TPU v7x, 32 devices: a whole 2x2x4 slice. The times are simulated.
32 devices in a mesh: dp: 8 (over z, y), head: 4 (over x, core).
Axes of the slice: x: 2, y: 2, z: 4, core: 2. Of those that a mesh axis runs over, the one named last changes fastest.
Arguments:
- block_input: bfloat16 [16384, 768], P(('dp', 'head')), may hold values from -6 to 6
- gain_one: float32 [768], replicated, may hold values from 0.5 to 1.5
- gain_two: float32 [768], replicated, may hold values from 0.5 to 1.5
- qkv_weight: float32 [3, 768, 768], P(None, 'dp', 'head'), may hold values from -0.3125 to 0.3125
- out_weight: float32 [768, 768], P('head', 'dp'), may hold values from -0.875 to 0.875
- gate_weight: float32 [768, 8], replicated, may hold values from -0.15625 to 0.15625
- frozen_in: float32 [8, 768, 1536], P('dp', None, 'head'), may hold values from -0.21875 to 0.21875
- frozen_out: float32 [8, 1536, 768], P('dp', 'head'), may hold values from -0.109375 to 0.109375
- fresh_in: float32 [8, 768, 1536], P('dp', None, 'head'), may hold values from -0.21875 to 0.21875
- fresh_out: float32 [8, 1536, 768], P('dp', 'head'), may hold values from -0.109375 to 0.109375
- routes: int32 [16384, 2], P('dp'), may hold values from 0 to 7, all different within a row; in each aligned block of 2048 rows (0 to 2047, 2048 to 4095, ...) at most 768 rows name the same one
- doc_lengths: int32 [8, 4], P('dp'), may hold values from 1 to 2045, as said below
- cotangent: bfloat16 [16384, 768], P(('dp', 'head')), may hold values from -6 to 6
Outputs:
- block_output: bfloat16 [16384, 768], P(('dp', 'head'))
- grad_input: float32 [16384, 768], P(('dp', 'head'))
- grad_gain_one: float32 [768], replicated
- grad_gain_two: float32 [768], replicated
- grad_qkv: float32 [3, 768, 768], P(None, 'dp', 'head')
- grad_out_weight: float32 [768, 768], P('head', 'dp')
- grad_gate: float32 [768, 8], replicated
- grad_fresh_in: float32 [8, 768, 1536], P('dp', None, 'head')
- grad_fresh_out: float32 [8, 1536, 768], P('dp', 'head')
Inputs may be any that keep to these rules, and one draw needn't show every extreme that they name: `routes`: in each aligned block of 2048 rows (the tokens of one group) every row names two different experts, no expert is named by more than 768 rows, a bound that some block reaches. `doc_lengths`: each row holds the lengths, in order, of the 4 documents of one group and sums to 2048; the second document begins within the group's first 512 tokens and ends within its last 512.
All inputs are finite; a program needn't handle non-finite values.
Results may differ from a plain program's by a relative error of at most 0.013.
The roundings to bfloat16 on the way count: a program that leaves them out, or rounds other values in their place, can miss the bound.
Values may be sent and summed in bfloat16 or wider, within the bound.
No kernel may reach another device: no remote copies, remote signals or barrier semaphores. Data moves between devices by JAX's collectives and lax.ppermute only.
A program may use at most 320 MiB of HBM per device.

v0:
```python
import jax
import jax.numpy as jnp
from jax import lax
from jax.sharding import PartitionSpec as P

HD = 64


EPS = 1e-05
MASKED = -1000000000.0
ROOT_HALF = 0.7071067811865476
INV_ROOT_TAU = 0.3989422804014327


def gelu_value(inputs):
    return 0.5 * inputs * (1.0 + lax.erf(inputs * ROOT_HALF))


def gelu_slope(inputs):
    return (
        0.5 * (1.0 + lax.erf(inputs * ROOT_HALF))
        + inputs * jnp.exp(-0.5 * inputs * inputs) * INV_ROOT_TAU
    )


def layer_norm(values, gain):
    centred = values - jnp.mean(values, axis=-1, keepdims=True)
    rstd = lax.rsqrt(jnp.mean(centred * centred, axis=-1, keepdims=True) + EPS)
    normed = centred * rstd
    return (normed * gain, normed, rstd)


def norm_back(grad_out, normed, rstd, gain):
    scaled = grad_out * gain
    mean_plain = jnp.mean(scaled, axis=-1, keepdims=True)
    mean_normed = jnp.mean(scaled * normed, axis=-1, keepdims=True)
    return (rstd * (scaled - mean_plain - normed * mean_normed), jnp.sum(grad_out * normed, axis=0))


def segment_ids(lengths, row_total):
    doc_ends = jnp.cumsum(lengths)
    places = jnp.arange(row_total, dtype=jnp.int32)
    return jnp.sum((places[:, None] >= doc_ends[None, :]).astype(jnp.int32), axis=1)


def slot_places(group_routes, expert_count, capacity):
    flat_ids = group_routes.reshape(-1)
    pair_count = expert_count // 2
    hit_table = (flat_ids[:, None] == jnp.arange(expert_count, dtype=jnp.int32)[None, :]).astype(
        jnp.int32
    )
    slot_index = jnp.sum((jnp.cumsum(hit_table, axis=0) - 1) * hit_table, axis=1)
    kind_index = flat_ids // pair_count
    places = (flat_ids % pair_count * 2 + kind_index) * capacity + slot_index
    route_total = flat_ids.shape[0]
    table = (
        jnp.full((expert_count * capacity,), route_total, jnp.int32)
        .at[places]
        .set(jnp.arange(route_total, dtype=jnp.int32))
    )
    return (places, table)


def block_scores(query_block, key_rows, segments, first_row, score_scale):
    row_count = query_block.shape[0]
    scores = (
        jnp.einsum("qhd,khd->hqk", query_block, key_rows, preferred_element_type=jnp.float32)
        * score_scale
    )
    seg_block = segments[first_row : first_row + row_count]
    pos_block = first_row + jnp.arange(row_count, dtype=jnp.int32)
    pos_keys = jnp.arange(key_rows.shape[0], dtype=jnp.int32)
    allowed = (seg_block[:, None] == segments[None, :]) & (pos_keys[None, :] <= pos_block[:, None])
    return jnp.where(allowed[None], scores, MASKED)


def group_rows(piece_rows):
    return lax.all_gather(piece_rows, "head", axis=0, tiled=True)


def project_rows(source, weight):
    return lax.psum_scatter(
        jnp.dot(source, weight, preferred_element_type=jnp.float32),
        "head",
        scatter_dimension=0,
        tiled=True,
    )


def to_experts(rows_by_pair):
    pair_count = rows_by_pair.shape[0]
    doubled = jnp.broadcast_to(rows_by_pair[:, None], (pair_count, 2) + rows_by_pair.shape[1:])
    return lax.all_to_all(
        doubled.reshape((2 * pair_count,) + rows_by_pair.shape[1:]),
        "dp",
        split_axis=0,
        concat_axis=0,
        tiled=True,
    )


def from_experts(pieces):
    source_count, capacity, feature_count = (pieces.shape[0], pieces.shape[2], pieces.shape[3])
    pair_count = source_count // 2
    returned = lax.all_to_all(pieces, "dp", split_axis=0, concat_axis=0, tiled=True)
    grouped = returned.reshape(pair_count, 2, 2, capacity, feature_count)
    summed = grouped[:, 0].astype(jnp.float32) + grouped[:, 1].astype(jnp.float32)
    return summed.reshape(pair_count * 2 * capacity, feature_count)


def body(
    block_input,
    gain_one,
    gain_two,
    qkv_weight,
    out_weight,
    gate_weight,
    frozen_in,
    frozen_out,
    fresh_in,
    fresh_out,
    routes,
    doc_lengths,
    cotangent,
):
    own_rows = block_input.shape[0]
    feature_count = block_input.shape[1]
    head_count = lax.axis_size("head")
    group_total = own_rows * head_count
    expert_count = gate_weight.shape[1]
    capacity = 3 * group_total // expert_count
    pair_count = expert_count // 2
    local_width = qkv_weight.shape[2]
    local_heads = local_width // HD
    block_rows = min(512, group_total)
    score_scale = HD ** (-0.5)
    head_index = lax.axis_index("head")
    qkv_full, out_full = (
        lax.all_gather(qkv_weight.astype(jnp.bfloat16), "dp", axis=1, tiled=True),
        lax.all_gather(out_weight.astype(jnp.bfloat16), "dp", axis=1, tiled=True),
    )
    inputs = block_input.astype(jnp.float32)
    ln_one, normed_one, rstd_one = layer_norm(inputs, gain_one)
    ln_one_rows = group_rows(ln_one.astype(jnp.bfloat16))
    projected = jnp.einsum(
        "rd,kdc->krc", ln_one_rows, qkv_full, preferred_element_type=jnp.float32
    ).astype(jnp.bfloat16)
    queries = projected[0].reshape(group_total, local_heads, HD)
    key_rows = projected[1].reshape(group_total, local_heads, HD)
    value_rows = projected[2].reshape(group_total, local_heads, HD)
    segments = segment_ids(doc_lengths[0], group_total)
    context_parts = []
    log_totals = []
    for block_start in range(0, group_total, block_rows):
        query_block = queries[block_start : block_start + block_rows]
        scores = block_scores(query_block, key_rows, segments, block_start, score_scale)
        row_max = jnp.max(scores, axis=-1, keepdims=True)
        raised = jnp.exp(scores - row_max)
        row_sum = jnp.sum(raised, axis=-1, keepdims=True)
        attn_probs = (raised / row_sum).astype(jnp.bfloat16)
        context_parts.append(
            jnp.einsum("hqk,khd->qhd", attn_probs, value_rows, preferred_element_type=jnp.float32)
        )
        log_totals.append(row_max + jnp.log(row_sum))
    context = (
        jnp.concatenate(context_parts, axis=0)
        .reshape(group_total, local_width)
        .astype(jnp.bfloat16)
    )
    attn_own = project_rows(context, out_full)
    x_one = inputs + attn_own
    ln_two, normed_two, rstd_two = layer_norm(x_one, gain_two)
    ln_two_low = ln_two.astype(jnp.bfloat16)
    gate_low = gate_weight.astype(jnp.bfloat16)
    logits = jnp.dot(ln_two_low, gate_low, preferred_element_type=jnp.float32)
    own_routes = lax.dynamic_slice_in_dim(routes, head_index * own_rows, own_rows, 0)
    route_hot = (
        own_routes[:, :, None] == jnp.arange(expert_count, dtype=jnp.int32)[None, None, :]
    ).astype(jnp.float32)
    chosen = jnp.sum(route_hot * logits[:, None, :], axis=-1)
    gate_max = jnp.max(chosen, axis=1, keepdims=True)
    gate_raised = jnp.exp(chosen - gate_max)
    gate_values = gate_raised / jnp.sum(gate_raised, axis=1, keepdims=True)
    ln_two_rows = group_rows(ln_two_low)
    places, table = slot_places(routes, expert_count, capacity)
    table_grid = table.reshape(pair_count, 2, capacity)
    padded_rows = jnp.concatenate(
        [ln_two_rows, jnp.zeros((1, feature_count), jnp.bfloat16)], axis=0
    )
    received = to_experts(padded_rows[table_grid // 2])
    first_pair = jnp.concatenate([frozen_in, fresh_in], axis=0).astype(jnp.bfloat16)
    second_pair = jnp.concatenate([frozen_out, fresh_out], axis=0).astype(jnp.bfloat16)
    first_use, second_use = (first_pair, second_pair)
    hidden = jnp.einsum("skcd,kdf->skcf", received, first_use, preferred_element_type=jnp.float32)
    activated = gelu_value(hidden).astype(jnp.bfloat16)
    expert_out = jnp.einsum(
        "skcf,kfd->skcd", activated, second_use, preferred_element_type=jnp.float32
    ).astype(jnp.bfloat16)
    combined = from_experts(expert_out)
    route_out = combined[places].reshape(group_total, 2, feature_count)
    own_out = lax.psum_scatter(route_out, "head", scatter_dimension=0, tiled=True)
    mixture = jnp.sum(gate_values[:, :, None] * own_out, axis=1)
    result = (x_one + mixture).astype(jnp.bfloat16)
    upstream = cotangent.astype(jnp.float32)
    gate_grads = jnp.sum(own_out * upstream[:, None, :], axis=-1)
    chosen_grads = gate_values * (
        gate_grads - jnp.sum(gate_values * gate_grads, axis=1, keepdims=True)
    )
    logit_grads = jnp.sum(chosen_grads[:, :, None] * route_hot, axis=1)
    route_grads_own = (gate_values[:, :, None] * upstream[:, None, :]).astype(jnp.bfloat16)
    route_grads_rows = lax.all_gather(route_grads_own, "head", axis=0, tiled=True)
    padded_grads = jnp.concatenate(
        [
            route_grads_rows.reshape(2 * group_total, feature_count),
            jnp.zeros((1, feature_count), jnp.bfloat16),
        ],
        axis=0,
    )
    grads_received = to_experts(padded_grads[table_grid])
    act_grads = jnp.einsum(
        "skcd,kfd->skcf", grads_received, second_use, preferred_element_type=jnp.float32
    )
    hidden_grads = (act_grads * gelu_slope(hidden)).astype(jnp.bfloat16)
    fresh_out_local = jnp.einsum(
        "scf,scd->fd", activated[:, 1], grads_received[:, 1], preferred_element_type=jnp.float32
    )
    fresh_in_local = jnp.einsum(
        "scd,scf->df", received[:, 1], hidden_grads[:, 1], preferred_element_type=jnp.float32
    )
    input_parts = jnp.einsum(
        "skcf,kdf->skcd", hidden_grads, first_use, preferred_element_type=jnp.float32
    ).astype(jnp.bfloat16)
    returned_rows = from_experts(input_parts)
    route_back = returned_rows[places].reshape(group_total, 2, feature_count)
    expert_back = lax.psum_scatter(
        jnp.sum(route_back, axis=1), "head", scatter_dimension=0, tiled=True
    )
    grad_fresh_in = fresh_in_local[None]
    grad_fresh_out = fresh_out_local[None]
    ln_two_grads = expert_back + jnp.dot(
        logit_grads, gate_low.astype(jnp.float32).T, precision=lax.Precision.HIGHEST
    )
    grad_gate = jnp.dot(
        ln_two_low.astype(jnp.float32).T, logit_grads, precision=lax.Precision.HIGHEST
    )
    x_one_back, grad_gain_two = norm_back(ln_two_grads, normed_two, rstd_two, gain_two)
    x_one_grads = upstream + x_one_back
    attn_rows_grads = group_rows(x_one_grads.astype(jnp.bfloat16))
    context_grads = (
        jnp.einsum("rd,cd->rc", attn_rows_grads, out_full, preferred_element_type=jnp.float32)
        .astype(jnp.bfloat16)
        .reshape(group_total, local_heads, HD)
    )
    grad_out_local = jnp.einsum(
        "rc,rd->cd", context, attn_rows_grads, preferred_element_type=jnp.float32
    )
    query_parts = []
    key_grads = jnp.zeros((group_total, local_heads, HD), jnp.float32)
    value_grads = jnp.zeros((group_total, local_heads, HD), jnp.float32)
    for block_index, block_start in enumerate(range(0, group_total, block_rows)):
        query_block = queries[block_start : block_start + block_rows]
        scores = block_scores(query_block, key_rows, segments, block_start, score_scale)
        attn_probs = jnp.exp(scores - log_totals[block_index])
        grad_block = context_grads[block_start : block_start + block_rows]
        prob_grads = jnp.einsum(
            "qhd,khd->hqk", grad_block, value_rows, preferred_element_type=jnp.float32
        )
        value_grads = value_grads + jnp.einsum(
            "hqk,qhd->khd",
            attn_probs.astype(jnp.bfloat16),
            grad_block,
            preferred_element_type=jnp.float32,
        )
        row_delta = jnp.sum(attn_probs * prob_grads, axis=-1, keepdims=True)
        score_grads = (attn_probs * (prob_grads - row_delta)).astype(jnp.bfloat16)
        query_parts.append(
            jnp.einsum("hqk,khd->qhd", score_grads, key_rows, preferred_element_type=jnp.float32)
            * score_scale
        )
        key_grads = (
            key_grads
            + jnp.einsum(
                "hqk,qhd->khd", score_grads, query_block, preferred_element_type=jnp.float32
            )
            * score_scale
        )
    query_grads = jnp.concatenate(query_parts, axis=0).astype(jnp.bfloat16)
    qkv_grads = jnp.stack(
        [query_grads, key_grads.astype(jnp.bfloat16), value_grads.astype(jnp.bfloat16)], axis=0
    ).reshape(3, group_total, local_width)
    grad_qkv_local = jnp.einsum(
        "rd,krc->kdc", ln_one_rows, qkv_grads, preferred_element_type=jnp.float32
    )
    stacked_source = qkv_grads.transpose(1, 0, 2).reshape(group_total, 3 * local_width)
    back_weight = qkv_full.transpose(0, 2, 1).reshape(3 * local_width, feature_count)
    ln_one_grads = project_rows(stacked_source, back_weight)
    input_back, grad_gain_one = norm_back(ln_one_grads, normed_one, rstd_one, gain_one)
    grad_input = x_one_grads + input_back
    grad_qkv, grad_out_weight = (
        lax.psum_scatter(grad_qkv_local, "dp", scatter_dimension=1, tiled=True),
        lax.psum_scatter(grad_out_local, "dp", scatter_dimension=1, tiled=True),
    )
    grad_gain_one, grad_gain_two, grad_gate = lax.psum(
        (grad_gain_one, grad_gain_two, grad_gate), ("dp", "head")
    )
    return (
        result,
        grad_input,
        grad_gain_one,
        grad_gain_two,
        grad_qkv,
        grad_out_weight,
        grad_gate,
        grad_fresh_in,
        grad_fresh_out,
    )


def solution(mesh):
    return jax.shard_map(
        body,
        mesh=mesh,
        in_specs=(
            P(("dp", "head"), None),
            P(),
            P(),
            P(None, "dp", "head"),
            P("head", "dp"),
            P(),
            P("dp", None, "head"),
            P("dp", "head", None),
            P("dp", None, "head"),
            P("dp", "head", None),
            P("dp", None),
            P("dp", None),
            P(("dp", "head"), None),
        ),
        out_specs=(
            P(("dp", "head"), None),
            P(("dp", "head"), None),
            P(),
            P(),
            P(None, "dp", "head"),
            P("head", "dp"),
            P(),
            P("dp", None, "head"),
            P("dp", "head", None),
        ),
        check_vma=False,
    )
```

profile of v0, /device:TPU:0, one launch (start us, length us, event | category | flops | bytes accessed | tf_op | source)
XLA Modules:
  0.0 2999.4 jit_solution(12216054860415370483)
XLA Ops:
  15.2 38.6 %all_gather.19 = bf16[3,768,192]{2,0,1:T(4,128)(2,1)S(1)} all-gather(bf16[3,96,192]{2,0,1:T(4,128)(2,1)S(1)} %copy.148), channel_id=1, replica_groups=mesh['dp'=8,'head'=4] {'dp'}, dimensions={1}, use_global_device_ids=true | all-gather | bytes 995328 | tf_op jit(solution)/shard_map/all_gather | solution.py:139
  56.1 31.0 %all_gather.20 = bf16[192,768]{0,1:T(8,128)(2,1)S(1)} all-gather(bf16[192,96]{0,1:T(8,128)(2,1)S(1)} %copy.150), channel_id=1, replica_groups=mesh['dp'=8,'head'=4] {'dp'}, dimensions={1}, use_global_device_ids=true | all-gather | bytes 331776 | tf_op jit(solution)/shard_map/all_gather | solution.py:140
  87.1 4.9 fusion.38
  92.0 4.1 fusion.119
  140.1 3.7 fusion.120
  143.9 57.9 %reduce-scatter.10.cloned.1.call-done = f32[512,768]{1,0:T(8,128)} async-done(((f32[2048,768]{1,0:T(8,128)}), f32[512,768]{1,0:T(8,128)}) %reduce-scatter.10.cloned.1.call-update) | async-done | bytes 1572880 | tf_op jit(solution)/shard_map/reduce_scatter | solution.py:82
  211.5 15.5 scatter_custom_fusion
  227.8 7.2 all-gather.7.cloned.1.call-done
  237.2 26.1 gather_fusion
  263.3 12.5 broadcast_in_dim.62
  275.8 6.6 all-to-all-start
  285.8 405.0 %all-to-all-done = bf16[8,2,768,768]{3,2,1,0:T(8,128)(2,1)} async-done(((bf16[8,2,768,768]{3,2,1,0:T(8,128)(2,1)}), bf16[8,2,768,768]{3,2,1,0:T(8,128)(2,1)}, u32[]{:S(2)}, u32[]{:S(2)}) %all-to-all-start) | async-done | bytes 18874400 | tf_op jit(solution)/shard_map/all_to_all | solution.py:93
  690.8 18.3 fusion.7
  709.2 16.7 convert_bitcast_fusion.1
  725.8 16.9 copy.161
  742.7 5.9 all-to-all-start.1
  748.7 407.6 %all-to-all-done.1 = bf16[8,2,768,768]{2,3,1,0:T(8,128)(2,1)} async-done(((bf16[8,2,768,768]{2,3,1,0:T(8,128)(2,1)}), bf16[8,2,768,768]{2,3,1,0:T(8,128)(2,1)}, u32[]{:S(2)}, u32[]{:S(2)}) %all-to-all-start.1) | async-done | bytes 18874400 | tf_op jit(solution)/shard_map/all_to_all | solution.py:105
  1156.3 14.0 fusion.110
  1170.3 12.6 copy.194
  1182.9 12.6 copy.195
  1195.6 12.7 convert_add_fusion.1
  1208.3 26.6 gather_fusion.1
  1234.9 15.1 reshape.774
  1254.3 214.6 %all-reduce.6.cloned.1.call-done = f32[2048,2,768]{2,1,0:T(2,128)} async-done(((f32[2048,2,768]{2,1,0:T(2,128)}), f32[2048,2,768]{2,1,0:T(2,128)}) %all-reduce.6.cloned.1.call-update) | async-done | bytes 12582928
  1469.0 12.6 multiply_reduce_fusion.4
  1481.6 46.6 %all-gather.9.cloned.1.call-done = bf16[2048,2,768]{2,1,0:T(2,128)(2,1)} async-done(((bf16[512,2,768]{2,1,0:T(2,128)(2,1)}), bf16[2048,2,768]{2,1,0:T(2,128)(2,1)}) %all-gather.9.cloned.1.call-update) | async-done | bytes 6291472 | tf_op jit(solution)/shard_map/all_gather | solution.py:211
  1528.3 13.8 reshape.775
  1542.0 5.8 concatenate.43
  1547.8 31.7 %gather_fusion.2 = bf16[6144,768]{1,0:T(8,128)(2,1)} fusion(bf16[4097,768]{1,0:T(8,128)(2,1)} %concatenate.43, s32[6144]{0:T(1024)S(1)} %broadcast_clamp_fusion), kind=kCustom, calls=%fused_computation.2 | custom fusion | bytes 18898944 | tf_op jit(solution)/shard_map/gather | solution.py:219
  1579.5 7.6 broadcast_in_dim.63
  1587.2 413.9 %all_to_all.20 = bf16[8,2,768,768]{3,2,1,0:T(8,128)(2,1)} all-to-all(bf16[8,2,768,768]{3,2,1,0:T(8,128)(2,1)S(1)} %bitcast.238), channel_id=1, replica_groups=mesh['dp'=8,'head'=4] {'dp'}, dimensions={0} | all-to-all | bytes 37748736 | tf_op jit(solution)/shard_map/all_to_all | solution.py:93
  2001.1 20.5 fusion.5
  2021.6 16.8 convert_bitcast_fusion
  2038.4 17.0 copy.168
  2055.4 413.0 %all_to_all.21 = bf16[8,2,768,768]{2,3,1,0:T(8,128)(2,1)S(1)} all-to-all(bf16[8,2,768,768]{2,3,1,0:T(8,128)(2,1)} %copy.168), channel_id=1, replica_groups=mesh['dp'=8,'head'=4] {'dp'}, dimensions={0} | all-to-all | bytes 37748736 | tf_op jit(solution)/shard_map/all_to_all | solution.py:105
  2468.4 6.7 fusion.109
  2475.1 12.6 copy.196
  2487.8 12.6 copy.197
  2500.4 12.7 convert_add_fusion
  2513.1 26.6 gather_fusion.3
  2539.7 15.1 reshape.778
  2554.8 36.4 %reduce_sum.259 = f32[2048,768]{1,0:T(8,128)} reduce(f32[2048,2,768]{2,1,0:T(2,128)} %reshape.778, f32[]{:T(128)} %constant.48.clone.1), dimensions={1}, to_apply=%region_24.25 | reduce | flops 1572864 | bytes 18874372 | tf_op jit(solution)/shard_map/reduce_sum | solution.py:236
  2592.4 54.8 %reduce-scatter.12.cloned.1.call-done = f32[512,768]{1,0:T(8,128)} async-done(((f32[2048,768]{1,0:T(8,128)}), f32[512,768]{1,0:T(8,128)}) %reduce-scatter.12.cloned.1.call-update) | async-done | bytes 1572880 | tf_op jit(solution)/shard_map/reduce_scatter | solution.py:235
  2650.6 3.8 fusion.107
  2657.4 25.8 all-gather.11.cloned.1.call-done
  2686.3 19.7 multiply_reduce_fusion.3
  2706.1 9.6 multiply_convert_fusion.3
  2715.7 5.0 fusion.77
  2726.4 6.6 multiply_reduce_fusion.2
  2733.0 3.3 fusion.24
  2736.3 6.6 multiply_reduce_fusion.1
  2746.2 6.2 multiply_reduce_fusion
  2754.8 10.4 multiply_convert_fusion.2
  2768.6 10.2 multiply_convert_fusion.1
  2778.9 5.4 convolution_add_fusion.1
  2784.3 10.1 multiply_convert_fusion
  2794.5 4.6 fusion.57
  2807.4 3.3 fusion.72
  2816.5 7.1 convolution_bitcast_fusion
  2825.2 10.1 fusion.75
  2835.3 10.2 fusion.76
  2847.2 40.0 %reduce-scatter.16.cloned.1.call-done = f32[96,576]{1,0:T(8,128)} async-done(((f32[768,576]{1,0:T(8,128)}), f32[96,576]{1,0:T(8,128)}) %reduce-scatter.16.cloned.1.call-update) | async-done | bytes 221200
  2889.1 57.8 %reduce-scatter.14.cloned.1.call-done = f32[512,768]{1,0:T(8,128)} async-done(((f32[2048,768]{1,0:T(8,128)}), f32[512,768]{1,0:T(8,128)}) %reduce-scatter.14.cloned.1.call-update) | async-done | bytes 1572880 | tf_op jit(solution)/shard_map/reduce_scatter | solution.py:82
  2949.0 40.3 %all-reduce.3 = (f32[768]{0:T(1024)}, f32[768]{0:T(1024)}, f32[768,8]{0,1:T(8,128)}) all-reduce(f32[768]{0:T(1024)S(1)} %get-tuple-element.67, f32[768]{0:T(1024)S(1)} %copy-done.86, f32[768,8]{0,1:T(8,128)S(1)} %fusion.122), channel_id=1, replica_groups=mesh['dp'=8,'head'=4] {'dp','head'}, use_global_device_ids=true, to_apply=%region_39.40 | all-reduce | flops 7680 | bytes 61440 | tf_op jit(solution)/shard_map/psum | solution.py:303
  (355 shorter events, 122.9 us)
Async XLA Ops:
  7.2 48.7 %copy-start.88 = (s32[1,4]{1,0:T(1,128)S(1)}, s32[1,4]{1,0:T(1,128)}, u32[]{:S(2)}) copy-start(s32[1,4]{1,0:T(1,128)} %param.24) | copy-start | bytes 52
  7.2 84.8 %all-gather.5.cloned.1.call-start = ((), (), s32[]{:S(2)}) async-start(), calls=%async_computation.9 | async-start | bytes 3932160 | tf_op jit(solution)/shard_map/all_gather | solution.py:78
  13.0 188.8 %reduce-scatter.10.cloned.1.call-start = ((), (), s32[]{:S(2)}) async-start(), calls=%async_computation.10 | async-start | bytes 7864320 | tf_op jit(solution)/shard_map/reduce_scatter | solution.py:82
  87.1 52.1 %copy-start.23 = (bf16[192,768]{0,1:T(8,128)(2,1)}, bf16[192,768]{0,1:T(8,128)(2,1)S(1)}, u32[]{:S(2)}) copy-start(bf16[192,768]{0,1:T(8,128)(2,1)S(1)} %all_gather.20) | copy-start | bytes 884740
  96.6 11.3 copy-start.42
  96.6 21.6 copy-start.38
  96.6 32.1 %copy-start.40 = (bf16[1,512,192]{1,2,0:T(8,128)(2,1)}, bf16[1,512,192]{1,2,0:T(8,128)(2,1)S(1)}, u32[]{:S(2)}) copy-start(bf16[1,512,192]{1,2,0:T(8,128)(2,1)S(1)} %get-tuple-element.85) | copy-start | bytes 589828
  96.8 32.0 %copy-start.12 = (bf16[1,2048,192]{1,2,0:T(8,128)(2,1)}, bf16[1,2048,192]{1,2,0:T(8,128)(2,1)S(1)}, u32[]{:S(2)}) copy-start(bf16[1,2048,192]{1,2,0:T(8,128)(2,1)S(1)} %get-tuple-element.86) | copy-start | bytes 2359300
  96.8 36.6 %copy-start.8 = (bf16[1,2048,192]{1,2,0:T(8,128)(2,1)}, bf16[1,2048,192]{1,2,0:T(8,128)(2,1)S(1)}, u32[]{:S(2)}) copy-start(bf16[1,2048,192]{1,2,0:T(8,128)(2,1)S(1)} %get-tuple-element.87) | copy-start | bytes 2359300
  140.1 61.7 %copy-start.10 = (bf16[512,768]{1,0:T(8,128)(2,1)S(1)}, bf16[512,768]{1,0:T(8,128)(2,1)}, u32[]{:S(2)}) copy-start(bf16[512,768]{1,0:T(8,128)(2,1)} %param.13) | copy-start | bytes 2359300
  143.8 61.4 %copy-start.66 = (f32[768]{0:T(1024)S(1)}, f32[768]{0:T(1024)}, u32[]{:S(2)}) copy-start(f32[768]{0:T(1024)} %param.15) | copy-start | bytes 9220
  143.8 62.5 %copy-start.85 = (s32[2048,2]{0,1:T(2,128)S(1)}, s32[2048,2]{0,1:T(2,128)}, u32[]{:S(2)}) copy-start(s32[2048,2]{0,1:T(2,128)} %param.23) | copy-start | bytes 49156
  143.9 91.2 %all-gather.7.cloned.1.call-start = ((), (), s32[]{:S(2)}) async-start(), calls=%async_computation.11 | async-start | bytes 3932160 | tf_op jit(solution)/shard_map/all_gather | solution.py:78
  275.8 415.0 %all-to-all-start = ((bf16[8,2,768,768]{3,2,1,0:T(8,128)(2,1)}), bf16[8,2,768,768]{3,2,1,0:T(8,128)(2,1)}, u32[]{:S(2)}, u32[]{:S(2)}) async-start(bf16[8,2,768,768]{3,2,1,0:T(8,128)(2,1)} %bitcast.236), calls=%async_computation.1 | async-start | bytes 37748736 | tf_op jit(solution)/shard_map/all_to_all | solution.py:93
  283.8 425.4 %copy-start.47 = (bf16[1,384,768]{1,2,0:T(8,128)(2,1)}, bf16[1,384,768]{1,2,0:T(8,128)(2,1)S(1)}, u32[]{:S(2)}) copy-start(bf16[1,384,768]{1,2,0:T(8,128)(2,1)S(1)} %copy.152) | copy-start | bytes 1769476
  284.0 425.1 %copy-start.45 = (bf16[1,768,384]{1,2,0:T(8,128)(2,1)}, bf16[1,768,384]{1,2,0:T(8,128)(2,1)S(1)}, u32[]{:S(2)}) copy-start(bf16[1,768,384]{1,2,0:T(8,128)(2,1)S(1)} %copy.155) | copy-start | bytes 1769476
  285.8 423.3 %copy-start.49 = (bf16[1,384,768]{1,2,0:T(8,128)(2,1)}, bf16[1,384,768]{1,2,0:T(8,128)(2,1)S(1)}, u32[]{:S(2)}) copy-start(bf16[1,384,768]{1,2,0:T(8,128)(2,1)S(1)} %copy.153) | copy-start | bytes 1769476
  742.7 413.6 %all-to-all-start.1 = ((bf16[8,2,768,768]{2,3,1,0:T(8,128)(2,1)}), bf16[8,2,768,768]{2,3,1,0:T(8,128)(2,1)}, u32[]{:S(2)}, u32[]{:S(2)}) async-start(bf16[8,2,768,768]{2,3,1,0:T(8,128)(2,1)} %copy.161), calls=%async_computation.2 | async-start | bytes 37748736 | tf_op jit(solution)/shard_map/all_to_all | solution.py:105
  748.6 720.3 %all-reduce.6.cloned.1.call-start = ((), (), s32[]{:S(2)}) async-start(), calls=%async_computation.18 | async-start | bytes 25165824
  748.7 459.6 %copy-start.55 = (s32[4096]{0:T(1024)}, s32[4096]{0:T(1024)S(1)}, u32[]{:S(2)}) copy-start(s32[4096]{0:T(1024)S(1)} %broadcast_clamp_fusion.2) | copy-start | bytes 49156
  1250.0 278.3 %all-gather.9.cloned.1.call-start = ((), (), s32[]{:S(2)}) async-start(), calls=%async_computation.12 | async-start | bytes 7864320 | tf_op jit(solution)/shard_map/all_gather | solution.py:211
  1251.1 230.5 %copy-start.59 = (s32[4,2,768,1]{2,1,0,3:T(2,128)S(1)}, s32[4,2,768,1]{2,1,0,3:T(2,128)}, u32[]{:S(2)}) copy-start(s32[4,2,768,1]{2,1,0,3:T(2,128)} %get-tuple-element.94) | copy-start | bytes 73732
  1253.2 288.8 %copy-start.69 = (s32[512,2]{0,1:T(2,128)}, s32[512,2]{0,1:T(2,128)S(1)}, u32[]{:S(2)}) copy-start(s32[512,2]{0,1:T(2,128)S(1)} %constant_dynamic-slice_fusion) | copy-start | bytes 12292
  1254.2 287.9 %copy-start.83 = (f32[512]{0:T(512)}, f32[512]{0:T(512)S(1)}, u32[]{:S(2)}) copy-start(f32[512]{0:T(512)S(1)} %fusion.101) | copy-start | bytes 6148
  1481.5 1165.7 %reduce-scatter.12.cloned.1.call-start = ((), (), s32[]{:S(2)}) async-start(), calls=%async_computation.13 | async-start | bytes 7864320 | tf_op jit(solution)/shard_map/reduce_scatter | solution.py:235
  1587.1 413.9 %copy-start.48 = (bf16[1,384,768]{1,2,0:T(8,128)(2,1)S(1)}, bf16[1,384,768]{1,2,0:T(8,128)(2,1)}, u32[]{:S(2)}) copy-start(bf16[1,384,768]{1,2,0:T(8,128)(2,1)} %copy-done.47) | copy-start | bytes 1769476
  1587.2 413.9 %copy-start.50 = (bf16[1,384,768]{1,2,0:T(8,128)(2,1)S(1)}, bf16[1,384,768]{1,2,0:T(8,128)(2,1)}, u32[]{:S(2)}) copy-start(bf16[1,384,768]{1,2,0:T(8,128)(2,1)} %copy-done.49) | copy-start | bytes 1769476
  2001.1 20.5 copy-start.44
  2001.1 20.5 copy-start.46
  2500.4 12.7 copy-start.56
  2591.3 56.0 %copy-start.7 = (f32[512,768]{1,0:T(8,128)S(1)}, f32[512,768]{1,0:T(8,128)}, u32[]{:S(2)}) copy-start(f32[512,768]{1,0:T(8,128)} %copy-done.6) | copy-start | bytes 4718596
  2591.3 56.0 %copy-start.58 = (f32[768,8]{0,1:T(8,128)S(1)}, f32[768,8]{0,1:T(8,128)}, u32[]{:S(2)}) copy-start(f32[768,8]{0,1:T(8,128)} %param.18) | copy-start | bytes 73732
  2591.3 56.0 %copy-start.63 = (f32[512]{0:T(512)S(1)}, f32[512]{0:T(512)}, u32[]{:S(2)}) copy-start(f32[512]{0:T(512)} %copy-done.62) | copy-start | bytes 6148
  2591.3 56.0 %copy-start.67 = (f32[768]{0:T(1024)S(1)}, f32[768]{0:T(1024)}, u32[]{:S(2)}) copy-start(f32[768]{0:T(1024)} %param.15) | copy-start | bytes 9220
  2591.3 56.0 %copy-start.74 = (f32[512]{0:T(512)S(1)}, f32[512]{0:T(512)}, u32[]{:S(2)}) copy-start(f32[512]{0:T(512)} %copy-done.73) | copy-start | bytes 6148
  2591.3 59.3 %copy-start.26 = (bf16[512,768]{1,0:T(8,128)(2,1)S(1)}, bf16[512,768]{1,0:T(8,128)(2,1)}, u32[]{:S(2)}) copy-start(bf16[512,768]{1,0:T(8,128)(2,1)} %param.25) | copy-start | bytes 2359300
  2591.4 91.8 %all-gather.11.cloned.1.call-start = ((), (), s32[]{:S(2)}) async-start(), calls=%async_computation.14 | async-start | bytes 3932160 | tf_op jit(solution)/shard_map/all_gather | solution.py:78
  2592.4 90.8 %copy-start.24 = (bf16[192,768]{0,1:T(8,128)(2,1)S(1)}, bf16[192,768]{0,1:T(8,128)(2,1)}, u32[]{:S(2)}) copy-start(bf16[192,768]{0,1:T(8,128)(2,1)} %copy-done.23) | copy-start | bytes 884740
  2650.6 35.7 %copy-start.9 = (bf16[1,2048,192]{1,2,0:T(8,128)(2,1)S(1)}, bf16[1,2048,192]{1,2,0:T(8,128)(2,1)}, u32[]{:S(2)}) copy-start(bf16[1,2048,192]{1,2,0:T(8,128)(2,1)} %copy-done.8) | copy-start | bytes 2359300
  2654.4 191.1 %reduce-scatter.18.cloned.1.call-start = ((), (), s32[]{:S(2)}) async-start(), calls=%async_computation.17 | async-start | bytes 884736
  2686.3 19.8 slice-start.15
  2686.3 19.7 slice-start.16
  2686.3 19.7 slice-start.17
  2686.3 36.7 %slice-start.12 = ((s8[12582912]{0:T(1024)(128)(4,1)}), s8[4194304]{0:T(1024)(128)(4,1)S(1)}, s32[]{:S(2)}) async-start(s8[12582912]{0:T(1024)(128)(4,1)} %bitcast.230), calls=%async_computation.31 | async-start | bytes 8388608
  2686.3 36.7 %slice-start.13 = ((s8[12582912]{0:T(1024)(128)(4,1)}), s8[4194304]{0:T(1024)(128)(4,1)S(1)}, s32[]{:S(2)}) async-start(s8[12582912]{0:T(1024)(128)(4,1)} %bitcast.230), calls=%async_computation.32 | async-start | bytes 8388608
  2706.1 17.0 slice-start.14
  2754.7 132.5 %reduce-scatter.16.cloned.1.call-start = ((), (), s32[]{:S(2)}) async-start(), calls=%async_computation.16 | async-start | bytes 2211840
  2754.8 13.8 slice-start.9
  2754.8 13.8 slice-start.10
  2768.5 15.7 slice-start.3
  2768.6 10.3 copy-start.39
  2768.6 15.7 slice-start.4
  2768.6 15.7 slice-start.5
  2778.9 20.3 slice-start.18
  2784.3 14.8 slice-start.19
  2784.3 14.8 slice-start.20
  2784.3 14.8 copy-start.18
  2816.5 130.4 %reduce-scatter.14.cloned.1.call-start = ((), (), s32[]{:S(2)}) async-start(), calls=%async_computation.15 | async-start | bytes 7864320 | tf_op jit(solution)/shard_map/reduce_scatter | solution.py:82
  2835.3 111.6 %copy-start.11 = (bf16[512,768]{1,0:T(8,128)(2,1)S(1)}, bf16[512,768]{1,0:T(8,128)(2,1)}, u32[]{:S(2)}) copy-start(bf16[512,768]{1,0:T(8,128)(2,1)} %param.13) | copy-start | bytes 2359300
  2835.3 111.6 %copy-start.61 = (f32[512]{0:T(512)S(1)}, f32[512]{0:T(512)}, u32[]{:S(2)}) copy-start(f32[512]{0:T(512)} %copy-done.60) | copy-start | bytes 6148
  2835.3 111.6 %copy-start.68 = (f32[768]{0:T(1024)S(1)}, f32[768]{0:T(1024)}, u32[]{:S(2)}) copy-start(f32[768]{0:T(1024)} %param.14) | copy-start | bytes 9220
  2835.3 111.6 %copy-start.72 = (f32[512]{0:T(512)S(1)}, f32[512]{0:T(512)}, u32[]{:S(2)}) copy-start(f32[512]{0:T(512)} %copy-done.71) | copy-start | bytes 6148
  2835.3 113.7 %copy-start.86 = (f32[768]{0:T(1024)S(1)}, f32[768]{0:T(1024)}, u32[]{:S(2)}) copy-start(f32[768]{0:T(1024)} %get-tuple-element.65) | copy-start | bytes 9220
  2835.3 154.0 %copy-start.19 = (f32[512,768]{1,0:T(8,128)S(1)}, f32[512,768]{1,0:T(8,128)}, u32[]{:S(2)}) copy-start(f32[512,768]{1,0:T(8,128)} %get-tuple-element.75) | copy-start | bytes 4718596
  (61 other events, 243.2 us)
Sparse Core Ops, SparseCore 0:
  13.1 31.2 all-gather.4
  144.0 57.7 reduce-scatter.9
  206.5 28.5 all-gather.6
  1250.1 218.7 all-reduce.5
  1481.7 46.5 all-gather.8
  2591.5 55.7 reduce-scatter.11
  2654.6 28.5 all-gather.10
  2754.8 62.5 reduce-scatter.17
  2821.3 65.8 reduce-scatter.15
  2889.6 57.2 reduce-scatter.13
where the time goes:
time: 3010 us; the launch traced here: 3000 us
  waiting for transfers between devices  1320 us (44%)
  blocking collectives  937 us (31%)
  local copies, waits for them, and re-layouts  343 us (11%)
  matrix products  220 us (7%)
  other arithmetic  153 us (5%)
    all_to_all x1, blocking collectives, to_experts(): lax.all_to_all(doubled.reshape((2 * pair_count,) + rows_by_pair.shape[1:]...  414 us
    all_to_all x1, blocking collectives, from_experts(): lax.all_to_all(pieces, 'dp', split_axis=0, concat_axis=0, tiled=True)  413 us
    all_to_all x1, waiting for transfers between devices, from_experts(): lax.all_to_all(pieces, 'dp', split_axis=0, concat_axis=0, tiled=True)  408 us
    all_to_all x1, waiting for transfers between devices, to_experts(): lax.all_to_all(doubled.reshape((2 * pair_count,) + rows_by_pair.shape[1:]...  405 us
    unnamed x13, waiting for transfers between devices  255 us
    reduce_scatter x2, waiting for transfers between devices, project_rows(): lax.psum_scatter(jnp.dot(source, weight, preferred_element_type=jnp.float...  116 us
    unnamed x242, local copies, waits for them, and re-layouts  84.8 us
  transfers between devices with their start and end apart: 12, of which 10 were waited for; matrix products, arithmetic and copies ran while one was open for 4% of the time, Pallas kernels for 0%

commit v1 on v0

v1 whole, which is shorter than its diff:
```python
import functools

import jax
import jax.numpy as jnp
from jax import lax
from jax.experimental import pallas as pl
from jax.experimental.pallas import tpu as pltpu
from jax.sharding import PartitionSpec as P

HD = 64
EPS = 1e-05
MASKED = -1000000000.0
ROOT_HALF = 0.7071067811865476
INV_ROOT_TAU = 0.3989422804014327
BLOCK = 256
LOW = jnp.bfloat16
WIDE = jnp.float32
NT = (((1,), (1,)), ((), ()))
TN = (((0,), (0,)), ((), ()))


def mm(a, b):
    return jnp.dot(a, b, preferred_element_type=WIDE)


def mm_nt(a, b):
    return lax.dot_general(a, b, NT, preferred_element_type=WIDE)


def mm_tn(a, b):
    return lax.dot_general(a, b, TN, preferred_element_type=WIDE)


def flip(array, axis, bits):
    size = lax.axis_size(axis)
    return lax.ppermute(array, axis, [(i, i ^ bits) for i in range(size)])


def norm_parts(values):
    centred = values - jnp.mean(values, axis=-1, keepdims=True)
    rstd = lax.rsqrt(jnp.mean(centred * centred, axis=-1, keepdims=True) + EPS)
    return centred * rstd, rstd


def norm_back(grad_out, normed, rstd, gain):
    scaled = grad_out * gain
    mean_plain = jnp.mean(scaled, axis=-1, keepdims=True)
    mean_normed = jnp.mean(scaled * normed, axis=-1, keepdims=True)
    return rstd * (scaled - mean_plain - normed * mean_normed)


def head_pieces(piece):
    far = flip(piece, "head", 2)
    near = flip(piece, "head", 1)
    return [piece, near, far, flip(far, "head", 1)]


def in_order(pieces, index):
    rows = pieces[0].shape[0]
    out = jnp.zeros((rows * len(pieces),) + pieces[0].shape[1:], pieces[0].dtype)
    for k, piece in enumerate(pieces):
        out = lax.dynamic_update_slice_in_dim(out, piece, (index ^ k) * rows, 0)
    return out


def over_dp(piece, axis):
    size, index = lax.axis_size("dp"), lax.axis_index("dp")
    bits, span, width = size // 2, 1, piece.shape[axis]
    held = {0: piece}
    while bits:
        joined = flip(jnp.stack(list(held.values())), "dp", bits)
        held.update({k ^ bits: joined[n] for n, k in enumerate(list(held))})
        bits //= 2
    shape = list(piece.shape)
    shape[axis] *= size
    out = jnp.zeros(shape, piece.dtype)
    for k, one in held.items():
        out = lax.dynamic_update_slice_in_dim(out, one, (index ^ k) * width, axis)
    return out


def sum_everywhere(value):
    for axis in ("head", "dp"):
        bits = 1
        while bits < lax.axis_size(axis):
            value = value + flip(value, axis, bits)
            bits *= 2
    return value


def sum_over_dp_scattered(value, axis):
    size, index = lax.axis_size("dp"), lax.axis_index("dp")
    width = value.shape[axis] // size
    held = {
        k: lax.dynamic_slice_in_dim(value, (index ^ k) * width, width, axis) for k in range(size)
    }
    bits = 1
    while bits < size:
        keep = [k for k in held if not k & bits]
        come = flip(jnp.stack([held[k ^ bits].astype(LOW) for k in keep]), "dp", bits)
        held = {k: held[k] + come[n].astype(WIDE) for n, k in enumerate(keep)}
        bits *= 2
    return held[0]


def sum_over_head(partial):
    near = lax.axis_index("head") % 2
    half = partial.shape[0] // 2
    mine = lax.dynamic_slice_in_dim(partial, near * half, half, 0)
    other = lax.dynamic_slice_in_dim(partial, (1 - near) * half, half, 0)
    mine = (mine + flip(other.astype(LOW), "head", 1).astype(WIDE)).astype(LOW)
    mine = mine.astype(WIDE) + flip(mine, "head", 2).astype(WIDE)
    mine = mine.astype(LOW)
    back = flip(mine, "head", 1)
    return jnp.concatenate(
        [jnp.where(near == 0, mine, back), jnp.where(near == 0, back, mine)], axis=0
    ).astype(WIDE)


def own_sum_over_head(partial):
    index, size = lax.axis_index("head"), lax.axis_size("head")
    rows = partial.shape[0] // size
    cut = [lax.dynamic_slice_in_dim(partial, (index ^ k) * rows, rows, 0) for k in range(size)]
    come = flip(jnp.stack([cut[1], cut[3]]).astype(LOW), "head", 1).astype(WIDE)
    far = flip((cut[2] + come[1]).astype(LOW), "head", 2).astype(WIDE)
    return cut[0] + come[0] + far


def attend_kernel(first_ref, start_ref, qt_ref, k_ref, vt_ref, ctx_ref, ctxt_ref, lse_ref):
    step = pl.program_id(0)
    heads = qt_ref.shape[0]
    start = start_ref[...]
    key_iota = lax.broadcasted_iota(jnp.int32, (BLOCK, BLOCK), 0)
    query_iota = lax.broadcasted_iota(jnp.int32, (BLOCK, BLOCK), 1)

    def block(j, carry, last):
        base = pl.multiple_of(j * BLOCK, BLOCK)
        allowed = key_iota + base >= start
        if last:
            allowed = allowed & (key_iota <= query_iota)
        out = []
        for h in range(heads):
            top, total, acc = carry[h]
            scores = mm(k_ref[h, pl.ds(base, BLOCK), :], qt_ref[h])
            scores = jnp.where(allowed, scores, MASKED)
            peak = jnp.maximum(top, jnp.max(scores, axis=0, keepdims=True))
            raised = jnp.exp(scores - peak)
            fade = jnp.exp(top - peak)
            total = total * fade + jnp.sum(raised, axis=0, keepdims=True)
            acc = acc * fade + mm(vt_ref[h, :, pl.ds(base, BLOCK)], raised.astype(LOW))
            out.append((peak, total, acc))
        return tuple(out)

    carry = tuple(
        (
            jnp.full((1, BLOCK), MASKED, WIDE),
            jnp.zeros((1, BLOCK), WIDE),
            jnp.zeros((HD, BLOCK), WIDE),
        )
        for _ in range(heads)
    )
    carry = lax.fori_loop(first_ref[step], step, lambda j, c: block(j, c, False), carry)
    carry = block(step, carry, True)
    parts = []
    for h in range(heads):
        top, total, acc = carry[h]
        acc = acc / total
        ctxt_ref[h] = acc
        lse_ref[h] = top + jnp.log(total)
        parts.append(acc.T)
    ctx_ref[...] = jnp.concatenate(parts, axis=1).astype(LOW)


def attend(first, start, qt, keys, vt):
    heads, _, rows = qt.shape
    grid_spec = pltpu.PrefetchScalarGridSpec(
        num_scalar_prefetch=1,
        grid=(rows // BLOCK,),
        in_specs=[
            pl.BlockSpec((1, BLOCK), lambda i, f: (0, i)),
            pl.BlockSpec((heads, HD, BLOCK), lambda i, f: (0, 0, i)),
            pl.BlockSpec((heads, rows, HD), lambda i, f: (0, 0, 0)),
            pl.BlockSpec((heads, HD, rows), lambda i, f: (0, 0, 0)),
        ],
        out_specs=[
            pl.BlockSpec((BLOCK, heads * HD), lambda i, f: (i, 0)),
            pl.BlockSpec((heads, HD, BLOCK), lambda i, f: (0, 0, i)),
            pl.BlockSpec((heads, 1, BLOCK), lambda i, f: (0, 0, i)),
        ],
    )
    return pl.pallas_call(
        attend_kernel,
        grid_spec=grid_spec,
        out_shape=[
            jax.ShapeDtypeStruct((rows, heads * HD), LOW),
            jax.ShapeDtypeStruct((heads, HD, rows), WIDE),
            jax.ShapeDtypeStruct((heads, 1, rows), WIDE),
        ],
        compiler_params=pltpu.CompilerParams(vmem_limit_bytes=40 * 2**20),
        cost_estimate=pl.CostEstimate(
            flops=8 * rows * rows * HD * heads, bytes_accessed=8 * 2**20, transcendentals=0
        ),
    )(first, start, qt, keys, vt)


def attend_back_kernel(
    first_ref, start_ref, qt_ref, q_ref, k_ref, kt_ref, v_ref, gt_ref, g_ref, ctxt_ref, lse_ref,
    dq_ref, dk_ref, dv_ref, dk_acc, dv_acc,
):
    step = pl.program_id(0)
    heads = qt_ref.shape[0]
    start = start_ref[...]
    key_iota = lax.broadcasted_iota(jnp.int32, (BLOCK, BLOCK), 0)
    query_iota = lax.broadcasted_iota(jnp.int32, (BLOCK, BLOCK), 1)

    @pl.when(step == 0)
    def _():
        dk_acc[...] = jnp.zeros_like(dk_acc)
        dv_acc[...] = jnp.zeros_like(dv_acc)

    delta = [
        jnp.sum(gt_ref[h].astype(WIDE) * ctxt_ref[h], axis=0, keepdims=True) for h in range(heads)
    ]

    def block(j, carry, last):
        base = pl.multiple_of(j * BLOCK, BLOCK)
        rows = pl.ds(base, BLOCK)
        allowed = key_iota + base >= start
        if last:
            allowed = allowed & (key_iota <= query_iota)
        out = []
        for h in range(heads):
            scores = mm(k_ref[h, rows, :], qt_ref[h])
            probs = jnp.where(allowed, jnp.exp(scores - lse_ref[h]), 0.0)
            slopes = mm(v_ref[h, rows, :], gt_ref[h])
            score_grads = (probs * (slopes - delta[h])).astype(LOW)
            dv_acc[h, rows, :] += mm(probs.astype(LOW), g_ref[h])
            dk_acc[h, rows, :] += mm(score_grads, q_ref[h])
            out.append(carry[h] + mm(kt_ref[h, :, rows], score_grads))
        return tuple(out)

    carry = tuple(jnp.zeros((HD, BLOCK), WIDE) for _ in range(heads))
    carry = lax.fori_loop(first_ref[step], step, lambda j, c: block(j, c, False), carry)
    carry = block(step, carry, True)
    scale = HD**-0.5
    dq_ref[...] = jnp.concatenate([(c * scale).T for c in carry], axis=1).astype(LOW)

    @pl.when(step == pl.num_programs(0) - 1)
    def _():
        for n in range(dk_acc.shape[1] // BLOCK):
            rows = slice(n * BLOCK, (n + 1) * BLOCK)
            dk_ref[rows, :] = jnp.concatenate(
                [dk_acc[h, rows, :] for h in range(heads)], axis=1
            ).astype(LOW)
            dv_ref[rows, :] = jnp.concatenate(
                [dv_acc[h, rows, :] for h in range(heads)], axis=1
            ).astype(LOW)


def attend_back(first, start, qt, q, keys, kt, values, gt, g, ctxt, lse):
    heads, _, rows = qt.shape
    by_column = pl.BlockSpec((heads, HD, BLOCK), lambda i, f: (0, 0, i))
    by_row = pl.BlockSpec((heads, BLOCK, HD), lambda i, f: (0, i, 0))
    all_rows = pl.BlockSpec((heads, rows, HD), lambda i, f: (0, 0, 0))
    all_columns = pl.BlockSpec((heads, HD, rows), lambda i, f: (0, 0, 0))
    whole = pl.BlockSpec((rows, heads * HD), lambda i, f: (0, 0))
    grid_spec = pltpu.PrefetchScalarGridSpec(
        num_scalar_prefetch=1,
        grid=(rows // BLOCK,),
        in_specs=[
            pl.BlockSpec((1, BLOCK), lambda i, f: (0, i)),
            by_column,
            by_row,
            all_rows,
            all_columns,
            all_rows,
            by_column,
            by_row,
            by_column,
            pl.BlockSpec((heads, 1, BLOCK), lambda i, f: (0, 0, i)),
        ],
        out_specs=[pl.BlockSpec((BLOCK, heads * HD), lambda i, f: (i, 0)), whole, whole],
        scratch_shapes=[pltpu.VMEM((heads, rows, HD), WIDE)] * 2,
    )
    return pl.pallas_call(
        attend_back_kernel,
        grid_spec=grid_spec,
        out_shape=[jax.ShapeDtypeStruct((rows, heads * HD), LOW)] * 3,
        compiler_params=pltpu.CompilerParams(vmem_limit_bytes=50 * 2**20),
        cost_estimate=pl.CostEstimate(
            flops=20 * rows * rows * HD * heads, bytes_accessed=8 * 2**20, transcendentals=0
        ),
    )(first, start, qt, q, keys, kt, values, gt, g, ctxt, lse)


def expert_kernel(
    own_ref, x_ref, c_ref, pair_ref, wg_ref, w1_ref, w2_ref,
    a_ref, du_ref, dx_ref, dy_ref, mark_ref, gate_ref, acc, dots, others,
):
    step = pl.program_id(0)
    rows, kinds = x_ref.shape[0], wg_ref.shape[1]
    lanes = lax.broadcasted_iota(jnp.int32, (rows, kinds), 1)
    own = own_ref[0]

    @pl.when(step == 0)
    def _():
        logits = mm(x_ref[...], wg_ref[...])
        here, there = lanes == own, lanes == pair_ref[...] - own
        mine = jnp.sum(jnp.where(here, logits, 0.0), axis=1, keepdims=True)
        theirs = jnp.sum(jnp.where(there, logits, 0.0), axis=1, keepdims=True)
        peak = jnp.maximum(mine, theirs)
        mine, theirs = jnp.exp(mine - peak), jnp.exp(theirs - peak)
        gate_ref[...] = mine / (mine + theirs)
        others[...] = theirs / (mine + theirs)
        dy_ref[...] = (gate_ref[...] * c_ref[...].astype(WIDE)).astype(LOW)
        acc[...] = jnp.zeros_like(acc)
        dots[...] = jnp.zeros_like(dots)

    size = 128
    for n in range(rows // size):
        part = slice(n * size, (n + 1) * size)
        u = mm(x_ref[part, :], w1_ref[0])
        da = mm_nt(c_ref[part, :], w2_ref[0])
        share = 0.5 * (1.0 + lax.erf(u * ROOT_HALF))
        a = (u * share).astype(LOW)
        slope = share + u * jnp.exp(-0.5 * u * u) * INV_ROOT_TAU
        dots[part, :] += jnp.sum(a.astype(WIDE) * da, axis=1, keepdims=True)
        du = (gate_ref[part, :] * da * slope).astype(LOW)
        a_ref[part, :] = a
        du_ref[part, :] = du
        acc[part, :] += mm_nt(du, w1_ref[0])

    @pl.when(step == pl.num_programs(0) - 1)
    def _():
        pull = gate_ref[...] * others[...] * dots[...]
        here, there = lanes == own, lanes == pair_ref[...] - own
        marks = jnp.where(here, pull, 0.0) - jnp.where(there, pull, 0.0)
        mark_ref[...] = marks
        high = marks.astype(LOW)
        rest = (marks - high.astype(WIDE)).astype(LOW)
        dx_ref[...] = (acc[...] + mm_nt(high, wg_ref[...]) + mm_nt(rest, wg_ref[...])).astype(LOW)


def run_experts(own, x, c, pairs, gate_low, first, second):
    rows, features = x.shape
    count, _, units = first.shape
    kinds = gate_low.shape[1]
    whole = lambda *shape: pl.BlockSpec(shape, lambda p, o: (0,) * len(shape))
    by_piece = pl.BlockSpec((rows, units), lambda p, o: (0, p))
    grid_spec = pltpu.PrefetchScalarGridSpec(
        num_scalar_prefetch=1,
        grid=(count,),
        in_specs=[
            whole(rows, features),
            whole(rows, features),
            whole(rows, 1),
            whole(features, kinds),
            pl.BlockSpec((1, features, units), lambda p, o: (p, 0, 0)),
            pl.BlockSpec((1, units, features), lambda p, o: (p, 0, 0)),
        ],
        out_specs=[
            by_piece,
            by_piece,
            whole(rows, features),
            whole(rows, features),
            whole(rows, kinds),
            whole(rows, 1),
        ],
        scratch_shapes=[
            pltpu.VMEM((rows, features), WIDE),
            pltpu.VMEM((rows, 1), WIDE),
            pltpu.VMEM((rows, 1), WIDE),
        ],
    )
    return pl.pallas_call(
        expert_kernel,
        grid_spec=grid_spec,
        out_shape=[
            jax.ShapeDtypeStruct((rows, count * units), LOW),
            jax.ShapeDtypeStruct((rows, count * units), LOW),
            jax.ShapeDtypeStruct((rows, features), LOW),
            jax.ShapeDtypeStruct((rows, features), LOW),
            jax.ShapeDtypeStruct((rows, kinds), WIDE),
            jax.ShapeDtypeStruct((rows, 1), WIDE),
        ],
        compiler_params=pltpu.CompilerParams(vmem_limit_bytes=50 * 2**20),
        cost_estimate=pl.CostEstimate(
            flops=10 * rows * features * count * units,
            bytes_accessed=24 * 2**20,
            transcendentals=0,
        ),
    )(own, x, c, pairs, gate_low, first, second)


def split_dot(a, marks):
    high = marks.astype(LOW)
    rest = (marks - high.astype(WIDE)).astype(LOW)
    return mm_tn(a, high) + mm_tn(a, rest)


def body(
    block_input,
    gain_one,
    gain_two,
    qkv_weight,
    out_weight,
    gate_weight,
    frozen_in,
    frozen_out,
    fresh_in,
    fresh_out,
    routes,
    doc_lengths,
    cotangent,
):
    own_rows, features = block_input.shape
    head_count, dp_count = lax.axis_size("head"), lax.axis_size("dp")
    head_index, dp_index = lax.axis_index("head"), lax.axis_index("dp")
    total = own_rows * head_count
    kinds = gate_weight.shape[1]
    share = 3 * total // kinds // head_count
    width = qkv_weight.shape[2]
    heads = width // HD
    first_own = head_index * own_rows

    def own_part(array):
        return lax.dynamic_slice_in_dim(array, first_own, own_rows, 0)

    rows_in = in_order(head_pieces(block_input), head_index).astype(WIDE)
    qkv = over_dp(qkv_weight.astype(LOW), 1)

    tokens = jnp.arange(total, dtype=jnp.int32)
    hits = (routes[:, :, None] == jnp.arange(kinds, dtype=jnp.int32)).astype(LOW)
    earlier = (tokens[:, None] > tokens[None, :]).astype(LOW)
    counts = mm(earlier, hits.reshape(total, 2 * kinds)).reshape(total, 2, kinds)
    counts = counts + jnp.sum(hits[:, 0].astype(WIDE), axis=0)[None, None] * jnp.array([0.0, 1.0])[None, :, None]
    slots = jnp.sum(counts * hits.astype(WIDE), axis=2).astype(jnp.int32)
    hosts = routes % (kinds // 2) * 2 + routes // (kinds // 2)
    places = (hosts ^ dp_index) * share + slots // head_count
    places = jnp.where(slots % head_count == head_index, places, -1)
    spots = jnp.arange(dp_count * share, dtype=jnp.int32)[:, None]
    picks = ((places[:, 0][None] == spots) | (places[:, 1][None] == spots)).astype(LOW)
    pair_sums = jnp.sum(routes, axis=1).astype(LOW)
    pairs_out = mm(picks, pair_sums[:, None]).reshape(dp_count, share)

    def exchange(rows):
        parts = rows.reshape(dp_count, share, rows.shape[-1])
        return [parts[0]] + [flip(parts[k], "dp", k) for k in range(1, dp_count)]

    order = dp_index ^ jnp.arange(dp_count, dtype=jnp.int32)
    pairs_out = jnp.sum(
        jnp.where((order[:, None] == jnp.arange(dp_count)[None])[:, :, None], pairs_out[:, None], 0.0), axis=0
    )
    pairs_in = lax.all_to_all(pairs_out, "dp", 0, 0, tiled=True)
    pairs_in = jnp.sum(
        jnp.where((order[:, None] == jnp.arange(dp_count)[None])[:, :, None], pairs_in[None], 0.0), axis=1
    )
    pairs_in = pairs_in.reshape(dp_count * share, 1).astype(jnp.int32)

    upstream_rows = in_order(head_pieces(cotangent), head_index)
    c_parts = exchange(mm(picks, upstream_rows).astype(LOW))

    odd = dp_index % 2
    keep_in = jnp.where(odd == 0, frozen_in[0], fresh_in[0]).astype(LOW)
    keep_out = jnp.where(odd == 0, frozen_out[0], fresh_out[0]).astype(LOW)
    give_in = jnp.where(odd == 0, fresh_in[0], frozen_in[0]).astype(LOW)
    give_out = jnp.where(odd == 0, fresh_out[0], frozen_out[0]).astype(LOW)
    half_in = jnp.stack([keep_in, flip(give_in, "dp", 1)])
    half_out = jnp.stack([keep_out, flip(give_out, "dp", 1)])
    first = jnp.concatenate(head_pieces(half_in))
    second = jnp.concatenate(head_pieces(half_out))
    own_kind = dp_index // 2 + odd * (kinds // 2)

    normed_one, rstd_one = norm_parts(rows_in)
    h_one = (normed_one * gain_one).astype(LOW)
    by_head = qkv.reshape(3, features, heads, HD)
    scale = HD**-0.5

    def columns(weight):
        return jnp.einsum("dhe,rd->her", weight, h_one, preferred_element_type=WIDE).astype(LOW)

    def lines(weight):
        return jnp.einsum("rd,dhe->hre", h_one, weight, preferred_element_type=WIDE).astype(LOW)

    qt, queries = columns(by_head[0]) * scale, lines(by_head[0]) * scale
    kt, keys = columns(by_head[1]), lines(by_head[1])
    vt, values = columns(by_head[2]), lines(by_head[2])
    qt, queries = qt.astype(LOW), queries.astype(LOW)
    ends = jnp.cumsum(doc_lengths[0])
    start = jnp.max(jnp.where(tokens[:, None] >= ends[None], ends[None], 0), axis=1)
    first_block = start[::BLOCK] // BLOCK
    start = start[None]
    context, context_t, log_totals = attend(first_block, start, qt, keys, vt)

    out_full = over_dp(out_weight.astype(LOW), 1)
    out_pieces = jnp.concatenate(head_pieces(out_full))
    contexts = jnp.concatenate(head_pieces(context), axis=1)
    x_one = rows_in + mm(contexts, out_pieces)
    normed_two, rstd_two = norm_parts(x_one)
    h_two = (normed_two * gain_two).astype(LOW)

    gate_low = gate_weight.astype(LOW)
    x_parts = exchange(mm(picks, h_two).astype(LOW))
    per = dp_count // 4
    own_list = own_kind.astype(jnp.int32)[None]
    done = []
    for n in range(4):
        ks = range(n * per, (n + 1) * per)
        x = jnp.concatenate([x_parts[k] for k in ks])
        c = jnp.concatenate([c_parts[k] for k in ks])
        done.append(
            (x,) + tuple(run_experts(
                own_list, x, c, pairs_in[n * per * share : (n + 1) * per * share], gate_low, first, second
            ))
        )
    dx_parts = []
    for n in range(4):
        for m in range(per):
            k = n * per + m
            part = done[n][3][m * share : (m + 1) * share]
            dx_parts.append(part if k == 0 else flip(part, "dp", k))
    dx_rows = jnp.concatenate(dx_parts)
    dh_two = sum_over_head(mm_tn(picks, dx_rows))

    hidden_low = jnp.concatenate([d[1] for d in done])
    hidden_grads = jnp.concatenate([d[2] for d in done])
    x_all = jnp.concatenate([d[0] for d in done])
    dy_all = jnp.concatenate([d[4] for d in done])
    marks = jnp.concatenate([d[5] for d in done])
    gates = jnp.concatenate([d[6] for d in done])
    units = first.shape[2]
    gated = (mm(hidden_low, second.reshape(-1, features)) * gates).astype(LOW)
    gated = jnp.concatenate(exchange(gated))
    mixture = own_sum_over_head(mm_tn(picks, gated))
    result = (own_part(x_one) + mixture).astype(LOW)
    grad_second = mm_tn(hidden_low, dy_all).reshape(head_count, 2, units, features)
    grad_first = jnp.stack(
        [
            mm_tn(x_all, hidden_grads[:, n * units : (n + 1) * units])
            for n in range(2 * head_count)
        ]
    ).reshape(head_count, 2, features, units)

    def home(grad):
        come = flip(jnp.stack([grad[1], grad[3]]).astype(LOW), "head", 1).astype(WIDE)
        far = flip((grad[2] + come[1]).astype(LOW), "head", 2).astype(WIDE)
        both = grad[0] + come[0] + far
        other = flip(both[1].astype(LOW), "dp", 1).astype(WIDE)
        return jnp.where(odd == 1, both[0], other)[None]

    grad_fresh_in, grad_fresh_out = home(grad_first), home(grad_second)
    grad_gate = split_dot(x_all, marks)

    upstream = upstream_rows.astype(WIDE)
    dx_one = upstream + norm_back(dh_two, normed_two, rstd_two, gain_two)
    grad_gain_two = jnp.sum(own_part(dh_two) * own_part(normed_two), axis=0)
    dattn = dx_one.astype(LOW)
    out_heads = out_full.reshape(heads, HD, features)
    gt = jnp.einsum("hed,rd->her", out_heads, dattn, preferred_element_type=WIDE).astype(LOW)
    g = jnp.einsum("rd,hed->hre", dattn, out_heads, preferred_element_type=WIDE).astype(LOW)
    dq, dk, dv = attend_back(
        first_block, start, qt, queries, keys, kt, values, gt, g, context_t, log_totals
    )
    grad_out_weight = sum_over_dp_scattered(mm_tn(context, dattn), 1)
    dqkv = jnp.concatenate([dq, dk, dv], axis=1)
    back_weight = qkv.transpose(1, 0, 2).reshape(features, 3 * width)
    dh_one = own_sum_over_head(mm_nt(dqkv, back_weight))
    grad_qkv = mm_tn(h_one, dqkv).reshape(features, 3, width).transpose(1, 0, 2)
    grad_qkv = sum_over_dp_scattered(grad_qkv, 1)
    own_normed, own_rstd = own_part(normed_one), own_part(rstd_one)
    grad_input = own_part(dx_one) + norm_back(dh_one, own_normed, own_rstd, gain_one)
    grad_gain_one = jnp.sum(dh_one * own_normed, axis=0)
    small = sum_everywhere(jnp.concatenate([grad_gain_two[None], grad_gate.T]))
    grad_gain_one = sum_everywhere(grad_gain_one)
    return (
        result,
        grad_input,
        grad_gain_one,
        small[0],
        grad_qkv,
        grad_out_weight,
        small[1:].T,
        grad_fresh_in,
        grad_fresh_out,
    )


def solution(mesh):
    return jax.shard_map(
        body,
        mesh=mesh,
        in_specs=(
            P(("dp", "head"), None),
            P(),
            P(),
            P(None, "dp", "head"),
            P("head", "dp"),
            P(),
            P("dp", None, "head"),
            P("dp", "head", None),
            P("dp", None, "head"),
            P("dp", "head", None),
            P("dp", None),
            P("dp", None),
            P(("dp", "head"), None),
        ),
        out_specs=(
            P(("dp", "head"), None),
            P(("dp", "head"), None),
            P(),
            P(),
            P(None, "dp", "head"),
            P("head", "dp"),
            P(),
            P("dp", None, "head"),
            P("dp", "head", None),
        ),
        check_vma=False,
    )
```

time: 3010 us -> 848 us (0.28)
  waiting for transfers between devices: 1320 us -> 204 us
  blocking collectives: 937 us -> 0 us
  local copies, waits for them, and re-layouts: 343 us -> 179 us
  Pallas kernels: 0 us -> 142 us
  matrix products: 220 us -> 105 us
  starting transfers between devices: 12.9 us -> 120 us
  other arithmetic: 153 us -> 87 us
    all_to_all x2 -> x0, blocking collectives: 827 us -> none  [the longest x1 414 us: to_experts(): lax.all_to_all(doubled.reshape((2 * pair_count,) + rows_by_pair.shape[1:]...]
    all_to_all x2 -> x1, waiting for transfers between devices: 813 us -> 0.01 us  [body(): pairs_in = lax.all_to_all(pairs_out, 'dp', 0, 0, tiled=True)]
    unnamed x13 -> x0, waiting for transfers between devices: 255 us -> none
    ppermute x0 -> x83, waiting for transfers between devices: none -> 204 us  [flip(): return lax.ppermute(array, axis, [(i, i ^ bits) for i in range(size)])]
    reduce_scatter x3 -> x0, waiting for transfers between devices: 171 us -> none  [the longest x2 116 us: project_rows(): lax.psum_scatter(jnp.dot(source, weight, preferred_element_type=jnp.float...]
    pallas_call x0 -> x6, Pallas kernels: none -> 142 us  [the longest x4 71.7 us: run_experts(): pl.pallas_call(expert_kernel, grid_spec=grid_spec, out_shape=[jax.ShapeDt...]
    ppermute x0 -> x83, starting transfers between devices: none -> 116 us  [flip(): return lax.ppermute(array, axis, [(i, i ^ bits) for i in range(size)])]
    gather x4 -> x0, local copies, waits for them, and re-layouts: 111 us -> none  [the longest x1 31.7 us: body(): grads_received = to_experts(padded_grads[table_grid])]
  transfers between devices with their start and end apart: 12 -> 84, of which waited for: 10 -> 23; matrix products, arithmetic and copies ran while one was open for 4% -> 36% of each run, Pallas kernels for 0% -> 10%
where the time goes in v1:
time: 848 us; the launch traced here: 841 us
  waiting for transfers between devices  204 us (24%)
  local copies, waits for them, and re-layouts  179 us (21%)
  Pallas kernels  142 us (17%)
  starting transfers between devices  120 us (14%)
  matrix products  105 us (12%)
  other arithmetic  87 us (10%)
    ppermute x83, waiting for transfers between devices, flip(): return lax.ppermute(array, axis, [(i, i ^ bits) for i in range(size)])  204 us
    ppermute x83, starting transfers between devices, flip(): return lax.ppermute(array, axis, [(i, i ^ bits) for i in range(size)])  116 us
    pallas_call x4, Pallas kernels, run_experts(): pl.pallas_call(expert_kernel, grid_spec=grid_spec, out_shape=[jax.ShapeDt...  71.7 us
    unnamed x274, local copies, waits for them, and re-layouts  60.7 us
    dot_general x15, matrix products, mm_tn(): return lax.dot_general(a, b, TN, preferred_element_type=WIDE)  54.5 us
    dot_general x6, matrix products, mm(): return jnp.dot(a, b, preferred_element_type=WIDE)  39.3 us
    pallas_call x1, Pallas kernels, attend_back(): pl.pallas_call(attend_back_kernel, grid_spec=grid_spec, out_shape=[jax.Sh...  36.4 us
    pallas_call x1, Pallas kernels, attend(): pl.pallas_call(attend_kernel, grid_spec=grid_spec, out_shape=[jax.ShapeDt...  34.3 us
  transfers between devices with their start and end apart: 84, of which 23 were waited for; matrix products, arithmetic and copies ran while one was open for 36% of the time, Pallas kernels for 10%

profile of v1, /device:TPU:0, one launch (start us, length us, event | category | flops | bytes accessed | tf_op | source)
XLA Modules:
  0.0 841.4 jit_solution(9606589632552835730)
XLA Ops:
  2.9 2.9 collective-permute-start.17
  6.8 2.6 collective-permute-start.9
  16.2 4.3 all-to-all-start
  20.5 3.0 collective-permute-start.3
  80.1 2.6 dynamic_update_slice.78
  82.7 2.6 dynamic_update_slice.79
  95.1 9.2 %collective-permute-done.5 = bf16[4,3,96,192]{3,2,1,0:T(8,128)(2,1)S(1)} collective-permute-done((bf16[4,3,96,192]{3,2,1,0:T(8,128)(2,1)S(1)}, bf16[4,3,96,192]{3,2,1,0:T(8,128)(2,1)S(1)}, u32[]{:S(2)}, u32[]{:S(2)}) %collective-permute-start.5) | collective-permute-done | bytes 442400 | tf_op jit(solution)/shard_map/ppermute | solution.py:36
  115.1 2.6 dynamic_update_slice.81
  117.7 2.6 dynamic_update_slice.82
  141.0 3.3 fusion.44.kt_ref
  145.2 3.8 fusion.159
  153.5 9.7 %fusion.22 = bf16[1536,768]{1,0:T(8,128)(2,1)} fusion(bf16[2048,768]{0,1:T(8,128)(2,1)} %constant_dynamic-update-slice_fusion.40, s32[2048]{0:T(1024)S(1)} %bitcast.390, s32[2048]{0:T(1024)S(1)} %bitcast.385), kind=kOutput, calls=%fused_computation.30 | convolution fusion | flops 4842455040 | bytes 5521408 | tf_op jit(solution)/shard_map/dot_general | solution.py:23
  164.6 34.3 %shard_map.205 = (bf16[2048,192]{1,0:T(8,128)(2,1)S(1)}, f32[3,64,2048]{2,1,0:T(8,128)S(1)}, f32[3,1,2048]{2,1,0:T(1,128)S(1)}) custom-call(s32[8]{0:T(128)S(1)} %and_select_fusion.4.first_ref, s32[1,2048]{1,0:T(1,128)S(1)} %bitcast.355, bf16[3,64,2048]{2,1,0:T(8,128)(2,1)S(1)} %copy.253.qt_ref, bf16[3,2048,64]{2,1,0:T(8,128)(2,1)S(1)} %copy.254.k_ref, ...), custom_call_target="tpu_custom_call" | custom-call | flops 6442450944 | bytes 8388608 | tf_op jit(solution)/shard_map/pallas_call | solution.py:191
  201.4 3.0 fusion.165
  207.7 3.6 fusion.5
  217.7 16.5 %collective-permute-start.34 = (bf16[192,768]{1,0:T(8,128)(2,1)S(1)}, bf16[192,768]{1,0:T(8,128)(2,1)S(1)}, u32[]{:S(2)}, u32[]{:S(2)}) collective-permute-start(bf16[192,768]{1,0:T(8,128)(2,1)S(1)} %copy-done.83), channel_id=1, source_target_pairs={{0,16},{4,20},{8,24},{12,28},{16,0},{20,4},{24,8},{28,12},{1,17},{... | collective-permute-start | bytes 884744 | tf_op jit(solution)/shard_map/ppermute | solution.py:36
  234.3 14.1 %collective-permute-start.31 = (bf16[192,768]{1,0:T(8,128)(2,1)S(1)}, bf16[192,768]{1,0:T(8,128)(2,1)S(1)}, u32[]{:S(2)}, u32[]{:S(2)}) collective-permute-start(bf16[192,768]{1,0:T(8,128)(2,1)S(1)} %copy-done.82), channel_id=1, source_target_pairs={{0,12},{4,8},{8,4},{12,0},{16,28},{20,24},{24,20},{28,16},{1,13},{... | collective-permute-start | bytes 884744 | tf_op jit(solution)/shard_map/ppermute | solution.py:36
  255.6 2.7 collective-permute-done.34
  258.2 6.3 collective-permute-done.31
  266.6 4.1 collective-permute-done.30
  278.6 6.3 fusion.174
  288.4 7.1 fusion.19
  307.0 3.6 collective-permute-start.32
  310.7 18.2 %shard_map.206 = (bf16[384,3072]{1,0:T(8,128)(2,1)}, bf16[384,3072]{1,0:T(8,128)(2,1)}, bf16[384,768]{1,0:T(8,128)(2,1)S(1)}, bf16[384,768]{1,0:T(8,128)(2,1)S(1...) custom-call(s32[1]{0:T(128)} %bitcast.32.own_ref, bf16[384,768]{1,0:T(8,128)(2,1)S(1)} %pad_maximum_fusion.11.x_ref, ...), custom_call_target="tpu_custom_call" | custom-call | flops 9059696640 | bytes 25165824 | tf_op jit(solution)/shard_map/pallas_call | solution.py:375
  329.8 3.4 constant_dynamic-update-slice_fusion.13
  333.1 17.6 %collective-permute-done.33 = bf16[192,768]{1,0:T(8,128)(2,1)S(1)} collective-permute-done((bf16[192,768]{1,0:T(8,128)(2,1)S(1)}, bf16[192,768]{1,0:T(8,128)(2,1)S(1)}, u32[]{:S(2)}, u32[]{:S(2)}) %collective-permute-start.33) | collective-permute-done | bytes 294944 | tf_op jit(solution)/shard_map/ppermute | solution.py:36
  350.7 4.8 collective-permute-done.32
  355.6 18.0 %shard_map.208 = (bf16[384,3072]{1,0:T(8,128)(2,1)}, bf16[384,3072]{1,0:T(8,128)(2,1)}, bf16[384,768]{1,0:T(8,128)(2,1)S(1)}, bf16[384,768]{1,0:T(8,128)(2,1)S(1...) custom-call(s32[1]{0:T(128)} %bitcast.32.own_ref, bf16[384,768]{1,0:T(8,128)(2,1)S(1)} %pad_maximum_fusion.15.x_ref, ...), custom_call_target="tpu_custom_call" | custom-call | flops 9059696640 | bytes 25165824 | tf_op jit(solution)/shard_map/pallas_call | solution.py:375
  375.4 17.6 %shard_map.207 = (bf16[384,3072]{1,0:T(8,128)(2,1)}, bf16[384,3072]{1,0:T(8,128)(2,1)}, bf16[384,768]{1,0:T(8,128)(2,1)S(1)}, bf16[384,768]{1,0:T(8,128)(2,1)S(1...) custom-call(s32[1]{0:T(128)} %bitcast.32.own_ref, bf16[384,768]{1,0:T(8,128)(2,1)S(1)} %pad_maximum_fusion.13.x_ref, ...), custom_call_target="tpu_custom_call" | custom-call | flops 9059696640 | bytes 25165824 | tf_op jit(solution)/shard_map/pallas_call | solution.py:375
  393.1 5.5 constant_dynamic-update-slice_fusion.12
  400.2 17.8 %shard_map.209 = (bf16[384,3072]{1,0:T(8,128)(2,1)}, bf16[384,3072]{1,0:T(8,128)(2,1)}, bf16[384,768]{1,0:T(8,128)(2,1)S(1)}, bf16[384,768]{1,0:T(8,128)(2,1)S(1...) custom-call(s32[1]{0:T(128)} %bitcast.32.own_ref, bf16[384,768]{1,0:T(8,128)(2,1)S(1)} %pad_maximum_fusion.17.x_ref, ...), custom_call_target="tpu_custom_call" | custom-call | flops 9059696640 | bytes 25165824 | tf_op jit(solution)/shard_map/pallas_call | solution.py:375
  418.1 3.6 constant_dynamic-update-slice_fusion.36
  421.9 4.4 fusion.91
  458.8 11.4 %multiply_convert_fusion.2 = bf16[1536,768]{1,0:T(8,128)(2,1)S(1)} fusion(bf16[1536,3072]{1,0:T(8,128)(2,1)} %constant_dynamic-update-slice_fusion.10, bf16[3072,768]{1,0:T(8,128)(2,1)} %bitcast.380, f32[1536]{0:T(1024)S(1)} %maximum_reduce_fusion), kind=kOutput, calls=%fused_computation.24 | convolution fusion | flops 7250116608 | bytes 16521216 | tf_op jit(solution)/shard_map/dot_general | solution.py:23
  471.9 10.8 %fusion.175 = (bf16[3072,768]{1,0:T(8,128)(2,1)S(1)}, f32[3072,768]{1,0:T(8,128)S(1)}) fusion(bf16[1536,3072]{1,0:T(8,128)(2,1)} %constant_dynamic-update-slice_fusion.10, bf16[384,768]{1,0:T(8,128)(2,1)S(1)} %copy-done.38, bf16[384,768]{1,0:T(8,128)(2,1)S(1)} %copy-done.34, bf16[384,768]{1,0:T(8,128)(2,1)S(1)} %copy-done.36, ...), kind=kOutput, calls=%fused_computation.375 | convolution fusion | flops 7259553792 | bytes 25952256 | tf_op jit(solution)/shard_map/dot_general | solution.py:31
  490.7 2.6 collective-permute-start.53
  493.3 2.6 collective-permute-start.46
  495.9 19.7 %collective-permute-done.52 = bf16[192,768]{1,0:T(8,128)(2,1)S(1)} collective-permute-done((bf16[192,768]{1,0:T(8,128)(2,1)S(1)}, bf16[192,768]{1,0:T(8,128)(2,1)S(1)}, u32[]{:S(2)}, u32[]{:S(2)}) %collective-permute-start.52) | collective-permute-done | bytes 294944 | tf_op jit(solution)/shard_map/ppermute | solution.py:36
  517.8 10.9 %collective-permute-done.53 = bf16[192,768]{1,0:T(8,128)(2,1)S(1)} collective-permute-done((bf16[192,768]{1,0:T(8,128)(2,1)S(1)}, bf16[192,768]{1,0:T(8,128)(2,1)S(1)}, u32[]{:S(2)}, u32[]{:S(2)}) %collective-permute-start.53) | collective-permute-done | bytes 294944 | tf_op jit(solution)/shard_map/ppermute | solution.py:36
  532.5 5.9 fusion.11
  538.7 6.2 collective-permute-done.40
  544.8 3.9 collective-permute-start.43
  549.6 19.6 %collective-permute-done.43 = bf16[192,768]{1,0:T(8,128)(2,1)S(1)} collective-permute-done((bf16[192,768]{1,0:T(8,128)(2,1)S(1)}, bf16[192,768]{1,0:T(8,128)(2,1)S(1)}, u32[]{:S(2)}, u32[]{:S(2)}) %collective-permute-start.43) | collective-permute-done | bytes 294944 | tf_op jit(solution)/shard_map/ppermute | solution.py:36
  569.2 6.3 collective-permute-done.44
  575.6 6.1 fusion.13
  587.6 3.7 convolution_bitcast_fusion.3
  605.5 18.0 %collective-permute-done.57 = bf16[1024,768]{0,1:T(8,128)(2,1)} collective-permute-done((bf16[1024,768]{0,1:T(8,128)(2,1)S(1)}, bf16[1024,768]{0,1:T(8,128)(2,1)}, u32[]{:S(2)}, u32[]{:S(2)}) %collective-permute-start.57) | collective-permute-done | bytes 1572896 | tf_op jit(solution)/shard_map/ppermute | solution.py:36
  623.4 3.3 add_convert_fusion
  626.7 21.9 %collective-permute-done.81 = bf16[2,384,768]{2,1,0:T(8,128)(2,1)S(1)} collective-permute-done((bf16[2,384,768]{2,1,0:T(8,128)(2,1)S(1)}, bf16[2,384,768]{2,1,0:T(8,128)(2,1)S(1)}, u32[]{:S(2)}, u32[]{:S(2)}) %collective-permute-start.81) | collective-permute-done | bytes 1179680 | tf_op jit(solution)/shard_map/ppermute | solution.py:36
  650.8 23.1 %collective-permute-done.78 = bf16[2,768,384]{2,1,0:T(8,128)(2,1)S(1)} collective-permute-done((bf16[2,768,384]{2,1,0:T(8,128)(2,1)S(1)}, bf16[2,768,384]{2,1,0:T(8,128)(2,1)S(1)}, u32[]{:S(2)}, u32[]{:S(2)}) %collective-permute-start.78) | collective-permute-done | bytes 1179680 | tf_op jit(solution)/shard_map/ppermute | solution.py:36
  676.0 13.7 %collective-permute-done.48 = bf16[512,768]{0,1:T(8,128)(2,1)S(1)} collective-permute-done((bf16[512,768]{0,1:T(8,128)(2,1)S(1)}, bf16[512,768]{0,1:T(8,128)(2,1)S(1)}, u32[]{:S(2)}, u32[]{:S(2)}) %collective-permute-start.48) | collective-permute-done | bytes 786464 | tf_op jit(solution)/shard_map/ppermute | solution.py:36
  689.8 3.1 fusion.84
  695.2 2.7 fusion.93
  704.5 3.4 fusion.160
  708.0 4.0 multiply_add_fusion
  712.0 2.6 fusion.85
  718.3 36.4 %shard_map.210 = (bf16[2048,192]{1,0:T(8,128)(2,1)S(1)}, bf16[2048,192]{1,0:T(8,128)(2,1)}, bf16[2048,192]{1,0:T(8,128)(2,1)}) custom-call(s32[8]{0:T(128)S(1)} %and_select_fusion.4.first_ref, s32[1,2048]{1,0:T(1,128)S(1)} %bitcast.356, bf16[3,64,2048]{2,1,0:T(8,128)(2,1)S(1)} %copy.253.qt_ref, bf16[3,2048,64]{2,1,0:T(8,128)(2,1)} %get-tuple-element.169.q_ref, ...), custom_call_target="tpu_custom_call" | custom-call | flops 16106127360 | bytes 8388608 | tf_op jit(solution)/shard_map/pallas_call | solution.py:285
  754.8 4.4 fusion.114
  759.2 2.8 fusion.115
  774.3 3.1 collective-permute-done.68
  803.2 3.6 collective-permute-done.71
  810.5 4.2 collective-permute-done.72
  834.6 3.0 multiply_add_fusion.1
  837.6 3.0 copy.297
  (607 shorter events, 310.9 us)
Async XLA Ops:
  2.9 127.1 %collective-permute-start.17 = (bf16[512,768]{0,1:T(8,128)(2,1)}, bf16[512,768]{0,1:T(8,128)(2,1)}, u32[]{:S(2)}, u32[]{:S(2)}) collective-permute-start(bf16[512,768]{0,1:T(8,128)(2,1)} %copy.260), channel_id=1, source_target_pairs={{0,2},{1,3},{2,0},{3,1},{4,6},{5,7},{6,4},{7,5},{8,10},{9,11},{10,... | collective-permute-start | bytes 2359304 | tf_op jit(solution)/shard_map/ppermute | solution.py:36
  5.9 121.7 %collective-permute-start.16 = (bf16[512,768]{0,1:T(8,128)(2,1)}, bf16[512,768]{0,1:T(8,128)(2,1)}, u32[]{:S(2)}, u32[]{:S(2)}) collective-permute-start(bf16[512,768]{0,1:T(8,128)(2,1)} %copy.260), channel_id=1, source_target_pairs={{0,1},{1,0},{2,3},{3,2},{4,5},{5,4},{6,7},{7,6},{8,9},{9,8},{10,11... | collective-permute-start | bytes 2359304 | tf_op jit(solution)/shard_map/ppermute | solution.py:36
  6.8 38.7 %collective-permute-start.9 = (bf16[1,192,96]{2,1,0:T(8,128)(2,1)S(1)}, bf16[1,192,96]{2,1,0:T(8,128)(2,1)S(1)}, u32[]{:S(2)}, u32[]{:S(2)}) collective-permute-start(bf16[1,192,96]{2,1,0:T(8,128)(2,1)S(1)} %convert_bitcast_fusion.5), channel_id=1, source_target_pairs={{0,16},{4,20},{8,24},{12,28},{16,0},{20,4},{24,8},{28,12},{1,17},{... | collective-permute-start | bytes 110600 | tf_op jit(solution)/shard_map/ppermute | solution.py:36
  16.2 29.2 %all-to-all-start = ((f32[8,1,192]{2,1,0:T(1,128)}), f32[8,1,192]{2,1,0:T(1,128)S(1)}, u32[]{:S(2)}, u32[]{:S(2)}) async-start(f32[8,1,192]{2,1,0:T(1,128)} %copy.263), calls=%async_computation | async-start | bytes 16384 | tf_op jit(solution)/shard_map/all_to_all | solution.py:454
  20.5 35.5 %collective-permute-start.3 = (bf16[1,3,96,192]{3,2,1,0:T(8,128)(2,1)S(1)}, bf16[1,3,96,192]{3,2,1,0:T(8,128)(2,1)}, u32[]{:S(2)}, u32[]{:S(2)}) collective-permute-start(bf16[1,3,96,192]{3,2,1,0:T(8,128)(2,1)S(1)} %convert_bitcast_fusion.4), channel_id=1, source_target_pairs={{0,16},{4,20},{8,24},{12,28},{16,0},{20,4},{24,8},{28,12},{1,17},{... | collective-permute-start | bytes 331784 | tf_op jit(solution)/shard_map/ppermute | solution.py:36
  24.7 81.1 %collective-permute-start.1 = (bf16[512,768]{0,1:T(8,128)(2,1)}, bf16[512,768]{0,1:T(8,128)(2,1)}, u32[]{:S(2)}, u32[]{:S(2)}) collective-permute-start(bf16[512,768]{0,1:T(8,128)(2,1)} %copy.238), channel_id=1, source_target_pairs={{0,2},{1,3},{2,0},{3,1},{4,6},{5,7},{6,4},{7,5},{8,10},{9,11},{10,... | collective-permute-start | bytes 2359304 | tf_op jit(solution)/shard_map/ppermute | solution.py:36
  56.0 30.4 %collective-permute-start.20 = (bf16[768,384]{1,0:T(8,128)(2,1)}, bf16[768,384]{1,0:T(8,128)(2,1)}, u32[]{:S(2)}, u32[]{:S(2)}) collective-permute-start(bf16[768,384]{1,0:T(8,128)(2,1)} %get-tuple-element.160), channel_id=1, source_target_pairs={{0,4},{4,0},{8,12},{12,8},{16,20},{20,16},{24,28},{28,24},{1,5},{5... | collective-permute-start | bytes 1769480 | tf_op jit(solution)/shard_map/ppermute | solution.py:36
  73.4 15.2 %collective-permute-start.24 = (bf16[384,768]{1,0:T(8,128)(2,1)}, bf16[384,768]{1,0:T(8,128)(2,1)}, u32[]{:S(2)}, u32[]{:S(2)}) collective-permute-start(bf16[384,768]{1,0:T(8,128)(2,1)} %get-tuple-element.159), channel_id=1, source_target_pairs={{0,4},{4,0},{8,12},{12,8},{16,20},{20,16},{24,28},{28,24},{1,5},{5... | collective-permute-start | bytes 1769480 | tf_op jit(solution)/shard_map/ppermute | solution.py:36
  86.5 38.1 %collective-permute-start = (bf16[512,768]{0,1:T(8,128)(2,1)}, bf16[512,768]{0,1:T(8,128)(2,1)}, u32[]{:S(2)}, u32[]{:S(2)}) collective-permute-start(bf16[512,768]{0,1:T(8,128)(2,1)} %copy.238), channel_id=1, source_target_pairs={{0,1},{1,0},{2,3},{3,2},{4,5},{5,4},{6,7},{7,6},{8,9},{9,8},{10,11... | collective-permute-start | bytes 2359304 | tf_op jit(solution)/shard_map/ppermute | solution.py:36
  88.6 15.7 %collective-permute-start.5 = (bf16[4,3,96,192]{3,2,1,0:T(8,128)(2,1)S(1)}, bf16[4,3,96,192]{3,2,1,0:T(8,128)(2,1)S(1)}, u32[]{:S(2)}, u32[]{:S(2)}) collective-permute-start(bf16[4,3,96,192]{3,2,1,0:T(8,128)(2,1)S(1)} %pad_maximum_fusion.10), channel_id=1, source_target_pairs={{0,4},{4,0},{8,12},{12,8},{16,20},{20,16},{24,28},{28,24},{1,5},{5... | collective-permute-start | bytes 1327112 | tf_op jit(solution)/shard_map/ppermute | solution.py:36
  104.3 100.1 %collective-permute-start.13 = (bf16[192,768]{1,0:T(8,128)(2,1)}, bf16[192,768]{1,0:T(8,128)(2,1)}, u32[]{:S(2)}, u32[]{:S(2)}) collective-permute-start(bf16[192,768]{1,0:T(8,128)(2,1)} %dynamic_update_slice.91), channel_id=1, source_target_pairs={{0,2},{1,3},{2,0},{3,1},{4,6},{5,7},{6,4},{7,5},{8,10},{9,11},{10,... | collective-permute-start | bytes 884744 | tf_op jit(solution)/shard_map/ppermute | solution.py:36
  105.8 27.9 %collective-permute-start.2 = (bf16[512,768]{0,1:T(8,128)(2,1)}, bf16[512,768]{0,1:T(8,128)(2,1)}, u32[]{:S(2)}, u32[]{:S(2)}) collective-permute-start(bf16[512,768]{0,1:T(8,128)(2,1)} %collective-permute-done.1), channel_id=1, source_target_pairs={{0,1},{1,0},{2,3},{3,2},{4,5},{5,4},{6,7},{7,6},{8,9},{9,8},{10,11... | collective-permute-start | bytes 2359304 | tf_op jit(solution)/shard_map/ppermute | solution.py:36
  124.6 80.5 %collective-permute-start.22 = (bf16[2,768,384]{2,1,0:T(8,128)(2,1)}, bf16[2,768,384]{2,1,0:T(8,128)(2,1)}, u32[]{:S(2)}, u32[]{:S(2)}) collective-permute-start(bf16[2,768,384]{2,1,0:T(8,128)(2,1)} %pad_maximum_fusion.6), channel_id=1, source_target_pairs={{0,2},{1,3},{2,0},{3,1},{4,6},{5,7},{6,4},{7,5},{8,10},{9,11},{10,... | collective-permute-start | bytes 3538952 | tf_op jit(solution)/shard_map/ppermute | solution.py:36
  127.6 77.7 %collective-permute-start.21 = (bf16[2,768,384]{2,1,0:T(8,128)(2,1)}, bf16[2,768,384]{2,1,0:T(8,128)(2,1)}, u32[]{:S(2)}, u32[]{:S(2)}) collective-permute-start(bf16[2,768,384]{2,1,0:T(8,128)(2,1)} %pad_maximum_fusion.6), channel_id=1, source_target_pairs={{0,1},{1,0},{2,3},{3,2},{4,5},{5,4},{6,7},{7,6},{8,9},{9,8},{10,11... | collective-permute-start | bytes 3538952 | tf_op jit(solution)/shard_map/ppermute | solution.py:36
  130.1 83.7 %collective-permute-start.26 = (bf16[2,384,768]{2,1,0:T(8,128)(2,1)}, bf16[2,384,768]{2,1,0:T(8,128)(2,1)}, u32[]{:S(2)}, u32[]{:S(2)}) collective-permute-start(bf16[2,384,768]{2,1,0:T(8,128)(2,1)} %pad_maximum_fusion.7), channel_id=1, source_target_pairs={{0,2},{1,3},{2,0},{3,1},{4,6},{5,7},{6,4},{7,5},{8,10},{9,11},{10,... | collective-permute-start | bytes 3538952 | tf_op jit(solution)/shard_map/ppermute | solution.py:36
  133.7 17.1 %collective-permute-start.18 = (bf16[512,768]{0,1:T(8,128)(2,1)}, bf16[512,768]{0,1:T(8,128)(2,1)}, u32[]{:S(2)}, u32[]{:S(2)}) collective-permute-start(bf16[512,768]{0,1:T(8,128)(2,1)} %collective-permute-done.17), channel_id=1, source_target_pairs={{0,1},{1,0},{2,3},{3,2},{4,5},{5,4},{6,7},{7,6},{8,9},{9,8},{10,11... | collective-permute-start | bytes 2359304 | tf_op jit(solution)/shard_map/ppermute | solution.py:36
  150.8 66.9 %collective-permute-start.25 = (bf16[2,384,768]{2,1,0:T(8,128)(2,1)}, bf16[2,384,768]{2,1,0:T(8,128)(2,1)}, u32[]{:S(2)}, u32[]{:S(2)}) collective-permute-start(bf16[2,384,768]{2,1,0:T(8,128)(2,1)} %pad_maximum_fusion.7), channel_id=1, source_target_pairs={{0,1},{1,0},{2,3},{3,2},{4,5},{5,4},{6,7},{7,6},{8,9},{9,8},{10,11... | collective-permute-start | bytes 3538952 | tf_op jit(solution)/shard_map/ppermute | solution.py:36
  204.4 43.9 %collective-permute-start.7 = (bf16[2048,192]{0,1:T(8,128)(2,1)}, bf16[2048,192]{0,1:T(8,128)(2,1)}, u32[]{:S(2)}, u32[]{:S(2)}) collective-permute-start(bf16[2048,192]{0,1:T(8,128)(2,1)} %copy.255), channel_id=1, source_target_pairs={{0,2},{1,3},{2,0},{3,1},{4,6},{5,7},{6,4},{7,5},{8,10},{9,11},{10,... | collective-permute-start | bytes 2359304 | tf_op jit(solution)/shard_map/ppermute | solution.py:36
  205.3 28.9 %collective-permute-start.39 = (bf16[192,768]{1,0:T(8,128)(2,1)}, bf16[192,768]{1,0:T(8,128)(2,1)}, u32[]{:S(2)}, u32[]{:S(2)}) collective-permute-start(bf16[192,768]{1,0:T(8,128)(2,1)} %get-tuple-element.152), channel_id=1, source_target_pairs={{0,28},{4,24},{8,20},{12,16},{16,12},{20,8},{24,4},{28,0},{1,29},{... | collective-permute-start | bytes 884744 | tf_op jit(solution)/shard_map/ppermute | solution.py:36
  213.7 39.5 %collective-permute-start.35 = (bf16[192,768]{1,0:T(8,128)(2,1)}, bf16[192,768]{1,0:T(8,128)(2,1)S(1)}, u32[]{:S(2)}, u32[]{:S(2)}) collective-permute-start(bf16[192,768]{1,0:T(8,128)(2,1)} %get-tuple-element.153), channel_id=1, source_target_pairs={{0,20},{4,16},{8,28},{12,24},{16,4},{20,0},{24,12},{28,8},{1,21},{... | collective-permute-start | bytes 884744 | tf_op jit(solution)/shard_map/ppermute | solution.py:36
  217.7 55.9 %collective-permute-start.6 = (bf16[2048,192]{0,1:T(8,128)(2,1)}, bf16[2048,192]{0,1:T(8,128)(2,1)}, u32[]{:S(2)}, u32[]{:S(2)}) collective-permute-start(bf16[2048,192]{0,1:T(8,128)(2,1)} %copy.255), channel_id=1, source_target_pairs={{0,1},{1,0},{2,3},{3,2},{4,5},{5,4},{6,7},{7,6},{8,9},{9,8},{10,11... | collective-permute-start | bytes 2359304 | tf_op jit(solution)/shard_map/ppermute | solution.py:36
  217.7 40.5 %collective-permute-start.34 = (bf16[192,768]{1,0:T(8,128)(2,1)S(1)}, bf16[192,768]{1,0:T(8,128)(2,1)S(1)}, u32[]{:S(2)}, u32[]{:S(2)}) collective-permute-start(bf16[192,768]{1,0:T(8,128)(2,1)S(1)} %copy-done.83), channel_id=1, source_target_pairs={{0,16},{4,20},{8,24},{12,28},{16,0},{20,4},{24,8},{28,12},{1,17},{... | collective-permute-start | bytes 884744 | tf_op jit(solution)/shard_map/ppermute | solution.py:36
  234.3 30.3 %collective-permute-start.31 = (bf16[192,768]{1,0:T(8,128)(2,1)S(1)}, bf16[192,768]{1,0:T(8,128)(2,1)S(1)}, u32[]{:S(2)}, u32[]{:S(2)}) collective-permute-start(bf16[192,768]{1,0:T(8,128)(2,1)S(1)} %copy-done.82), channel_id=1, source_target_pairs={{0,12},{4,8},{8,4},{12,0},{16,28},{20,24},{24,20},{28,16},{1,13},{... | collective-permute-start | bytes 884744 | tf_op jit(solution)/shard_map/ppermute | solution.py:36
  248.3 27.5 %collective-permute-start.8 = (bf16[2048,192]{0,1:T(8,128)(2,1)}, bf16[2048,192]{0,1:T(8,128)(2,1)}, u32[]{:S(2)}, u32[]{:S(2)}) collective-permute-start(bf16[2048,192]{0,1:T(8,128)(2,1)} %collective-permute-done.7), channel_id=1, source_target_pairs={{0,1},{1,0},{2,3},{3,2},{4,5},{5,4},{6,7},{7,6},{8,9},{9,8},{10,11... | collective-permute-start | bytes 2359304 | tf_op jit(solution)/shard_map/ppermute | solution.py:36
  253.2 17.4 %collective-permute-start.30 = (bf16[192,768]{1,0:T(8,128)(2,1)S(1)}, bf16[192,768]{1,0:T(8,128)(2,1)S(1)}, u32[]{:S(2)}, u32[]{:S(2)}) collective-permute-start(bf16[192,768]{1,0:T(8,128)(2,1)S(1)} %get-tuple-element.156), channel_id=1, source_target_pairs={{0,8},{4,12},{8,0},{12,4},{16,24},{20,28},{24,16},{28,20},{1,9},{5... | collective-permute-start | bytes 884744 | tf_op jit(solution)/shard_map/ppermute | solution.py:36
  258.2 20.3 %collective-permute-start.12 = (bf16[192,768]{1,0:T(8,128)(2,1)}, bf16[192,768]{1,0:T(8,128)(2,1)}, u32[]{:S(2)}, u32[]{:S(2)}) collective-permute-start(bf16[192,768]{1,0:T(8,128)(2,1)} %dynamic_update_slice.91), channel_id=1, source_target_pairs={{0,1},{1,0},{2,3},{3,2},{4,5},{5,4},{6,7},{7,6},{8,9},{9,8},{10,11... | collective-permute-start | bytes 884744 | tf_op jit(solution)/shard_map/ppermute | solution.py:36
  264.6 14.0 %collective-permute-start.14 = (bf16[192,768]{1,0:T(8,128)(2,1)}, bf16[192,768]{1,0:T(8,128)(2,1)}, u32[]{:S(2)}, u32[]{:S(2)}) collective-permute-start(bf16[192,768]{1,0:T(8,128)(2,1)} %collective-permute-done.13), channel_id=1, source_target_pairs={{0,1},{1,0},{2,3},{3,2},{4,5},{5,4},{6,7},{7,6},{8,9},{9,8},{10,11... | collective-permute-start | bytes 884744 | tf_op jit(solution)/shard_map/ppermute | solution.py:36
  270.6 26.4 %collective-permute-start.19 = (bf16[192,768]{1,0:T(8,128)(2,1)}, bf16[192,768]{1,0:T(8,128)(2,1)}, u32[]{:S(2)}, u32[]{:S(2)}) collective-permute-start(bf16[192,768]{1,0:T(8,128)(2,1)} %get-tuple-element.157), channel_id=1, source_target_pairs={{0,4},{4,0},{8,12},{12,8},{16,20},{20,16},{24,28},{28,24},{1,5},{5... | collective-permute-start | bytes 884744 | tf_op jit(solution)/shard_map/ppermute | solution.py:36
  273.6 24.4 %collective-permute-start.23 = (bf16[2,768,384]{2,1,0:T(8,128)(2,1)}, bf16[2,768,384]{2,1,0:T(8,128)(2,1)}, u32[]{:S(2)}, u32[]{:S(2)}) collective-permute-start(bf16[2,768,384]{2,1,0:T(8,128)(2,1)} %collective-permute-done.22), channel_id=1, source_target_pairs={{0,1},{1,0},{2,3},{3,2},{4,5},{5,4},{6,7},{7,6},{8,9},{9,8},{10,11... | collective-permute-start | bytes 3538952 | tf_op jit(solution)/shard_map/ppermute | solution.py:36
  275.9 24.6 %collective-permute-start.27 = (bf16[2,384,768]{2,1,0:T(8,128)(2,1)}, bf16[2,384,768]{2,1,0:T(8,128)(2,1)}, u32[]{:S(2)}, u32[]{:S(2)}) collective-permute-start(bf16[2,384,768]{2,1,0:T(8,128)(2,1)} %collective-permute-done.26), channel_id=1, source_target_pairs={{0,1},{1,0},{2,3},{3,2},{4,5},{5,4},{6,7},{7,6},{8,9},{9,8},{10,11... | collective-permute-start | bytes 3538952 | tf_op jit(solution)/shard_map/ppermute | solution.py:36
  295.7 14.9 %collective-permute-start.15 = (bf16[192,768]{1,0:T(8,128)(2,1)S(1)}, bf16[192,768]{1,0:T(8,128)(2,1)S(1)}, u32[]{:S(2)}, u32[]{:S(2)}) collective-permute-start(bf16[192,768]{1,0:T(8,128)(2,1)S(1)} %get-tuple-element.141), channel_id=1, source_target_pairs={{0,4},{4,0},{8,12},{12,8},{16,20},{20,16},{24,28},{28,24},{1,5},{5... | collective-permute-start | bytes 884744 | tf_op jit(solution)/shard_map/ppermute | solution.py:36
  302.9 97.2 %collective-permute-start.37 = (bf16[192,768]{1,0:T(8,128)(2,1)S(1)}, bf16[192,768]{1,0:T(8,128)(2,1)S(1)}, u32[]{:S(2)}, u32[]{:S(2)}) collective-permute-start(bf16[192,768]{1,0:T(8,128)(2,1)S(1)} %get-tuple-element.135), channel_id=1, source_target_pairs={{0,28},{4,24},{8,20},{12,16},{16,12},{20,8},{24,4},{28,0},{1,29},{... | collective-permute-start | bytes 884744 | tf_op jit(solution)/shard_map/ppermute | solution.py:36
  304.5 95.7 %collective-permute-start.36 = (bf16[192,768]{1,0:T(8,128)(2,1)S(1)}, bf16[192,768]{1,0:T(8,128)(2,1)S(1)}, u32[]{:S(2)}, u32[]{:S(2)}) collective-permute-start(bf16[192,768]{1,0:T(8,128)(2,1)S(1)} %get-tuple-element.136), channel_id=1, source_target_pairs={{0,24},{4,28},{8,16},{12,20},{16,8},{20,12},{24,0},{28,4},{1,25},{... | collective-permute-start | bytes 884744 | tf_op jit(solution)/shard_map/ppermute | solution.py:36
  307.0 43.8 %collective-permute-start.33 = (bf16[192,768]{1,0:T(8,128)(2,1)S(1)}, bf16[192,768]{1,0:T(8,128)(2,1)S(1)}, u32[]{:S(2)}, u32[]{:S(2)}) collective-permute-start(bf16[192,768]{1,0:T(8,128)(2,1)S(1)} %get-tuple-element.137), channel_id=1, source_target_pairs={{0,20},{4,16},{8,28},{12,24},{16,4},{20,0},{24,12},{28,8},{1,21},{... | collective-permute-start | bytes 884744 | tf_op jit(solution)/shard_map/ppermute | solution.py:36
  307.0 48.5 %collective-permute-start.32 = (bf16[192,768]{1,0:T(8,128)(2,1)S(1)}, bf16[192,768]{1,0:T(8,128)(2,1)S(1)}, u32[]{:S(2)}, u32[]{:S(2)}) collective-permute-start(bf16[192,768]{1,0:T(8,128)(2,1)S(1)} %get-tuple-element.138), channel_id=1, source_target_pairs={{0,16},{4,20},{8,24},{12,28},{16,0},{20,4},{24,8},{28,12},{1,17},{... | collective-permute-start | bytes 884744 | tf_op jit(solution)/shard_map/ppermute | solution.py:36
  310.6 64.8 %collective-permute-start.29 = (bf16[192,768]{1,0:T(8,128)(2,1)S(1)}, bf16[192,768]{1,0:T(8,128)(2,1)S(1)}, u32[]{:S(2)}, u32[]{:S(2)}) collective-permute-start(bf16[192,768]{1,0:T(8,128)(2,1)S(1)} %get-tuple-element.139), channel_id=1, source_target_pairs={{0,12},{4,8},{8,4},{12,0},{16,28},{20,24},{24,20},{28,16},{1,13},{... | collective-permute-start | bytes 884744 | tf_op jit(solution)/shard_map/ppermute | solution.py:36
  350.7 24.7 %collective-permute-start.28 = (bf16[192,768]{1,0:T(8,128)(2,1)S(1)}, bf16[192,768]{1,0:T(8,128)(2,1)S(1)}, u32[]{:S(2)}, u32[]{:S(2)}) collective-permute-start(bf16[192,768]{1,0:T(8,128)(2,1)S(1)} %get-tuple-element.140), channel_id=1, source_target_pairs={{0,8},{4,12},{8,0},{12,4},{16,24},{20,28},{24,16},{28,20},{1,9},{5... | collective-permute-start | bytes 884744 | tf_op jit(solution)/shard_map/ppermute | solution.py:36
  443.0 88.3 %collective-permute-start.55 = (bf16[192,768]{1,0:T(8,128)(2,1)}, bf16[192,768]{1,0:T(8,128)(2,1)S(1)}, u32[]{:S(2)}, u32[]{:S(2)}) collective-permute-start(bf16[192,768]{1,0:T(8,128)(2,1)} %get-tuple-element.182), channel_id=1, source_target_pairs={{0,28},{4,24},{8,20},{12,16},{16,12},{20,8},{24,4},{28,0},{1,29},{... | collective-permute-start | bytes 884744 | tf_op jit(solution)/shard_map/ppermute | solution.py:36
  445.6 83.2 %collective-permute-start.54 = (bf16[192,768]{1,0:T(8,128)(2,1)}, bf16[192,768]{1,0:T(8,128)(2,1)S(1)}, u32[]{:S(2)}, u32[]{:S(2)}) collective-permute-start(bf16[192,768]{1,0:T(8,128)(2,1)} %get-tuple-element.183), channel_id=1, source_target_pairs={{0,24},{4,28},{8,16},{12,20},{16,8},{20,12},{24,0},{28,4},{1,25},{... | collective-permute-start | bytes 884744 | tf_op jit(solution)/shard_map/ppermute | solution.py:36
  450.3 42.9 %collective-permute-start.51 = (bf16[192,768]{1,0:T(8,128)(2,1)S(1)}, bf16[192,768]{1,0:T(8,128)(2,1)S(1)}, u32[]{:S(2)}, u32[]{:S(2)}) collective-permute-start(bf16[192,768]{1,0:T(8,128)(2,1)S(1)} %get-tuple-element.186), channel_id=1, source_target_pairs={{0,12},{4,8},{8,4},{12,0},{16,28},{20,24},{24,20},{28,16},{1,13},{... | collective-permute-start | bytes 884744 | tf_op jit(solution)/shard_map/ppermute | solution.py:36
  450.4 40.2 %collective-permute-start.50 = (bf16[192,768]{1,0:T(8,128)(2,1)S(1)}, bf16[192,768]{1,0:T(8,128)(2,1)S(1)}, u32[]{:S(2)}, u32[]{:S(2)}) collective-permute-start(bf16[192,768]{1,0:T(8,128)(2,1)S(1)} %get-tuple-element.187), channel_id=1, source_target_pairs={{0,8},{4,12},{8,0},{12,4},{16,24},{20,28},{24,16},{28,20},{1,9},{5... | collective-permute-start | bytes 884744 | tf_op jit(solution)/shard_map/ppermute | solution.py:36
  453.7 35.9 %collective-permute-start.49 = (bf16[192,768]{1,0:T(8,128)(2,1)S(1)}, bf16[192,768]{1,0:T(8,128)(2,1)S(1)}, u32[]{:S(2)}, u32[]{:S(2)}) collective-permute-start(bf16[192,768]{1,0:T(8,128)(2,1)S(1)} %get-tuple-element.188), channel_id=1, source_target_pairs={{0,4},{4,0},{8,12},{12,8},{16,20},{20,16},{24,28},{28,24},{1,5},{5... | collective-permute-start | bytes 884744 | tf_op jit(solution)/shard_map/ppermute | solution.py:36
  489.7 26.0 %collective-permute-start.52 = (bf16[192,768]{1,0:T(8,128)(2,1)S(1)}, bf16[192,768]{1,0:T(8,128)(2,1)S(1)}, u32[]{:S(2)}, u32[]{:S(2)}) collective-permute-start(bf16[192,768]{1,0:T(8,128)(2,1)S(1)} %copy-done.86), channel_id=1, source_target_pairs={{0,16},{4,20},{8,24},{12,28},{16,0},{20,4},{24,8},{28,12},{1,17},{... | collective-permute-start | bytes 884744 | tf_op jit(solution)/shard_map/ppermute | solution.py:36
  490.7 38.1 %collective-permute-start.53 = (bf16[192,768]{1,0:T(8,128)(2,1)S(1)}, bf16[192,768]{1,0:T(8,128)(2,1)S(1)}, u32[]{:S(2)}, u32[]{:S(2)}) collective-permute-start(bf16[192,768]{1,0:T(8,128)(2,1)S(1)} %copy-done.85), channel_id=1, source_target_pairs={{0,20},{4,16},{8,28},{12,24},{16,4},{20,0},{24,12},{28,8},{1,21},{... | collective-permute-start | bytes 884744 | tf_op jit(solution)/shard_map/ppermute | solution.py:36
  493.3 82.3 %collective-permute-start.46 = (bf16[192,768]{1,0:T(8,128)(2,1)S(1)}, bf16[192,768]{1,0:T(8,128)(2,1)S(1)}, u32[]{:S(2)}, u32[]{:S(2)}) collective-permute-start(bf16[192,768]{1,0:T(8,128)(2,1)S(1)} %get-tuple-element.143), channel_id=1, source_target_pairs={{0,28},{4,24},{8,20},{12,16},{16,12},{20,8},{24,4},{28,0},{1,29},{... | collective-permute-start | bytes 884744 | tf_op jit(solution)/shard_map/ppermute | solution.py:36
  515.6 59.9 %collective-permute-start.45 = (bf16[192,768]{1,0:T(8,128)(2,1)S(1)}, bf16[192,768]{1,0:T(8,128)(2,1)S(1)}, u32[]{:S(2)}, u32[]{:S(2)}) collective-permute-start(bf16[192,768]{1,0:T(8,128)(2,1)S(1)} %get-tuple-element.144), channel_id=1, source_target_pairs={{0,24},{4,28},{8,16},{12,20},{16,8},{20,12},{24,0},{28,4},{1,25},{... | collective-permute-start | bytes 884744 | tf_op jit(solution)/shard_map/ppermute | solution.py:36
  528.8 20.7 %collective-permute-start.42 = (bf16[192,768]{1,0:T(8,128)(2,1)S(1)}, bf16[192,768]{1,0:T(8,128)(2,1)S(1)}, u32[]{:S(2)}, u32[]{:S(2)}) collective-permute-start(bf16[192,768]{1,0:T(8,128)(2,1)S(1)} %get-tuple-element.147), channel_id=1, source_target_pairs={{0,12},{4,8},{8,4},{12,0},{16,28},{20,24},{24,20},{28,16},{1,13},{... | collective-permute-start | bytes 884744 | tf_op jit(solution)/shard_map/ppermute | solution.py:36
  528.8 19.9 %collective-permute-start.41 = (bf16[192,768]{1,0:T(8,128)(2,1)S(1)}, bf16[192,768]{1,0:T(8,128)(2,1)S(1)}, u32[]{:S(2)}, u32[]{:S(2)}) collective-permute-start(bf16[192,768]{1,0:T(8,128)(2,1)S(1)} %get-tuple-element.148), channel_id=1, source_target_pairs={{0,8},{4,12},{8,0},{12,4},{16,24},{20,28},{24,16},{28,20},{1,9},{5... | collective-permute-start | bytes 884744 | tf_op jit(solution)/shard_map/ppermute | solution.py:36
  531.3 13.5 %collective-permute-start.40 = (bf16[192,768]{1,0:T(8,128)(2,1)S(1)}, bf16[192,768]{1,0:T(8,128)(2,1)S(1)}, u32[]{:S(2)}, u32[]{:S(2)}) collective-permute-start(bf16[192,768]{1,0:T(8,128)(2,1)S(1)} %get-tuple-element.149), channel_id=1, source_target_pairs={{0,4},{4,0},{8,12},{12,8},{16,20},{20,16},{24,28},{28,24},{1,5},{5... | collective-permute-start | bytes 884744 | tf_op jit(solution)/shard_map/ppermute | solution.py:36
  544.8 24.3 %collective-permute-start.43 = (bf16[192,768]{1,0:T(8,128)(2,1)S(1)}, bf16[192,768]{1,0:T(8,128)(2,1)S(1)}, u32[]{:S(2)}, u32[]{:S(2)}) collective-permute-start(bf16[192,768]{1,0:T(8,128)(2,1)S(1)} %get-tuple-element.146), channel_id=1, source_target_pairs={{0,16},{4,20},{8,24},{12,28},{16,0},{20,4},{24,8},{28,12},{1,17},{... | collective-permute-start | bytes 884744 | tf_op jit(solution)/shard_map/ppermute | solution.py:36
  548.8 26.7 %collective-permute-start.44 = (bf16[192,768]{1,0:T(8,128)(2,1)S(1)}, bf16[192,768]{1,0:T(8,128)(2,1)S(1)}, u32[]{:S(2)}, u32[]{:S(2)}) collective-permute-start(bf16[192,768]{1,0:T(8,128)(2,1)S(1)} %get-tuple-element.145), channel_id=1, source_target_pairs={{0,20},{4,16},{8,28},{12,24},{16,4},{20,0},{24,12},{28,8},{1,21},{... | collective-permute-start | bytes 884744 | tf_op jit(solution)/shard_map/ppermute | solution.py:36
  549.5 44.3 %collective-permute-start.80 = (bf16[2,2,384,768]{3,2,1,0:T(8,128)(2,1)}, bf16[2,2,384,768]{3,2,1,0:T(8,128)(2,1)}, u32[]{:S(2)}, u32[]{:S(2)}) collective-permute-start(bf16[2,2,384,768]{3,2,1,0:T(8,128)(2,1)} %pad_maximum_fusion.3), channel_id=1, source_target_pairs={{0,1},{1,0},{2,3},{3,2},{4,5},{5,4},{6,7},{7,6},{8,9},{9,8},{10,11... | collective-permute-start | bytes 7077896 | tf_op jit(solution)/shard_map/ppermute | solution.py:36
  569.2 31.1 %collective-permute-start.77 = (bf16[2,2,768,384]{3,2,1,0:T(8,128)(2,1)}, bf16[2,2,768,384]{3,2,1,0:T(8,128)(2,1)}, u32[]{:S(2)}, u32[]{:S(2)}) collective-permute-start(bf16[2,2,768,384]{3,2,1,0:T(8,128)(2,1)} %pad_maximum_fusion.2), channel_id=1, source_target_pairs={{0,1},{1,0},{2,3},{3,2},{4,5},{5,4},{6,7},{7,6},{8,9},{9,8},{10,11... | collective-permute-start | bytes 7077896 | tf_op jit(solution)/shard_map/ppermute | solution.py:36
  584.8 13.4 %collective-permute-start.47 = (bf16[2,512,768]{1,2,0:T(8,128)(2,1)}, bf16[2,512,768]{1,2,0:T(8,128)(2,1)}, u32[]{:S(2)}, u32[]{:S(2)}) collective-permute-start(bf16[2,512,768]{1,2,0:T(8,128)(2,1)} %pad_maximum_fusion.4), channel_id=1, source_target_pairs={{0,1},{1,0},{2,3},{3,2},{4,5},{5,4},{6,7},{7,6},{8,9},{9,8},{10,11... | collective-permute-start | bytes 4718600 | tf_op jit(solution)/shard_map/ppermute | solution.py:36
  586.0 37.4 %collective-permute-start.57 = (bf16[1024,768]{0,1:T(8,128)(2,1)S(1)}, bf16[1024,768]{0,1:T(8,128)(2,1)}, u32[]{:S(2)}, u32[]{:S(2)}) collective-permute-start(bf16[1024,768]{0,1:T(8,128)(2,1)S(1)} %add_convert_fusion.1), channel_id=1, source_target_pairs={{0,2},{1,3},{2,0},{3,1},{4,6},{5,7},{6,4},{7,5},{8,10},{9,11},{10,... | collective-permute-start | bytes 4718600 | tf_op jit(solution)/shard_map/ppermute | solution.py:36
  596.5 52.1 %collective-permute-start.81 = (bf16[2,384,768]{2,1,0:T(8,128)(2,1)S(1)}, bf16[2,384,768]{2,1,0:T(8,128)(2,1)S(1)}, u32[]{:S(2)}, u32[]{:S(2)}) collective-permute-start(bf16[2,384,768]{2,1,0:T(8,128)(2,1)S(1)} %fusion.54), channel_id=1, source_target_pairs={{0,2},{1,3},{2,0},{3,1},{4,6},{5,7},{6,4},{7,5},{8,10},{9,11},{10,... | collective-permute-start | bytes 3538952 | tf_op jit(solution)/shard_map/ppermute | solution.py:36
  603.0 70.8 %collective-permute-start.78 = (bf16[2,768,384]{2,1,0:T(8,128)(2,1)S(1)}, bf16[2,768,384]{2,1,0:T(8,128)(2,1)S(1)}, u32[]{:S(2)}, u32[]{:S(2)}) collective-permute-start(bf16[2,768,384]{2,1,0:T(8,128)(2,1)S(1)} %fusion.58), channel_id=1, source_target_pairs={{0,2},{1,3},{2,0},{3,1},{4,6},{5,7},{6,4},{7,5},{8,10},{9,11},{10,... | collective-permute-start | bytes 3538952 | tf_op jit(solution)/shard_map/ppermute | solution.py:36
  604.2 85.6 %collective-permute-start.48 = (bf16[512,768]{0,1:T(8,128)(2,1)S(1)}, bf16[512,768]{0,1:T(8,128)(2,1)S(1)}, u32[]{:S(2)}, u32[]{:S(2)}) collective-permute-start(bf16[512,768]{0,1:T(8,128)(2,1)S(1)} %fusion.80), channel_id=1, source_target_pairs={{0,2},{1,3},{2,0},{3,1},{4,6},{5,7},{6,4},{7,5},{8,10},{9,11},{10,... | collective-permute-start | bytes 2359304 | tf_op jit(solution)/shard_map/ppermute | solution.py:36
  626.7 73.7 %collective-permute-start.58 = (bf16[1024,768]{0,1:T(8,128)(2,1)}, bf16[1024,768]{0,1:T(8,128)(2,1)}, u32[]{:S(2)}, u32[]{:S(2)}) collective-permute-start(bf16[1024,768]{0,1:T(8,128)(2,1)} %add_convert_fusion), channel_id=1, source_target_pairs={{0,1},{1,0},{2,3},{3,2},{4,5},{5,4},{6,7},{7,6},{8,9},{9,8},{10,11... | collective-permute-start | bytes 4718600 | tf_op jit(solution)/shard_map/ppermute | solution.py:36
  649.9 45.2 %collective-permute-start.82 = (bf16[384,768]{1,0:T(8,128)(2,1)}, bf16[384,768]{1,0:T(8,128)(2,1)}, u32[]{:S(2)}, u32[]{:S(2)}) collective-permute-start(bf16[384,768]{1,0:T(8,128)(2,1)} %fusion.123), channel_id=1, source_target_pairs={{0,4},{4,0},{8,12},{12,8},{16,20},{20,16},{24,28},{28,24},{1,5},{5... | collective-permute-start | bytes 1769480 | tf_op jit(solution)/shard_map/ppermute | solution.py:36
  675.2 22.7 %collective-permute-start.79 = (bf16[768,384]{1,0:T(8,128)(2,1)}, bf16[768,384]{1,0:T(8,128)(2,1)}, u32[]{:S(2)}, u32[]{:S(2)}) collective-permute-start(bf16[768,384]{1,0:T(8,128)(2,1)} %fusion.122), channel_id=1, source_target_pairs={{0,4},{4,0},{8,12},{12,8},{16,20},{20,16},{24,28},{28,24},{1,5},{5... | collective-permute-start | bytes 1769480 | tf_op jit(solution)/shard_map/ppermute | solution.py:36
  765.1 32.6 %collective-permute-start.59 = (bf16[2,512,768]{1,2,0:T(8,128)(2,1)}, bf16[2,512,768]{1,2,0:T(8,128)(2,1)}, u32[]{:S(2)}, u32[]{:S(2)}) collective-permute-start(bf16[2,512,768]{1,2,0:T(8,128)(2,1)} %pad_maximum_fusion.5), channel_id=1, source_target_pairs={{0,1},{1,0},{2,3},{3,2},{4,5},{5,4},{6,7},{7,6},{8,9},{9,8},{10,11... | collective-permute-start | bytes 4718600 | tf_op jit(solution)/shard_map/ppermute | solution.py:36
  778.2 18.5 %collective-permute-start.74 = (bf16[4,192,96]{2,1,0:T(8,128)(2,1)}, bf16[4,192,96]{2,1,0:T(8,128)(2,1)}, u32[]{:S(2)}, u32[]{:S(2)}) collective-permute-start(bf16[4,192,96]{2,1,0:T(8,128)(2,1)} %pad_maximum_fusion.23), channel_id=1, source_target_pairs={{0,4},{4,0},{8,12},{12,8},{16,20},{20,16},{24,28},{28,24},{1,5},{5... | collective-permute-start | bytes 442376 | tf_op jit(solution)/shard_map/ppermute | solution.py:36
  801.6 16.1 %collective-permute-start.60 = (bf16[512,768]{0,1:T(8,128)(2,1)S(1)}, bf16[512,768]{0,1:T(8,128)(2,1)S(1)}, u32[]{:S(2)}, u32[]{:S(2)}) collective-permute-start(bf16[512,768]{0,1:T(8,128)(2,1)S(1)} %fusion.76), channel_id=1, source_target_pairs={{0,2},{1,3},{2,0},{3,1},{4,6},{5,7},{6,4},{7,5},{8,10},{9,11},{10,... | collective-permute-start | bytes 2359304 | tf_op jit(solution)/shard_map/ppermute | solution.py:36
  (135 other events, 1316.4 us)

commit v2 on v1

v2 whole, which is shorter than its diff:
```python
import functools

import jax
import jax.numpy as jnp
from jax import lax
from jax.experimental import pallas as pl
from jax.experimental.pallas import tpu as pltpu
from jax.sharding import PartitionSpec as P

HD = 64
EPS = 1e-05
MASKED = -1000000000.0
ROOT_HALF = 0.7071067811865476
INV_ROOT_TAU = 0.3989422804014327
BLOCK = 512
LOW = jnp.bfloat16
WIDE = jnp.float32
LITTLE = pl.CostEstimate(flops=10**6, bytes_accessed=10**5, transcendentals=0)
NT = (((1,), (1,)), ((), ()))
TN = (((0,), (0,)), ((), ()))
ERF_P = 0.4
ERF_C = (
    0.11596113048765463,
    0.08091125192311208,
    0.23413842084756234,
    -0.1854556415158047,
    0.35457470270248115,
    -0.10012987827403336,
)


def mm(a, b):
    return jnp.dot(a, b, preferred_element_type=WIDE)


def mm_nt(a, b):
    return lax.dot_general(a, b, NT, preferred_element_type=WIDE)


def mm_tn(a, b):
    return lax.dot_general(a, b, TN, preferred_element_type=WIDE)


def spot_of(k):
    return (k % 2) * 2 + k // 2


def select_piece(spot, refs, out):
    for n, ref in enumerate(refs):

        @pl.when((spot == n) if n < 2 else (spot >= 2))
        def _(ref=ref):
            out[...] = ref[...]


def piece_specs(rows, features, spot):
    still = pl.BlockSpec((rows, features), lambda *i: (0, 0))
    return [still, still, pl.BlockSpec((rows, features), lambda *i: (jnp.maximum(spot(*i) - 2, 0), 0))]


def norm_parts(values):
    centred = values - jnp.mean(values, axis=-1, keepdims=True)
    rstd = lax.rsqrt(jnp.mean(centred * centred, axis=-1, keepdims=True) + EPS)
    return centred * rstd, rstd


def attend_kernel(
    meta_ref, start_ref, x_own_ref, x_far_ref, x_near_ref, gain_ref, w_ref,
    h_ref, qt_ref, q_ref, k_ref, kt_ref, v_ref, ctx_ref, ctxt_ref, lse_ref, k_all, vt_all, x_ref,
):
    step = pl.program_id(0)
    heads = qt_ref.shape[0]
    width = heads * HD
    start = start_ref[...]
    key_iota = lax.broadcasted_iota(jnp.int32, (BLOCK, BLOCK), 0)
    query_iota = lax.broadcasted_iota(jnp.int32, (BLOCK, BLOCK), 1)

    select_piece(spot_of(step ^ meta_ref[0]), (x_own_ref, x_far_ref, x_near_ref), x_ref)
    normed, _ = norm_parts(x_ref[...].astype(WIDE))
    h_one = (normed * gain_ref[...]).astype(LOW)
    h_ref[...] = h_one
    here = pl.ds(pl.multiple_of(step * BLOCK, BLOCK), BLOCK)
    q = mm(h_one, w_ref[:, :width]).astype(LOW) * (HD**-0.5)
    k = mm(h_one, w_ref[:, width : 2 * width]).astype(LOW)
    v = mm(h_one, w_ref[:, 2 * width : 3 * width]).astype(LOW)
    q = q.astype(LOW)
    q_t, k_t, v_t = q.T, k.T, v.T
    for h in range(heads):
        rows = slice(h * HD, (h + 1) * HD)
        qt_ref[h] = q_t[rows]
        q_ref[h] = q[:, rows]
        kt_ref[h] = k_t[rows]
        k_ref[h] = k[:, rows]
        k_all[h, here, :] = k[:, rows]
        v_ref[h] = v[:, rows]
        vt_all[h, :, here] = v_t[rows]

    def block(j, carry, last):
        base = pl.multiple_of(j * BLOCK, BLOCK)
        allowed = key_iota + base >= start
        if last:
            allowed = allowed & (key_iota <= query_iota)
        out = []
        for h in range(heads):
            top, total, acc = carry[h]
            scores = mm(k_all[h, pl.ds(base, BLOCK), :], qt_ref[h])
            scores = jnp.where(allowed, scores, MASKED)
            peak = jnp.maximum(top, jnp.max(scores, axis=0, keepdims=True))
            raised = jnp.exp(scores - peak)
            fade = jnp.exp(top - peak)
            total = total * fade + jnp.sum(raised, axis=0, keepdims=True)
            acc = acc * fade + mm(vt_all[h, :, pl.ds(base, BLOCK)], raised.astype(LOW))
            out.append((peak, total, acc))
        return tuple(out)

    carry = tuple(
        (
            jnp.full((1, BLOCK), MASKED, WIDE),
            jnp.zeros((1, BLOCK), WIDE),
            jnp.zeros((HD, BLOCK), WIDE),
        )
        for _ in range(heads)
    )
    carry = lax.fori_loop(meta_ref[1 + step], step, lambda j, c: block(j, c, False), carry)
    carry = block(step, carry, True)
    for h in range(heads):
        top, total, acc = carry[h]
        acc = acc / total
        ctxt_ref[h] = acc
        lse_ref[h] = top + jnp.log(total)
        ctx_ref[h * HD : (h + 1) * HD, :] = acc.astype(LOW)


def attend(meta, start, pieces, gain, weights, width):
    features = gain.shape[1]
    rows = 4 * BLOCK
    heads = width // HD
    spot = lambda i, m: spot_of(i ^ m[0])
    place = lambda i, m: (spot(i, m), 0)

    by_column = pl.BlockSpec((heads, HD, BLOCK), lambda i, m: (0, 0, i))
    by_row = pl.BlockSpec((heads, BLOCK, HD), lambda i, m: (0, i, 0))
    grid_spec = pltpu.PrefetchScalarGridSpec(
        num_scalar_prefetch=1,
        grid=(rows // BLOCK,),
        in_specs=[
            pl.BlockSpec((1, BLOCK), lambda i, m: (0, i)),
            *piece_specs(BLOCK, features, spot),
            pl.BlockSpec((1, features), lambda i, m: (0, 0)),
            pl.BlockSpec(weights.shape, lambda i, m: (0, 0)),
        ],
        out_specs=[
            pl.BlockSpec((BLOCK, features), place),
            by_column,
            by_row,
            by_row,
            by_column,
            by_row,
            pl.BlockSpec((width, BLOCK), lambda i, m: (0, spot(i, m))),
            by_column,
            pl.BlockSpec((heads, 1, BLOCK), lambda i, m: (0, 0, i)),
        ],
        scratch_shapes=[
            pltpu.VMEM((heads, rows, HD), LOW),
            pltpu.VMEM((heads, HD, rows), LOW),
            pltpu.VMEM((BLOCK, features), LOW),
        ],
    )
    tall = jax.ShapeDtypeStruct((heads, rows, HD), LOW)
    flat = jax.ShapeDtypeStruct((heads, HD, rows), LOW)
    return pl.pallas_call(
        attend_kernel,
        grid_spec=grid_spec,
        out_shape=[
            jax.ShapeDtypeStruct((rows, features), LOW),
            flat,
            tall,
            tall,
            flat,
            tall,
            jax.ShapeDtypeStruct((width, rows), LOW),
            jax.ShapeDtypeStruct((heads, HD, rows), WIDE),
            jax.ShapeDtypeStruct((heads, 1, rows), WIDE),
        ],
        compiler_params=pltpu.CompilerParams(vmem_limit_bytes=50 * 2**20),
        cost_estimate=LITTLE,
    )(meta, start, *pieces, gain, weights)


def attend_back_kernel(
    meta_ref, start_ref, x_ref, dh_mine_ref, dh_near_ref, c_own_ref, c_far_ref, c_near_ref,
    gain_ref, wo_ref, qt_ref, q_ref, k_ref, kt_ref, v_ref, ctxt_ref, lse_ref,
    d_ref, dx_ref, dgain_ref, dqkv_ref, dq_all, dk_acc, dv_acc, dh_ref, c_ref,
):
    step = pl.program_id(0)
    heads = qt_ref.shape[0]
    start = start_ref[...]
    key_iota = lax.broadcasted_iota(jnp.int32, (BLOCK, BLOCK), 0)
    query_iota = lax.broadcasted_iota(jnp.int32, (BLOCK, BLOCK), 1)

    @pl.when(step == 0)
    def _():
        dk_acc[...] = jnp.zeros_like(dk_acc)
        dv_acc[...] = jnp.zeros_like(dv_acc)

    spot = spot_of(step ^ meta_ref[0])
    select_piece(spot, (c_own_ref, c_far_ref, c_near_ref), c_ref)

    @pl.when(spot < 2)
    def _():
        dh_ref[...] = dh_mine_ref[...]

    @pl.when(spot >= 2)
    def _():
        dh_ref[...] = dh_near_ref[...]

    normed, rstd = norm_parts(x_ref[...])
    dh = dh_ref[...].astype(WIDE)
    scaled = dh * gain_ref[...]
    mean_plain = jnp.mean(scaled, axis=-1, keepdims=True)
    mean_normed = jnp.mean(scaled * normed, axis=-1, keepdims=True)
    dx = c_ref[...].astype(WIDE) + rstd * (scaled - mean_plain - normed * mean_normed)
    dattn = dx.astype(LOW)
    d_ref[...] = dattn

    @pl.when(step == meta_ref[0])
    def _():
        dx_ref[...] = dx
        dgain_ref[...] = jnp.sum(dh * normed, axis=0, keepdims=True)

    g_all = mm(dattn, wo_ref[:, 3 * heads * HD :]).astype(LOW)
    gt_all = g_all.T
    g = [g_all[:, h * HD : (h + 1) * HD] for h in range(heads)]
    gt = [gt_all[h * HD : (h + 1) * HD] for h in range(heads)]
    delta = [
        jnp.sum(gt[h].astype(WIDE) * ctxt_ref[h], axis=0, keepdims=True) for h in range(heads)
    ]

    def block(j, carry, last):
        base = pl.multiple_of(j * BLOCK, BLOCK)
        rows = pl.ds(base, BLOCK)
        allowed = key_iota + base >= start
        if last:
            allowed = allowed & (key_iota <= query_iota)
        out = []
        for h in range(heads):
            scores = mm(k_ref[h, rows, :], qt_ref[h])
            probs = jnp.where(allowed, jnp.exp(scores - lse_ref[h]), 0.0)
            slopes = mm(v_ref[h, rows, :], gt[h])
            score_grads = (probs * (slopes - delta[h])).astype(LOW)
            dv_acc[h, rows, :] += mm(probs.astype(LOW), g[h])
            dk_acc[h, rows, :] += mm(score_grads, q_ref[h])
            out.append(carry[h] + mm(kt_ref[h, :, rows], score_grads))
        return tuple(out)

    carry = tuple(jnp.zeros((HD, BLOCK), WIDE) for _ in range(heads))
    carry = lax.fori_loop(meta_ref[1 + step], step, lambda j, c: block(j, c, False), carry)
    carry = block(step, carry, True)
    here = pl.ds(pl.multiple_of(step * BLOCK, BLOCK), BLOCK)
    scale = HD**-0.5
    for h in range(heads):
        dq_all[h, here, :] = (carry[h] * scale).T

    @pl.when(step == pl.num_programs(0) - 1)
    def _():
        for n in range(4):
            rows = slice(n * BLOCK, (n + 1) * BLOCK)
            to = pl.ds(pl.multiple_of(spot_of(n ^ meta_ref[0]) * BLOCK, BLOCK), BLOCK)
            dqkv_ref[to, :] = jnp.concatenate(
                [part[h, rows, :] for part in (dq_all, dk_acc, dv_acc) for h in range(heads)],
                axis=1,
            ).astype(LOW)


def attend_back(meta, start, x_one, dh_pieces, c_pieces, gain, weights, qt, q, keys, kt, values, ctxt, lse):
    heads, _, rows = qt.shape
    features = x_one.shape[1]
    spot = lambda i, m: spot_of(i ^ m[0])
    place = lambda i, m: (spot(i, m), 0)

    by_column = pl.BlockSpec((heads, HD, BLOCK), lambda i, m: (0, 0, i))
    by_row = pl.BlockSpec((heads, BLOCK, HD), lambda i, m: (0, i, 0))
    by_place = pl.BlockSpec((BLOCK, features), place)
    whole = lambda *shape: pl.BlockSpec(shape, lambda i, m: (0,) * len(shape))
    grid_spec = pltpu.PrefetchScalarGridSpec(
        num_scalar_prefetch=1,
        grid=(rows // BLOCK,),
        in_specs=[
            pl.BlockSpec((1, BLOCK), lambda i, m: (0, i)),
            by_place,
            pl.BlockSpec((BLOCK, features), lambda i, m: (jnp.minimum(spot(i, m), 1), 0)),
            pl.BlockSpec((BLOCK, features), lambda i, m: (jnp.maximum(spot(i, m) - 2, 0), 0)),
            *piece_specs(BLOCK, features, spot),
            whole(1, features),
            whole(*weights.shape),
            by_column,
            by_row,
            whole(heads, rows, HD),
            whole(heads, HD, rows),
            whole(heads, rows, HD),
            by_column,
            pl.BlockSpec((heads, 1, BLOCK), lambda i, m: (0, 0, i)),
        ],
        out_specs=[
            by_place,
            whole(rows // 4, features),
            whole(1, features),
            whole(rows, 3 * heads * HD),
        ],
        scratch_shapes=[pltpu.VMEM((heads, rows, HD), WIDE)] * 3
        + [pltpu.VMEM((BLOCK, features), LOW)] * 2,
    )
    return pl.pallas_call(
        attend_back_kernel,
        grid_spec=grid_spec,
        out_shape=[
            jax.ShapeDtypeStruct((rows, features), LOW),
            jax.ShapeDtypeStruct((rows // 4, features), WIDE),
            jax.ShapeDtypeStruct((1, features), WIDE),
            jax.ShapeDtypeStruct((rows, 3 * heads * HD), LOW),
        ],
        compiler_params=pltpu.CompilerParams(vmem_limit_bytes=60 * 2**20),
        cost_estimate=LITTLE,
    )(meta, start, x_one, *dh_pieces, *c_pieces, gain, weights, qt, q, keys, kt, values, ctxt, lse)


def hot_rows(placed_ref, line, first, rows):
    spots = lax.broadcasted_iota(jnp.int32, (rows, placed_ref.shape[1]), 0) + first
    hot = (placed_ref[line : line + 1, :] == spots) | (placed_ref[line + 1 : line + 2, :] == spots)
    return jnp.where(hot, 1.0, 0.0).astype(LOW)


def send_kernel(
    index_ref, placed_ref, c_own_ref, c_far_ref, c_near_ref, c_ref, in_order_ref, picks_ref, rows_all
):
    step = pl.program_id(0)
    share = in_order_ref.shape[0]
    size = c_own_ref.shape[0]

    @pl.when(step == 0)
    def _():
        rows_all[:size, :] = c_own_ref[...]
        rows_all[size : 2 * size, :] = c_far_ref[...]
        rows_all[2 * size :, :] = c_near_ref[...]

    hot = hot_rows(placed_ref, 2, step * share, share)
    in_order_ref[...] = hot
    picks_ref[...] = hot
    c_ref[0, :share, :] = mm(hot, rows_all[...]).astype(LOW)
    sums = mm_nt(placed_ref[...].astype(WIDE).astype(LOW), hot)[4:5]
    line = jnp.concatenate(
        [sums, jnp.zeros((1, c_ref.shape[2] - share), WIDE)], axis=1
    ) if c_ref.shape[2] > share else sums
    c_ref[0, share:, :] = jnp.broadcast_to(line, (16, c_ref.shape[2])).astype(LOW)


def send_rows(index, placed, pieces, count, share):
    size, features = pieces[0].shape
    total = 4 * size
    whole = lambda *shape: pl.BlockSpec(shape, lambda p, o: (0,) * len(shape))
    grid_spec = pltpu.PrefetchScalarGridSpec(
        num_scalar_prefetch=1,
        grid=(count,),
        in_specs=[
            whole(*placed.shape),
            whole(size, features),
            whole(size, features),
            whole(2 * size, features),
        ],
        out_specs=[
            pl.BlockSpec((1, share + 16, features), lambda p, o: (p, 0, 0)),
            pl.BlockSpec((share, total), lambda p, o: (p, 0)),
            pl.BlockSpec((share, total), lambda p, o: (p ^ o[0], 0)),
        ],
        scratch_shapes=[pltpu.VMEM((total, features), LOW)],
    )
    return pl.pallas_call(
        send_kernel,
        grid_spec=grid_spec,
        out_shape=[
            jax.ShapeDtypeStruct((count, share + 16, features), LOW),
            jax.ShapeDtypeStruct((count * share, total), LOW),
            jax.ShapeDtypeStruct((count * share, total), LOW),
        ],
        compiler_params=pltpu.CompilerParams(vmem_limit_bytes=40 * 2**20),
        cost_estimate=LITTLE,
    )(index, placed, *pieces)


def halves_kernel(odd_ref, frozen_in_ref, frozen_out_ref, fresh_in_ref, fresh_out_ref, kept_ref, given_ref):
    units = frozen_out_ref.shape[1]

    def store(out, first, second):
        out[:units, :] = first[0].T.astype(LOW)
        out[units:, :] = second[0].astype(LOW)

    @pl.when(odd_ref[0] == 0)
    def _():
        store(kept_ref, frozen_in_ref, frozen_out_ref)
        store(given_ref, fresh_in_ref, fresh_out_ref)

    @pl.when(odd_ref[0] == 1)
    def _():
        store(kept_ref, fresh_in_ref, fresh_out_ref)
        store(given_ref, frozen_in_ref, frozen_out_ref)


def expert_halves(odd, frozen_in, frozen_out, fresh_in, fresh_out):
    _, features, units = frozen_in.shape
    grid_spec = pltpu.PrefetchScalarGridSpec(
        num_scalar_prefetch=1,
        grid=(1,),
        in_specs=[
            pl.BlockSpec(w.shape, lambda p, o: (0, 0, 0))
            for w in (frozen_in, frozen_out, fresh_in, fresh_out)
        ],
        out_specs=[pl.BlockSpec((2 * units, features), lambda p, o: (0, 0))] * 2,
    )
    return pl.pallas_call(
        halves_kernel,
        grid_spec=grid_spec,
        out_shape=[jax.ShapeDtypeStruct((2 * units, features), LOW)] * 2,
        compiler_params=pltpu.CompilerParams(vmem_limit_bytes=40 * 2**20),
        cost_estimate=LITTLE,
    )(odd, frozen_in, frozen_out, fresh_in, fresh_out)


def mix_kernel(count, gain_ref, placed_ref, *refs):
    context_refs, weight_refs, piece_refs = refs[:4], refs[4:8], refs[8:11]
    x_one_ref, taken_refs, x_ref, h_all = refs[11], refs[12 : 12 + count], refs[-2], refs[-1]
    step = pl.program_id(0)
    size = x_ref.shape[0]
    select_piece(step, piece_refs, x_ref)
    attn = mm(context_refs[0][...].T, weight_refs[0][...])
    for n in range(1, 4):
        attn = attn + mm(context_refs[n][...].T, weight_refs[n][...])
    x_one = x_ref[...].astype(WIDE) + attn
    x_one_ref[...] = x_one
    normed, _ = norm_parts(x_one)
    h_all[pl.ds(pl.multiple_of(step * size, size), size), :] = (normed * gain_ref[...]).astype(LOW)

    @pl.when(step == pl.num_programs(0) - 1)
    def _():
        share = taken_refs[0].shape[0]
        for k in range(count):
            hot = hot_rows(placed_ref, 0, k * share, share)
            taken_refs[k][...] = mm(hot, h_all[...]).astype(LOW)


def mix(placed, pieces, gain, contexts, weights, count, share):
    width, rows = contexts[0].shape
    features = gain.shape[1]
    size = rows // 4

    def context_spec(n):
        return pl.BlockSpec((width, size), lambda i: (0, i ^ n))

    def weight_spec(n):
        return pl.BlockSpec((width, features), lambda i: (n // 3, 0))

    return pl.pallas_call(
        functools.partial(mix_kernel, count),
        grid=(4,),
        in_specs=[
            pl.BlockSpec((1, features), lambda i: (0, 0)),
            pl.BlockSpec(placed.shape, lambda i: (0, 0)),
        ]
        + [context_spec(n) for n in range(4)]
        + [weight_spec(n) for n in range(4)]
        + piece_specs(size, features, lambda i: i),
        scratch_shapes=[pltpu.VMEM((size, features), LOW), pltpu.VMEM((rows, features), LOW)],
        out_specs=[pl.BlockSpec((size, features), lambda i: (i, 0))]
        + [pl.BlockSpec((share, features), lambda i: (0, 0))] * count,
        out_shape=[jax.ShapeDtypeStruct((rows, features), WIDE)]
        + [jax.ShapeDtypeStruct((share, features), LOW)] * count,
        compiler_params=pltpu.CompilerParams(vmem_limit_bytes=40 * 2**20),
        cost_estimate=LITTLE,
    )(gain, placed, *contexts, *weights, weights[2], *pieces)


def expert_kernel(count, meta_ref, *refs):
    x_refs, refs = refs[:count], refs[count:]
    c_refs, refs = refs[:count], refs[count:]
    wg_ref, weight_refs = refs[0], refs[1:9]
    refs = refs[-(15 + count) :]
    a_ref, du_ref, xs_ref, dy_ref, mark_ref, y_ref = refs[:6]
    dx_refs, refs = refs[6 : 6 + count], refs[6 + count :]
    cs, w1_all, w2_all, sems, acc, acc_y, dots, others, gate = refs
    step, steps = pl.program_id(0), pl.num_programs(0)
    rows, kinds = xs_ref.shape[0], wg_ref.shape[1]
    share = rows // count
    units = w1_all.shape[1] // 2
    lanes = lax.broadcasted_iota(jnp.int32, (rows, kinds), 1)
    own = meta_ref[0]

    def fetches(n):
        slot = n % 2
        for m in range(2):
            span = slice(m * units, (m + 1) * units)
            for p, target in enumerate((w1_all, w2_all)):
                yield pltpu.make_async_copy(
                    weight_refs[2 * n + m].at[p * units : (p + 1) * units],
                    target.at[slot, span],
                    sems.at[slot, 2 * m + p],
                )

    def kinds_of():
        sums = [
            c_refs[n][0, share : share + 16, : -(-share // 128) * 128].astype(WIDE).T[:share, :1]
            for n in range(count)
        ]
        sums = jnp.concatenate(sums, axis=0).astype(jnp.int32)
        return lanes == own, lanes == sums - own

    @pl.when(step == 0)
    def _():
        for copy in fetches(0):
            copy.start()
        for n in range(count):
            xs_ref[n * share : (n + 1) * share, :] = x_refs[n][...]
            cs[n * share : (n + 1) * share, :] = c_refs[n][0, :share, :]
        logits = mm(xs_ref[...], wg_ref[...].astype(LOW))
        here, there = kinds_of()
        mine = jnp.sum(jnp.where(here, logits, 0.0), axis=1, keepdims=True)
        theirs = jnp.sum(jnp.where(there, logits, 0.0), axis=1, keepdims=True)
        peak = jnp.maximum(mine, theirs)
        mine, theirs = jnp.exp(mine - peak), jnp.exp(theirs - peak)
        gate[...] = mine / (mine + theirs)
        others[...] = theirs / (mine + theirs)
        dy_ref[...] = (gate[...] * cs[...].astype(WIDE)).astype(LOW)
        acc[...] = jnp.zeros_like(acc)
        acc_y[...] = jnp.zeros_like(acc_y)
        dots[...] = jnp.zeros_like(dots)

    for n in range(4):

        @pl.when(step == n)
        def _(n=n):
            if n < 3:
                for copy in fetches(n + 1):
                    copy.start()
            for copy in fetches(n):
                copy.wait()

    w1, w2 = w1_all[step % 2], w2_all[step % 2]
    u = mm_nt(xs_ref[...], w1)
    da = mm_nt(cs[...], w2)
    bell = jnp.exp(u * u * -0.5)
    t = 1.0 / (1.0 + jnp.abs(u) * (ERF_P * ROOT_HALF))
    tail = ERF_C[-1] * t
    for coefficient in ERF_C[-2::-1]:
        tail = (tail + coefficient) * t
    tail = tail * bell
    part = jnp.where(u >= 0.0, 1.0 - tail, tail)
    a = (u * part).astype(LOW)
    slope = part + u * bell * INV_ROOT_TAU
    dots[...] += jnp.sum(a.astype(WIDE) * da, axis=1, keepdims=True)
    du = (gate[...] * da * slope).astype(LOW)
    a_ref[...] = a
    du_ref[...] = du
    acc_y[...] += mm(a, w2)
    acc[...] += mm(du, w1)

    @pl.when(step == steps - 1)
    def _():
        pull = gate[...] * others[...] * dots[...]
        here, there = kinds_of()
        marks = jnp.where(here, pull, 0.0) - jnp.where(there, pull, 0.0)
        mark_ref[...] = marks
        high = marks.astype(LOW)
        rest = (marks - high.astype(WIDE)).astype(LOW)
        gate_low = wg_ref[...].astype(LOW)
        dx = acc[...] + mm_nt(high, gate_low) + mm_nt(rest, gate_low)
        for n in range(count):
            dx_refs[n][...] = dx[n * share : (n + 1) * share].astype(LOW)
        y = (gate[...] * acc_y[...]).astype(LOW)
        for n in range(count):
            base = pl.multiple_of((meta_ref[1] % count ^ n) * share, 16)
            y_ref[pl.ds(base, share), :] = y[n * share : (n + 1) * share]


def run_experts(meta, xs, c, gate_weight, weights, chunk, chunks, held):
    count = len(xs)
    share, features = xs[0].shape
    rows = count * share
    units = weights[0].shape[0]
    kinds = gate_weight.shape[1]
    whole = lambda *shape: pl.BlockSpec(shape, lambda p, o: (0,) * len(shape))
    by_piece = pl.BlockSpec((rows, units), lambda p, o: (chunk, p))
    by_chunk = lambda width: pl.BlockSpec((rows, width), lambda p, o: (chunk, 0))
    anywhere = pl.BlockSpec(memory_space=pl.ANY)

    def c_spec(n):
        return pl.BlockSpec((1,) + c.shape[1:], lambda p, o: (o[1] ^ (chunk * count + n), 0, 0))

    operands = [meta, *xs, *([c] * count), gate_weight, *weights]
    in_specs = (
        [whole(share, features)] * count
        + [c_spec(n) for n in range(count)]
        + [whole(features, kinds)]
        + [anywhere] * 8
    )
    aliases = {}
    if held is not None:
        aliases = {len(operands) + n: n for n in range(6)}
        operands += held
        in_specs += [anywhere] * 6
    every = chunks * rows
    grid_spec = pltpu.PrefetchScalarGridSpec(
        num_scalar_prefetch=1,
        grid=(4,),
        in_specs=in_specs,
        out_specs=[
            by_piece,
            by_piece,
            by_chunk(features),
            by_chunk(features),
            by_chunk(kinds),
            pl.BlockSpec((rows, features), lambda p, o: (o[1] // count ^ chunk, 0)),
            *([whole(share, features)] * count),
        ],
        scratch_shapes=[
            pltpu.VMEM((rows, features), LOW),
            pltpu.VMEM((2, units, features), LOW),
            pltpu.VMEM((2, units, features), LOW),
            pltpu.SemaphoreType.DMA((2, 4)),
            pltpu.VMEM((rows, features), WIDE),
            pltpu.VMEM((rows, features), WIDE),
            pltpu.VMEM((rows, 1), WIDE),
            pltpu.VMEM((rows, 1), WIDE),
            pltpu.VMEM((rows, 1), WIDE),
        ],
    )
    out = pl.pallas_call(
        functools.partial(expert_kernel, count),
        grid_spec=grid_spec,
        out_shape=[
            jax.ShapeDtypeStruct((every, 4 * units), LOW),
            jax.ShapeDtypeStruct((every, 4 * units), LOW),
            jax.ShapeDtypeStruct((every, features), LOW),
            jax.ShapeDtypeStruct((every, features), LOW),
            jax.ShapeDtypeStruct((every, kinds), WIDE),
            jax.ShapeDtypeStruct((every, features), LOW),
            *([jax.ShapeDtypeStruct((share, features), LOW)] * count),
        ],
        input_output_aliases=aliases,
        compiler_params=pltpu.CompilerParams(vmem_limit_bytes=58 * 2**20),
        cost_estimate=LITTLE,
    )(*operands)
    return out[:6], out[6:]


def expert_grads_kernel(a_ref, du_ref, x_ref, dy_ref, give_ref, keep_ref):
    step = pl.program_id(0)
    units = a_ref.shape[1] // 2

    def store(out, kind):
        first = mm_tn(du_ref[...], x_ref[...])
        second = mm_tn(a_ref[...], dy_ref[...])
        for m in range(2):
            span = slice(m * units, (m + 1) * units)
            out[0, m, :units, :] = first[span].astype(kind)
            out[0, m, units:, :] = second[span].astype(kind)

    @pl.when(step < 2)
    def _():
        store(give_ref, LOW)

    @pl.when(step >= 2)
    def _():
        store(keep_ref, WIDE)


def expert_grads(hidden, hidden_grads, x, dy):
    rows, features = x.shape
    units = hidden.shape[1] // 4
    piece = pl.BlockSpec((rows, units), lambda p: (0, p ^ 2))
    all_rows = pl.BlockSpec((rows, features), lambda p: (0, 0))
    shape = (2, 2, units, features)
    return pl.pallas_call(
        expert_grads_kernel,
        grid=(4,),
        in_specs=[piece, piece, all_rows, all_rows],
        out_specs=[
            pl.BlockSpec((1,) + shape[1:], lambda p: (jnp.minimum(p, 1), 0, 0, 0)),
            pl.BlockSpec((1,) + shape[1:], lambda p: (jnp.maximum(p - 2, 0), 0, 0, 0)),
        ],
        out_shape=[jax.ShapeDtypeStruct(shape, LOW), jax.ShapeDtypeStruct(shape, WIDE)],
        compiler_params=pltpu.CompilerParams(vmem_limit_bytes=58 * 2**20),
        cost_estimate=LITTLE,
    )(hidden, hidden_grads, x, dy)


def weight_kernel(
    index_ref, h_ref, dqkv_ref, d_ref, ctx_ref, w_ref, keep_ref, give_ref, dots_ref, acc
):
    step = pl.program_id(0)
    width = dqkv_ref.shape[1]

    @pl.when(step == 0)
    def _():
        acc[...] = jnp.zeros_like(acc)

    acc[:, :width] += mm_tn(h_ref[...], dqkv_ref[...])
    acc[:, width:] += mm_tn(d_ref[...], ctx_ref[...].T)

    @pl.when(step == pl.num_programs(0) - 1)
    def _():
        count, size = 2 * keep_ref.shape[0], keep_ref.shape[1]
        dots_ref[...] = jnp.sum(
            acc[:, :width] * w_ref[:, :width].astype(WIDE), axis=1, keepdims=True
        )
        for n in range(count):
            k = sum(((n >> b) & 1) * (count >> 1 >> b) for b in range(count.bit_length() - 1))
            part = acc[pl.ds(pl.multiple_of((index_ref[0] ^ k) * size, 8), size), :]
            if n < count // 2:
                keep_ref[n] = part
            else:
                give_ref[n - count // 2] = part.astype(LOW)


def weight_grads(index, h_one, dqkv, dattn, context, weights, count):
    rows, features = h_one.shape
    width, narrow = dqkv.shape[1], context.shape[0]
    size = features // count
    by_row = lambda columns: pl.BlockSpec((BLOCK, columns), lambda i, o: (i, 0))
    share = pl.BlockSpec((count // 2, size, width + narrow), lambda i, o: (0, 0, 0))
    grid_spec = pltpu.PrefetchScalarGridSpec(
        num_scalar_prefetch=1,
        grid=(rows // BLOCK,),
        in_specs=[
            by_row(features),
            by_row(width),
            by_row(features),
            pl.BlockSpec((narrow, BLOCK), lambda i, o: (0, i)),
            pl.BlockSpec(weights.shape, lambda i, o: (0, 0)),
        ],
        out_specs=[share, share, pl.BlockSpec((features, 1), lambda i, o: (0, 0))],
        scratch_shapes=[pltpu.VMEM((features, width + narrow), WIDE)],
    )
    return pl.pallas_call(
        weight_kernel,
        grid_spec=grid_spec,
        out_shape=[
            jax.ShapeDtypeStruct((count // 2, size, width + narrow), WIDE),
            jax.ShapeDtypeStruct((count // 2, size, width + narrow), LOW),
            jax.ShapeDtypeStruct((features, 1), WIDE),
        ],
        compiler_params=pltpu.CompilerParams(vmem_limit_bytes=40 * 2**20),
        cost_estimate=LITTLE,
    )(index, h_one, dqkv, dattn, context, weights)


def finish_kernel(keep_ref, near_ref, far_ref, x_ref, gain_ref, dx_ref, out_ref):
    dh = keep_ref[...] + near_ref[...].astype(WIDE) + far_ref[...].astype(WIDE)
    normed, rstd = norm_parts(x_ref[...].astype(WIDE))
    scaled = dh * gain_ref[...]
    mean_plain = jnp.mean(scaled, axis=-1, keepdims=True)
    mean_normed = jnp.mean(scaled * normed, axis=-1, keepdims=True)
    out_ref[...] = dx_ref[...] + rstd * (scaled - mean_plain - normed * mean_normed)


def finish(keep, near, far, x, gain, dx):
    rows, features = x.shape
    size = 256
    by_row = pl.BlockSpec((size, features), lambda i: (i, 0))
    return pl.pallas_call(
        finish_kernel,
        grid=(rows // size,),
        in_specs=[by_row] * 4 + [pl.BlockSpec((1, features), lambda i: (0, 0)), by_row],
        out_specs=by_row,
        out_shape=jax.ShapeDtypeStruct((rows, features), WIDE),
        cost_estimate=LITTLE,
    )(keep, near, far, x, gain, dx)


def flip(array, axis, bits):
    size = lax.axis_size(axis)
    return lax.ppermute(array, axis, [(i, i ^ bits) for i in range(size)])


def flip_head_where(array, bits, odd):
    heads, rest = lax.axis_size("head"), lax.axis_size("dp")
    pairs = [
        (d * heads + h, d * heads + (h ^ bits)) for d in range(odd, rest, 2) for h in range(heads)
    ]
    return lax.ppermute(array, ("dp", "head"), pairs)


def after(value, *others):
    return lax.optimization_barrier((value, *others))[0]


def joined(pieces):
    return jnp.concatenate(pieces, axis=0)


def sum_everywhere(value):
    for axis in ("head", "dp"):
        bits = 1
        while bits < lax.axis_size(axis):
            value = value + flip(value, axis, bits)
            bits *= 2
    return value


def sum_over_dp_scattered(keep, give):
    bits = 1
    while True:
        keep = keep + flip(give, "dp", bits).astype(WIDE)
        count = keep.shape[0]
        if count == 1:
            return keep[0]
        keep, give = keep[: count // 2], keep[count // 2 :].astype(LOW)
        bits *= 2


def split_dot(a, marks):
    high = marks.astype(LOW)
    rest = (marks - high.astype(WIDE)).astype(LOW)
    return mm_tn(a, high) + mm_tn(a, rest)


def body(
    block_input,
    gain_one,
    gain_two,
    qkv_weight,
    out_weight,
    gate_weight,
    frozen_in,
    frozen_out,
    fresh_in,
    fresh_out,
    routes,
    doc_lengths,
    cotangent,
):
    own_rows, features = block_input.shape
    head_count, dp_count = lax.axis_size("head"), lax.axis_size("dp")
    head_index, dp_index = lax.axis_index("head"), lax.axis_index("dp")
    total = own_rows * head_count
    half = total // 2
    kinds = gate_weight.shape[1]
    share = 3 * total // kinds // head_count
    width = qkv_weight.shape[2]
    odd = dp_index % 2
    gain_one, gain_two = gain_one[None], gain_two[None]

    c_far = flip(cotangent, "head", 2)
    c_near = flip(joined([cotangent, c_far]), "head", 1)
    c_pieces = [cotangent, c_far, c_near]
    x_far = flip(after(block_input, c_far), "head", 2)

    piece = jnp.concatenate(
        [qkv_weight[0], qkv_weight[1], qkv_weight[2], out_weight.T], axis=1
    ).astype(LOW)
    weights = lax.all_to_all(
        jnp.broadcast_to(piece[None], (dp_count,) + piece.shape), "dp", 0, 0, tiled=True
    ).reshape(features, 4 * width)

    tokens = jnp.arange(total, dtype=jnp.int32)
    hits = (routes[:, :, None] == jnp.arange(kinds, dtype=jnp.int32)).astype(LOW)
    earlier = (tokens[:, None] > tokens[None, :]).astype(LOW)
    counts = mm(earlier, hits.reshape(total, 2 * kinds)).reshape(total, 2, kinds)
    firsts = jnp.sum(hits[:, 0].astype(WIDE), axis=0)
    counts = counts + jnp.stack([jnp.zeros_like(firsts), firsts])[None]
    slots = jnp.sum(counts * hits.astype(WIDE), axis=2).astype(jnp.int32)
    hosts = routes % (kinds // 2) * 2 + routes // (kinds // 2)
    held_here = slots % head_count == head_index
    near_places = jnp.where(held_here, (hosts ^ dp_index) * share + slots // head_count, -1)
    places = jnp.where(held_here, hosts * share + slots // head_count, -1)
    placed = jnp.concatenate([near_places, places, jnp.sum(routes, axis=1, keepdims=True)], axis=1)
    placed = placed.reshape(head_count, own_rows, 5)
    placed = joined(
        [
            lax.dynamic_index_in_dim(placed, head_index ^ k, 0, keepdims=False)
            for k in (0, 2, 1, 3)
        ]
    ).T
    placed = jnp.pad(placed, ((0, 3), (0, 0)))
    here_dp = dp_index.astype(jnp.int32)[None]

    kept, given = expert_halves(
        odd.astype(jnp.int32)[None], frozen_in, frozen_out, fresh_in, fresh_out
    )

    c_out, in_order, picks = send_rows(here_dp, placed, after(c_pieces, kept), dp_count, share)
    x_far = after(x_far, c_out)
    x_near = flip(joined([block_input, x_far]), "head", 1)
    x_pieces = [block_input, x_far, x_near]
    c_in = lax.all_to_all(c_out, "dp", 0, 0, tiled=True)

    come = flip(after(given, weights), "dp", 1)
    kept_far = flip(after(kept, x_far), "head", 2)

    near_kept = flip(kept, "head", 1)
    out = weights[:, 3 * width :].T
    out_far = flip(out, "head", 2)
    out_near = flip(joined([out, out_far]), "head", 1)

    ends = jnp.cumsum(doc_lengths[0])
    start = jnp.max(jnp.where(tokens[:, None] >= ends[None], ends[None], 0), axis=1)
    meta = jnp.concatenate([head_index[None], start[::BLOCK] // BLOCK]).astype(jnp.int32)
    start = start[None]
    h_one, qt, queries, keys, kt, values, context, context_t, log_totals = attend(
        meta, start, x_pieces, gain_one, weights, width
    )
    near_context = flip(context, "head", 1)
    far_context = flip(after(context, kept_far, out_far, near_kept), "head", 2)
    last_context = flip(far_context, "head", 1)
    come_far = flip(after(come, far_context), "head", 2)
    near_come = flip(come, "head", 1)
    last_kept = flip(kept_far, "head", 1)
    per = dp_count // 4
    x_one, *x_out = mix(
        placed, x_pieces, after(gain_two, c_in, near_come, last_kept),
        [context, far_context, near_context, last_context], [out, out_far, out_near],
        dp_count, share,
    )
    last_come = flip(after(come_far, x_one), "head", 1)
    halves = [kept, come, kept_far, come_far, near_kept, near_come, last_kept, last_come]

    x_parts = [x_out[0]] + [flip(x_out[k], "dp", k) for k in range(1, 3 * per)]
    held, dx_parts = None, []
    own_kind = dp_index // 2 + odd * (kinds // 2)
    expert_meta = jnp.stack([own_kind, dp_index]).astype(jnp.int32)
    for n in range(4):
        ks = range(n * per, (n + 1) * per)
        xs = [x_parts[k] for k in ks]
        if n >= 2:
            xs[0] = after(xs[0], *dx_parts[(n - 2) * per : (n - 1) * per])
        held, dx = run_experts(
            expert_meta, xs, c_in, gate_weight, halves, n, 4, held
        )
        dx_parts += [part if k == 0 else flip(part, "dp", k) for k, part in zip(ks, dx)]
        if n == 0:
            ready = x_parts[2 * per :]
            x_parts += [
                flip(after(x_out[k], dx[0], *ready), "dp", k) for k in range(3 * per, dp_count)
            ]

    hidden, hidden_grads, x_all, dy_all, marks, gated = held
    cut = 2 * per * share
    early = joined(dx_parts[: 2 * per])
    there = mm_tn(picks[:cut, half:], early)
    here = mm_tn(picks[:cut, :half], early)
    give, keep = expert_grads(hidden, hidden_grads, after(x_all, there, here), dy_all)
    late = joined([after(dx_parts[2 * per], give), *dx_parts[2 * per + 1 :]])
    there = (there + mm_tn(picks[cut:, half:], late)).astype(LOW)
    sent = flip(there, "head", 1)
    here = (here + mm_tn(picks[cut:, :half], late) + sent.astype(WIDE)).astype(LOW)
    across = flip(here, "head", 2)

    give = [flip(after(give[:, n], here), "head", 1) for n in (1, 0)]
    leave = [(keep[n, 1] + give[0][n].astype(WIDE)).astype(LOW) for n in (1, 0)]
    gated = after(gated, *leave)
    leave = [flip(part, "dp", 1) for part in leave]
    across = across.astype(WIDE)
    dh_mine = (here.astype(WIDE) + joined([across[own_rows:], across[:own_rows]])).astype(LOW)
    dh_near = flip(dh_mine, "head", 1)
    stay = (keep[1, 0] + give[1][1].astype(WIDE)).astype(LOW)
    crossed = flip_head_where(after(stay, dh_mine), 2, 1) + flip_head_where(after(leave[0], dh_mine), 2, 0)
    home = jnp.where(odd == 1, keep[0, 0] + give[1][0].astype(WIDE), leave[1].astype(WIDE))

    dattn, dx_one, grad_gain_two, dqkv = attend_back(
        meta, start, x_one, [dh_mine, dh_near], c_pieces, gain_two, weights,
        qt, queries, keys, kt, values, context_t, log_totals,
    )
    back = weights[:, : 3 * width]
    keep, give, dots = weight_grads(
        dp_index.astype(jnp.int32)[None], h_one, dqkv, dattn, context, weights, dp_count
    )
    sent = flip(mm_nt(after(dqkv, give)[half:], back).astype(LOW), "head", 1)
    mine = mm_nt(dqkv[:half], back)
    far = flip((mine[own_rows:] + sent[own_rows:].astype(WIDE)).astype(LOW), "head", 2)
    grad_input = finish(mine[:own_rows], sent[:own_rows], far, block_input, gain_one, dx_one)
    grads = sum_over_dp_scattered(keep, give)
    grad_qkv = jnp.stack([grads[:, n * width : (n + 1) * width] for n in range(3)])
    grad_out_weight = grads[:, 3 * width :].T

    gated = lax.all_to_all(
        gated.reshape(dp_count, share, features), "dp", 0, 0, tiled=True
    ).reshape(dp_count * share, features)
    gated = after(gated, mine)
    sent = flip(mm_tn(in_order[:, half:], gated).astype(LOW), "head", 1).astype(WIDE)
    mine = mm_tn(in_order[:, :half], gated) + sent
    mixture = mine[:own_rows] + flip(mine[own_rows:].astype(LOW), "head", 2).astype(WIDE)
    result = (x_one[:own_rows] + mixture).astype(LOW)
    home = home + after(crossed, mine).astype(WIDE)
    units = home.shape[0] // 2
    grad_fresh_in, grad_fresh_out = home[:units].T[None], home[units:][None]
    grad_gate = split_dot(after(x_all, give), marks)
    small = sum_everywhere(joined([dots[:, 0][None] / gain_one, grad_gain_two, grad_gate.T]))
    return (
        result,
        grad_input,
        small[0],
        small[1],
        grad_qkv,
        grad_out_weight,
        small[2:].T,
        grad_fresh_in,
        grad_fresh_out,
    )


def solution(mesh):
    return jax.shard_map(
        body,
        mesh=mesh,
        in_specs=(
            P(("dp", "head"), None),
            P(),
            P(),
            P(None, "dp", "head"),
            P("head", "dp"),
            P(),
            P("dp", None, "head"),
            P("dp", "head", None),
            P("dp", None, "head"),
            P("dp", "head", None),
            P("dp", None),
            P("dp", None),
            P(("dp", "head"), None),
        ),
        out_specs=(
            P(("dp", "head"), None),
            P(("dp", "head"), None),
            P(),
            P(),
            P(None, "dp", "head"),
            P("head", "dp"),
            P(),
            P("dp", None, "head"),
            P("dp", "head", None),
        ),
        check_vma=False,
    )
```

time: 848 us -> 521 us (0.61)
  local copies, waits for them, and re-layouts: 179 us -> 43.1 us
  waiting for transfers between devices: 204 us -> 135 us
  matrix products: 105 us -> 38.8 us
  other arithmetic: 87 us -> 22.2 us
  Pallas kernels: 142 us -> 192 us
  starting transfers between devices: 120 us -> 78.2 us
    ppermute x83 -> x49, waiting for transfers between devices: 204 us -> 124 us  [flip(): return lax.ppermute(array, axis, [(i, i ^ bits) for i in range(size)])]
    ppermute x83 -> x49, starting transfers between devices: 116 us -> 54.1 us  [flip(): return lax.ppermute(array, axis, [(i, i ^ bits) for i in range(size)])]
    pallas_call x4 -> x10, Pallas kernels: 71.7 us -> 127 us  [the longest x4 68.7 us: run_experts(): pl.pallas_call(functools.partial(expert_kernel, count), grid_spec=grid_sp...]
    dynamic_update_slice x24 -> x0, local copies, waits for them, and re-layouts: 46.1 us -> none  [the longest x16 32.5 us: over_dp(): out = lax.dynamic_update_slice_in_dim(out, one, (index ^ k) * width, axis)]
    dot_general x6 -> x1, matrix products: 39.3 us -> 1.55 us  [mm(): return jnp.dot(a, b, preferred_element_type=WIDE)]
    unnamed x274 -> x150, local copies, waits for them, and re-layouts: 60.7 us -> 31.7 us
    dot_general x15 -> x8, matrix products: 54.5 us -> 31.6 us  [mm_tn(): return lax.dot_general(a, b, TN, preferred_element_type=WIDE)]
    another operation x21 -> x3, other arithmetic: 20.9 us -> 1.49 us  [the longest x1 0.73 us: body(): jnp.stack([grads[:, n * width:(n + 1) * width] for n in range(3)])]
  transfers between devices with their start and end apart: 84 -> 54, of which waited for: 23 -> 24; matrix products, arithmetic and copies ran while one was open for 36% -> 14% of each run, Pallas kernels for 10% -> 34%
where the time goes in v2:
time: 521 us; the launch traced here: 512 us
  Pallas kernels  192 us (37%)
  waiting for transfers between devices  135 us (26%)
  starting transfers between devices  78.2 us (15%)
  local copies, waits for them, and re-layouts  43.1 us (8%)
  matrix products  38.8 us (7%)
  other arithmetic  22.2 us (4%)
    ppermute x49, waiting for transfers between devices, flip(): return lax.ppermute(array, axis, [(i, i ^ bits) for i in range(size)])  124 us
    pallas_call x4, Pallas kernels, run_experts(): pl.pallas_call(functools.partial(expert_kernel, count), grid_spec=grid_sp...  68.7 us
    ppermute x49, starting transfers between devices, flip(): return lax.ppermute(array, axis, [(i, i ^ bits) for i in range(size)])  54.1 us
    pallas_call x1, Pallas kernels, attend_back(): pl.pallas_call(attend_back_kernel, grid_spec=grid_spec, out_shape=[jax.Sh...  39.7 us
    unnamed x150, local copies, waits for them, and re-layouts  31.7 us
    dot_general x8, matrix products, mm_tn(): return lax.dot_general(a, b, TN, preferred_element_type=WIDE)  31.6 us
    pallas_call x1, Pallas kernels, attend(): pl.pallas_call(attend_kernel, grid_spec=grid_spec, out_shape=[jax.ShapeDt...  25.7 us
    pallas_call x1, Pallas kernels, expert_grads(): pl.pallas_call(expert_grads_kernel, grid=(4,), in_specs=[piece, piece, al...  22.3 us
  transfers between devices with their start and end apart: 54, of which 24 were waited for; matrix products, arithmetic and copies ran while one was open for 14% of the time, Pallas kernels for 34%

profile of v2, /device:TPU:0, one launch (start us, length us, event | category | flops | bytes accessed | tf_op | source)
XLA Modules:
  0.0 511.7 jit_solution(8637447676349187113)
XLA Ops:
  0.6 3.0 collective-permute-start
  7.0 5.8 %all-to-all-start.1 = ((bf16[8,96,768]{2,1,0:T(8,128)(2,1)}), bf16[8,96,768]{2,1,0:T(8,128)(2,1)S(1)}, u32[]{:S(2)}, u32[]{:S(2)}) async-start(bf16[8,96,768]{2,1,0:T(8,128)(2,1)} %broadcast_in_dim.56), calls=%async_computation.1 | async-start | bytes 2359296 | tf_op jit(solution)/shard_map/all_to_all | solution.py:858
  12.8 8.6 %collective-permute-done.c_far_ref = bf16[512,768]{1,0:T(8,128)(2,1)S(1)} collective-permute-done((bf16[512,768]{1,0:T(8,128)(2,1)}, bf16[512,768]{1,0:T(8,128)(2,1)S(1)}, u32[]{:S(2)}, u32[]{:S(2)}) %collective-permute-start) | collective-permute-done | bytes 786464 | tf_op jit(solution)/shard_map/ppermute | solution.py:779
  33.4 10.3 %shard_map.197 = (bf16[8,208,768]{2,1,0:T(8,128)(2,1)S(1)}, bf16[1536,2048]{1,0:T(8,128)(2,1)S(1)}, bf16[1536,2048]{1,0:T(8,128)(2,1)}) custom-call(s32[1]{0:T(128)} %bitcast.index_ref, s32[8,2048]{1,0:T(8,128)S(1)} %pad.5.placed_ref, bf16[512,768]{1,0:T(8,128)(2,1)S(1)} %copy-done.5, bf16[512,768]{1,0:T(8,128)(2,1)S(1)} %copy-done.7, ...), custom_call_target="tpu_custom_call" | custom-call | flops 1000000 | bytes 100000 | tf_op jit(solution)/shard_map/pallas_call | solution.py:377
  45.1 2.6 copy-done.27
  47.7 5.8 %all-to-all-start = ((bf16[8,208,768]{2,1,0:T(8,128)(2,1)}), bf16[8,208,768]{2,1,0:T(8,128)(2,1)}, u32[]{:S(2)}, u32[]{:S(2)}) async-start(bf16[8,208,768]{2,1,0:T(8,128)(2,1)} %copy-done.12), calls=%async_computation | async-start | bytes 5111808 | tf_op jit(solution)/shard_map/all_to_all | solution.py:892
  53.6 2.4 pad_maximum_fusion.1
  57.4 2.0 collective-permute-start.2
  61.4 25.7 %shard_map.198 = (bf16[2048,768]{1,0:T(8,128)(2,1)}, bf16[3,64,2048]{2,1,0:T(8,128)(2,1)S(1)}, bf16[3,2048,64]{2,1,0:T(8,128)(2,1)}, bf16[3,2048,64]{2,1,0:T(8,1...) custom-call(s32[5]{0:T(128)S(1)} %pad_add_fusion.1.meta_ref, ...), custom_call_target="tpu_custom_call" | custom-call | flops 1000000 | bytes 100000 | tf_op jit(solution)/shard_map/pallas_call | solution.py:171
  88.0 4.8 collective-permute-done.8
  93.6 15.4 %collective-permute-done.2.refs_6_ = bf16[768,768]{1,0:T(8,128)(2,1)} collective-permute-done((bf16[768,768]{1,0:T(8,128)(2,1)}, bf16[768,768]{1,0:T(8,128)(2,1)}, u32[]{:S(2)}, u32[]{:S(2)}) %collective-permute-start.2) | collective-permute-done | bytes 1179680 | tf_op jit(solution)/shard_map/ppermute | solution.py:779
  109.6 2.1 collective-permute-done.10.refs_1_
  117.3 15.1 %shard_map.199 = (f32[2048,768]{1,0:T(8,128)}, bf16[192,768]{1,0:T(8,128)(2,1)S(1)}, bf16[192,768]{1,0:T(8,128)(2,1)S(1)}, bf16[192,768]{1,0:T(8,128)(2,1)}, bf1...) custom-call(f32[1,768]{1,0:T(1,128)S(1)} %broadcast_in_dim.31.gain_r, ...), custom_call_target="tpu_custom_call" | custom-call | flops 1000000 | bytes 100000 | tf_op jit(solution)/shard_map/pallas_call | solution.py:461
  134.6 3.7 collective-permute-done.15.refs_8_
  138.3 2.0 collective-permute-start.14
  140.3 2.3 collective-permute-start.17
  142.7 1.9 collective-permute-start.20
  144.6 3.4 collective-permute-done.14.refs_1_
  148.0 2.5 collective-permute-start.21
  153.8 17.1 %shard_map.200 = (bf16[1536,3072]{1,0:T(8,128)(2,1)}, bf16[1536,3072]{1,0:T(8,128)(2,1)}, bf16[1536,768]{1,0:T(8,128)(2,1)}, bf16[1536,768]{1,0:T(8,128)(2,1)}, ...) custom-call(s32[2]{0:T(128)} %pad_add_fusion.2.meta_ref, ...), custom_call_target="tpu_custom_call" | custom-call | flops 1000000 | bytes 100000 | tf_op jit(solution)/shard_map/pallas_call | solution.py:634
  171.0 2.4 collective-permute-start.19
  174.2 17.3 %shard_map.201 = (bf16[1536,3072]{1,0:T(8,128)(2,1)}, bf16[1536,3072]{1,0:T(8,128)(2,1)}, bf16[1536,768]{1,0:T(8,128)(2,1)}, bf16[1536,768]{1,0:T(8,128)(2,1)}, ...) custom-call(s32[2]{0:T(128)} %pad_add_fusion.2.meta_ref, ...), custom_call_target="tpu_custom_call", output_to_operand_aliasing={{0}: (14, {}), {1}: (15, {}), {2}: (16, {}), {3}: (17, {}),... | custom-call | flops 1000000 | bytes 100000 | tf_op jit(solution)/shard_map/pallas_call | solution.py:634
  192.2 1.8 collective-permute-start.23
  196.7 5.0 collective-permute-done.22
  201.7 7.0 %collective-permute-done.23 = bf16[192,768]{1,0:T(8,128)(2,1)S(1)} collective-permute-done((bf16[192,768]{1,0:T(8,128)(2,1)}, bf16[192,768]{1,0:T(8,128)(2,1)S(1)}, u32[]{:S(2)}, u32[]{:S(2)}) %collective-permute-start.23) | collective-permute-done | bytes 294944 | tf_op jit(solution)/shard_map/ppermute | solution.py:779
  209.0 17.0 %shard_map.202 = (bf16[1536,3072]{1,0:T(8,128)(2,1)}, bf16[1536,3072]{1,0:T(8,128)(2,1)}, bf16[1536,768]{1,0:T(8,128)(2,1)}, bf16[1536,768]{1,0:T(8,128)(2,1)}, ...) custom-call(s32[2]{0:T(128)} %pad_add_fusion.2.meta_ref, ...), custom_call_target="tpu_custom_call", output_to_operand_aliasing={{0}: (14, {}), {1}: (15, {}), {2}: (16, {}), {3}: (17, {}),... | custom-call | flops 1000000 | bytes 100000 | tf_op jit(solution)/shard_map/pallas_call | solution.py:634
  226.7 17.3 %shard_map.203 = (bf16[1536,3072]{1,0:T(8,128)(2,1)}, bf16[1536,3072]{1,0:T(8,128)(2,1)}, bf16[1536,768]{1,0:T(8,128)(2,1)}, bf16[1536,768]{1,0:T(8,128)(2,1)}, ...) custom-call(s32[2]{0:T(128)} %pad_add_fusion.2.meta_ref, ...), custom_call_target="tpu_custom_call", output_to_operand_aliasing={{0}: (14, {}), {1}: (15, {}), {2}: (16, {}), {3}: (17, {}),... | custom-call | flops 1000000 | bytes 100000 | tf_op jit(solution)/shard_map/pallas_call | solution.py:634
  245.1 6.5 %collective-permute-start.26 = (bf16[192,768]{1,0:T(8,128)(2,1)S(1)}, bf16[192,768]{1,0:T(8,128)(2,1)S(1)}, u32[]{:S(2)}, u32[]{:S(2)}) collective-permute-start(bf16[192,768]{1,0:T(8,128)(2,1)S(1)} %copy-done.62), channel_id=1, source_target_pairs={{0,16},{4,20},{8,24},{12,28},{16,0},{20,4},{24,8},{28,12},{1,17},{... | collective-permute-start | bytes 884744 | tf_op jit(solution)/shard_map/ppermute | solution.py:779
  252.0 4.5 fusion.30
  256.5 4.5 fusion.32
  262.7 22.3 %shard_map.204 = (bf16[2,2,768,768]{3,2,1,0:T(8,128)(2,1)}, f32[2,2,768,768]{3,2,1,0:T(8,128)}) custom-call(bf16[1536,3072]{1,0:T(8,128)(2,1)} %get-tuple-element.151.a_ref, bf16[1536,3072]{1,0:T(8,128)(2,1)} %get-tuple-element.152.du_ref, bf16[1536,768]{1,0:T(8,128)(2,1)} %get-tuple-element.183.x_ref, bf16[1536,768]{1,0:T(8,128)(2,1)} %get-tuple-element.156.dy_ref), custom_call_target="tpu_custom_call" | custom-call | flops 1000000 | bytes 100000 | tf_op jit(solution)/shard_map/pallas_call | solution.py:680
  285.0 5.9 %collective-permute-done.27 = bf16[192,768]{1,0:T(8,128)(2,1)S(1)} collective-permute-done((bf16[192,768]{1,0:T(8,128)(2,1)S(1)}, bf16[192,768]{1,0:T(8,128)(2,1)S(1)}, u32[]{:S(2)}, u32[]{:S(2)}) %collective-permute-start.27) | collective-permute-done | bytes 294944 | tf_op jit(solution)/shard_map/ppermute | solution.py:779
  291.1 3.9 add_convert_fusion.1
  295.5 3.0 fusion.28
  300.4 3.5 collective-permute-done.31
  303.9 3.4 collective-permute-done.46
  307.3 2.6 fusion.11
  309.9 9.3 %all-to-all-start.2 = ((bf16[8,192,768]{2,1,0:T(8,128)(2,1)}), bf16[8,192,768]{2,1,0:T(8,128)(2,1)}, u32[]{:S(2)}, u32[]{:S(2)}) async-start(bf16[8,192,768]{2,1,0:T(8,128)(2,1)} %bitcast.31), calls=%async_computation.2 | async-start | bytes 4718592 | tf_op jit(solution)/shard_map/all_to_all | solution.py:982
  319.2 17.4 %collective-permute-done.32 = bf16[1024,768]{1,0:T(8,128)(2,1)S(1)} collective-permute-done((bf16[1024,768]{1,0:T(8,128)(2,1)S(1)}, bf16[1024,768]{1,0:T(8,128)(2,1)S(1)}, u32[]{:S(2)}, u32[]{:S(2)}) %collective-permute-start.32) | collective-permute-done | bytes 1572896 | tf_op jit(solution)/shard_map/ppermute | solution.py:779
  338.6 2.0 collective-permute-done.33.dh_near_ref
  341.8 39.7 %shard_map.205 = (bf16[2048,768]{1,0:T(8,128)(2,1)}, f32[512,768]{1,0:T(8,128)}, f32[1,768]{1,0:T(1,128)}, bf16[2048,576]{1,0:T(8,128)(2,1)}) custom-call(s32[5]{0:T(128)} %copy-done.26, s32[1,2048]{1,0:T(1,128)} %bitcast.118, f32[2048,768]{1,0:T(8,128)} %get-tuple-element.112.x_ref, bf16[1024,768]{1,0:T(8,128)(2,1)} %copy-done.36, ...), custom_call_target="tpu_custom_call" | custom-call | flops 1000000 | bytes 100000 | tf_op jit(solution)/shard_map/pallas_call | solution.py:313
  381.5 1.9 copy-done.8
  383.4 1.9 copy-done.9
  387.1 6.0 %shard_map.206 = (f32[4,96,768]{2,1,0:T(8,128)S(1)}, bf16[4,96,768]{2,1,0:T(8,128)(2,1)S(1)}, f32[768,1]{1,0:T(8,128)S(1)}) custom-call(s32[1]{0:T(128)} %bitcast.index_ref, bf16[2048,768]{1,0:T(8,128)(2,1)S(1)} %copy-done.8, bf16[2048,576]{1,0:T(8,128)(2,1)S(1)} %copy-done.10, bf16[2048,768]{1,0:T(8,128)(2,1)S(1)} %copy-done.9, ...), custom_call_target="tpu_custom_call" | custom-call | flops 1000000 | bytes 100000 | tf_op jit(solution)/shard_map/pallas_call | solution.py:741
  394.7 2.7 fusion.42
  399.4 2.6 convolution_convert_fusion
  402.0 3.2 fusion.35
  405.2 3.4 collective-permute-done.43
  409.8 6.8 %collective-permute-start.44 = (bf16[2,96,768]{2,1,0:T(8,128)(2,1)S(1)}, bf16[2,96,768]{2,1,0:T(8,128)(2,1)S(1)}, u32[]{:S(2)}, u32[]{:S(2)}) collective-permute-start(bf16[2,96,768]{2,1,0:T(8,128)(2,1)S(1)} %slice.301), channel_id=1, source_target_pairs={{0,8},{4,12},{8,0},{12,4},{16,24},{20,28},{24,16},{28,20},{1,9},{5... | collective-permute-start | bytes 884744 | tf_op jit(solution)/shard_map/ppermute | solution.py:779
  416.6 6.5 %fusion.21 = bf16[1024,768]{1,0:T(8,128)(2,1)} fusion(bf16[1536,768]{1,0:T(8,128)(2,1)} %bitcast.32, bf16[1536,2048]{1,0:T(8,128)(2,1)} %copy-done.27), kind=kOutput, calls=%fused_computation.26 | convolution fusion | flops 2416705536 | bytes 7077888 | tf_op jit(solution)/shard_map/dot_general | solution.py:41
  423.8 3.6 collective-permute-done.39
  428.7 2.8 collective-permute-done.40
  431.6 4.1 collective-permute-done.41
  435.8 5.0 collective-permute-done.42
  444.2 5.1 collective-permute-done.45
  449.3 2.5 collective-permute-start.50
  452.0 2.9 fusion.24
  456.3 5.8 %convert_add_fusion = f32[1024,768]{1,0:T(8,128)S(1)} fusion(bf16[1024,768]{1,0:T(8,128)(2,1)} %collective-permute-done.34, bf16[1536,768]{1,0:T(8,128)(2,1)} %bitcast.32, bf16[1536,2048]{1,0:T(8,128)(2,1)} %copy-done.27), kind=kOutput, calls=%fused_computation.5 | convolution fusion | flops 2417491968 | bytes 10223616 | tf_op jit(solution)/shard_map/dot_general | solution.py:41
  466.9 2.1 slice.208.near_ref
  469.0 11.4 %collective-permute-done.50 = bf16[768,768]{1,0:T(8,128)(2,1)} collective-permute-done((bf16[768,768]{1,0:T(8,128)(2,1)}, bf16[768,768]{1,0:T(8,128)(2,1)}, u32[]{:S(2)}, u32[]{:S(2)}) %collective-permute-start.50) | collective-permute-done | bytes 1179680 | tf_op jit(solution)/shard_map/ppermute | solution.py:787
  482.0 15.3 %collective-permute-done.37.far_ref = bf16[512,768]{1,0:T(8,128)(2,1)} collective-permute-done((bf16[512,768]{1,0:T(8,128)(2,1)}, bf16[512,768]{1,0:T(8,128)(2,1)}, u32[]{:S(2)}, u32[]{:S(2)}) %collective-permute-start.37) | collective-permute-done | bytes 786464 | tf_op jit(solution)/shard_map/ppermute | solution.py:779
  497.3 4.2 shard_map.207
  501.5 2.5 fusion.10
  508.2 3.3 fusion.26
  (282 shorter events, 71.5 us)
Async XLA Ops:
  0.6 20.8 %collective-permute-start = (bf16[512,768]{1,0:T(8,128)(2,1)}, bf16[512,768]{1,0:T(8,128)(2,1)S(1)}, u32[]{:S(2)}, u32[]{:S(2)}) collective-permute-start(bf16[512,768]{1,0:T(8,128)(2,1)} %c_own_ref.2), channel_id=1, source_target_pairs={{0,2},{1,3},{2,0},{3,1},{4,6},{5,7},{6,4},{7,5},{8,10},{9,11},{10,... | collective-permute-start | bytes 2359304 | tf_op jit(solution)/shard_map/ppermute | solution.py:779
  7.0 40.7 %all-to-all-start.1 = ((bf16[8,96,768]{2,1,0:T(8,128)(2,1)}), bf16[8,96,768]{2,1,0:T(8,128)(2,1)S(1)}, u32[]{:S(2)}, u32[]{:S(2)}) async-start(bf16[8,96,768]{2,1,0:T(8,128)(2,1)} %broadcast_in_dim.56), calls=%async_computation.1 | async-start | bytes 2359296 | tf_op jit(solution)/shard_map/all_to_all | solution.py:858
  22.9 9.5 %collective-permute-start.1 = (bf16[1024,768]{1,0:T(8,128)(2,1)}, bf16[1024,768]{1,0:T(8,128)(2,1)}, u32[]{:S(2)}, u32[]{:S(2)}) collective-permute-start(bf16[1024,768]{1,0:T(8,128)(2,1)} %pad_maximum_fusion), channel_id=1, source_target_pairs={{0,1},{1,0},{2,3},{3,2},{4,5},{5,4},{6,7},{7,6},{8,9},{9,8},{10,11... | collective-permute-start | bytes 4718600 | tf_op jit(solution)/shard_map/ppermute | solution.py:779
  25.0 28.6 %collective-permute-start.4 = (bf16[512,768]{1,0:T(8,128)(2,1)S(1)}, bf16[512,768]{1,0:T(8,128)(2,1)}, u32[]{:S(2)}, u32[]{:S(2)}) collective-permute-start(bf16[512,768]{1,0:T(8,128)(2,1)S(1)} %copy-done.3), channel_id=1, source_target_pairs={{0,2},{1,3},{2,0},{3,1},{4,6},{5,7},{6,4},{7,5},{8,10},{9,11},{10,... | collective-permute-start | bytes 2359304 | tf_op jit(solution)/shard_map/ppermute | solution.py:779
  47.7 68.7 %all-to-all-start = ((bf16[8,208,768]{2,1,0:T(8,128)(2,1)}), bf16[8,208,768]{2,1,0:T(8,128)(2,1)}, u32[]{:S(2)}, u32[]{:S(2)}) async-start(bf16[8,208,768]{2,1,0:T(8,128)(2,1)} %copy-done.12), calls=%async_computation | async-start | bytes 5111808 | tf_op jit(solution)/shard_map/all_to_all | solution.py:892
  56.0 5.4 %collective-permute-start.7 = (bf16[1024,768]{1,0:T(8,128)(2,1)}, bf16[1024,768]{1,0:T(8,128)(2,1)}, u32[]{:S(2)}, u32[]{:S(2)}) collective-permute-start(bf16[1024,768]{1,0:T(8,128)(2,1)} %pad_maximum_fusion.1), channel_id=1, source_target_pairs={{0,1},{1,0},{2,3},{3,2},{4,5},{5,4},{6,7},{7,6},{8,9},{9,8},{10,11... | collective-permute-start | bytes 4718600 | tf_op jit(solution)/shard_map/ppermute | solution.py:779
  56.0 32.0 %collective-permute-start.9 = (bf16[768,768]{1,0:T(8,128)(2,1)S(1)}, bf16[768,768]{1,0:T(8,128)(2,1)}, u32[]{:S(2)}, u32[]{:S(2)}) collective-permute-start(bf16[768,768]{1,0:T(8,128)(2,1)S(1)} %get-tuple-element.108.refs_5_), channel_id=1, source_target_pairs={{0,1},{1,0},{2,3},{3,2},{4,5},{5,4},{6,7},{7,6},{8,9},{9,8},{10,11... | collective-permute-start | bytes 3538952 | tf_op jit(solution)/shard_map/ppermute | solution.py:779
  56.5 36.3 %collective-permute-start.5 = (bf16[768,768]{1,0:T(8,128)(2,1)S(1)}, bf16[768,768]{1,0:T(8,128)(2,1)}, u32[]{:S(2)}, u32[]{:S(2)}) collective-permute-start(bf16[768,768]{1,0:T(8,128)(2,1)S(1)} %get-tuple-element.108.refs_5_), channel_id=1, source_target_pairs={{0,2},{1,3},{2,0},{3,1},{4,6},{5,7},{6,4},{7,5},{8,10},{9,11},{10,... | collective-permute-start | bytes 3538952 | tf_op jit(solution)/shard_map/ppermute | solution.py:779
  57.2 29.9 %copy-start.24 = (f32[1,768]{1,0:T(1,128)}, f32[1,768]{1,0:T(1,128)S(1)}, u32[]{:S(2)}) copy-start(f32[1,768]{1,0:T(1,128)S(1)} %broadcast_in_dim.60.gain_ref) | copy-start | bytes 9220
  57.3 29.8 %copy-start.22 = (s32[2048]{0:T(1024)}, s32[2048]{0:T(1024)S(1)}, u32[]{:S(2)}) copy-start(s32[2048]{0:T(1024)S(1)} %select_reduce_fusion) | copy-start | bytes 24580
  57.4 51.7 %collective-permute-start.2 = (bf16[768,768]{1,0:T(8,128)(2,1)}, bf16[768,768]{1,0:T(8,128)(2,1)}, u32[]{:S(2)}, u32[]{:S(2)}) collective-permute-start(bf16[768,768]{1,0:T(8,128)(2,1)} %copy-done.28), channel_id=1, source_target_pairs={{0,4},{4,0},{8,12},{12,8},{16,20},{20,16},{24,28},{28,24},{1,5},{5... | collective-permute-start | bytes 3538952 | tf_op jit(solution)/shard_map/ppermute | solution.py:779
  59.6 33.7 %copy-start.37 = (bf16[192,768]{0,1:T(8,128)(2,1)}, bf16[192,768]{0,1:T(8,128)(2,1)S(1)}, u32[]{:S(2)}) copy-start(bf16[192,768]{0,1:T(8,128)(2,1)S(1)} %slice_bitcast_fusion.8) | copy-start | bytes 884740
  59.6 33.1 %collective-permute-start.8 = (bf16[192,768]{0,1:T(8,128)(2,1)S(1)}, bf16[192,768]{0,1:T(8,128)(2,1)S(1)}, u32[]{:S(2)}, u32[]{:S(2)}) collective-permute-start(bf16[192,768]{0,1:T(8,128)(2,1)S(1)} %slice_bitcast_fusion.8), channel_id=1, source_target_pairs={{0,2},{1,3},{2,0},{3,1},{4,6},{5,7},{6,4},{7,5},{8,10},{9,11},{10,... | collective-permute-start | bytes 884744 | tf_op jit(solution)/shard_map/ppermute | solution.py:779
  61.3 25.8 %copy-start.26 = (s32[5]{0:T(128)}, s32[5]{0:T(128)S(1)}, u32[]{:S(2)}) copy-start(s32[5]{0:T(128)S(1)} %pad_add_fusion.1.meta_ref) | copy-start | bytes 64
  61.4 51.4 %copy-start.59 = (f32[768]{0:T(1024)S(1)}, f32[768]{0:T(1024)}, u32[]{:S(2)}) copy-start(f32[768]{0:T(1024)} %param.15) | copy-start | bytes 9220
  88.0 24.8 %copy-start.25 = (f32[3,1,2048]{2,1,0:T(1,128)}, f32[3,1,2048]{2,1,0:T(1,128)S(1)}, u32[]{:S(2)}) copy-start(f32[3,1,2048]{2,1,0:T(1,128)S(1)} %get-tuple-element.172.lse_ref) | copy-start | bytes 73732
  92.8 18.9 %collective-permute-start.10 = (bf16[192,2048]{1,0:T(8,128)(2,1)}, bf16[192,2048]{1,0:T(8,128)(2,1)S(1)}, u32[]{:S(2)}, u32[]{:S(2)}) collective-permute-start(bf16[192,2048]{1,0:T(8,128)(2,1)} %get-tuple-element.111.refs_0_.ctx_ref), channel_id=1, source_target_pairs={{0,2},{1,3},{2,0},{3,1},{4,6},{5,7},{6,4},{7,5},{8,10},{9,11},{10,... | collective-permute-start | bytes 2359304 | tf_op jit(solution)/shard_map/ppermute | solution.py:779
  93.5 18.7 %collective-permute-start.13 = (bf16[384,768]{0,1:T(8,128)(2,1)S(1)}, bf16[384,768]{0,1:T(8,128)(2,1)S(1)}, u32[]{:S(2)}, u32[]{:S(2)}) collective-permute-start(bf16[384,768]{0,1:T(8,128)(2,1)S(1)} %pad_maximum_fusion.2), channel_id=1, source_target_pairs={{0,1},{1,0},{2,3},{3,2},{4,5},{5,4},{6,7},{7,6},{8,9},{9,8},{10,11... | collective-permute-start | bytes 1769480 | tf_op jit(solution)/shard_map/ppermute | solution.py:779
  109.1 7.4 %collective-permute-start.3 = (bf16[768,768]{1,0:T(8,128)(2,1)}, bf16[768,768]{1,0:T(8,128)(2,1)}, u32[]{:S(2)}, u32[]{:S(2)}) collective-permute-start(bf16[768,768]{1,0:T(8,128)(2,1)} %collective-permute-done.2.refs_6_), channel_id=1, source_target_pairs={{0,1},{1,0},{2,3},{3,2},{4,5},{5,4},{6,7},{7,6},{8,9},{9,8},{10,11... | collective-permute-start | bytes 3538952 | tf_op jit(solution)/shard_map/ppermute | solution.py:779
  109.1 7.4 %collective-permute-start.6 = (bf16[768,768]{1,0:T(8,128)(2,1)}, bf16[768,768]{1,0:T(8,128)(2,1)}, u32[]{:S(2)}, u32[]{:S(2)}) collective-permute-start(bf16[768,768]{1,0:T(8,128)(2,1)} %collective-permute-done.5.refs_7_), channel_id=1, source_target_pairs={{0,1},{1,0},{2,3},{3,2},{4,5},{5,4},{6,7},{7,6},{8,9},{9,8},{10,11... | collective-permute-start | bytes 3538952 | tf_op jit(solution)/shard_map/ppermute | solution.py:779
  111.7 26.6 %collective-permute-start.15 = (bf16[768,768]{1,0:T(8,128)(2,1)}, bf16[768,768]{1,0:T(8,128)(2,1)}, u32[]{:S(2)}, u32[]{:S(2)}) collective-permute-start(bf16[768,768]{1,0:T(8,128)(2,1)} %collective-permute-done.2.refs_6_), channel_id=1, source_target_pairs={{0,2},{1,3},{2,0},{3,1},{4,6},{5,7},{6,4},{7,5},{8,10},{9,11},{10,... | collective-permute-start | bytes 3538952 | tf_op jit(solution)/shard_map/ppermute | solution.py:779
  112.2 4.2 collective-permute-start.11
  112.3 4.2 collective-permute-start.12
  138.3 14.5 %collective-permute-start.16 = (bf16[768,768]{1,0:T(8,128)(2,1)}, bf16[768,768]{1,0:T(8,128)(2,1)S(1)}, u32[]{:S(2)}, u32[]{:S(2)}) collective-permute-start(bf16[768,768]{1,0:T(8,128)(2,1)} %collective-permute-done.15.refs_8_), channel_id=1, source_target_pairs={{0,1},{1,0},{2,3},{3,2},{4,5},{5,4},{6,7},{7,6},{8,9},{9,8},{10,11... | collective-permute-start | bytes 3538952 | tf_op jit(solution)/shard_map/ppermute | solution.py:779
  138.3 9.7 %collective-permute-start.14 = (bf16[192,768]{1,0:T(8,128)(2,1)S(1)}, bf16[192,768]{1,0:T(8,128)(2,1)S(1)}, u32[]{:S(2)}, u32[]{:S(2)}) collective-permute-start(bf16[192,768]{1,0:T(8,128)(2,1)S(1)} %get-tuple-element.116), channel_id=1, source_target_pairs={{0,4},{4,0},{8,12},{12,8},{16,20},{20,16},{24,28},{28,24},{1,5},{5... | collective-permute-start | bytes 884744 | tf_op jit(solution)/shard_map/ppermute | solution.py:779
  140.3 30.6 %collective-permute-start.17 = (bf16[192,768]{1,0:T(8,128)(2,1)}, bf16[192,768]{1,0:T(8,128)(2,1)S(1)}, u32[]{:S(2)}, u32[]{:S(2)}) collective-permute-start(bf16[192,768]{1,0:T(8,128)(2,1)} %get-tuple-element.120), channel_id=1, source_target_pairs={{0,16},{4,20},{8,24},{12,28},{16,0},{20,4},{24,8},{28,12},{1,17},{... | collective-permute-start | bytes 884744 | tf_op jit(solution)/shard_map/ppermute | solution.py:779
  142.6 28.4 %collective-permute-start.18 = (bf16[192,768]{1,0:T(8,128)(2,1)}, bf16[192,768]{1,0:T(8,128)(2,1)S(1)}, u32[]{:S(2)}, u32[]{:S(2)}) collective-permute-start(bf16[192,768]{1,0:T(8,128)(2,1)} %get-tuple-element.121), channel_id=1, source_target_pairs={{0,20},{4,16},{8,28},{12,24},{16,4},{20,0},{24,12},{28,8},{1,21},{... | collective-permute-start | bytes 884744 | tf_op jit(solution)/shard_map/ppermute | solution.py:779
  142.7 30.7 %collective-permute-start.20 = (bf16[192,768]{1,0:T(8,128)(2,1)}, bf16[192,768]{1,0:T(8,128)(2,1)S(1)}, u32[]{:S(2)}, u32[]{:S(2)}) collective-permute-start(bf16[192,768]{1,0:T(8,128)(2,1)} %get-tuple-element.123), channel_id=1, source_target_pairs={{0,8},{4,12},{8,0},{12,4},{16,24},{20,28},{24,16},{28,20},{1,9},{5... | collective-permute-start | bytes 884744 | tf_op jit(solution)/shard_map/ppermute | solution.py:779
  148.0 25.4 %collective-permute-start.21 = (bf16[192,768]{1,0:T(8,128)(2,1)}, bf16[192,768]{1,0:T(8,128)(2,1)S(1)}, u32[]{:S(2)}, u32[]{:S(2)}) collective-permute-start(bf16[192,768]{1,0:T(8,128)(2,1)} %get-tuple-element.124), channel_id=1, source_target_pairs={{0,12},{4,8},{8,4},{12,0},{16,28},{20,24},{24,20},{28,16},{1,13},{... | collective-permute-start | bytes 884744 | tf_op jit(solution)/shard_map/ppermute | solution.py:779
  171.0 25.7 %collective-permute-start.19 = (bf16[192,768]{1,0:T(8,128)(2,1)S(1)}, bf16[192,768]{1,0:T(8,128)(2,1)S(1)}, u32[]{:S(2)}, u32[]{:S(2)}) collective-permute-start(bf16[192,768]{1,0:T(8,128)(2,1)S(1)} %copy-done.32), channel_id=1, source_target_pairs={{0,24},{4,28},{8,16},{12,20},{16,8},{20,12},{24,0},{28,4},{1,25},{... | collective-permute-start | bytes 884744 | tf_op jit(solution)/shard_map/ppermute | solution.py:779
  191.5 10.2 %collective-permute-start.22 = (bf16[192,768]{1,0:T(8,128)(2,1)}, bf16[192,768]{1,0:T(8,128)(2,1)S(1)}, u32[]{:S(2)}, u32[]{:S(2)}) collective-permute-start(bf16[192,768]{1,0:T(8,128)(2,1)} %get-tuple-element.131), channel_id=1, source_target_pairs={{0,8},{4,12},{8,0},{12,4},{16,24},{20,28},{24,16},{28,20},{1,9},{5... | collective-permute-start | bytes 884744 | tf_op jit(solution)/shard_map/ppermute | solution.py:779
  192.2 16.5 %collective-permute-start.23 = (bf16[192,768]{1,0:T(8,128)(2,1)}, bf16[192,768]{1,0:T(8,128)(2,1)S(1)}, u32[]{:S(2)}, u32[]{:S(2)}) collective-permute-start(bf16[192,768]{1,0:T(8,128)(2,1)} %get-tuple-element.132), channel_id=1, source_target_pairs={{0,12},{4,8},{8,4},{12,0},{16,28},{20,24},{24,20},{28,16},{1,13},{... | collective-permute-start | bytes 884744 | tf_op jit(solution)/shard_map/ppermute | solution.py:779
  194.0 15.0 %collective-permute-start.25 = (bf16[192,768]{1,0:T(8,128)(2,1)S(1)}, bf16[192,768]{1,0:T(8,128)(2,1)S(1)}, u32[]{:S(2)}, u32[]{:S(2)}) collective-permute-start(bf16[192,768]{1,0:T(8,128)(2,1)S(1)} %copy-done.63), channel_id=1, source_target_pairs={{0,4},{4,0},{8,12},{12,8},{16,20},{20,16},{24,28},{28,24},{1,5},{5... | collective-permute-start | bytes 884744 | tf_op jit(solution)/shard_map/ppermute | solution.py:779
  195.1 30.9 %collective-permute-start.24 = (bf16[192,768]{1,0:T(8,128)(2,1)S(1)}, bf16[192,768]{1,0:T(8,128)(2,1)S(1)}, u32[]{:S(2)}, u32[]{:S(2)}) collective-permute-start(bf16[192,768]{1,0:T(8,128)(2,1)S(1)} %copy-done.30), channel_id=1, source_target_pairs={{0,28},{4,24},{8,20},{12,16},{16,12},{20,8},{24,4},{28,0},{1,29},{... | collective-permute-start | bytes 884744 | tf_op jit(solution)/shard_map/ppermute | solution.py:779
  196.7 29.3 %copy-start.51 = (bf16[192,768]{1,0:T(8,128)(2,1)}, bf16[192,768]{1,0:T(8,128)(2,1)S(1)}, u32[]{:S(2)}) copy-start(bf16[192,768]{1,0:T(8,128)(2,1)S(1)} %collective-permute-done.19.refs_0_) | copy-start | bytes 884740
  226.7 24.9 %copy-start.60 = (bf16[192,768]{1,0:T(8,128)(2,1)S(1)}, bf16[192,768]{1,0:T(8,128)(2,1)}, u32[]{:S(2)}) copy-start(bf16[192,768]{1,0:T(8,128)(2,1)} %get-tuple-element.161) | copy-start | bytes 884740
  244.0 47.0 %collective-permute-start.28 = (bf16[192,768]{1,0:T(8,128)(2,1)}, bf16[192,768]{1,0:T(8,128)(2,1)S(1)}, u32[]{:S(2)}, u32[]{:S(2)}) collective-permute-start(bf16[192,768]{1,0:T(8,128)(2,1)} %get-tuple-element.162), channel_id=1, source_target_pairs={{0,24},{4,28},{8,16},{12,20},{16,8},{20,12},{24,0},{28,4},{1,25},{... | collective-permute-start | bytes 884744 | tf_op jit(solution)/shard_map/ppermute | solution.py:779
  245.1 39.9 %collective-permute-start.26 = (bf16[192,768]{1,0:T(8,128)(2,1)S(1)}, bf16[192,768]{1,0:T(8,128)(2,1)S(1)}, u32[]{:S(2)}, u32[]{:S(2)}) collective-permute-start(bf16[192,768]{1,0:T(8,128)(2,1)S(1)} %copy-done.62), channel_id=1, source_target_pairs={{0,16},{4,20},{8,24},{12,28},{16,0},{20,4},{24,8},{28,12},{1,17},{... | collective-permute-start | bytes 884744 | tf_op jit(solution)/shard_map/ppermute | solution.py:779
  251.6 39.4 %collective-permute-start.27 = (bf16[192,768]{1,0:T(8,128)(2,1)S(1)}, bf16[192,768]{1,0:T(8,128)(2,1)S(1)}, u32[]{:S(2)}, u32[]{:S(2)}) collective-permute-start(bf16[192,768]{1,0:T(8,128)(2,1)S(1)} %copy-done.60), channel_id=1, source_target_pairs={{0,20},{4,16},{8,28},{12,24},{16,4},{20,0},{24,12},{28,8},{1,21},{... | collective-permute-start | bytes 884744 | tf_op jit(solution)/shard_map/ppermute | solution.py:779
  261.0 30.0 %collective-permute-start.29 = (bf16[192,768]{1,0:T(8,128)(2,1)S(1)}, bf16[192,768]{1,0:T(8,128)(2,1)S(1)}, u32[]{:S(2)}, u32[]{:S(2)}) collective-permute-start(bf16[192,768]{1,0:T(8,128)(2,1)S(1)} %copy-done.61), channel_id=1, source_target_pairs={{0,28},{4,24},{8,20},{12,16},{16,12},{20,8},{24,4},{28,0},{1,29},{... | collective-permute-start | bytes 884744 | tf_op jit(solution)/shard_map/ppermute | solution.py:779
  295.0 3.5 collective-permute-start.30
  299.2 4.7 collective-permute-start.31
  299.8 7.5 %collective-permute-start.46 = (bf16[2,768,768]{2,1,0:T(8,128)(2,1)S(1)}, bf16[2,768,768]{2,1,0:T(8,128)(2,1)S(1)}, u32[]{:S(2)}, u32[]{:S(2)}) collective-permute-start(bf16[2,768,768]{2,1,0:T(8,128)(2,1)S(1)} %get-tuple-element.185), channel_id=1, source_target_pairs={{0,1},{1,0},{2,3},{3,2},{4,5},{5,4},{6,7},{7,6},{8,9},{9,8},{10,11... | collective-permute-start | bytes 7077896 | tf_op jit(solution)/shard_map/ppermute | solution.py:779
  299.8 36.7 %collective-permute-start.32 = (bf16[1024,768]{1,0:T(8,128)(2,1)S(1)}, bf16[1024,768]{1,0:T(8,128)(2,1)S(1)}, u32[]{:S(2)}, u32[]{:S(2)}) collective-permute-start(bf16[1024,768]{1,0:T(8,128)(2,1)S(1)} %add_convert_fusion), channel_id=1, source_target_pairs={{0,2},{1,3},{2,0},{3,1},{4,6},{5,7},{6,4},{7,5},{8,10},{9,11},{10,... | collective-permute-start | bytes 4718600 | tf_op jit(solution)/shard_map/ppermute | solution.py:779
  309.9 106.7 %all-to-all-start.2 = ((bf16[8,192,768]{2,1,0:T(8,128)(2,1)}), bf16[8,192,768]{2,1,0:T(8,128)(2,1)}, u32[]{:S(2)}, u32[]{:S(2)}) async-start(bf16[8,192,768]{2,1,0:T(8,128)(2,1)} %bitcast.31), calls=%async_computation.2 | async-start | bytes 4718592 | tf_op jit(solution)/shard_map/all_to_all | solution.py:982
  337.2 3.5 collective-permute-start.33
  337.3 106.2 %collective-permute-start.49 = (bf16[768,768]{1,0:T(8,128)(2,1)}, bf16[768,768]{1,0:T(8,128)(2,1)}, u32[]{:S(2)}, u32[]{:S(2)}) collective-permute-start(bf16[768,768]{1,0:T(8,128)(2,1)} %get-tuple-element.223), channel_id=1, source_target_pairs={{0,4},{4,0},{8,12},{12,8},{16,20},{20,16},{24,28},{28,24},{1,5},{5... | collective-permute-start | bytes 3538952 | tf_op jit(solution)/shard_map/ppermute | solution.py:779
  341.8 39.7 %copy-start.1 = (bf16[8,96,768]{2,1,0:T(8,128)(2,1)S(1)}, bf16[8,96,768]{2,1,0:T(8,128)(2,1)}, u32[]{:S(2)}) copy-start(bf16[8,96,768]{2,1,0:T(8,128)(2,1)} %copy-done) | copy-start | bytes 3538948
  393.1 15.5 %collective-permute-start.43 = (bf16[4,96,768]{2,1,0:T(8,128)(2,1)S(1)}, bf16[4,96,768]{2,1,0:T(8,128)(2,1)}, u32[]{:S(2)}, u32[]{:S(2)}) collective-permute-start(bf16[4,96,768]{2,1,0:T(8,128)(2,1)S(1)} %get-tuple-element.177), channel_id=1, source_target_pairs={{0,4},{4,0},{8,12},{12,8},{16,20},{20,16},{24,28},{28,24},{1,5},{5... | collective-permute-start | bytes 1769480 | tf_op jit(solution)/shard_map/ppermute | solution.py:779
  398.4 24.7 %collective-permute-start.38 = (f32[10,768]{1,0:T(8,128)S(1)}, f32[10,768]{1,0:T(8,128)S(1)}, u32[]{:S(2)}, u32[]{:S(2)}) collective-permute-start(f32[10,768]{1,0:T(8,128)S(1)} %pad_maximum_fusion.5), channel_id=1, source_target_pairs={{0,1},{1,0},{2,3},{3,2},{4,5},{5,4},{6,7},{7,6},{8,9},{9,8},{10,11... | collective-permute-start | bytes 92168 | tf_op jit(solution)/shard_map/ppermute | solution.py:779
  402.0 50.0 %collective-permute-start.36 = (bf16[1024,768]{1,0:T(8,128)(2,1)}, bf16[1024,768]{1,0:T(8,128)(2,1)}, u32[]{:S(2)}, u32[]{:S(2)}) collective-permute-start(bf16[1024,768]{1,0:T(8,128)(2,1)} %convolution_convert_fusion), channel_id=1, source_target_pairs={{0,1},{1,0},{2,3},{3,2},{4,5},{5,4},{6,7},{7,6},{8,9},{9,8},{10,11... | collective-permute-start | bytes 4718600 | tf_op jit(solution)/shard_map/ppermute | solution.py:779
  409.8 32.3 %collective-permute-start.44 = (bf16[2,96,768]{2,1,0:T(8,128)(2,1)S(1)}, bf16[2,96,768]{2,1,0:T(8,128)(2,1)S(1)}, u32[]{:S(2)}, u32[]{:S(2)}) collective-permute-start(bf16[2,96,768]{2,1,0:T(8,128)(2,1)S(1)} %slice.301), channel_id=1, source_target_pairs={{0,8},{4,12},{8,0},{12,4},{16,24},{20,28},{24,16},{28,20},{1,9},{5... | collective-permute-start | bytes 884744 | tf_op jit(solution)/shard_map/ppermute | solution.py:779
  416.6 26.9 %copy-start.45 = (bf16[768,768]{1,0:T(8,128)(2,1)S(1)}, bf16[768,768]{1,0:T(8,128)(2,1)}, u32[]{:S(2)}) copy-start(bf16[768,768]{1,0:T(8,128)(2,1)} %get-tuple-element.186) | copy-start | bytes 3538948
  423.1 33.2 %collective-permute-start.34 = (bf16[1024,768]{1,0:T(8,128)(2,1)}, bf16[1024,768]{1,0:T(8,128)(2,1)}, u32[]{:S(2)}, u32[]{:S(2)}) collective-permute-start(bf16[1024,768]{1,0:T(8,128)(2,1)} %fusion.21), channel_id=1, source_target_pairs={{0,1},{1,0},{2,3},{3,2},{4,5},{5,4},{6,7},{7,6},{8,9},{9,8},{10,11... | collective-permute-start | bytes 4718600 | tf_op jit(solution)/shard_map/ppermute | solution.py:779
  423.1 4.2 collective-permute-start.39
  427.4 4.1 collective-permute-start.40
  431.5 4.2 collective-permute-start.41
  435.7 5.0 collective-permute-start.42
  440.7 60.7 %collective-permute-start.47 = (bf16[768,768]{1,0:T(8,128)(2,1)}, bf16[768,768]{1,0:T(8,128)(2,1)}, u32[]{:S(2)}, u32[]{:S(2)}) collective-permute-start(bf16[768,768]{1,0:T(8,128)(2,1)} %get-tuple-element.222), channel_id=1, source_target_pairs={{0,4},{4,0},{8,12},{12,8},{16,20},{20,16},{24,28},{28,24},{1,5},{5... | collective-permute-start | bytes 3538952 | tf_op jit(solution)/shard_map/ppermute | solution.py:779
  442.2 7.2 %collective-permute-start.45 = (bf16[1,96,768]{2,1,0:T(8,128)(2,1)S(1)}, bf16[1,96,768]{2,1,0:T(8,128)(2,1)S(1)}, u32[]{:S(2)}, u32[]{:S(2)}) collective-permute-start(bf16[1,96,768]{2,1,0:T(8,128)(2,1)S(1)} %slice.302), channel_id=1, source_target_pairs={{0,16},{4,20},{8,24},{12,28},{16,0},{20,4},{24,8},{28,12},{1,17},{... | collective-permute-start | bytes 442376 | tf_op jit(solution)/shard_map/ppermute | solution.py:779
  443.5 25.5 %collective-permute-start.48 = (bf16[768,768]{1,0:T(8,128)(2,1)S(1)}, bf16[768,768]{1,0:T(8,128)(2,1)S(1)}, u32[]{:S(2)}, u32[]{:S(2)}) collective-permute-start(bf16[768,768]{1,0:T(8,128)(2,1)S(1)} %copy-done.45), channel_id=1, source_target_pairs={{4,6},{5,7},{6,4},{7,5},{12,14},{13,15},{14,12},{15,13},{20,22},{2... | collective-permute-start | bytes 3538952 | tf_op jit(solution)/shard_map/ppermute | solution.py:787
  449.3 31.1 %collective-permute-start.50 = (bf16[768,768]{1,0:T(8,128)(2,1)}, bf16[768,768]{1,0:T(8,128)(2,1)}, u32[]{:S(2)}, u32[]{:S(2)}) collective-permute-start(bf16[768,768]{1,0:T(8,128)(2,1)} %collective-permute-done.49), channel_id=1, source_target_pairs={{0,2},{1,3},{2,0},{3,1},{8,10},{9,11},{10,8},{11,9},{16,18},{17,19... | collective-permute-start | bytes 3538952 | tf_op jit(solution)/shard_map/ppermute | solution.py:787
  454.9 42.4 %collective-permute-start.37 = (bf16[512,768]{1,0:T(8,128)(2,1)}, bf16[512,768]{1,0:T(8,128)(2,1)}, u32[]{:S(2)}, u32[]{:S(2)}) collective-permute-start(bf16[512,768]{1,0:T(8,128)(2,1)} %get-tuple-element.227), channel_id=1, source_target_pairs={{0,2},{1,3},{2,0},{3,1},{4,6},{5,7},{6,4},{7,5},{8,10},{9,11},{10,... | collective-permute-start | bytes 2359304 | tf_op jit(solution)/shard_map/ppermute | solution.py:779
  464.8 43.4 %collective-permute-start.35 = (bf16[512,768]{1,0:T(8,128)(2,1)}, bf16[512,768]{1,0:T(8,128)(2,1)}, u32[]{:S(2)}, u32[]{:S(2)}) collective-permute-start(bf16[512,768]{1,0:T(8,128)(2,1)} %slice.300), channel_id=1, source_target_pairs={{0,2},{1,3},{2,0},{3,1},{4,6},{5,7},{6,4},{7,5},{8,10},{9,11},{10,... | collective-permute-start | bytes 2359304 | tf_op jit(solution)/shard_map/ppermute | solution.py:779
  (60 other events, 403.5 us)

commit v3 on v2

--- a/solution.py
+++ b/solution.py
@@ -48,14 +48,13 @@
 def select_piece(spot, refs, out):
     for n, ref in enumerate(refs):
 
-        @pl.when((spot == n) if n < 2 else (spot >= 2))
+        @pl.when(spot == n)
         def _(ref=ref):
             out[...] = ref[...]
 
 
-def piece_specs(rows, features, spot):
-    still = pl.BlockSpec((rows, features), lambda *i: (0, 0))
-    return [still, still, pl.BlockSpec((rows, features), lambda *i: (jnp.maximum(spot(*i) - 2, 0), 0))]
+def piece_specs(rows, features):
+    return [pl.BlockSpec((rows, features), lambda *i: (0, 0))] * 4
 
 
 def norm_parts(values):
@@ -65,7 +64,7 @@
 
 
 def attend_kernel(
-    meta_ref, start_ref, x_own_ref, x_far_ref, x_near_ref, gain_ref, w_ref,
+    meta_ref, start_ref, x_0_ref, x_1_ref, x_2_ref, x_3_ref, gain_ref, w_ref,
     h_ref, qt_ref, q_ref, k_ref, kt_ref, v_ref, ctx_ref, ctxt_ref, lse_ref, k_all, vt_all, x_ref,
 ):
     step = pl.program_id(0)
@@ -75,7 +74,7 @@
     key_iota = lax.broadcasted_iota(jnp.int32, (BLOCK, BLOCK), 0)
     query_iota = lax.broadcasted_iota(jnp.int32, (BLOCK, BLOCK), 1)
 
-    select_piece(spot_of(step ^ meta_ref[0]), (x_own_ref, x_far_ref, x_near_ref), x_ref)
+    select_piece(spot_of(step ^ meta_ref[0]), (x_0_ref, x_1_ref, x_2_ref, x_3_ref), x_ref)
     normed, _ = norm_parts(x_ref[...].astype(WIDE))
     h_one = (normed * gain_ref[...]).astype(LOW)
     h_ref[...] = h_one
@@ -145,7 +144,7 @@
         grid=(rows // BLOCK,),
         in_specs=[
             pl.BlockSpec((1, BLOCK), lambda i, m: (0, i)),
-            *piece_specs(BLOCK, features, spot),
+            *piece_specs(BLOCK, features),
             pl.BlockSpec((1, features), lambda i, m: (0, 0)),
             pl.BlockSpec(weights.shape, lambda i, m: (0, 0)),
         ],
@@ -188,109 +187,156 @@
 
 
 def attend_back_kernel(
-    meta_ref, start_ref, x_ref, dh_mine_ref, dh_near_ref, c_own_ref, c_far_ref, c_near_ref,
-    gain_ref, wo_ref, qt_ref, q_ref, k_ref, kt_ref, v_ref, ctxt_ref, lse_ref,
-    d_ref, dx_ref, dgain_ref, dqkv_ref, dq_all, dk_acc, dv_acc, dh_ref, c_ref,
+    meta_ref, start_ref, x_ref, dh_mine_ref, dh_near_ref, c_0_ref, c_1_ref, c_2_ref, c_3_ref,
+    gain_ref, w_ref, qt_ref, q_ref, k_ref, kt_ref, v_ref, ctxt_ref, lse_ref, h_ref, ctx_ref,
+    dx_ref, dgain_ref, send_ref, mine_ref, keep_ref, give_ref, dots_ref,
+    dk_acc, dv_acc, dh_ref, c_ref, dqkv, d_all, acc,
 ):
     step = pl.program_id(0)
     heads = qt_ref.shape[0]
-    start = start_ref[...]
-    key_iota = lax.broadcasted_iota(jnp.int32, (BLOCK, BLOCK), 0)
-    query_iota = lax.broadcasted_iota(jnp.int32, (BLOCK, BLOCK), 1)
+    width = heads * HD
 
     @pl.when(step == 0)
     def _():
         dk_acc[...] = jnp.zeros_like(dk_acc)
         dv_acc[...] = jnp.zeros_like(dv_acc)
-
-    spot = spot_of(step ^ meta_ref[0])
-    select_piece(spot, (c_own_ref, c_far_ref, c_near_ref), c_ref)
-
-    @pl.when(spot < 2)
-    def _():
-        dh_ref[...] = dh_mine_ref[...]
-
-    @pl.when(spot >= 2)
-    def _():
-        dh_ref[...] = dh_near_ref[...]
-
-    normed, rstd = norm_parts(x_ref[...])
-    dh = dh_ref[...].astype(WIDE)
-    scaled = dh * gain_ref[...]
-    mean_plain = jnp.mean(scaled, axis=-1, keepdims=True)
-    mean_normed = jnp.mean(scaled * normed, axis=-1, keepdims=True)
-    dx = c_ref[...].astype(WIDE) + rstd * (scaled - mean_plain - normed * mean_normed)
-    dattn = dx.astype(LOW)
-    d_ref[...] = dattn
-
-    @pl.when(step == meta_ref[0])
-    def _():
-        dx_ref[...] = dx
-        dgain_ref[...] = jnp.sum(dh * normed, axis=0, keepdims=True)
-
-    g_all = mm(dattn, wo_ref[:, 3 * heads * HD :]).astype(LOW)
-    gt_all = g_all.T
-    g = [g_all[:, h * HD : (h + 1) * HD] for h in range(heads)]
-    gt = [gt_all[h * HD : (h + 1) * HD] for h in range(heads)]
-    delta = [
-        jnp.sum(gt[h].astype(WIDE) * ctxt_ref[h], axis=0, keepdims=True) for h in range(heads)
-    ]
-
-    def block(j, carry, last):
-        base = pl.multiple_of(j * BLOCK, BLOCK)
-        rows = pl.ds(base, BLOCK)
-        allowed = key_iota + base >= start
-        if last:
-            allowed = allowed & (key_iota <= query_iota)
-        out = []
-        for h in range(heads):
-            scores = mm(k_ref[h, rows, :], qt_ref[h])
-            probs = jnp.where(allowed, jnp.exp(scores - lse_ref[h]), 0.0)
-            slopes = mm(v_ref[h, rows, :], gt[h])
-            score_grads = (probs * (slopes - delta[h])).astype(LOW)
-            dv_acc[h, rows, :] += mm(probs.astype(LOW), g[h])
-            dk_acc[h, rows, :] += mm(score_grads, q_ref[h])
-            out.append(carry[h] + mm(kt_ref[h, :, rows], score_grads))
-        return tuple(out)
-
-    carry = tuple(jnp.zeros((HD, BLOCK), WIDE) for _ in range(heads))
-    carry = lax.fori_loop(meta_ref[1 + step], step, lambda j, c: block(j, c, False), carry)
-    carry = block(step, carry, True)
-    here = pl.ds(pl.multiple_of(step * BLOCK, BLOCK), BLOCK)
-    scale = HD**-0.5
-    for h in range(heads):
-        dq_all[h, here, :] = (carry[h] * scale).T
-
-    @pl.when(step == pl.num_programs(0) - 1)
+        acc[...] = jnp.zeros_like(acc)
+
+    def place(piece):
+        return pl.ds(pl.multiple_of(spot_of(piece ^ meta_ref[0]) * BLOCK, BLOCK), BLOCK)
+
+    @pl.when(step < 4)
+    def _():
+        start = start_ref[...]
+        key_iota = lax.broadcasted_iota(jnp.int32, (BLOCK, BLOCK), 0)
+        query_iota = lax.broadcasted_iota(jnp.int32, (BLOCK, BLOCK), 1)
+        spot = spot_of(step ^ meta_ref[0])
+        select_piece(spot, (c_0_ref, c_1_ref, c_2_ref, c_3_ref), c_ref)
+
+        @pl.when(spot < 2)
+        def _():
+            dh_ref[...] = dh_mine_ref[...]
+
+        @pl.when(spot >= 2)
+        def _():
+            dh_ref[...] = dh_near_ref[...]
+
+        normed, rstd = norm_parts(x_ref[...])
+        dh = dh_ref[...].astype(WIDE)
+        scaled = dh * gain_ref[...]
+        mean_plain = jnp.mean(scaled, axis=-1, keepdims=True)
+        mean_normed = jnp.mean(scaled * normed, axis=-1, keepdims=True)
+        dx = c_ref[...].astype(WIDE) + rstd * (scaled - mean_plain - normed * mean_normed)
+        dattn = dx.astype(LOW)
+        d_all[place(step), :] = dattn
+
+        @pl.when(step == meta_ref[0])
+        def _():
+            dx_ref[...] = dx
+            dgain_ref[...] = jnp.sum(dh * normed, axis=0, keepdims=True)
+
+        g_all = mm(dattn, w_ref[:, 3 * width :]).astype(LOW)
+        gt_all = g_all.T
+        g = [g_all[:, h * HD : (h + 1) * HD] for h in range(heads)]
+        gt = [gt_all[h * HD : (h + 1) * HD] for h in range(heads)]
+        delta = [
+            jnp.sum(gt[h].astype(WIDE) * ctxt_ref[h], axis=0, keepdims=True)
+            for h in range(heads)
+        ]
+
+        def block(j, carry, last):
+            base = pl.multiple_of(j * BLOCK, BLOCK)
+            rows = pl.ds(base, BLOCK)
+            allowed = key_iota + base >= start
+            if last:
+                allowed = allowed & (key_iota <= query_iota)
+            out = []
+            for h in range(heads):
+                scores = mm(k_ref[h, rows, :], qt_ref[h])
+                probs = jnp.where(allowed, jnp.exp(scores - lse_ref[h]), 0.0)
+                slopes = mm(v_ref[h, rows, :], gt[h])
+                score_grads = (probs * (slopes - delta[h])).astype(LOW)
+                dv_acc[h, rows, :] += mm(probs.astype(LOW), g[h])
+                dk_acc[h, rows, :] += mm(score_grads, q_ref[h])
+                out.append(carry[h] + mm(kt_ref[h, :, rows], score_grads))
+            return tuple(out)
+
+        carry = tuple(jnp.zeros((HD, BLOCK), WIDE) for _ in range(heads))
+        carry = lax.fori_loop(meta_ref[1 + step], step, lambda j, c: block(j, c, False), carry)
+        carry = block(step, carry, True)
+        scale = HD**-0.5
+        dqkv[place(step), :width] = jnp.concatenate(
+            [(c * scale).T for c in carry], axis=1
+        ).astype(LOW)
+
+    @pl.when(step == 3)
     def _():
         for n in range(4):
             rows = slice(n * BLOCK, (n + 1) * BLOCK)
-            to = pl.ds(pl.multiple_of(spot_of(n ^ meta_ref[0]) * BLOCK, BLOCK), BLOCK)
-            dqkv_ref[to, :] = jnp.concatenate(
-                [part[h, rows, :] for part in (dq_all, dk_acc, dv_acc) for h in range(heads)],
-                axis=1,
+            dqkv[place(n), width:] = jnp.concatenate(
+                [part[h, rows, :] for part in (dk_acc, dv_acc) for h in range(heads)], axis=1
             ).astype(LOW)
 
-
-def attend_back(meta, start, x_one, dh_pieces, c_pieces, gain, weights, qt, q, keys, kt, values, ctxt, lse):
+    def rest(out, kind):
+        rows = pl.ds(pl.multiple_of(((step - 4) ^ 2) * BLOCK, BLOCK), BLOCK)
+        grads = dqkv[rows, :]
+        out[...] = mm_nt(grads, w_ref[:, : 3 * width]).astype(kind)
+        acc[:, : 3 * width] += mm_tn(h_ref[...], grads)
+        acc[:, 3 * width :] += mm_tn(d_all[rows, :], ctx_ref[...].T)
+
+    @pl.when((step == 4) | (step == 5))
+    def _():
+        rest(send_ref, LOW)
+
+    @pl.when(step >= 6)
+    def _():
+        rest(mine_ref, WIDE)
+
+    @pl.when(step == 7)
+    def _():
+        dots_ref[...] = jnp.sum(
+            acc[:, : 3 * width] * w_ref[:, : 3 * width].astype(WIDE), axis=1, keepdims=True
+        )
+        count, size = 2 * keep_ref.shape[0], keep_ref.shape[1]
+        for n in range(count):
+            k = sum(((n >> b) & 1) * (count >> 1 >> b) for b in range(count.bit_length() - 1))
+            part = acc[pl.ds(pl.multiple_of((meta_ref[5] ^ k) * size, 8), size), :]
+            if n < count // 2:
+                keep_ref[n] = part
+            else:
+                give_ref[n - count // 2] = part.astype(LOW)
+
+
+def attend_back(
+    meta, start, x_one, dh_pieces, c_pieces, gain, weights,
+    qt, q, keys, kt, values, ctxt, lse, h_one, context, count,
+):
     heads, _, rows = qt.shape
     features = x_one.shape[1]
-    spot = lambda i, m: spot_of(i ^ m[0])
-    place = lambda i, m: (spot(i, m), 0)
-
-    by_column = pl.BlockSpec((heads, HD, BLOCK), lambda i, m: (0, 0, i))
-    by_row = pl.BlockSpec((heads, BLOCK, HD), lambda i, m: (0, i, 0))
-    by_place = pl.BlockSpec((BLOCK, features), place)
-    whole = lambda *shape: pl.BlockSpec(shape, lambda i, m: (0,) * len(shape))
+    every = weights.shape[1]
+    low = lambda i: jnp.minimum(i, 3)
+    high = lambda i: jnp.maximum(i - 4, 0) ^ 2
+    spot = lambda i, m: spot_of(low(i) ^ m[0])
+    once = pl.Buffered(1)
+    by_column = pl.BlockSpec((heads, HD, BLOCK), lambda i, m: (0, 0, low(i)))
+    by_row = pl.BlockSpec((heads, BLOCK, HD), lambda i, m: (0, low(i), 0))
+
+    def whole(*shape):
+        return pl.BlockSpec(shape, lambda i, m: (0,) * len(shape), pipeline_mode=once)
+
+    def out(*shape):
+        return pl.BlockSpec(shape, lambda i, m: (0,) * len(shape))
+
+    share = (count // 2, features // count, every)
     grid_spec = pltpu.PrefetchScalarGridSpec(
         num_scalar_prefetch=1,
-        grid=(rows // BLOCK,),
+        grid=(8,),
         in_specs=[
-            pl.BlockSpec((1, BLOCK), lambda i, m: (0, i)),
-            by_place,
+            pl.BlockSpec((1, BLOCK), lambda i, m: (0, low(i))),
+            pl.BlockSpec((BLOCK, features), lambda i, m: (spot(i, m), 0)),
             pl.BlockSpec((BLOCK, features), lambda i, m: (jnp.minimum(spot(i, m), 1), 0)),
             pl.BlockSpec((BLOCK, features), lambda i, m: (jnp.maximum(spot(i, m) - 2, 0), 0)),
-            *piece_specs(BLOCK, features, spot),
+            *([whole(BLOCK, features)] * 4),
             whole(1, features),
             whole(*weights.shape),
             by_column,
@@ -299,29 +345,45 @@
             whole(heads, HD, rows),
             whole(heads, rows, HD),
             by_column,
-            pl.BlockSpec((heads, 1, BLOCK), lambda i, m: (0, 0, i)),
+            pl.BlockSpec((heads, 1, BLOCK), lambda i, m: (0, 0, low(i))),
+            pl.BlockSpec((BLOCK, features), lambda i, m: (high(i), 0)),
+            pl.BlockSpec((heads * HD, BLOCK), lambda i, m: (0, high(i))),
         ],
         out_specs=[
-            by_place,
-            whole(rows // 4, features),
-            whole(1, features),
-            whole(rows, 3 * heads * HD),
-        ],
-        scratch_shapes=[pltpu.VMEM((heads, rows, HD), WIDE)] * 3
-        + [pltpu.VMEM((BLOCK, features), LOW)] * 2,
+            out(BLOCK, features),
+            out(1, features),
+            pl.BlockSpec((BLOCK, features), lambda i, m: (jnp.clip(i - 4, 0, 1), 0)),
+            pl.BlockSpec((BLOCK, features), lambda i, m: (jnp.clip(i - 6, 0, 1), 0)),
+            out(*share),
+            out(*share),
+            out(features, 1),
+        ],
+        scratch_shapes=[pltpu.VMEM((heads, rows, HD), WIDE)] * 2
+        + [pltpu.VMEM((BLOCK, features), LOW)] * 2
+        + [
+            pltpu.VMEM((rows, 3 * heads * HD), LOW),
+            pltpu.VMEM((rows, features), LOW),
+            pltpu.VMEM((features, every), WIDE),
+        ],
     )
     return pl.pallas_call(
         attend_back_kernel,
         grid_spec=grid_spec,
         out_shape=[
-            jax.ShapeDtypeStruct((rows, features), LOW),
-            jax.ShapeDtypeStruct((rows // 4, features), WIDE),
+            jax.ShapeDtypeStruct((BLOCK, features), WIDE),
             jax.ShapeDtypeStruct((1, features), WIDE),
-            jax.ShapeDtypeStruct((rows, 3 * heads * HD), LOW),
-        ],
-        compiler_params=pltpu.CompilerParams(vmem_limit_bytes=60 * 2**20),
+            jax.ShapeDtypeStruct((2 * BLOCK, features), LOW),
+            jax.ShapeDtypeStruct((2 * BLOCK, features), WIDE),
+            jax.ShapeDtypeStruct(share, WIDE),
+            jax.ShapeDtypeStruct(share, LOW),
+            jax.ShapeDtypeStruct((features, 1), WIDE),
+        ],
+        compiler_params=pltpu.CompilerParams(vmem_limit_bytes=61 * 2**20),
         cost_estimate=LITTLE,
-    )(meta, start, x_one, *dh_pieces, *c_pieces, gain, weights, qt, q, keys, kt, values, ctxt, lse)
+    )(
+        meta, start, x_one, *dh_pieces, *c_pieces, gain, weights,
+        qt, q, keys, kt, values, ctxt, lse, h_one, context,
+    )
 
 
 def hot_rows(placed_ref, line, first, rows):
@@ -331,17 +393,16 @@
 
 
 def send_kernel(
-    index_ref, placed_ref, c_own_ref, c_far_ref, c_near_ref, c_ref, in_order_ref, picks_ref, rows_all
+    index_ref, placed_ref, c_0_ref, c_1_ref, c_2_ref, c_3_ref, c_ref, in_order_ref, picks_ref, rows_all
 ):
     step = pl.program_id(0)
     share = in_order_ref.shape[0]
-    size = c_own_ref.shape[0]
+    size = c_0_ref.shape[0]
 
     @pl.when(step == 0)
     def _():
-        rows_all[:size, :] = c_own_ref[...]
-        rows_all[size : 2 * size, :] = c_far_ref[...]
-        rows_all[2 * size :, :] = c_near_ref[...]
+        for n, ref in enumerate((c_0_ref, c_1_ref, c_2_ref, c_3_ref)):
+            rows_all[n * size : (n + 1) * size, :] = ref[...]
 
     hot = hot_rows(placed_ref, 2, step * share, share)
     in_order_ref[...] = hot
@@ -363,9 +424,7 @@
         grid=(count,),
         in_specs=[
             whole(*placed.shape),
-            whole(size, features),
-            whole(size, features),
-            whole(2 * size, features),
+            *([whole(size, features)] * 4),
         ],
         out_specs=[
             pl.BlockSpec((1, share + 16, features), lambda p, o: (p, 0, 0)),
@@ -383,7 +442,7 @@
             jax.ShapeDtypeStruct((count * share, total), LOW),
         ],
         compiler_params=pltpu.CompilerParams(vmem_limit_bytes=40 * 2**20),
-        cost_estimate=LITTLE,
+        cost_estimate=pl.CostEstimate(flops=4 * 10**10, bytes_accessed=10**7, transcendentals=0),
     )(index, placed, *pieces)
 
 
@@ -426,14 +485,14 @@
 
 
 def mix_kernel(count, gain_ref, placed_ref, *refs):
-    context_refs, weight_refs, piece_refs = refs[:4], refs[4:8], refs[8:11]
-    x_one_ref, taken_refs, x_ref, h_all = refs[11], refs[12 : 12 + count], refs[-2], refs[-1]
+    context_refs, weight_refs, piece_refs = refs[:4], refs[4:8], refs[8:12]
+    x_one_ref, taken_refs, x_ref, h_all = refs[12], refs[13 : 13 + count], refs[-2], refs[-1]
     step = pl.program_id(0)
     size = x_ref.shape[0]
     select_piece(step, piece_refs, x_ref)
-    attn = mm(context_refs[0][...].T, weight_refs[0][...])
+    attn = mm_nt(context_refs[0][...].T, weight_refs[0][...])
     for n in range(1, 4):
-        attn = attn + mm(context_refs[n][...].T, weight_refs[n][...])
+        attn = attn + mm_nt(context_refs[n][...].T, weight_refs[n][...])
     x_one = x_ref[...].astype(WIDE) + attn
     x_one_ref[...] = x_one
     normed, _ = norm_parts(x_one)
@@ -454,9 +513,6 @@
 
     def context_spec(n):
         return pl.BlockSpec((width, size), lambda i: (0, i ^ n))
-
-    def weight_spec(n):
-        return pl.BlockSpec((width, features), lambda i: (n // 3, 0))
 
     return pl.pallas_call(
         functools.partial(mix_kernel, count),
@@ -466,16 +522,16 @@
             pl.BlockSpec(placed.shape, lambda i: (0, 0)),
         ]
         + [context_spec(n) for n in range(4)]
-        + [weight_spec(n) for n in range(4)]
-        + piece_specs(size, features, lambda i: i),
+        + [pl.BlockSpec((features, width), lambda i: (0, 0))] * 4
+        + piece_specs(size, features),
         scratch_shapes=[pltpu.VMEM((size, features), LOW), pltpu.VMEM((rows, features), LOW)],
         out_specs=[pl.BlockSpec((size, features), lambda i: (i, 0))]
         + [pl.BlockSpec((share, features), lambda i: (0, 0))] * count,
         out_shape=[jax.ShapeDtypeStruct((rows, features), WIDE)]
         + [jax.ShapeDtypeStruct((share, features), LOW)] * count,
-        compiler_params=pltpu.CompilerParams(vmem_limit_bytes=40 * 2**20),
+        compiler_params=pltpu.CompilerParams(vmem_limit_bytes=60 * 2**20),
         cost_estimate=LITTLE,
-    )(gain, placed, *contexts, *weights, weights[2], *pieces)
+    )(gain, placed, *contexts, *weights, *pieces)
 
 
 def expert_kernel(count, meta_ref, *refs):
@@ -487,11 +543,11 @@
     dx_refs, refs = refs[6 : 6 + count], refs[6 + count :]
     cs, w1_all, w2_all, sems, acc, acc_y, dots, others, gate = refs
     step, steps = pl.program_id(0), pl.num_programs(0)
-    rows, kinds = xs_ref.shape[0], wg_ref.shape[1]
+    rows, kinds = xs_ref.shape[0], wg_ref.shape[0]
     share = rows // count
     units = w1_all.shape[1] // 2
     lanes = lax.broadcasted_iota(jnp.int32, (rows, kinds), 1)
-    own = meta_ref[0]
+    own = meta_ref[6]
 
     def fetches(n):
         slot = n % 2
@@ -519,7 +575,7 @@
         for n in range(count):
             xs_ref[n * share : (n + 1) * share, :] = x_refs[n][...]
             cs[n * share : (n + 1) * share, :] = c_refs[n][0, :share, :]
-        logits = mm(xs_ref[...], wg_ref[...].astype(LOW))
+        logits = mm_nt(xs_ref[...], wg_ref[...].astype(LOW))
         here, there = kinds_of()
         mine = jnp.sum(jnp.where(here, logits, 0.0), axis=1, keepdims=True)
         theirs = jnp.sum(jnp.where(there, logits, 0.0), axis=1, keepdims=True)
@@ -570,12 +626,12 @@
         high = marks.astype(LOW)
         rest = (marks - high.astype(WIDE)).astype(LOW)
         gate_low = wg_ref[...].astype(LOW)
-        dx = acc[...] + mm_nt(high, gate_low) + mm_nt(rest, gate_low)
+        dx = acc[...] + mm(high, gate_low) + mm(rest, gate_low)
         for n in range(count):
             dx_refs[n][...] = dx[n * share : (n + 1) * share].astype(LOW)
         y = (gate[...] * acc_y[...]).astype(LOW)
         for n in range(count):
-            base = pl.multiple_of((meta_ref[1] % count ^ n) * share, 16)
+            base = pl.multiple_of((meta_ref[5] % count ^ n) * share, 16)
             y_ref[pl.ds(base, share), :] = y[n * share : (n + 1) * share]
 
 
@@ -584,20 +640,20 @@
     share, features = xs[0].shape
     rows = count * share
     units = weights[0].shape[0]
-    kinds = gate_weight.shape[1]
+    kinds = gate_weight.shape[0]
     whole = lambda *shape: pl.BlockSpec(shape, lambda p, o: (0,) * len(shape))
     by_piece = pl.BlockSpec((rows, units), lambda p, o: (chunk, p))
     by_chunk = lambda width: pl.BlockSpec((rows, width), lambda p, o: (chunk, 0))
     anywhere = pl.BlockSpec(memory_space=pl.ANY)
 
     def c_spec(n):
-        return pl.BlockSpec((1,) + c.shape[1:], lambda p, o: (o[1] ^ (chunk * count + n), 0, 0))
+        return pl.BlockSpec((1,) + c.shape[1:], lambda p, o: (o[5] ^ (chunk * count + n), 0, 0))
 
     operands = [meta, *xs, *([c] * count), gate_weight, *weights]
     in_specs = (
         [whole(share, features)] * count
         + [c_spec(n) for n in range(count)]
-        + [whole(features, kinds)]
+        + [whole(kinds, features)]
         + [anywhere] * 8
     )
     aliases = {}
@@ -616,7 +672,7 @@
             by_chunk(features),
             by_chunk(features),
             by_chunk(kinds),
-            pl.BlockSpec((rows, features), lambda p, o: (o[1] // count ^ chunk, 0)),
+            pl.BlockSpec((rows, features), lambda p, o: (o[5] // count ^ chunk, 0)),
             *([whole(share, features)] * count),
         ],
         scratch_shapes=[
@@ -650,28 +706,38 @@
     return out[:6], out[6:]
 
 
-def expert_grads_kernel(a_ref, du_ref, x_ref, dy_ref, give_ref, keep_ref):
+def expert_grads_kernel(a_ref, du_ref, x_ref, dy_ref, marks_ref, *refs):
+    give_refs, (keep_ref, gate_ref) = refs[:4], refs[4:]
     step = pl.program_id(0)
+
+    @pl.when(step == 0)
+    def _():
+        high = marks_ref[...].astype(LOW)
+        rest = (marks_ref[...] - high.astype(WIDE)).astype(LOW)
+        gate_ref[...] = mm_tn(x_ref[...], high) + mm_tn(x_ref[...], rest)
+
     units = a_ref.shape[1] // 2
 
-    def store(out, kind):
+    def store(outs, kind):
         first = mm_tn(du_ref[...], x_ref[...])
         second = mm_tn(a_ref[...], dy_ref[...])
-        for m in range(2):
+        for m, out in enumerate(outs):
             span = slice(m * units, (m + 1) * units)
-            out[0, m, :units, :] = first[span].astype(kind)
-            out[0, m, units:, :] = second[span].astype(kind)
-
-    @pl.when(step < 2)
-    def _():
-        store(give_ref, LOW)
+            out[:units, :] = first[span].astype(kind)
+            out[units:, :] = second[span].astype(kind)
+
+    for n in range(2):
+
+        @pl.when(step == n)
+        def _(n=n):
+            store(give_refs[2 * n : 2 * n + 2], LOW)
 
     @pl.when(step >= 2)
     def _():
-        store(keep_ref, WIDE)
-
-
-def expert_grads(hidden, hidden_grads, x, dy):
+        store((keep_ref.at[0, 0], keep_ref.at[0, 1]), WIDE)
+
+
+def expert_grads(hidden, hidden_grads, x, dy, marks):
     rows, features = x.shape
     units = hidden.shape[1] // 4
     piece = pl.BlockSpec((rows, units), lambda p: (0, p ^ 2))
@@ -680,75 +746,148 @@
     return pl.pallas_call(
         expert_grads_kernel,
         grid=(4,),
-        in_specs=[piece, piece, all_rows, all_rows],
+        in_specs=[piece, piece, all_rows, all_rows, pl.BlockSpec(marks.shape, lambda p: (0, 0))],
         out_specs=[
-            pl.BlockSpec((1,) + shape[1:], lambda p: (jnp.minimum(p, 1), 0, 0, 0)),
+            *([pl.BlockSpec(shape[2:], lambda p: (0, 0))] * 4),
             pl.BlockSpec((1,) + shape[1:], lambda p: (jnp.maximum(p - 2, 0), 0, 0, 0)),
-        ],
-        out_shape=[jax.ShapeDtypeStruct(shape, LOW), jax.ShapeDtypeStruct(shape, WIDE)],
+            pl.BlockSpec((features, marks.shape[1]), lambda p: (0, 0)),
+        ],
+        out_shape=[
+            *([jax.ShapeDtypeStruct(shape[2:], LOW)] * 4),
+            jax.ShapeDtypeStruct(shape, WIDE),
+            jax.ShapeDtypeStruct((features, marks.shape[1]), WIDE),
+        ],
         compiler_params=pltpu.CompilerParams(vmem_limit_bytes=58 * 2**20),
         cost_estimate=LITTLE,
-    )(hidden, hidden_grads, x, dy)
-
-
-def weight_kernel(
-    index_ref, h_ref, dqkv_ref, d_ref, ctx_ref, w_ref, keep_ref, give_ref, dots_ref, acc
-):
-    step = pl.program_id(0)
-    width = dqkv_ref.shape[1]
-
-    @pl.when(step == 0)
-    def _():
-        acc[...] = jnp.zeros_like(acc)
-
-    acc[:, :width] += mm_tn(h_ref[...], dqkv_ref[...])
-    acc[:, width:] += mm_tn(d_ref[...], ctx_ref[...].T)
-
-    @pl.when(step == pl.num_programs(0) - 1)
-    def _():
-        count, size = 2 * keep_ref.shape[0], keep_ref.shape[1]
-        dots_ref[...] = jnp.sum(
-            acc[:, :width] * w_ref[:, :width].astype(WIDE), axis=1, keepdims=True
-        )
-        for n in range(count):
-            k = sum(((n >> b) & 1) * (count >> 1 >> b) for b in range(count.bit_length() - 1))
-            part = acc[pl.ds(pl.multiple_of((index_ref[0] ^ k) * size, 8), size), :]
-            if n < count // 2:
-                keep_ref[n] = part
-            else:
-                give_ref[n - count // 2] = part.astype(LOW)
-
-
-def weight_grads(index, h_one, dqkv, dattn, context, weights, count):
-    rows, features = h_one.shape
-    width, narrow = dqkv.shape[1], context.shape[0]
-    size = features // count
-    by_row = lambda columns: pl.BlockSpec((BLOCK, columns), lambda i, o: (i, 0))
-    share = pl.BlockSpec((count // 2, size, width + narrow), lambda i, o: (0, 0, 0))
+    )(hidden, hidden_grads, x, dy, marks)
+
+
+def leave_kernel(keep_ref, give_0_ref, give_1_ref, out_ref):
+    for n, give_ref in enumerate((give_0_ref, give_1_ref)):
+
+        @pl.when(pl.program_id(0) == n)
+        def _(give_ref=give_ref):
+            out_ref[0] = (keep_ref[0, 0] + give_ref[...].astype(WIDE)).astype(LOW)
+
+
+def far_sum(keep, give):
+    _, halves, rows, features = keep.shape
+    whole = pl.BlockSpec((rows, features), lambda m: (0, 0))
+    return pl.pallas_call(
+        leave_kernel,
+        grid=(halves,),
+        in_specs=[pl.BlockSpec((1, 1, rows, features), lambda m: (1, m, 0, 0)), whole, whole],
+        out_specs=pl.BlockSpec((1, rows, features), lambda m: (m, 0, 0)),
+        out_shape=jax.ShapeDtypeStruct((halves, rows, features), LOW),
+        compiler_params=pltpu.CompilerParams(vmem_limit_bytes=40 * 2**20),
+        cost_estimate=LITTLE,
+    )(keep, *give)
+
+
+def home_kernel(keep_ref, give_0_ref, give_1_ref, far_ref, kept_ref, other_ref):
+    held = keep_ref[0, 0] + far_ref[0].astype(WIDE)
+
+    @pl.when(pl.program_id(0) == 0)
+    def _():
+        other_ref[...] = (held + give_1_ref[...].astype(WIDE)).astype(LOW)
+
+    @pl.when(pl.program_id(0) == 1)
+    def _():
+        kept_ref[...] = held + give_0_ref[...].astype(WIDE)
+
+
+def home_sum(keep, give, far):
+    _, halves, rows, features = keep.shape
+    whole = pl.BlockSpec((rows, features), lambda m: (0, 0))
+    return pl.pallas_call(
+        home_kernel,
+        grid=(halves,),
+        in_specs=[
+            pl.BlockSpec((1, 1, rows, features), lambda m: (0, 1 - m, 0, 0)),
+            whole,
+            whole,
+            pl.BlockSpec((1, rows, features), lambda m: (1 - m, 0, 0)),
+        ],
+        out_specs=[whole, whole],
+        out_shape=[
+            jax.ShapeDtypeStruct((rows, features), WIDE),
+            jax.ShapeDtypeStruct((rows, features), LOW),
+        ],
+        compiler_params=pltpu.CompilerParams(vmem_limit_bytes=40 * 2**20),
+        cost_estimate=LITTLE,
+    )(keep, *give, far)
+
+
+def choose_kernel(odd_ref, kept_ref, other_ref, first_ref, second_ref):
+    units = second_ref.shape[1]
+
+    def store(value):
+        first_ref[0] = value[:units].T
+        second_ref[0] = value[units:]
+
+    @pl.when(odd_ref[0] == 1)
+    def _():
+        store(kept_ref[...])
+
+    @pl.when(odd_ref[0] == 0)
+    def _():
+        store(other_ref[...].astype(WIDE))
+
+
+def choose(odd, kept, other):
+    rows, features = kept.shape
+    units = rows // 2
+    whole = lambda *shape: pl.BlockSpec(shape, lambda i, o: (0,) * len(shape))
     grid_spec = pltpu.PrefetchScalarGridSpec(
         num_scalar_prefetch=1,
-        grid=(rows // BLOCK,),
-        in_specs=[
-            by_row(features),
-            by_row(width),
-            by_row(features),
-            pl.BlockSpec((narrow, BLOCK), lambda i, o: (0, i)),
-            pl.BlockSpec(weights.shape, lambda i, o: (0, 0)),
-        ],
-        out_specs=[share, share, pl.BlockSpec((features, 1), lambda i, o: (0, 0))],
-        scratch_shapes=[pltpu.VMEM((features, width + narrow), WIDE)],
+        grid=(1,),
+        in_specs=[whole(rows, features), whole(rows, features)],
+        out_specs=[whole(1, features, units), whole(1, units, features)],
     )
     return pl.pallas_call(
-        weight_kernel,
+        choose_kernel,
         grid_spec=grid_spec,
         out_shape=[
-            jax.ShapeDtypeStruct((count // 2, size, width + narrow), WIDE),
-            jax.ShapeDtypeStruct((count // 2, size, width + narrow), LOW),
-            jax.ShapeDtypeStruct((features, 1), WIDE),
+            jax.ShapeDtypeStruct((1, features, units), WIDE),
+            jax.ShapeDtypeStruct((1, units, features), WIDE),
         ],
         compiler_params=pltpu.CompilerParams(vmem_limit_bytes=40 * 2**20),
         cost_estimate=LITTLE,
-    )(index, h_one, dqkv, dattn, context, weights)
+    )(odd, kept, other)
+
+
+def tokens_kernel(hot_ref, rows_ref, send_ref, keep_ref):
+    total = mm_tn(hot_ref[...], rows_ref[...])
+
+    @pl.when(pl.program_id(0) < 2)
+    def _():
+        send_ref[...] = total.astype(LOW)
+
+    @pl.when(pl.program_id(0) >= 2)
+    def _():
+        keep_ref[...] = total
+
+
+def to_tokens(hot, rows):
+    count, features = rows.shape
+    return pl.pallas_call(
+        tokens_kernel,
+        grid=(4,),
+        in_specs=[
+            pl.BlockSpec((count, BLOCK), lambda i: (0, i ^ 2)),
+            pl.BlockSpec((count, features), lambda i: (0, 0)),
+        ],
+        out_specs=[
+            pl.BlockSpec((BLOCK, features), lambda i: (jnp.minimum(i, 1), 0)),
+            pl.BlockSpec((BLOCK, features), lambda i: (jnp.maximum(i - 2, 0), 0)),
+        ],
+        out_shape=[
+            jax.ShapeDtypeStruct((2 * BLOCK, features), LOW),
+            jax.ShapeDtypeStruct((2 * BLOCK, features), WIDE),
+        ],
+        compiler_params=pltpu.CompilerParams(vmem_limit_bytes=40 * 2**20),
+        cost_estimate=LITTLE,
+    )(hot, rows)
 
 
 def finish_kernel(keep_ref, near_ref, far_ref, x_ref, gain_ref, dx_ref, out_ref):
@@ -795,30 +934,19 @@
     return jnp.concatenate(pieces, axis=0)
 
 
-def sum_everywhere(value):
-    for axis in ("head", "dp"):
-        bits = 1
-        while bits < lax.axis_size(axis):
-            value = value + flip(value, axis, bits)
-            bits *= 2
-    return value
-
-
-def sum_over_dp_scattered(keep, give):
-    bits = 1
+def sum_over_dp_scattered(keep, give, other):
+    bits, first = 1, None
     while True:
-        keep = keep + flip(give, "dp", bits).astype(WIDE)
+        come = flip(give, "dp", bits)
+        if first is None:
+            come = after(come, other)
+        keep = keep + come.astype(WIDE)
+        first = keep if first is None else first
         count = keep.shape[0]
         if count == 1:
-            return keep[0]
+            return keep[0], first
         keep, give = keep[: count // 2], keep[count // 2 :].astype(LOW)
         bits *= 2
-
-
-def split_dot(a, marks):
-    high = marks.astype(LOW)
-    rest = (marks - high.astype(WIDE)).astype(LOW)
-    return mm_tn(a, high) + mm_tn(a, rest)
 
 
 def body(
@@ -848,8 +976,7 @@
     gain_one, gain_two = gain_one[None], gain_two[None]
 
     c_far = flip(cotangent, "head", 2)
-    c_near = flip(joined([cotangent, c_far]), "head", 1)
-    c_pieces = [cotangent, c_far, c_near]
+    c_near, x_near = flip(cotangent, "head", 1), flip(block_input, "head", 1)
     x_far = flip(after(block_input, c_far), "head", 2)
 
     piece = jnp.concatenate(
@@ -882,116 +1009,124 @@
     here_dp = dp_index.astype(jnp.int32)[None]
 
     kept, given = expert_halves(
-        odd.astype(jnp.int32)[None], frozen_in, frozen_out, fresh_in, fresh_out
-    )
-
-    c_out, in_order, picks = send_rows(here_dp, placed, after(c_pieces, kept), dp_count, share)
+        after(odd.astype(jnp.int32)[None], c_far), frozen_in, frozen_out, fresh_in, fresh_out
+    )
+
+    come = flip(given, "dp", 1)
+
+    c_pieces = [cotangent, c_far, c_near, flip(after(c_far, kept), "head", 1)]
+    c_out, in_order, picks = send_rows(here_dp, placed, c_pieces, dp_count, share)
     x_far = after(x_far, c_out)
-    x_near = flip(joined([block_input, x_far]), "head", 1)
-    x_pieces = [block_input, x_far, x_near]
-    c_in = lax.all_to_all(c_out, "dp", 0, 0, tiled=True)
-
-    come = flip(after(given, weights), "dp", 1)
+    x_pieces = [block_input, x_far, x_near, flip(x_far, "head", 1)]
+
     kept_far = flip(after(kept, x_far), "head", 2)
 
     near_kept = flip(kept, "head", 1)
-    out = weights[:, 3 * width :].T
-    out_far = flip(out, "head", 2)
-    out_near = flip(joined([out, out_far]), "head", 1)
+    out = weights[:, 3 * width :]
+    out_far, out_near = flip(out, "head", 2), flip(out, "head", 1)
+    out_last = flip(out_far, "head", 1)
 
     ends = jnp.cumsum(doc_lengths[0])
     start = jnp.max(jnp.where(tokens[:, None] >= ends[None], ends[None], 0), axis=1)
-    meta = jnp.concatenate([head_index[None], start[::BLOCK] // BLOCK]).astype(jnp.int32)
+    own_kind = dp_index // 2 + odd * (kinds // 2)
+    meta = jnp.concatenate(
+        [head_index[None], start[::BLOCK] // BLOCK, dp_index[None], own_kind[None]]
+    ).astype(jnp.int32)
     start = start[None]
     h_one, qt, queries, keys, kt, values, context, context_t, log_totals = attend(
         meta, start, x_pieces, gain_one, weights, width
     )
     near_context = flip(context, "head", 1)
-    far_context = flip(after(context, kept_far, out_far, near_kept), "head", 2)
-    last_context = flip(far_context, "head", 1)
+    far_context = flip(after(context, kept_far, near_kept, out_far), "head", 2)
+    c_in = lax.all_to_all(c_out, "dp", 0, 0, tiled=True)
+    last_context = flip(after(far_context, come), "head", 1)
     come_far = flip(after(come, far_context), "head", 2)
-    near_come = flip(come, "head", 1)
     last_kept = flip(kept_far, "head", 1)
     per = dp_count // 4
     x_one, *x_out = mix(
-        placed, x_pieces, after(gain_two, c_in, near_come, last_kept),
-        [context, far_context, near_context, last_context], [out, out_far, out_near],
+        placed, x_pieces, after(gain_two, last_kept),
+        [context, far_context, near_context, last_context], [out, out_far, out_near, out_last],
         dp_count, share,
     )
-    last_come = flip(after(come_far, x_one), "head", 1)
+    near_come, last_come = (flip(after(w, x_one), "head", 1) for w in (come, come_far))
     halves = [kept, come, kept_far, come_far, near_kept, near_come, last_kept, last_come]
 
-    x_parts = [x_out[0]] + [flip(x_out[k], "dp", k) for k in range(1, 3 * per)]
-    held, dx_parts = None, []
-    own_kind = dp_index // 2 + odd * (kinds // 2)
-    expert_meta = jnp.stack([own_kind, dp_index]).astype(jnp.int32)
-    for n in range(4):
-        ks = range(n * per, (n + 1) * per)
+    groups = [range(n * per, (n + 1) * per) for n in range(4)]
+    x_parts = {k: flip(x_out[k], "dp", k) if k else x_out[0] for k in range(2 * per)}
+    x_parts.update({k: flip(after(x_out[k], x_parts[1]), "dp", k) for k in groups[2]})
+    held, dx_parts = None, {}
+    for n, ks in enumerate(groups):
         xs = [x_parts[k] for k in ks]
-        if n >= 2:
-            xs[0] = after(xs[0], *dx_parts[(n - 2) * per : (n - 1) * per])
-        held, dx = run_experts(
-            expert_meta, xs, c_in, gate_weight, halves, n, 4, held
-        )
-        dx_parts += [part if k == 0 else flip(part, "dp", k) for k, part in zip(ks, dx)]
+        if n == 3:
+            xs[0] = after(xs[0], *[dx_parts[k] for k in (*groups[0], *groups[1])])
+        held, dx = run_experts(meta, xs, c_in, gate_weight.T, halves, n, 4, held)
+        if n == 2:
+            back = flip(joined(dx), "dp", n * per)
+            for r, k in enumerate(ks):
+                part = back[r * share : (r + 1) * share]
+                dx_parts[k] = flip(part, "dp", r) if r else part
+        else:
+            dx_parts.update({k: part if k == 0 else flip(part, "dp", k) for k, part in zip(ks, dx)})
         if n == 0:
-            ready = x_parts[2 * per :]
-            x_parts += [
-                flip(after(x_out[k], dx[0], *ready), "dp", k) for k in range(3 * per, dp_count)
-            ]
-
-    hidden, hidden_grads, x_all, dy_all, marks, gated = held
+            x_parts.update({k: flip(after(x_out[k], dx[0]), "dp", k) for k in groups[3]})
+
     cut = 2 * per * share
-    early = joined(dx_parts[: 2 * per])
+    early = joined([dx_parts[k] for k in range(2 * per)])
     there = mm_tn(picks[:cut, half:], early)
     here = mm_tn(picks[:cut, :half], early)
-    give, keep = expert_grads(hidden, hidden_grads, after(x_all, there, here), dy_all)
-    late = joined([after(dx_parts[2 * per], give), *dx_parts[2 * per + 1 :]])
+    late = [dx_parts[k] for k in (*groups[2], *groups[3])]
+    late = joined([after(late[0], there, here), *late[1:]])
     there = (there + mm_tn(picks[cut:, half:], late)).astype(LOW)
     sent = flip(there, "head", 1)
     here = (here + mm_tn(picks[cut:, :half], late) + sent.astype(WIDE)).astype(LOW)
     across = flip(here, "head", 2)
 
-    give = [flip(after(give[:, n], here), "head", 1) for n in (1, 0)]
-    leave = [(keep[n, 1] + give[0][n].astype(WIDE)).astype(LOW) for n in (1, 0)]
-    gated = after(gated, *leave)
-    leave = [flip(part, "dp", 1) for part in leave]
-    across = across.astype(WIDE)
-    dh_mine = (here.astype(WIDE) + joined([across[own_rows:], across[:own_rows]])).astype(LOW)
+    hidden, hidden_grads, x_all, dy_all, marks, gated = held
+    *give, keep, grad_gate = expert_grads(hidden, hidden_grads, after(x_all, here), dy_all, marks)
+    give = [flip(part, "head", 1) for part in give]
+    leave = far_sum(keep, give[2:])
+    gated = after(gated, leave)
+    dh_mine = (
+        here.astype(WIDE) + joined([across[own_rows:], across[:own_rows]]).astype(WIDE)
+    ).astype(LOW)
     dh_near = flip(dh_mine, "head", 1)
-    stay = (keep[1, 0] + give[1][1].astype(WIDE)).astype(LOW)
-    crossed = flip_head_where(after(stay, dh_mine), 2, 1) + flip_head_where(after(leave[0], dh_mine), 2, 0)
-    home = jnp.where(odd == 1, keep[0, 0] + give[1][0].astype(WIDE), leave[1].astype(WIDE))
-
-    dattn, dx_one, grad_gain_two, dqkv = attend_back(
+    crossed = flip_head_where(after(leave, dh_mine), 2, 1)
+    keep_home, give_home = keep, give[:2]
+
+    dx_one, grad_gain_two, send, mine, keep, give, dots = attend_back(
         meta, start, x_one, [dh_mine, dh_near], c_pieces, gain_two, weights,
-        qt, queries, keys, kt, values, context_t, log_totals,
-    )
-    back = weights[:, : 3 * width]
-    keep, give, dots = weight_grads(
-        dp_index.astype(jnp.int32)[None], h_one, dqkv, dattn, context, weights, dp_count
-    )
-    sent = flip(mm_nt(after(dqkv, give)[half:], back).astype(LOW), "head", 1)
-    mine = mm_nt(dqkv[:half], back)
-    far = flip((mine[own_rows:] + sent[own_rows:].astype(WIDE)).astype(LOW), "head", 2)
-    grad_input = finish(mine[:own_rows], sent[:own_rows], far, block_input, gain_one, dx_one)
-    grads = sum_over_dp_scattered(keep, give)
+        qt, queries, keys, kt, values, context_t, log_totals, h_one, context, dp_count,
+    )
+    send = flip(after(send, crossed), "head", 1)
+    far_out = (mine[own_rows:] + send[own_rows:].astype(WIDE)).astype(LOW)
+    far = flip(far_out, "head", 2)
+    grad_input = finish(mine[:own_rows], send[:own_rows], far, block_input, gain_one, dx_one)
+    grads, once_summed = sum_over_dp_scattered(keep, give, far_out)
     grad_qkv = jnp.stack([grads[:, n * width : (n + 1) * width] for n in range(3)])
     grad_out_weight = grads[:, 3 * width :].T
 
     gated = lax.all_to_all(
         gated.reshape(dp_count, share, features), "dp", 0, 0, tiled=True
     ).reshape(dp_count * share, features)
-    gated = after(gated, mine)
-    sent = flip(mm_tn(in_order[:, half:], gated).astype(LOW), "head", 1).astype(WIDE)
-    mine = mm_tn(in_order[:, :half], gated) + sent
-    mixture = mine[:own_rows] + flip(mine[own_rows:].astype(LOW), "head", 2).astype(WIDE)
+    small = joined([dots[:, 0][None] / gain_one, grad_gain_two, grad_gate.T])
+    for bits in (1, 2):
+        small = small + flip(small, "head", bits)
+    small = after(small, once_summed)
+    small = small + flip(small, "dp", 1)
+    kept_home, other = home_sum(keep_home, give_home, after(crossed, far_out, once_summed))
+    over = flip(after(other, small), "dp", 1)
+    send, mine = to_tokens(in_order, after(gated, other))
+    send = flip(send, "head", 1)
+    y_out = (mine[own_rows:] + send[own_rows:].astype(WIDE)).astype(LOW)
+    y_far = flip(y_out, "head", 2)
+    mixture = mine[:own_rows] + send[:own_rows].astype(WIDE) + y_far.astype(WIDE)
     result = (x_one[:own_rows] + mixture).astype(LOW)
-    home = home + after(crossed, mine).astype(WIDE)
-    units = home.shape[0] // 2
-    grad_fresh_in, grad_fresh_out = home[:units].T[None], home[units:][None]
-    grad_gate = split_dot(after(x_all, give), marks)
-    small = sum_everywhere(joined([dots[:, 0][None] / gain_one, grad_gain_two, grad_gate.T]))
+    small = after(small, y_out)
+    bits = 2
+    while bits < dp_count:
+        small = small + flip(small, "dp", bits)
+        bits *= 2
+    grad_fresh_in, grad_fresh_out = choose(odd.astype(jnp.int32)[None], kept_home, over)
     return (
         result,
         grad_input,

time: 521 us -> 457 us (0.88)
  waiting for transfers between devices: 135 us -> 96.7 us
  matrix products: 38.8 us -> 9.04 us
  Pallas kernels: 192 us -> 214 us
  local copies, waits for them, and re-layouts: 43.1 us -> 35.2 us
  starting transfers between devices: 78.2 us -> 72.9 us
    ppermute x49 -> x53, waiting for transfers between devices: 124 us -> 94.8 us  [flip(): return lax.ppermute(array, axis, [(i, i ^ bits) for i in range(size)])]
    dot_general x8 -> x4, matrix products: 31.6 us -> 7.49 us  [mm_tn(): return lax.dot_general(a, b, TN, preferred_element_type=WIDE)]
    ppermute x2 -> x1, waiting for transfers between devices: 11.5 us -> 0.01 us  [flip_head_where(): return lax.ppermute(array, ('dp', 'head'), pairs)]
    pallas_call x1 -> x4, Pallas kernels: 5.99 us -> 15.7 us  [the longest x1 7.55 us: to_tokens(): pl.pallas_call(tokens_kernel, grid=(4,), in_specs=[pl.BlockSpec((count, B...]
    pallas_call x1, Pallas kernels: 39.7 us -> 49.2 us  [attend_back(): pl.pallas_call(attend_back_kernel, grid_spec=grid_spec, out_shape=[jax.Sh...]
    dot_general x2 -> x0, matrix products: 5.73 us -> none  [mm_nt(): return lax.dot_general(a, b, NT, preferred_element_type=WIDE)]
    unnamed x150 -> x124, local copies, waits for them, and re-layouts: 31.7 us -> 26.6 us
    ppermute x49 -> x53, starting transfers between devices: 54.1 us -> 52.2 us  [flip(): return lax.ppermute(array, axis, [(i, i ^ bits) for i in range(size)])]
  transfers between devices with their start and end apart: 54 -> 57, of which waited for: 24 -> 25; matrix products, arithmetic and copies ran while one was open for 14% -> 7% of each run, Pallas kernels for 34% -> 46%
where the time goes in v3:
time: 457 us; the launch traced here: 448 us
  Pallas kernels  214 us (47%)
  waiting for transfers between devices  96.7 us (21%)
  starting transfers between devices  72.9 us (16%)
  local copies, waits for them, and re-layouts  35.2 us (8%)
  other arithmetic  18.2 us (4%)
  matrix products  9.04 us (2%)
    ppermute x53, waiting for transfers between devices, flip(): return lax.ppermute(array, axis, [(i, i ^ bits) for i in range(size)])  94.8 us
    pallas_call x4, Pallas kernels, run_experts(): pl.pallas_call(functools.partial(expert_kernel, count), grid_spec=grid_sp...  68.1 us
    ppermute x53, starting transfers between devices, flip(): return lax.ppermute(array, axis, [(i, i ^ bits) for i in range(size)])  52.2 us
    pallas_call x1, Pallas kernels, attend_back(): pl.pallas_call(attend_back_kernel, grid_spec=grid_spec, out_shape=[jax.Sh...  49.2 us
    unnamed x124, local copies, waits for them, and re-layouts  26.6 us
    pallas_call x1, Pallas kernels, attend(): pl.pallas_call(attend_kernel, grid_spec=grid_spec, out_shape=[jax.ShapeDt...  25.7 us
    pallas_call x1, Pallas kernels, expert_grads(): pl.pallas_call(expert_grads_kernel, grid=(4,), in_specs=[piece, piece, al...  24.7 us
    pallas_call x1, Pallas kernels, mix(): pl.pallas_call(functools.partial(mix_kernel, count), grid=(4,), in_specs=...  16.4 us
  transfers between devices with their start and end apart: 57, of which 25 were waited for; matrix products, arithmetic and copies ran while one was open for 7% of the time, Pallas kernels for 46%

profile of v3, /device:TPU:0, one launch (start us, length us, event | category | flops | bytes accessed | tf_op | source)
XLA Modules:
  0.0 448.3 jit_solution(12384225513739043456)
XLA Ops:
  0.6 3.0 collective-permute-start
  7.0 5.8 %all-to-all-start = ((bf16[8,96,768]{2,1,0:T(8,128)(2,1)}), bf16[8,96,768]{2,1,0:T(8,128)(2,1)}, u32[]{:S(2)}, u32[]{:S(2)}) async-start(bf16[8,96,768]{2,1,0:T(8,128)(2,1)} %broadcast_in_dim.59), calls=%async_computation | async-start | bytes 2359296 | tf_op jit(solution)/shard_map/all_to_all | solution.py:985
  13.2 1.5 fusion.16
  14.9 6.5 %collective-permute-done.c_1_ref = bf16[512,768]{1,0:T(8,128)(2,1)S(1)} collective-permute-done((bf16[512,768]{1,0:T(8,128)(2,1)}, bf16[512,768]{1,0:T(8,128)(2,1)S(1)}, u32[]{:S(2)}, u32[]{:S(2)}) %collective-permute-start) | collective-permute-done | bytes 786464 | tf_op jit(solution)/shard_map/ppermute | solution.py:918
  22.9 1.7 collective-permute-start.1
  24.7 10.0 %shard_map.197 = (bf16[8,208,768]{2,1,0:T(8,128)(2,1)S(1)}, bf16[1536,2048]{1,0:T(8,128)(2,1)S(1)}, bf16[1536,2048]{1,0:T(8,128)(2,1)}) custom-call(s32[1]{0:T(128)} %bitcast.1.index_ref, s32[8,2048]{1,0:T(8,128)S(1)} %pad.5.placed_ref, bf16[512,768]{1,0:T(8,128)(2,1)S(1)} %copy-done.16, bf16[512,768]{1,0:T(8,128)(2,1)S(1)} %collective-permute-done.c_1_ref, ...), custom_call_target="tpu_custom_call" | custom-call | flops 40000000000 | bytes 10000000 | tf_op jit(solution)/shard_map/pallas_call | solution.py:436
  34.7 2.6 copy-done.3
  40.3 1.9 all-to-all-done
  42.2 4.6 %all-to-all-start.1 = ((bf16[8,208,768]{2,1,0:T(8,128)(2,1)}), bf16[8,208,768]{2,1,0:T(8,128)(2,1)}, u32[]{:S(2)}, u32[]{:S(2)}) async-start(bf16[8,208,768]{2,1,0:T(8,128)(2,1)} %copy-done.9), calls=%async_computation.1 | async-start | bytes 5111808 | tf_op jit(solution)/shard_map/all_to_all | solution.py:1041
  48.4 2.0 collective-permute-start.12
  54.3 25.7 %shard_map.198 = (bf16[2048,768]{1,0:T(8,128)(2,1)}, bf16[3,64,2048]{2,1,0:T(8,128)(2,1)S(1)}, bf16[3,2048,64]{2,1,0:T(8,128)(2,1)}, bf16[3,2048,64]{2,1,0:T(8,1...) custom-call(s32[7]{0:T(128)S(1)} %pad_add_fusion.1.meta_ref, ...), custom_call_target="tpu_custom_call" | custom-call | flops 1000000 | bytes 100000 | tf_op jit(solution)/shard_map/pallas_call | solution.py:170
  84.5 17.1 %collective-permute-done.12.refs_6_ = bf16[768,768]{1,0:T(8,128)(2,1)} collective-permute-done((bf16[768,768]{1,0:T(8,128)(2,1)}, bf16[768,768]{1,0:T(8,128)(2,1)}, u32[]{:S(2)}, u32[]{:S(2)}) %collective-permute-start.12) | collective-permute-done | bytes 1179680 | tf_op jit(solution)/shard_map/ppermute | solution.py:918
  105.3 2.4 collective-permute-done.14.refs_6_
  110.0 16.4 %shard_map.199 = (f32[2048,768]{1,0:T(8,128)}, bf16[192,768]{1,0:T(8,128)(2,1)}, bf16[192,768]{1,0:T(8,128)(2,1)}, bf16[192,768]{1,0:T(8,128)(2,1)}, bf16[192,76...) custom-call(f32[1,768]{1,0:T(1,128)} %broadcast_in_dim.29.gain_ref, ...), custom_call_target="tpu_custom_call" | custom-call | flops 1000000 | bytes 100000 | tf_op jit(solution)/shard_map/pallas_call | solution.py:517
  126.6 3.5 collective-permute-done.17.refs_8_
  130.1 1.9 collective-permute-start.16
  133.6 6.3 %collective-permute-done.16.refs_1_ = bf16[192,768]{1,0:T(8,128)(2,1)S(1)} collective-permute-done((bf16[192,768]{1,0:T(8,128)(2,1)}, bf16[192,768]{1,0:T(8,128)(2,1)S(1)}, u32[]{:S(2)}, u32[]{:S(2)}) %collective-permute-start.16) | collective-permute-done | bytes 294944 | tf_op jit(solution)/shard_map/ppermute | solution.py:918
  139.8 2.6 collective-permute-start.27
  142.4 1.6 collective-permute-start.28
  145.0 16.9 %shard_map.200 = (bf16[1536,3072]{1,0:T(8,128)(2,1)}, bf16[1536,3072]{1,0:T(8,128)(2,1)}, bf16[1536,768]{1,0:T(8,128)(2,1)}, bf16[1536,768]{1,0:T(8,128)(2,1)}, ...) custom-call(s32[7]{0:T(128)} %copy-done.24, ...), custom_call_target="tpu_custom_call" | custom-call | flops 1000000 | bytes 100000 | tf_op jit(solution)/shard_map/pallas_call | solution.py:690
  162.0 3.4 collective-permute-start.20
  165.9 17.3 %shard_map.201 = (bf16[1536,3072]{1,0:T(8,128)(2,1)}, bf16[1536,3072]{1,0:T(8,128)(2,1)}, bf16[1536,768]{1,0:T(8,128)(2,1)}, bf16[1536,768]{1,0:T(8,128)(2,1)}, ...) custom-call(s32[7]{0:T(128)} %copy-done.24, ...), custom_call_target="tpu_custom_call", output_to_operand_aliasing={{0}: (14, {}), {1}: (15, {}), {2}: (16, {}), {3}: (17, {}),... | custom-call | flops 1000000 | bytes 100000 | tf_op jit(solution)/shard_map/pallas_call | solution.py:690
  183.4 2.9 collective-permute-start.25
  186.8 16.9 %shard_map.202 = (bf16[1536,3072]{1,0:T(8,128)(2,1)}, bf16[1536,3072]{1,0:T(8,128)(2,1)}, bf16[1536,768]{1,0:T(8,128)(2,1)}, bf16[1536,768]{1,0:T(8,128)(2,1)}, ...) custom-call(s32[7]{0:T(128)} %copy-done.24, ...), custom_call_target="tpu_custom_call", output_to_operand_aliasing={{0}: (14, {}), {1}: (15, {}), {2}: (16, {}), {3}: (17, {}),... | custom-call | flops 1000000 | bytes 100000 | tf_op jit(solution)/shard_map/pallas_call | solution.py:690
  206.9 17.0 %shard_map.203 = (bf16[1536,3072]{1,0:T(8,128)(2,1)}, bf16[1536,3072]{1,0:T(8,128)(2,1)}, bf16[1536,768]{1,0:T(8,128)(2,1)}, bf16[1536,768]{1,0:T(8,128)(2,1)}, ...) custom-call(s32[7]{0:T(128)} %copy-done.24, ...), custom_call_target="tpu_custom_call", output_to_operand_aliasing={{0}: (14, {}), {1}: (15, {}), {2}: (16, {}), {3}: (17, {}),... | custom-call | flops 1000000 | bytes 100000 | tf_op jit(solution)/shard_map/pallas_call | solution.py:690
  223.9 2.7 collective-permute-start.31
  226.6 3.0 fusion.10
  229.6 9.1 %collective-permute-done.29 = bf16[384,768]{1,0:T(8,128)(2,1)S(1)} collective-permute-done((bf16[384,768]{1,0:T(8,128)(2,1)S(1)}, bf16[384,768]{1,0:T(8,128)(2,1)S(1)}, u32[]{:S(2)}, u32[]{:S(2)}) %collective-permute-start.29) | collective-permute-done | bytes 589856 | tf_op jit(solution)/shard_map/ppermute | solution.py:918
  238.8 1.5 collective-permute-start.30
  241.8 1.6 collective-permute-start.32
  243.4 9.7 %collective-permute-done.30 = bf16[192,768]{1,0:T(8,128)(2,1)S(1)} collective-permute-done((bf16[192,768]{1,0:T(8,128)(2,1)S(1)}, bf16[192,768]{1,0:T(8,128)(2,1)S(1)}, u32[]{:S(2)}, u32[]{:S(2)}) %collective-permute-start.30) | collective-permute-done | bytes 294944 | tf_op jit(solution)/shard_map/ppermute | solution.py:918
  253.2 1.6 add_convert_fusion.2
  256.3 1.9 collective-permute-done.33
  259.9 24.7 %shard_map.204 = (bf16[768,768]{1,0:T(8,128)(2,1)}, bf16[768,768]{1,0:T(8,128)(2,1)}, bf16[768,768]{1,0:T(8,128)(2,1)}, bf16[768,768]{1,0:T(8,128)(2,1)}, f32[2,2,768,768]{3,2,1,0:T(8,128)}, /*index=5*/f32[768,8]{1,0:T(8,128)}) custom-call(bf16[1536,3072]{1,0:T(8,128)(2,1)} %get-tuple-element.163.a_ref, bf16[1536,3072]{1,0:T(8,128)(2,1)} %get-tuple-element.164.du_ref, ...), custom_call_target="tpu_custom_call" | custom-call | flops 1000000 | bytes 100000 | tf_op jit(solution)/shard_map/pallas_call | solution.py:746
  285.1 2.5 collective-permute-done.34.give_0_ref
  287.7 1.7 collective-permute-done.35.give_1_ref
  289.4 3.7 copy-done
  293.1 1.6 shard_map.205
  295.5 1.6 add_convert_fusion.dh_mine_ref
  297.0 2.1 collective-permute-start.39
  299.1 8.3 %all-to-all-start.2 = ((bf16[8,192,768]{2,1,0:T(8,128)(2,1)}), bf16[8,192,768]{2,1,0:T(8,128)(2,1)S(1)}, u32[]{:S(2)}, u32[]{:S(2)}) async-start(bf16[8,192,768]{2,1,0:T(8,128)(2,1)} %bitcast.72), calls=%async_computation.2 | async-start | bytes 4718592 | tf_op jit(solution)/shard_map/all_to_all | solution.py:1108
  307.4 3.7 collective-permute-done.40.dh_near_ref
  311.2 49.2 %shard_map.206 = (f32[512,768]{1,0:T(8,128)}, f32[1,768]{1,0:T(1,128)}, bf16[1024,768]{1,0:T(8,128)(2,1)}, f32[1024,768]{1,0:T(8,128)}, f32[4,96,768]{2,1,0:T(8,...) custom-call(s32[7]{0:T(128)} %copy-done.24, s32[1,2048]{1,0:T(1,128)} %bitcast.71, ...), custom_call_target="tpu_custom_call" | custom-call | flops 1000000 | bytes 100000 | tf_op jit(solution)/shard_map/pallas_call | solution.py:369
  361.1 2.0 collective-permute-start.42
  364.0 4.2 fusion.31
  368.2 8.9 %collective-permute-done.42 = bf16[4,96,768]{2,1,0:T(8,128)(2,1)S(1)} collective-permute-done((bf16[4,96,768]{2,1,0:T(8,128)(2,1)}, bf16[4,96,768]{2,1,0:T(8,128)(2,1)S(1)}, u32[]{:S(2)}, u32[]{:S(2)}) %collective-permute-start.42) | collective-permute-done | bytes 589856 | tf_op jit(solution)/shard_map/ppermute | solution.py:918
  378.3 3.6 shard_map.207
  384.3 2.8 copy-done.4
  387.1 7.6 %shard_map.208 = (bf16[1024,768]{1,0:T(8,128)(2,1)}, f32[1024,768]{1,0:T(8,128)S(1)}) custom-call(bf16[1536,2048]{1,0:T(8,128)(2,1)S(1)} %copy-done.4, bf16[1536,768]{1,0:T(8,128)(2,1)S(1)} %bitcast.69), custom_call_target="tpu_custom_call" | custom-call | flops 1000000 | bytes 100000 | tf_op jit(solution)/shard_map/pallas_call | solution.py:873
  394.7 1.7 copy-done.7
  398.4 1.8 collective-permute-start.51
  401.4 3.0 collective-permute-done.47
  406.0 2.6 collective-permute-done.48
  411.2 2.1 slice.153.near_ref
  414.4 2.4 collective-permute-start.52
  416.9 2.2 add_convert_fusion.4
  420.0 2.2 collective-permute-done.52
  422.7 3.7 collective-permute-done.49
  426.4 2.3 collective-permute-start.50
  430.9 4.1 shard_map.209
  435.0 1.7 copy-done.11
  436.7 2.9 shard_map.210
  440.8 3.9 collective-permute-done.44
  444.8 3.0 add_convert_fusion.3
  (249 shorter events, 56.0 us)
Async XLA Ops:
  0.6 20.8 %collective-permute-start = (bf16[512,768]{1,0:T(8,128)(2,1)}, bf16[512,768]{1,0:T(8,128)(2,1)S(1)}, u32[]{:S(2)}, u32[]{:S(2)}) collective-permute-start(bf16[512,768]{1,0:T(8,128)(2,1)} %c_0_ref.3), channel_id=1, source_target_pairs={{0,2},{1,3},{2,0},{3,1},{4,6},{5,7},{6,4},{7,5},{8,10},{9,11},{10,... | collective-permute-start | bytes 2359304 | tf_op jit(solution)/shard_map/ppermute | solution.py:918
  3.6 21.0 %collective-permute-start.2 = (bf16[512,768]{1,0:T(8,128)(2,1)}, bf16[512,768]{1,0:T(8,128)(2,1)}, u32[]{:S(2)}, u32[]{:S(2)}) collective-permute-start(bf16[512,768]{1,0:T(8,128)(2,1)} %c_0_ref.3), channel_id=1, source_target_pairs={{0,1},{1,0},{2,3},{3,2},{4,5},{5,4},{6,7},{7,6},{8,9},{9,8},{10,11... | collective-permute-start | bytes 2359304 | tf_op jit(solution)/shard_map/ppermute | solution.py:918
  7.0 35.2 %all-to-all-start = ((bf16[8,96,768]{2,1,0:T(8,128)(2,1)}), bf16[8,96,768]{2,1,0:T(8,128)(2,1)}, u32[]{:S(2)}, u32[]{:S(2)}) async-start(bf16[8,96,768]{2,1,0:T(8,128)(2,1)} %broadcast_in_dim.59), calls=%async_computation | async-start | bytes 2359296 | tf_op jit(solution)/shard_map/all_to_all | solution.py:985
  21.9 2.7 collective-permute-start.3
  22.9 23.9 %collective-permute-start.1 = (bf16[512,768]{1,0:T(8,128)(2,1)S(1)}, bf16[512,768]{1,0:T(8,128)(2,1)S(1)}, u32[]{:S(2)}, u32[]{:S(2)}) collective-permute-start(bf16[512,768]{1,0:T(8,128)(2,1)S(1)} %copy-done.2), channel_id=1, source_target_pairs={{0,2},{1,3},{2,0},{3,1},{4,6},{5,7},{6,4},{7,5},{8,10},{9,11},{10,... | collective-permute-start | bytes 2359304 | tf_op jit(solution)/shard_map/ppermute | solution.py:918
  42.2 101.8 %all-to-all-start.1 = ((bf16[8,208,768]{2,1,0:T(8,128)(2,1)}), bf16[8,208,768]{2,1,0:T(8,128)(2,1)}, u32[]{:S(2)}, u32[]{:S(2)}) async-start(bf16[8,208,768]{2,1,0:T(8,128)(2,1)} %copy-done.9), calls=%async_computation.1 | async-start | bytes 5111808 | tf_op jit(solution)/shard_map/all_to_all | solution.py:1041
  46.8 35.6 %collective-permute-start.8 = (bf16[768,768]{1,0:T(8,128)(2,1)S(1)}, bf16[768,768]{1,0:T(8,128)(2,1)}, u32[]{:S(2)}, u32[]{:S(2)}) collective-permute-start(bf16[768,768]{1,0:T(8,128)(2,1)S(1)} %get-tuple-element.116.refs_5_), channel_id=1, source_target_pairs={{0,1},{1,0},{2,3},{3,2},{4,5},{5,4},{6,7},{7,6},{8,9},{9,8},{10,11... | collective-permute-start | bytes 3538952 | tf_op jit(solution)/shard_map/ppermute | solution.py:918
  46.9 33.1 %copy-start.6 = (bf16[512,768]{1,0:T(8,128)(2,1)}, bf16[512,768]{1,0:T(8,128)(2,1)S(1)}, u32[]{:S(2)}) copy-start(bf16[512,768]{1,0:T(8,128)(2,1)S(1)} %collective-permute-done.1.x_1_ref.refs_9_) | copy-start | bytes 2359300
  46.9 36.8 %collective-permute-start.4 = (bf16[768,768]{1,0:T(8,128)(2,1)S(1)}, bf16[768,768]{1,0:T(8,128)(2,1)}, u32[]{:S(2)}, u32[]{:S(2)}) collective-permute-start(bf16[768,768]{1,0:T(8,128)(2,1)S(1)} %get-tuple-element.116.refs_5_), channel_id=1, source_target_pairs={{0,2},{1,3},{2,0},{3,1},{4,6},{5,7},{6,4},{7,5},{8,10},{9,11},{10,... | collective-permute-start | bytes 3538952 | tf_op jit(solution)/shard_map/ppermute | solution.py:918
  47.7 4.6 %collective-permute-start.6 = (bf16[512,768]{1,0:T(8,128)(2,1)S(1)}, bf16[512,768]{1,0:T(8,128)(2,1)S(1)}, u32[]{:S(2)}, u32[]{:S(2)}) collective-permute-start(bf16[512,768]{1,0:T(8,128)(2,1)S(1)} %copy-done.2), channel_id=1, source_target_pairs={{0,1},{1,0},{2,3},{3,2},{4,5},{5,4},{6,7},{7,6},{8,9},{9,8},{10,11... | collective-permute-start | bytes 2359304 | tf_op jit(solution)/shard_map/ppermute | solution.py:918
  47.9 6.3 %collective-permute-start.7 = (bf16[512,768]{1,0:T(8,128)(2,1)S(1)}, bf16[512,768]{1,0:T(8,128)(2,1)}, u32[]{:S(2)}, u32[]{:S(2)}) collective-permute-start(bf16[512,768]{1,0:T(8,128)(2,1)S(1)} %collective-permute-done.1.x_1_ref.refs_9_), channel_id=1, source_target_pairs={{0,1},{1,0},{2,3},{3,2},{4,5},{5,4},{6,7},{7,6},{8,9},{9,8},{10,11... | collective-permute-start | bytes 2359304 | tf_op jit(solution)/shard_map/ppermute | solution.py:918
  48.4 53.2 %collective-permute-start.12 = (bf16[768,768]{1,0:T(8,128)(2,1)}, bf16[768,768]{1,0:T(8,128)(2,1)}, u32[]{:S(2)}, u32[]{:S(2)}) collective-permute-start(bf16[768,768]{1,0:T(8,128)(2,1)} %copy-done.26), channel_id=1, source_target_pairs={{0,4},{4,0},{8,12},{12,8},{16,20},{20,16},{24,28},{28,24},{1,5},{5... | collective-permute-start | bytes 3538952 | tf_op jit(solution)/shard_map/ppermute | solution.py:918
  50.5 29.4 %copy-start.22 = (s32[2048]{0:T(1024)}, s32[2048]{0:T(1024)S(1)}, u32[]{:S(2)}) copy-start(s32[2048]{0:T(1024)S(1)} %select_reduce_fusion) | copy-start | bytes 24580
  51.1 28.8 %copy-start.23 = (f32[1,768]{1,0:T(1,128)}, f32[1,768]{1,0:T(1,128)S(1)}, u32[]{:S(2)}) copy-start(f32[1,768]{1,0:T(1,128)S(1)} %broadcast_in_dim.58.gain_ref) | copy-start | bytes 9220
  52.3 57.6 %copy-start.33 = (bf16[768,192]{1,0:T(8,128)(2,1)}, bf16[768,192]{1,0:T(8,128)(2,1)S(1)}, u32[]{:S(2)}) copy-start(bf16[768,192]{1,0:T(8,128)(2,1)S(1)} %slice.145.refs_4_) | copy-start | bytes 884740
  52.4 31.3 %collective-permute-start.9 = (bf16[768,192]{1,0:T(8,128)(2,1)S(1)}, bf16[768,192]{1,0:T(8,128)(2,1)S(1)}, u32[]{:S(2)}, u32[]{:S(2)}) collective-permute-start(bf16[768,192]{1,0:T(8,128)(2,1)S(1)} %slice.145.refs_4_), channel_id=1, source_target_pairs={{0,2},{1,3},{2,0},{3,1},{4,6},{5,7},{6,4},{7,5},{8,10},{9,11},{10,... | collective-permute-start | bytes 884744 | tf_op jit(solution)/shard_map/ppermute | solution.py:918
  54.2 25.7 %copy-start.24 = (s32[7]{0:T(128)}, s32[7]{0:T(128)S(1)}, u32[]{:S(2)}) copy-start(s32[7]{0:T(128)S(1)} %pad_add_fusion.1.meta_ref) | copy-start | bytes 88
  54.2 50.5 %copy-start.51 = (f32[768]{0:T(1024)S(1)}, f32[768]{0:T(1024)}, u32[]{:S(2)}) copy-start(f32[768]{0:T(1024)} %param.15) | copy-start | bytes 9220
  82.4 27.6 %copy-start.5 = (bf16[192,2048]{1,0:T(8,128)(2,1)}, bf16[192,2048]{1,0:T(8,128)(2,1)S(1)}, u32[]{:S(2)}) copy-start(bf16[192,2048]{1,0:T(8,128)(2,1)S(1)} %get-tuple-element.119.refs_0_.ctx_ref) | copy-start | bytes 2359300
  83.7 19.2 %collective-permute-start.10 = (bf16[192,2048]{1,0:T(8,128)(2,1)S(1)}, bf16[192,2048]{1,0:T(8,128)(2,1)S(1)}, u32[]{:S(2)}, u32[]{:S(2)}) collective-permute-start(bf16[192,2048]{1,0:T(8,128)(2,1)S(1)} %get-tuple-element.119.refs_0_.ctx_ref), channel_id=1, source_target_pairs={{0,2},{1,3},{2,0},{3,1},{4,6},{5,7},{6,4},{7,5},{8,10},{9,11},{10,... | collective-permute-start | bytes 2359304 | tf_op jit(solution)/shard_map/ppermute | solution.py:918
  84.5 19.8 %collective-permute-start.5 = (bf16[768,768]{1,0:T(8,128)(2,1)}, bf16[768,768]{1,0:T(8,128)(2,1)S(1)}, u32[]{:S(2)}, u32[]{:S(2)}) collective-permute-start(bf16[768,768]{1,0:T(8,128)(2,1)} %collective-permute-done.4.refs_7_), channel_id=1, source_target_pairs={{0,1},{1,0},{2,3},{3,2},{4,5},{5,4},{6,7},{7,6},{8,9},{9,8},{10,11... | collective-permute-start | bytes 3538952 | tf_op jit(solution)/shard_map/ppermute | solution.py:918
  102.9 27.1 %collective-permute-start.17 = (bf16[768,768]{1,0:T(8,128)(2,1)}, bf16[768,768]{1,0:T(8,128)(2,1)S(1)}, u32[]{:S(2)}, u32[]{:S(2)}) collective-permute-start(bf16[768,768]{1,0:T(8,128)(2,1)} %collective-permute-done.12.refs_6_), channel_id=1, source_target_pairs={{0,2},{1,3},{2,0},{3,1},{4,6},{5,7},{6,4},{7,5},{8,10},{9,11},{10,... | collective-permute-start | bytes 3538952 | tf_op jit(solution)/shard_map/ppermute | solution.py:918
  103.7 4.5 %collective-permute-start.11 = (bf16[192,2048]{1,0:T(8,128)(2,1)S(1)}, bf16[192,2048]{1,0:T(8,128)(2,1)S(1)}, u32[]{:S(2)}, u32[]{:S(2)}) collective-permute-start(bf16[192,2048]{1,0:T(8,128)(2,1)S(1)} %get-tuple-element.119.refs_0_.ctx_ref), channel_id=1, source_target_pairs={{0,1},{1,0},{2,3},{3,2},{4,5},{5,4},{6,7},{7,6},{8,9},{9,8},{10,11... | collective-permute-start | bytes 2359304 | tf_op jit(solution)/shard_map/ppermute | solution.py:918
  103.7 6.2 %collective-permute-start.13 = (bf16[192,2048]{1,0:T(8,128)(2,1)S(1)}, bf16[192,2048]{1,0:T(8,128)(2,1)}, u32[]{:S(2)}, u32[]{:S(2)}) collective-permute-start(bf16[192,2048]{1,0:T(8,128)(2,1)S(1)} %collective-permute-done.10.refs_1_), channel_id=1, source_target_pairs={{0,1},{1,0},{2,3},{3,2},{4,5},{5,4},{6,7},{7,6},{8,9},{9,8},{10,11... | collective-permute-start | bytes 2359304 | tf_op jit(solution)/shard_map/ppermute | solution.py:918
  104.2 3.5 collective-permute-start.14
  104.3 4.0 collective-permute-start.15
  126.4 16.0 %collective-permute-start.18 = (bf16[768,768]{1,0:T(8,128)(2,1)}, bf16[768,768]{1,0:T(8,128)(2,1)S(1)}, u32[]{:S(2)}, u32[]{:S(2)}) collective-permute-start(bf16[768,768]{1,0:T(8,128)(2,1)} %collective-permute-done.12.refs_6_), channel_id=1, source_target_pairs={{0,1},{1,0},{2,3},{3,2},{4,5},{5,4},{6,7},{7,6},{8,9},{9,8},{10,11... | collective-permute-start | bytes 3538952 | tf_op jit(solution)/shard_map/ppermute | solution.py:918
  130.0 13.9 %collective-permute-start.19 = (bf16[768,768]{1,0:T(8,128)(2,1)S(1)}, bf16[768,768]{1,0:T(8,128)(2,1)S(1)}, u32[]{:S(2)}, u32[]{:S(2)}) collective-permute-start(bf16[768,768]{1,0:T(8,128)(2,1)S(1)} %collective-permute-done.17.refs_8_), channel_id=1, source_target_pairs={{0,1},{1,0},{2,3},{3,2},{4,5},{5,4},{6,7},{7,6},{8,9},{9,8},{10,11... | collective-permute-start | bytes 3538952 | tf_op jit(solution)/shard_map/ppermute | solution.py:918
  130.1 9.8 %collective-permute-start.16 = (bf16[192,768]{1,0:T(8,128)(2,1)}, bf16[192,768]{1,0:T(8,128)(2,1)S(1)}, u32[]{:S(2)}, u32[]{:S(2)}) collective-permute-start(bf16[192,768]{1,0:T(8,128)(2,1)} %get-tuple-element.126), channel_id=1, source_target_pairs={{0,4},{4,0},{8,12},{12,8},{16,20},{20,16},{24,28},{28,24},{1,5},{5... | collective-permute-start | bytes 884744 | tf_op jit(solution)/shard_map/ppermute | solution.py:918
  131.9 33.4 %collective-permute-start.22 = (bf16[192,768]{1,0:T(8,128)(2,1)}, bf16[192,768]{1,0:T(8,128)(2,1)}, u32[]{:S(2)}, u32[]{:S(2)}) collective-permute-start(bf16[192,768]{1,0:T(8,128)(2,1)} %get-tuple-element.133), channel_id=1, source_target_pairs={{0,8},{4,12},{8,0},{12,4},{16,24},{20,28},{24,16},{28,20},{1,9},{5... | collective-permute-start | bytes 884744 | tf_op jit(solution)/shard_map/ppermute | solution.py:918
  133.3 32.6 %collective-permute-start.23 = (bf16[192,768]{1,0:T(8,128)(2,1)}, bf16[192,768]{1,0:T(8,128)(2,1)}, u32[]{:S(2)}, u32[]{:S(2)}) collective-permute-start(bf16[192,768]{1,0:T(8,128)(2,1)} %get-tuple-element.134), channel_id=1, source_target_pairs={{0,12},{4,8},{8,4},{12,0},{16,28},{20,24},{24,20},{28,16},{1,13},{... | collective-permute-start | bytes 884744 | tf_op jit(solution)/shard_map/ppermute | solution.py:918
  139.8 43.5 %collective-permute-start.27 = (bf16[192,768]{1,0:T(8,128)(2,1)}, bf16[192,768]{1,0:T(8,128)(2,1)}, u32[]{:S(2)}, u32[]{:S(2)}) collective-permute-start(bf16[192,768]{1,0:T(8,128)(2,1)} %get-tuple-element.147), channel_id=1, source_target_pairs={{0,16},{4,20},{8,24},{12,28},{16,0},{20,4},{24,8},{28,12},{1,17},{... | collective-permute-start | bytes 884744 | tf_op jit(solution)/shard_map/ppermute | solution.py:918
  142.4 43.9 %collective-permute-start.28 = (bf16[192,768]{1,0:T(8,128)(2,1)}, bf16[192,768]{1,0:T(8,128)(2,1)}, u32[]{:S(2)}, u32[]{:S(2)}) collective-permute-start(bf16[192,768]{1,0:T(8,128)(2,1)} %get-tuple-element.149), channel_id=1, source_target_pairs={{0,20},{4,16},{8,28},{12,24},{16,4},{20,0},{24,12},{28,8},{1,21},{... | collective-permute-start | bytes 884744 | tf_op jit(solution)/shard_map/ppermute | solution.py:918
  162.0 42.9 %collective-permute-start.20 = (bf16[192,768]{1,0:T(8,128)(2,1)S(1)}, bf16[192,768]{1,0:T(8,128)(2,1)S(1)}, u32[]{:S(2)}, u32[]{:S(2)}) collective-permute-start(bf16[192,768]{1,0:T(8,128)(2,1)S(1)} %copy-done.53), channel_id=1, source_target_pairs={{0,24},{4,28},{8,16},{12,20},{16,8},{20,12},{24,0},{28,4},{1,25},{... | collective-permute-start | bytes 884744 | tf_op jit(solution)/shard_map/ppermute | solution.py:918
  165.3 40.6 %collective-permute-start.21 = (bf16[192,768]{1,0:T(8,128)(2,1)}, bf16[192,768]{1,0:T(8,128)(2,1)S(1)}, u32[]{:S(2)}, u32[]{:S(2)}) collective-permute-start(bf16[192,768]{1,0:T(8,128)(2,1)} %get-tuple-element.132), channel_id=1, source_target_pairs={{0,4},{4,0},{8,12},{12,8},{16,20},{20,16},{24,28},{28,24},{1,5},{5... | collective-permute-start | bytes 884744 | tf_op jit(solution)/shard_map/ppermute | solution.py:918
  183.3 22.7 %collective-permute-start.24 = (bf16[192,768]{1,0:T(8,128)(2,1)}, bf16[192,768]{1,0:T(8,128)(2,1)S(1)}, u32[]{:S(2)}, u32[]{:S(2)}) collective-permute-start(bf16[192,768]{1,0:T(8,128)(2,1)} %get-tuple-element.141), channel_id=1, source_target_pairs={{0,8},{4,12},{8,0},{12,4},{16,24},{20,28},{24,16},{28,20},{1,9},{5... | collective-permute-start | bytes 884744 | tf_op jit(solution)/shard_map/ppermute | solution.py:918
  183.4 22.6 %collective-permute-start.25 = (bf16[192,768]{1,0:T(8,128)(2,1)}, bf16[192,768]{1,0:T(8,128)(2,1)S(1)}, u32[]{:S(2)}, u32[]{:S(2)}) collective-permute-start(bf16[192,768]{1,0:T(8,128)(2,1)} %get-tuple-element.142), channel_id=1, source_target_pairs={{0,12},{4,8},{8,4},{12,0},{16,28},{20,24},{24,20},{28,16},{1,13},{... | collective-permute-start | bytes 884744 | tf_op jit(solution)/shard_map/ppermute | solution.py:918
  186.3 19.9 %collective-permute-start.26 = (bf16[192,768]{1,0:T(8,128)(2,1)S(1)}, bf16[192,768]{1,0:T(8,128)(2,1)S(1)}, u32[]{:S(2)}, u32[]{:S(2)}) collective-permute-start(bf16[192,768]{1,0:T(8,128)(2,1)S(1)} %copy-done.52), channel_id=1, source_target_pairs={{0,28},{4,24},{8,20},{12,16},{16,12},{20,8},{24,4},{28,0},{1,29},{... | collective-permute-start | bytes 884744 | tf_op jit(solution)/shard_map/ppermute | solution.py:918
  204.9 33.8 %collective-permute-start.29 = (bf16[384,768]{1,0:T(8,128)(2,1)S(1)}, bf16[384,768]{1,0:T(8,128)(2,1)S(1)}, u32[]{:S(2)}, u32[]{:S(2)}) collective-permute-start(bf16[384,768]{1,0:T(8,128)(2,1)S(1)} %pad_maximum_fusion), channel_id=1, source_target_pairs={{0,16},{4,20},{8,24},{12,28},{16,0},{20,4},{24,8},{28,12},{1,17},{... | collective-permute-start | bytes 1769480 | tf_op jit(solution)/shard_map/ppermute | solution.py:918
  223.9 29.3 %collective-permute-start.31 = (bf16[192,768]{1,0:T(8,128)(2,1)}, bf16[192,768]{1,0:T(8,128)(2,1)S(1)}, u32[]{:S(2)}, u32[]{:S(2)}) collective-permute-start(bf16[192,768]{1,0:T(8,128)(2,1)} %get-tuple-element.170), channel_id=1, source_target_pairs={{0,24},{4,28},{8,16},{12,20},{16,8},{20,12},{24,0},{28,4},{1,25},{... | collective-permute-start | bytes 884744 | tf_op jit(solution)/shard_map/ppermute | solution.py:918
  238.8 14.3 %collective-permute-start.30 = (bf16[192,768]{1,0:T(8,128)(2,1)S(1)}, bf16[192,768]{1,0:T(8,128)(2,1)S(1)}, u32[]{:S(2)}, u32[]{:S(2)}) collective-permute-start(bf16[192,768]{1,0:T(8,128)(2,1)S(1)} %get-tuple-element.257), channel_id=1, source_target_pairs={{0,4},{4,0},{8,12},{12,8},{16,20},{20,16},{24,28},{28,24},{1,5},{5... | collective-permute-start | bytes 884744 | tf_op jit(solution)/shard_map/ppermute | solution.py:918
  241.8 11.4 %collective-permute-start.32 = (bf16[192,768]{1,0:T(8,128)(2,1)S(1)}, bf16[192,768]{1,0:T(8,128)(2,1)S(1)}, u32[]{:S(2)}, u32[]{:S(2)}) collective-permute-start(bf16[192,768]{1,0:T(8,128)(2,1)S(1)} %copy-done.54), channel_id=1, source_target_pairs={{0,28},{4,24},{8,20},{12,16},{16,12},{20,8},{24,4},{28,0},{1,29},{... | collective-permute-start | bytes 884744 | tf_op jit(solution)/shard_map/ppermute | solution.py:918
  254.8 3.5 collective-permute-start.33
  258.9 36.5 %collective-permute-start.38 = (bf16[1024,768]{1,0:T(8,128)(2,1)S(1)}, bf16[1024,768]{1,0:T(8,128)(2,1)S(1)}, u32[]{:S(2)}, u32[]{:S(2)}) collective-permute-start(bf16[1024,768]{1,0:T(8,128)(2,1)S(1)} %add_convert_fusion.1), channel_id=1, source_target_pairs={{0,2},{1,3},{2,0},{3,1},{4,6},{5,7},{6,4},{7,5},{8,10},{9,11},{10,... | collective-permute-start | bytes 4718600 | tf_op jit(solution)/shard_map/ppermute | solution.py:918
  284.6 3.1 collective-permute-start.34
  284.6 4.7 %collective-permute-start.35 = (bf16[768,768]{1,0:T(8,128)(2,1)}, bf16[768,768]{1,0:T(8,128)(2,1)S(1)}, u32[]{:S(2)}, u32[]{:S(2)}) collective-permute-start(bf16[768,768]{1,0:T(8,128)(2,1)} %get-tuple-element.177), channel_id=1, source_target_pairs={{0,1},{1,0},{2,3},{3,2},{4,5},{5,4},{6,7},{7,6},{8,9},{9,8},{10,11... | collective-permute-start | bytes 3538952 | tf_op jit(solution)/shard_map/ppermute | solution.py:918
  297.0 63.3 %collective-permute-start.39 = (bf16[2,768,768]{2,1,0:T(8,128)(2,1)}, bf16[2,768,768]{2,1,0:T(8,128)(2,1)}, u32[]{:S(2)}, u32[]{:S(2)}) collective-permute-start(bf16[2,768,768]{2,1,0:T(8,128)(2,1)} %shard_map.205), channel_id=1, source_target_pairs={{4,6},{5,7},{6,4},{7,5},{12,14},{13,15},{14,12},{15,13},{20,22},{2... | collective-permute-start | bytes 7077896 | tf_op jit(solution)/shard_map/ppermute | solution.py:926
  299.1 85.3 %all-to-all-start.2 = ((bf16[8,192,768]{2,1,0:T(8,128)(2,1)}), bf16[8,192,768]{2,1,0:T(8,128)(2,1)S(1)}, u32[]{:S(2)}, u32[]{:S(2)}) async-start(bf16[8,192,768]{2,1,0:T(8,128)(2,1)} %bitcast.72), calls=%async_computation.2 | async-start | bytes 4718592 | tf_op jit(solution)/shard_map/all_to_all | solution.py:1108
  307.3 3.8 collective-permute-start.40
  360.4 3.7 collective-permute-start.41
  360.6 17.7 %collective-permute-start.36 = (bf16[768,768]{1,0:T(8,128)(2,1)}, bf16[768,768]{1,0:T(8,128)(2,1)S(1)}, u32[]{:S(2)}, u32[]{:S(2)}) collective-permute-start(bf16[768,768]{1,0:T(8,128)(2,1)} %get-tuple-element.179), channel_id=1, source_target_pairs={{0,1},{1,0},{2,3},{3,2},{4,5},{5,4},{6,7},{7,6},{8,9},{9,8},{10,11... | collective-permute-start | bytes 3538952 | tf_op jit(solution)/shard_map/ppermute | solution.py:918
  360.9 17.4 %collective-permute-start.37 = (bf16[768,768]{1,0:T(8,128)(2,1)}, bf16[768,768]{1,0:T(8,128)(2,1)S(1)}, u32[]{:S(2)}, u32[]{:S(2)}) collective-permute-start(bf16[768,768]{1,0:T(8,128)(2,1)} %get-tuple-element.180), channel_id=1, source_target_pairs={{0,1},{1,0},{2,3},{3,2},{4,5},{5,4},{6,7},{7,6},{8,9},{9,8},{10,11... | collective-permute-start | bytes 3538952 | tf_op jit(solution)/shard_map/ppermute | solution.py:918
  361.1 16.1 %collective-permute-start.42 = (bf16[4,96,768]{2,1,0:T(8,128)(2,1)}, bf16[4,96,768]{2,1,0:T(8,128)(2,1)S(1)}, u32[]{:S(2)}, u32[]{:S(2)}) collective-permute-start(bf16[4,96,768]{2,1,0:T(8,128)(2,1)} %get-tuple-element.194), channel_id=1, source_target_pairs={{0,4},{4,0},{8,12},{12,8},{16,20},{20,16},{24,28},{28,24},{1,5},{5... | collective-permute-start | bytes 1769480 | tf_op jit(solution)/shard_map/ppermute | solution.py:918
  396.4 20.5 %collective-permute-start.43 = (bf16[1024,768]{1,0:T(8,128)(2,1)}, bf16[1024,768]{1,0:T(8,128)(2,1)}, u32[]{:S(2)}, u32[]{:S(2)}) collective-permute-start(bf16[1024,768]{1,0:T(8,128)(2,1)} %get-tuple-element.200), channel_id=1, source_target_pairs={{0,1},{1,0},{2,3},{3,2},{4,5},{5,4},{6,7},{7,6},{8,9},{9,8},{10,11... | collective-permute-start | bytes 4718600 | tf_op jit(solution)/shard_map/ppermute | solution.py:918
  396.7 3.5 collective-permute-start.46
  398.4 14.9 %collective-permute-start.51 = (bf16[2,96,768]{2,1,0:T(8,128)(2,1)S(1)}, bf16[2,96,768]{2,1,0:T(8,128)(2,1)S(1)}, u32[]{:S(2)}, u32[]{:S(2)}) collective-permute-start(bf16[2,96,768]{2,1,0:T(8,128)(2,1)S(1)} %slice.197), channel_id=1, source_target_pairs={{0,8},{4,12},{8,0},{12,4},{16,24},{20,28},{24,16},{28,20},{1,9},{5... | collective-permute-start | bytes 884744 | tf_op jit(solution)/shard_map/ppermute | solution.py:918
  400.3 4.2 collective-permute-start.47
  404.4 4.2 collective-permute-start.48
  408.6 26.4 %collective-permute-start.53 = (bf16[768,768]{1,0:T(8,128)(2,1)}, bf16[768,768]{1,0:T(8,128)(2,1)}, u32[]{:S(2)}, u32[]{:S(2)}) collective-permute-start(bf16[768,768]{1,0:T(8,128)(2,1)} %copy-done.27), channel_id=1, source_target_pairs={{0,4},{4,0},{8,12},{12,8},{16,20},{20,16},{24,28},{28,24},{1,5},{5... | collective-permute-start | bytes 3538952 | tf_op jit(solution)/shard_map/ppermute | solution.py:918
  410.1 20.8 %collective-permute-start.45 = (bf16[512,768]{1,0:T(8,128)(2,1)}, bf16[512,768]{1,0:T(8,128)(2,1)}, u32[]{:S(2)}, u32[]{:S(2)}) collective-permute-start(bf16[512,768]{1,0:T(8,128)(2,1)} %get-tuple-element.254), channel_id=1, source_target_pairs={{0,2},{1,3},{2,0},{3,1},{4,6},{5,7},{6,4},{7,5},{8,10},{9,11},{10,... | collective-permute-start | bytes 2359304 | tf_op jit(solution)/shard_map/ppermute | solution.py:918
  414.4 7.8 %collective-permute-start.52 = (bf16[1,96,768]{2,1,0:T(8,128)(2,1)S(1)}, bf16[1,96,768]{2,1,0:T(8,128)(2,1)S(1)}, u32[]{:S(2)}, u32[]{:S(2)}) collective-permute-start(bf16[1,96,768]{2,1,0:T(8,128)(2,1)S(1)} %slice.198), channel_id=1, source_target_pairs={{0,16},{4,20},{8,24},{12,28},{16,0},{20,4},{24,8},{28,12},{1,17},{... | collective-permute-start | bytes 442376 | tf_op jit(solution)/shard_map/ppermute | solution.py:918
  419.0 25.7 %collective-permute-start.44 = (bf16[512,768]{1,0:T(8,128)(2,1)}, bf16[512,768]{1,0:T(8,128)(2,1)}, u32[]{:S(2)}, u32[]{:S(2)}) collective-permute-start(bf16[512,768]{1,0:T(8,128)(2,1)} %add_convert_fusion.4), channel_id=1, source_target_pairs={{0,2},{1,3},{2,0},{3,1},{4,6},{5,7},{6,4},{7,5},{8,10},{9,11},{10,... | collective-permute-start | bytes 2359304 | tf_op jit(solution)/shard_map/ppermute | solution.py:918
  422.3 4.2 collective-permute-start.49
  426.4 13.2 %collective-permute-start.50 = (f32[10,768]{1,0:T(8,128)S(1)}, f32[10,768]{1,0:T(8,128)S(1)}, u32[]{:S(2)}, u32[]{:S(2)}) collective-permute-start(f32[10,768]{1,0:T(8,128)S(1)} %add.132), channel_id=1, source_target_pairs={{0,16},{4,20},{8,24},{12,28},{16,0},{20,4},{24,8},{28,12},{1,17},{... | collective-permute-start | bytes 92168 | tf_op jit(solution)/shard_map/ppermute | solution.py:918
  (51 other events, 338.1 us)

commit v4 on v3

--- a/solution.py
+++ b/solution.py
@@ -189,7 +189,7 @@
 def attend_back_kernel(
     meta_ref, start_ref, x_ref, dh_mine_ref, dh_near_ref, c_0_ref, c_1_ref, c_2_ref, c_3_ref,
     gain_ref, w_ref, qt_ref, q_ref, k_ref, kt_ref, v_ref, ctxt_ref, lse_ref, h_ref, ctx_ref,
-    dx_ref, dgain_ref, send_ref, mine_ref, keep_ref, give_ref, dots_ref,
+    dx_ref, dgain_ref, send_own_ref, send_far_ref, own_ref, far_ref, keep_ref, give_ref, dots_ref,
     dk_acc, dv_acc, dh_ref, c_ref, dqkv, d_all, acc,
 ):
     step = pl.program_id(0)
@@ -284,13 +284,13 @@
         acc[:, : 3 * width] += mm_tn(h_ref[...], grads)
         acc[:, 3 * width :] += mm_tn(d_all[rows, :], ctx_ref[...].T)
 
-    @pl.when((step == 4) | (step == 5))
-    def _():
-        rest(send_ref, LOW)
-
-    @pl.when(step >= 6)
-    def _():
-        rest(mine_ref, WIDE)
+    for n, (out, kind) in enumerate(
+        ((send_own_ref, LOW), (send_far_ref, LOW), (own_ref, WIDE), (far_ref, WIDE))
+    ):
+
+        @pl.when(step == 4 + n)
+        def _(out=out, kind=kind):
+            rest(out, kind)
 
     @pl.when(step == 7)
     def _():
@@ -352,8 +352,7 @@
         out_specs=[
             out(BLOCK, features),
             out(1, features),
-            pl.BlockSpec((BLOCK, features), lambda i, m: (jnp.clip(i - 4, 0, 1), 0)),
-            pl.BlockSpec((BLOCK, features), lambda i, m: (jnp.clip(i - 6, 0, 1), 0)),
+            *([out(BLOCK, features)] * 4),
             out(*share),
             out(*share),
             out(features, 1),
@@ -372,8 +371,8 @@
         out_shape=[
             jax.ShapeDtypeStruct((BLOCK, features), WIDE),
             jax.ShapeDtypeStruct((1, features), WIDE),
-            jax.ShapeDtypeStruct((2 * BLOCK, features), LOW),
-            jax.ShapeDtypeStruct((2 * BLOCK, features), WIDE),
+            *([jax.ShapeDtypeStruct((BLOCK, features), LOW)] * 2),
+            *([jax.ShapeDtypeStruct((BLOCK, features), WIDE)] * 2),
             jax.ShapeDtypeStruct(share, WIDE),
             jax.ShapeDtypeStruct(share, LOW),
             jax.ShapeDtypeStruct((features, 1), WIDE),
@@ -784,12 +783,14 @@
     )(keep, *give)
 
 
-def home_kernel(keep_ref, give_0_ref, give_1_ref, far_ref, kept_ref, other_ref):
+def home_kernel(keep_ref, give_0_ref, give_1_ref, far_ref, kept_ref, *other_refs):
     held = keep_ref[0, 0] + far_ref[0].astype(WIDE)
 
     @pl.when(pl.program_id(0) == 0)
     def _():
-        other_ref[...] = (held + give_1_ref[...].astype(WIDE)).astype(LOW)
+        other = (held + give_1_ref[...].astype(WIDE)).astype(LOW)
+        for n, out in enumerate(other_refs):
+            out[...] = other[n * out.shape[0] : (n + 1) * out.shape[0]]
 
     @pl.when(pl.program_id(0) == 1)
     def _():
@@ -808,30 +809,26 @@
             whole,
             pl.BlockSpec((1, rows, features), lambda m: (1 - m, 0, 0)),
         ],
-        out_specs=[whole, whole],
-        out_shape=[
-            jax.ShapeDtypeStruct((rows, features), WIDE),
-            jax.ShapeDtypeStruct((rows, features), LOW),
-        ],
+        out_specs=[whole] + [pl.BlockSpec((rows // 2, features), lambda m: (0, 0))] * 2,
+        out_shape=[jax.ShapeDtypeStruct((rows, features), WIDE)]
+        + [jax.ShapeDtypeStruct((rows // 2, features), LOW)] * 2,
         compiler_params=pltpu.CompilerParams(vmem_limit_bytes=40 * 2**20),
         cost_estimate=LITTLE,
     )(keep, *give, far)
 
 
-def choose_kernel(odd_ref, kept_ref, other_ref, first_ref, second_ref):
+def choose_kernel(odd_ref, kept_ref, other_0_ref, other_1_ref, first_ref, second_ref):
     units = second_ref.shape[1]
 
-    def store(value):
-        first_ref[0] = value[:units].T
-        second_ref[0] = value[units:]
-
     @pl.when(odd_ref[0] == 1)
     def _():
-        store(kept_ref[...])
+        first_ref[0] = kept_ref[:units, :].T
+        second_ref[0] = kept_ref[units:, :]
 
     @pl.when(odd_ref[0] == 0)
     def _():
-        store(other_ref[...].astype(WIDE))
+        first_ref[0] = other_0_ref[...].astype(WIDE).T
+        second_ref[0] = other_1_ref[...].astype(WIDE)
 
 
 def choose(odd, kept, other):
@@ -841,7 +838,7 @@
     grid_spec = pltpu.PrefetchScalarGridSpec(
         num_scalar_prefetch=1,
         grid=(1,),
-        in_specs=[whole(rows, features), whole(rows, features)],
+        in_specs=[whole(rows, features)] + [whole(units, features)] * 2,
         out_specs=[whole(1, features, units), whole(1, units, features)],
     )
     return pl.pallas_call(
@@ -853,19 +850,16 @@
         ],
         compiler_params=pltpu.CompilerParams(vmem_limit_bytes=40 * 2**20),
         cost_estimate=LITTLE,
-    )(odd, kept, other)
-
-
-def tokens_kernel(hot_ref, rows_ref, send_ref, keep_ref):
+    )(odd, kept, *other)
+
+
+def tokens_kernel(hot_ref, rows_ref, *out_refs):
     total = mm_tn(hot_ref[...], rows_ref[...])
-
-    @pl.when(pl.program_id(0) < 2)
-    def _():
-        send_ref[...] = total.astype(LOW)
-
-    @pl.when(pl.program_id(0) >= 2)
-    def _():
-        keep_ref[...] = total
+    for n, out in enumerate(out_refs):
+
+        @pl.when(pl.program_id(0) == n)
+        def _(out=out):
+            out[...] = total.astype(out.dtype)
 
 
 def to_tokens(hot, rows):
@@ -877,14 +871,9 @@
             pl.BlockSpec((count, BLOCK), lambda i: (0, i ^ 2)),
             pl.BlockSpec((count, features), lambda i: (0, 0)),
         ],
-        out_specs=[
-            pl.BlockSpec((BLOCK, features), lambda i: (jnp.minimum(i, 1), 0)),
-            pl.BlockSpec((BLOCK, features), lambda i: (jnp.maximum(i - 2, 0), 0)),
-        ],
-        out_shape=[
-            jax.ShapeDtypeStruct((2 * BLOCK, features), LOW),
-            jax.ShapeDtypeStruct((2 * BLOCK, features), WIDE),
-        ],
+        out_specs=[pl.BlockSpec((BLOCK, features), lambda i: (0, 0))] * 4,
+        out_shape=[jax.ShapeDtypeStruct((BLOCK, features), LOW)] * 2
+        + [jax.ShapeDtypeStruct((BLOCK, features), WIDE)] * 2,
         compiler_params=pltpu.CompilerParams(vmem_limit_bytes=40 * 2**20),
         cost_estimate=LITTLE,
     )(hot, rows)
@@ -932,21 +921,6 @@
 
 def joined(pieces):
     return jnp.concatenate(pieces, axis=0)
-
-
-def sum_over_dp_scattered(keep, give, other):
-    bits, first = 1, None
-    while True:
-        come = flip(give, "dp", bits)
-        if first is None:
-            come = after(come, other)
-        keep = keep + come.astype(WIDE)
-        first = keep if first is None else first
-        count = keep.shape[0]
-        if count == 1:
-            return keep[0], first
-        keep, give = keep[: count // 2], keep[count // 2 :].astype(LOW)
-        bits *= 2
 
 
 def body(
@@ -1008,24 +982,6 @@
     placed = jnp.pad(placed, ((0, 3), (0, 0)))
     here_dp = dp_index.astype(jnp.int32)[None]
 
-    kept, given = expert_halves(
-        after(odd.astype(jnp.int32)[None], c_far), frozen_in, frozen_out, fresh_in, fresh_out
-    )
-
-    come = flip(given, "dp", 1)
-
-    c_pieces = [cotangent, c_far, c_near, flip(after(c_far, kept), "head", 1)]
-    c_out, in_order, picks = send_rows(here_dp, placed, c_pieces, dp_count, share)
-    x_far = after(x_far, c_out)
-    x_pieces = [block_input, x_far, x_near, flip(x_far, "head", 1)]
-
-    kept_far = flip(after(kept, x_far), "head", 2)
-
-    near_kept = flip(kept, "head", 1)
-    out = weights[:, 3 * width :]
-    out_far, out_near = flip(out, "head", 2), flip(out, "head", 1)
-    out_last = flip(out_far, "head", 1)
-
     ends = jnp.cumsum(doc_lengths[0])
     start = jnp.max(jnp.where(tokens[:, None] >= ends[None], ends[None], 0), axis=1)
     own_kind = dp_index // 2 + odd * (kinds // 2)
@@ -1033,13 +989,32 @@
         [head_index[None], start[::BLOCK] // BLOCK, dp_index[None], own_kind[None]]
     ).astype(jnp.int32)
     start = start[None]
+
+    kept, given = expert_halves(
+        after(odd.astype(jnp.int32)[None], c_far), frozen_in, frozen_out, fresh_in, fresh_out
+    )
+
+    come = flip(given, "dp", 1)
+
+    c_pieces = [cotangent, c_far, c_near, flip(after(c_far, kept), "head", 1)]
+    c_out, in_order, picks = send_rows(after(here_dp, meta, start), placed, c_pieces, dp_count, share)
+    x_far = after(x_far, c_out)
+    x_pieces = [block_input, x_far, x_near, flip(x_far, "head", 1)]
+
+    kept_far = flip(after(kept, x_far), "head", 2)
+
+    near_kept = flip(kept, "head", 1)
+    out = weights[:, 3 * width :]
+    out_far, out_near = flip(out, "head", 2), flip(out, "head", 1)
+    out_last = flip(out_far, "head", 1)
+
     h_one, qt, queries, keys, kt, values, context, context_t, log_totals = attend(
         meta, start, x_pieces, gain_one, weights, width
     )
     near_context = flip(context, "head", 1)
     far_context = flip(after(context, kept_far, near_kept, out_far), "head", 2)
     c_in = lax.all_to_all(c_out, "dp", 0, 0, tiled=True)
-    last_context = flip(after(far_context, come), "head", 1)
+    last_context = flip(after(far_context, come, out_near, out_last), "head", 1)
     come_far = flip(after(come, far_context), "head", 2)
     last_kept = flip(kept_far, "head", 1)
     per = dp_count // 4
@@ -1085,7 +1060,9 @@
     *give, keep, grad_gate = expert_grads(hidden, hidden_grads, after(x_all, here), dy_all, marks)
     give = [flip(part, "head", 1) for part in give]
     leave = far_sum(keep, give[2:])
-    gated = after(gated, leave)
+    gated = lax.all_to_all(
+        after(gated, keep).reshape(dp_count, share, features), "dp", 0, 0, tiled=True
+    ).reshape(dp_count * share, features)
     dh_mine = (
         here.astype(WIDE) + joined([across[own_rows:], across[:own_rows]]).astype(WIDE)
     ).astype(LOW)
@@ -1093,39 +1070,48 @@
     crossed = flip_head_where(after(leave, dh_mine), 2, 1)
     keep_home, give_home = keep, give[:2]
 
-    dx_one, grad_gain_two, send, mine, keep, give, dots = attend_back(
+    dx_one, grad_gain_two, send_own, send_far, own, far, keep, give, dots = attend_back(
         meta, start, x_one, [dh_mine, dh_near], c_pieces, gain_two, weights,
         qt, queries, keys, kt, values, context_t, log_totals, h_one, context, dp_count,
     )
-    send = flip(after(send, crossed), "head", 1)
-    far_out = (mine[own_rows:] + send[own_rows:].astype(WIDE)).astype(LOW)
+    send_far = flip(after(send_far, crossed), "head", 1)
+    send_own = flip(send_own, "head", 1)
+    far_out = (far + send_far.astype(WIDE)).astype(LOW)
     far = flip(far_out, "head", 2)
-    grad_input = finish(mine[:own_rows], send[:own_rows], far, block_input, gain_one, dx_one)
-    grads, once_summed = sum_over_dp_scattered(keep, give, far_out)
-    grad_qkv = jnp.stack([grads[:, n * width : (n + 1) * width] for n in range(3)])
-    grad_out_weight = grads[:, 3 * width :].T
-
-    gated = lax.all_to_all(
-        gated.reshape(dp_count, share, features), "dp", 0, 0, tiled=True
-    ).reshape(dp_count * share, features)
+    grad_input = finish(own, send_own, far, block_input, gain_one, dx_one)
+
+    y_send_own, y_send_far, y_own, y_far = to_tokens(in_order, after(gated, give))
+    tokens_done = y_own
+    y_send_far = flip(y_send_far, "head", 1)
+    y_send_own = flip(y_send_own, "head", 1)
+    y_out = (y_far + y_send_far.astype(WIDE)).astype(LOW)
+    y_far = flip(y_out, "head", 2)
+    mixture = y_own + y_send_own.astype(WIDE) + y_far.astype(WIDE)
+    result = (x_one[:own_rows] + mixture).astype(LOW)
+
+    dots = after(dots, send_far)
     small = joined([dots[:, 0][None] / gain_one, grad_gain_two, grad_gate.T])
     for bits in (1, 2):
         small = small + flip(small, "head", bits)
-    small = after(small, once_summed)
-    small = small + flip(small, "dp", 1)
-    kept_home, other = home_sum(keep_home, give_home, after(crossed, far_out, once_summed))
-    over = flip(after(other, small), "dp", 1)
-    send, mine = to_tokens(in_order, after(gated, other))
-    send = flip(send, "head", 1)
-    y_out = (mine[own_rows:] + send[own_rows:].astype(WIDE)).astype(LOW)
-    y_far = flip(y_out, "head", 2)
-    mixture = mine[:own_rows] + send[:own_rows].astype(WIDE) + y_far.astype(WIDE)
-    result = (x_one[:own_rows] + mixture).astype(LOW)
-    small = after(small, y_out)
-    bits = 2
+    keep = keep + after(flip(give, "dp", 1), far_out, small, tokens_done).astype(WIDE)
+    kept_home, *other = home_sum(keep_home, give_home, after(crossed, keep))
+    over = [flip(part, "dp", 1) for part in other]
+    bits, small = 2, after(small, over[0])
     while bits < dp_count:
+        count = keep.shape[0]
+        come = flip(keep[count // 2 :].astype(LOW), "dp", bits)
         small = small + flip(small, "dp", bits)
+        if bits == 2:
+            come = after(come, *other)
+        if count == 2:
+            small = after(small, y_out)
+            small = small + flip(small, "dp", 1)
+            come = after(come, y_far, small, grad_input)
+        keep = keep[: count // 2] + come.astype(WIDE)
         bits *= 2
+    grads = keep[0]
+    grad_qkv = jnp.stack([grads[:, n * width : (n + 1) * width] for n in range(3)])
+    grad_out_weight = grads[:, 3 * width :].T
     grad_fresh_in, grad_fresh_out = choose(odd.astype(jnp.int32)[None], kept_home, over)
     return (
         result,

time: 457 us -> 439 us (0.961)
  waiting for transfers between devices: 96.7 us -> 82.3 us
  local copies, waits for them, and re-layouts: 35.2 us -> 29.1 us
  starting transfers between devices: 72.9 us -> 77.9 us
    ppermute x53 -> x56, waiting for transfers between devices: 94.8 us -> 81 us  [flip(): return lax.ppermute(array, axis, [(i, i ^ bits) for i in range(size)])]
    ppermute x53 -> x56, starting transfers between devices: 52.2 us -> 58.6 us  [flip(): return lax.ppermute(array, axis, [(i, i ^ bits) for i in range(size)])]
    unnamed x124 -> x132, local copies, waits for them, and re-layouts: 26.6 us -> 22.9 us
  transfers between devices with their start and end apart: 57 -> 60, of which waited for: 25 -> 21; matrix products, arithmetic and copies ran while one was open for 7% -> 6% of each run, Pallas kernels for 46% -> 50%
where the time goes in v4:
time: 439 us; the launch traced here: 431 us
  Pallas kernels  217 us (49%)
  waiting for transfers between devices  82.3 us (19%)
  starting transfers between devices  77.9 us (18%)
  local copies, waits for them, and re-layouts  29.1 us (7%)
  other arithmetic  13.9 us (3%)
  matrix products  9.03 us (2%)
    ppermute x56, waiting for transfers between devices, flip(): return lax.ppermute(array, axis, [(i, i ^ bits) for i in range(size)])  81 us
    pallas_call x4, Pallas kernels, run_experts(): pl.pallas_call(functools.partial(expert_kernel, count), grid_spec=grid_sp...  68.2 us
    ppermute x56, starting transfers between devices, flip(): return lax.ppermute(array, axis, [(i, i ^ bits) for i in range(size)])  58.6 us
    pallas_call x1, Pallas kernels, attend_back(): pl.pallas_call(attend_back_kernel, grid_spec=grid_spec, out_shape=[jax.Sh...  50.6 us
    pallas_call x1, Pallas kernels, attend(): pl.pallas_call(attend_kernel, grid_spec=grid_spec, out_shape=[jax.ShapeDt...  25.7 us
    pallas_call x1, Pallas kernels, expert_grads(): pl.pallas_call(expert_grads_kernel, grid=(4,), in_specs=[piece, piece, al...  24.7 us
    unnamed x132, local copies, waits for them, and re-layouts  22.9 us
    pallas_call x1, Pallas kernels, mix(): pl.pallas_call(functools.partial(mix_kernel, count), grid=(4,), in_specs=...  16.3 us
  transfers between devices with their start and end apart: 60, of which 21 were waited for; matrix products, arithmetic and copies ran while one was open for 6% of the time, Pallas kernels for 50%

profile of v4, /device:TPU:0, one launch (start us, length us, event | category | flops | bytes accessed | tf_op | source)
XLA Modules:
  0.0 431.1 jit_solution(5049815123235083859)
XLA Ops:
  0.6 3.0 collective-permute-start
  7.0 5.8 %all-to-all-start = ((bf16[8,96,768]{2,1,0:T(8,128)(2,1)}), bf16[8,96,768]{2,1,0:T(8,128)(2,1)}, u32[]{:S(2)}, u32[]{:S(2)}) async-start(bf16[8,96,768]{2,1,0:T(8,128)(2,1)} %broadcast_in_dim.59), calls=%async_computation | async-start | bytes 2359296 | tf_op jit(solution)/shard_map/all_to_all | solution.py:959
  13.7 1.5 fusion.16
  15.4 6.0 %collective-permute-done.c_1_ref = bf16[512,768]{1,0:T(8,128)(2,1)S(1)} collective-permute-done((bf16[512,768]{1,0:T(8,128)(2,1)}, bf16[512,768]{1,0:T(8,128)(2,1)S(1)}, u32[]{:S(2)}, u32[]{:S(2)}) %collective-permute-start) | collective-permute-done | bytes 786464 | tf_op jit(solution)/shard_map/ppermute | solution.py:907
  23.1 1.8 collective-permute-start.1
  25.2 9.9 %shard_map.197 = (bf16[8,208,768]{2,1,0:T(8,128)(2,1)S(1)}, bf16[1536,2048]{1,0:T(8,128)(2,1)S(1)}, bf16[1536,2048]{1,0:T(8,128)(2,1)}) custom-call(s32[1]{0:T(128)} %bitcast.1.index_ref, s32[8,2048]{1,0:T(8,128)S(1)} %pad.5.placed_ref, bf16[512,768]{1,0:T(8,128)(2,1)S(1)} %copy-done.14, bf16[512,768]{1,0:T(8,128)(2,1)S(1)} %collective-permute-done.c_1_ref, ...), custom_call_target="tpu_custom_call" | custom-call | flops 40000000000 | bytes 10000000 | tf_op jit(solution)/shard_map/pallas_call | solution.py:435
  35.2 2.6 copy-done.3
  37.8 1.6 copy-done.7
  42.2 4.9 %all-to-all-start.1 = ((bf16[8,208,768]{2,1,0:T(8,128)(2,1)}), bf16[8,208,768]{2,1,0:T(8,128)(2,1)}, u32[]{:S(2)}, u32[]{:S(2)}) async-start(bf16[8,208,768]{2,1,0:T(8,128)(2,1)} %copy-done.7), calls=%async_computation.1 | async-start | bytes 5111808 | tf_op jit(solution)/shard_map/all_to_all | solution.py:1016
  47.1 1.6 collective-permute-start.4
  49.2 2.0 collective-permute-start.12
  54.2 25.7 %shard_map.198 = (bf16[2048,768]{1,0:T(8,128)(2,1)}, bf16[3,64,2048]{2,1,0:T(8,128)(2,1)S(1)}, bf16[3,2048,64]{2,1,0:T(8,128)(2,1)}, bf16[3,2048,64]{2,1,0:T(8,1...) custom-call(s32[7]{0:T(128)S(1)} %pad_add_fusion.1.meta_ref, ...), custom_call_target="tpu_custom_call" | custom-call | flops 1000000 | bytes 100000 | tf_op jit(solution)/shard_map/pallas_call | solution.py:170
  82.3 1.7 collective-permute-done.9.refs_5_
  84.0 1.6 collective-permute-start.10
  86.1 16.5 %collective-permute-done.12.refs_6_ = bf16[768,768]{1,0:T(8,128)(2,1)} collective-permute-done((bf16[768,768]{1,0:T(8,128)(2,1)}, bf16[768,768]{1,0:T(8,128)(2,1)}, u32[]{:S(2)}, u32[]{:S(2)}) %collective-permute-start.12) | collective-permute-done | bytes 1179680 | tf_op jit(solution)/shard_map/ppermute | solution.py:907
  108.3 16.3 %shard_map.199 = (f32[2048,768]{1,0:T(8,128)}, bf16[192,768]{1,0:T(8,128)(2,1)}, bf16[192,768]{1,0:T(8,128)(2,1)}, bf16[192,768]{1,0:T(8,128)(2,1)}, bf16[192,76...) custom-call(f32[1,768]{1,0:T(1,128)} %broadcast_in_dim.29.gain_ref, ...), custom_call_target="tpu_custom_call" | custom-call | flops 1000000 | bytes 100000 | tf_op jit(solution)/shard_map/pallas_call | solution.py:516
  124.9 5.5 %collective-permute-done.17.refs_8_ = bf16[768,768]{1,0:T(8,128)(2,1)S(1)} collective-permute-done((bf16[768,768]{1,0:T(8,128)(2,1)}, bf16[768,768]{1,0:T(8,128)(2,1)S(1)}, u32[]{:S(2)}, u32[]{:S(2)}) %collective-permute-start.17) | collective-permute-done | bytes 1179680 | tf_op jit(solution)/shard_map/ppermute | solution.py:907
  130.4 2.1 collective-permute-start.16
  134.0 6.4 %collective-permute-done.16.refs_1_ = bf16[192,768]{1,0:T(8,128)(2,1)S(1)} collective-permute-done((bf16[192,768]{1,0:T(8,128)(2,1)}, bf16[192,768]{1,0:T(8,128)(2,1)S(1)}, u32[]{:S(2)}, u32[]{:S(2)}) %collective-permute-start.16) | collective-permute-done | bytes 294944 | tf_op jit(solution)/shard_map/ppermute | solution.py:907
  140.3 2.5 collective-permute-start.27
  142.9 1.6 collective-permute-start.28
  144.5 16.9 %shard_map.200 = (bf16[1536,3072]{1,0:T(8,128)(2,1)}, bf16[1536,3072]{1,0:T(8,128)(2,1)}, bf16[1536,768]{1,0:T(8,128)(2,1)}, bf16[1536,768]{1,0:T(8,128)(2,1)}, ...) custom-call(s32[7]{0:T(128)} %copy-done.22, ...), custom_call_target="tpu_custom_call" | custom-call | flops 1000000 | bytes 100000 | tf_op jit(solution)/shard_map/pallas_call | solution.py:689
  161.5 3.3 collective-permute-start.20
  165.4 17.2 %shard_map.201 = (bf16[1536,3072]{1,0:T(8,128)(2,1)}, bf16[1536,3072]{1,0:T(8,128)(2,1)}, bf16[1536,768]{1,0:T(8,128)(2,1)}, bf16[1536,768]{1,0:T(8,128)(2,1)}, ...) custom-call(s32[7]{0:T(128)} %copy-done.22, ...), custom_call_target="tpu_custom_call", output_to_operand_aliasing={{0}: (14, {}), {1}: (15, {}), {2}: (16, {}), {3}: (17, {}),... | custom-call | flops 1000000 | bytes 100000 | tf_op jit(solution)/shard_map/pallas_call | solution.py:689
  182.6 2.9 collective-permute-start.25
  186.5 16.9 %shard_map.202 = (bf16[1536,3072]{1,0:T(8,128)(2,1)}, bf16[1536,3072]{1,0:T(8,128)(2,1)}, bf16[1536,768]{1,0:T(8,128)(2,1)}, bf16[1536,768]{1,0:T(8,128)(2,1)}, ...) custom-call(s32[7]{0:T(128)} %copy-done.22, ...), custom_call_target="tpu_custom_call", output_to_operand_aliasing={{0}: (14, {}), {1}: (15, {}), {2}: (16, {}), {3}: (17, {}),... | custom-call | flops 1000000 | bytes 100000 | tf_op jit(solution)/shard_map/pallas_call | solution.py:689
  206.1 17.2 %shard_map.203 = (bf16[1536,3072]{1,0:T(8,128)(2,1)}, bf16[1536,3072]{1,0:T(8,128)(2,1)}, bf16[1536,768]{1,0:T(8,128)(2,1)}, bf16[1536,768]{1,0:T(8,128)(2,1)}, ...) custom-call(s32[7]{0:T(128)} %copy-done.22, ...), custom_call_target="tpu_custom_call", output_to_operand_aliasing={{0}: (14, {}), {1}: (15, {}), {2}: (16, {}), {3}: (17, {}),... | custom-call | flops 1000000 | bytes 100000 | tf_op jit(solution)/shard_map/pallas_call | solution.py:689
  223.3 2.8 collective-permute-start.31
  226.2 3.0 fusion.10
  229.2 8.8 %collective-permute-done.29 = bf16[384,768]{1,0:T(8,128)(2,1)S(1)} collective-permute-done((bf16[384,768]{1,0:T(8,128)(2,1)S(1)}, bf16[384,768]{1,0:T(8,128)(2,1)S(1)}, u32[]{:S(2)}, u32[]{:S(2)}) %collective-permute-start.29) | collective-permute-done | bytes 589856 | tf_op jit(solution)/shard_map/ppermute | solution.py:907
  238.1 1.6 collective-permute-start.30
  241.1 1.6 collective-permute-start.32
  242.7 10.5 %collective-permute-done.30 = bf16[192,768]{1,0:T(8,128)(2,1)S(1)} collective-permute-done((bf16[192,768]{1,0:T(8,128)(2,1)S(1)}, bf16[192,768]{1,0:T(8,128)(2,1)S(1)}, u32[]{:S(2)}, u32[]{:S(2)}) %collective-permute-start.30) | collective-permute-done | bytes 294944 | tf_op jit(solution)/shard_map/ppermute | solution.py:907
  253.3 1.5 add_convert_fusion.2
  256.4 1.9 collective-permute-done.33
  258.4 1.8 add_convert_fusion.1
  260.2 1.5 collective-permute-start.34
  261.7 24.7 %shard_map.204 = (bf16[768,768]{1,0:T(8,128)(2,1)}, bf16[768,768]{1,0:T(8,128)(2,1)}, bf16[768,768]{1,0:T(8,128)(2,1)}, bf16[768,768]{1,0:T(8,128)(2,1)}, f32[2,2,768,768]{3,2,1,0:T(8,128)}, /*index=5*/f32[768,8]{1,0:T(8,128)}) custom-call(bf16[1536,3072]{1,0:T(8,128)(2,1)} %get-tuple-element.172.a_ref, bf16[1536,3072]{1,0:T(8,128)(2,1)} %get-tuple-element.173.du_ref, ...), custom_call_target="tpu_custom_call" | custom-call | flops 1000000 | bytes 100000 | tf_op jit(solution)/shard_map/pallas_call | solution.py:745
  286.9 6.4 %all-to-all-start.2 = ((bf16[8,192,768]{2,1,0:T(8,128)(2,1)}), bf16[8,192,768]{2,1,0:T(8,128)(2,1)S(1)}, u32[]{:S(2)}, u32[]{:S(2)}) async-start(bf16[8,192,768]{2,1,0:T(8,128)(2,1)} %bitcast.72), calls=%async_computation.2 | async-start | bytes 4718592 | tf_op jit(solution)/shard_map/all_to_all | solution.py:1063
  293.3 3.7 copy-done
  297.0 3.2 shard_map.207
  301.7 1.8 add_convert_fusion.dh_mine_ref
  303.6 2.2 collective-permute-start.42
  305.8 3.4 collective-permute-done.35.dh_near_ref
  310.3 50.6 %shard_map.205 = (f32[512,768]{1,0:T(8,128)}, f32[1,768]{1,0:T(1,128)}, bf16[512,768]{1,0:T(8,128)(2,1)}, bf16[512,768]{1,0:T(8,128)(2,1)}, f32[512,768]{1,0:T(8...) custom-call(s32[7]{0:T(128)} %copy-done.22, ...), custom_call_target="tpu_custom_call" | custom-call | flops 1000000 | bytes 100000 | tf_op jit(solution)/shard_map/pallas_call | solution.py:368
  361.8 2.4 collective-permute-start.49
  366.3 2.8 copy-done.4
  369.1 7.5 %shard_map.206 = (bf16[512,768]{1,0:T(8,128)(2,1)}, bf16[512,768]{1,0:T(8,128)(2,1)S(1)}, f32[512,768]{1,0:T(8,128)S(1)}, f32[512,768]{1,0:T(8,128)S(1)}) custom-call(bf16[1536,2048]{1,0:T(8,128)(2,1)S(1)} %copy-done.4, bf16[1536,768]{1,0:T(8,128)(2,1)S(1)} %bitcast.69), custom_call_target="tpu_custom_call" | custom-call | flops 1000000 | bytes 100000 | tf_op jit(solution)/shard_map/pallas_call | solution.py:867
  377.1 1.6 collective-permute-start.46
  381.4 4.4 %shard_map.209 = (f32[768,768]{1,0:T(8,128)S(1)}, bf16[384,768]{1,0:T(8,128)(2,1)S(1)}, bf16[384,768]{1,0:T(8,128)(2,1)S(1)}) custom-call(f32[2,2,768,768]{3,2,1,0:T(8,128)} %get-tuple-element.184.keep_ref, bf16[768,768]{1,0:T(8,128)(2,1)} %collective-permute-done.47.give_0_ref, bf16[768,768]{1,0:T(8,128)(2,1)} %collective-permute-done.48.give_1_ref, ...), custom_call_target="tpu_custom_call" | custom-call | flops 1000000 | bytes 100000 | tf_op jit(solution)/shard_map/pallas_call | solution.py:803
  385.7 1.9 collective-permute-start.50
  387.6 1.5 collective-permute-start.44
  389.1 1.6 collective-permute-start.54
  390.7 9.4 %collective-permute-done.50.other_0_ref = bf16[384,768]{1,0:T(8,128)(2,1)S(1)} collective-permute-done((bf16[384,768]{1,0:T(8,128)(2,1)S(1)}, bf16[384,768]{1,0:T(8,128)(2,1)S(1)}, u32[]{:S(2)}, u32[]{:S(2)}) %collective-permute-start.50) | collective-permute-done | bytes 589856 | tf_op jit(solution)/shard_map/ppermute | solution.py:907
  400.1 1.7 collective-permute-start.56
  401.8 1.5 collective-permute-start.51
  403.5 2.4 collective-permute-done.51
  405.9 1.5 collective-permute-start.38
  407.4 2.6 collective-permute-start.52
  410.0 2.5 collective-permute-done.52
  413.9 1.7 shard_map.210
  416.6 2.6 collective-permute-start.55
  421.7 4.1 shard_map.208
  427.6 3.1 add_convert_fusion.4
  (262 shorter events, 46.3 us)
Async XLA Ops:
  0.6 20.8 %collective-permute-start = (bf16[512,768]{1,0:T(8,128)(2,1)}, bf16[512,768]{1,0:T(8,128)(2,1)S(1)}, u32[]{:S(2)}, u32[]{:S(2)}) collective-permute-start(bf16[512,768]{1,0:T(8,128)(2,1)} %c_0_ref.3), channel_id=1, source_target_pairs={{0,2},{1,3},{2,0},{3,1},{4,6},{5,7},{6,4},{7,5},{8,10},{9,11},{10,... | collective-permute-start | bytes 2359304 | tf_op jit(solution)/shard_map/ppermute | solution.py:907
  3.6 21.2 %collective-permute-start.2 = (bf16[512,768]{1,0:T(8,128)(2,1)}, bf16[512,768]{1,0:T(8,128)(2,1)}, u32[]{:S(2)}, u32[]{:S(2)}) collective-permute-start(bf16[512,768]{1,0:T(8,128)(2,1)} %c_0_ref.3), channel_id=1, source_target_pairs={{0,1},{1,0},{2,3},{3,2},{4,5},{5,4},{6,7},{7,6},{8,9},{9,8},{10,11... | collective-permute-start | bytes 2359304 | tf_op jit(solution)/shard_map/ppermute | solution.py:907
  7.0 35.2 %all-to-all-start = ((bf16[8,96,768]{2,1,0:T(8,128)(2,1)}), bf16[8,96,768]{2,1,0:T(8,128)(2,1)}, u32[]{:S(2)}, u32[]{:S(2)}) async-start(bf16[8,96,768]{2,1,0:T(8,128)(2,1)} %broadcast_in_dim.59), calls=%async_computation | async-start | bytes 2359296 | tf_op jit(solution)/shard_map/all_to_all | solution.py:959
  13.1 39.9 %copy-start.20 = (s32[2048]{0:T(1024)}, s32[2048]{0:T(1024)S(1)}, u32[]{:S(2)}) copy-start(s32[2048]{0:T(1024)S(1)} %select_reduce_fusion) | copy-start | bytes 24580
  23.0 2.3 collective-permute-start.3
  23.1 24.0 %collective-permute-start.1 = (bf16[512,768]{1,0:T(8,128)(2,1)S(1)}, bf16[512,768]{1,0:T(8,128)(2,1)S(1)}, u32[]{:S(2)}, u32[]{:S(2)}) collective-permute-start(bf16[512,768]{1,0:T(8,128)(2,1)S(1)} %copy-done.2), channel_id=1, source_target_pairs={{0,2},{1,3},{2,0},{3,1},{4,6},{5,7},{6,4},{7,5},{8,10},{9,11},{10,... | collective-permute-start | bytes 2359304 | tf_op jit(solution)/shard_map/ppermute | solution.py:907
  42.2 102.3 %all-to-all-start.1 = ((bf16[8,208,768]{2,1,0:T(8,128)(2,1)}), bf16[8,208,768]{2,1,0:T(8,128)(2,1)}, u32[]{:S(2)}, u32[]{:S(2)}) async-start(bf16[8,208,768]{2,1,0:T(8,128)(2,1)} %copy-done.7), calls=%async_computation.1 | async-start | bytes 5111808 | tf_op jit(solution)/shard_map/all_to_all | solution.py:1016
  47.1 35.2 %collective-permute-start.8 = (bf16[768,768]{1,0:T(8,128)(2,1)S(1)}, bf16[768,768]{1,0:T(8,128)(2,1)S(1)}, u32[]{:S(2)}, u32[]{:S(2)}) collective-permute-start(bf16[768,768]{1,0:T(8,128)(2,1)S(1)} %get-tuple-element.125.refs_5_), channel_id=1, source_target_pairs={{0,1},{1,0},{2,3},{3,2},{4,5},{5,4},{6,7},{7,6},{8,9},{9,8},{10,11... | collective-permute-start | bytes 3538952 | tf_op jit(solution)/shard_map/ppermute | solution.py:907
  47.1 36.8 %collective-permute-start.4 = (bf16[768,768]{1,0:T(8,128)(2,1)S(1)}, bf16[768,768]{1,0:T(8,128)(2,1)S(1)}, u32[]{:S(2)}, u32[]{:S(2)}) collective-permute-start(bf16[768,768]{1,0:T(8,128)(2,1)S(1)} %get-tuple-element.125.refs_5_), channel_id=1, source_target_pairs={{0,2},{1,3},{2,0},{3,1},{4,6},{5,7},{6,4},{7,5},{8,10},{9,11},{10,... | collective-permute-start | bytes 3538952 | tf_op jit(solution)/shard_map/ppermute | solution.py:907
  48.7 3.7 collective-permute-start.6
  48.9 4.2 collective-permute-start.7
  49.2 53.3 %collective-permute-start.12 = (bf16[768,768]{1,0:T(8,128)(2,1)}, bf16[768,768]{1,0:T(8,128)(2,1)}, u32[]{:S(2)}, u32[]{:S(2)}) collective-permute-start(bf16[768,768]{1,0:T(8,128)(2,1)} %copy-done.24), channel_id=1, source_target_pairs={{0,4},{4,0},{8,12},{12,8},{16,20},{20,16},{24,28},{28,24},{1,5},{5... | collective-permute-start | bytes 3538952 | tf_op jit(solution)/shard_map/ppermute | solution.py:907
  52.4 55.9 %copy-start.33 = (bf16[768,192]{1,0:T(8,128)(2,1)}, bf16[768,192]{1,0:T(8,128)(2,1)S(1)}, u32[]{:S(2)}) copy-start(bf16[768,192]{1,0:T(8,128)(2,1)S(1)} %slice.113.refs_4_) | copy-start | bytes 884740
  52.4 31.5 %collective-permute-start.9 = (bf16[768,192]{1,0:T(8,128)(2,1)S(1)}, bf16[768,192]{1,0:T(8,128)(2,1)S(1)}, u32[]{:S(2)}, u32[]{:S(2)}) collective-permute-start(bf16[768,192]{1,0:T(8,128)(2,1)S(1)} %slice.113.refs_4_), channel_id=1, source_target_pairs={{0,2},{1,3},{2,0},{3,1},{4,6},{5,7},{6,4},{7,5},{8,10},{9,11},{10,... | collective-permute-start | bytes 884744 | tf_op jit(solution)/shard_map/ppermute | solution.py:907
  53.0 52.3 %copy-start.54 = (f32[768]{0:T(1024)S(1)}, f32[768]{0:T(1024)}, u32[]{:S(2)}) copy-start(f32[768]{0:T(1024)} %param.15) | copy-start | bytes 9220
  84.0 19.3 %collective-permute-start.10 = (bf16[192,2048]{1,0:T(8,128)(2,1)S(1)}, bf16[192,2048]{1,0:T(8,128)(2,1)S(1)}, u32[]{:S(2)}, u32[]{:S(2)}) collective-permute-start(bf16[192,2048]{1,0:T(8,128)(2,1)S(1)} %get-tuple-element.128.refs_0_.ctx_ref), channel_id=1, source_target_pairs={{0,2},{1,3},{2,0},{3,1},{4,6},{5,7},{6,4},{7,5},{8,10},{9,11},{10,... | collective-permute-start | bytes 2359304 | tf_op jit(solution)/shard_map/ppermute | solution.py:907
  85.5 20.4 %collective-permute-start.5 = (bf16[768,768]{1,0:T(8,128)(2,1)S(1)}, bf16[768,768]{1,0:T(8,128)(2,1)S(1)}, u32[]{:S(2)}, u32[]{:S(2)}) collective-permute-start(bf16[768,768]{1,0:T(8,128)(2,1)S(1)} %collective-permute-done.4.refs_7_), channel_id=1, source_target_pairs={{0,1},{1,0},{2,3},{3,2},{4,5},{5,4},{6,7},{7,6},{8,9},{9,8},{10,11... | collective-permute-start | bytes 3538952 | tf_op jit(solution)/shard_map/ppermute | solution.py:907
  85.5 19.2 %collective-permute-start.13 = (bf16[768,192]{1,0:T(8,128)(2,1)S(1)}, bf16[768,192]{1,0:T(8,128)(2,1)S(1)}, u32[]{:S(2)}, u32[]{:S(2)}) collective-permute-start(bf16[768,192]{1,0:T(8,128)(2,1)S(1)} %slice.113.refs_4_), channel_id=1, source_target_pairs={{0,1},{1,0},{2,3},{3,2},{4,5},{5,4},{6,7},{7,6},{8,9},{9,8},{10,11... | collective-permute-start | bytes 884744 | tf_op jit(solution)/shard_map/ppermute | solution.py:907
  86.1 18.7 %collective-permute-start.14 = (bf16[768,192]{1,0:T(8,128)(2,1)S(1)}, bf16[768,192]{1,0:T(8,128)(2,1)S(1)}, u32[]{:S(2)}, u32[]{:S(2)}) collective-permute-start(bf16[768,192]{1,0:T(8,128)(2,1)S(1)} %collective-permute-done.9.refs_5_), channel_id=1, source_target_pairs={{0,1},{1,0},{2,3},{3,2},{4,5},{5,4},{6,7},{7,6},{8,9},{9,8},{10,11... | collective-permute-start | bytes 884744 | tf_op jit(solution)/shard_map/ppermute | solution.py:907
  103.3 27.1 %collective-permute-start.17 = (bf16[768,768]{1,0:T(8,128)(2,1)}, bf16[768,768]{1,0:T(8,128)(2,1)S(1)}, u32[]{:S(2)}, u32[]{:S(2)}) collective-permute-start(bf16[768,768]{1,0:T(8,128)(2,1)} %collective-permute-done.12.refs_6_), channel_id=1, source_target_pairs={{0,2},{1,3},{2,0},{3,1},{4,6},{5,7},{6,4},{7,5},{8,10},{9,11},{10,... | collective-permute-start | bytes 3538952 | tf_op jit(solution)/shard_map/ppermute | solution.py:907
  104.8 2.4 collective-permute-start.11
  104.8 3.5 collective-permute-start.15
  124.7 18.2 %collective-permute-start.18 = (bf16[768,768]{1,0:T(8,128)(2,1)}, bf16[768,768]{1,0:T(8,128)(2,1)S(1)}, u32[]{:S(2)}, u32[]{:S(2)}) collective-permute-start(bf16[768,768]{1,0:T(8,128)(2,1)} %collective-permute-done.12.refs_6_), channel_id=1, source_target_pairs={{0,1},{1,0},{2,3},{3,2},{4,5},{5,4},{6,7},{7,6},{8,9},{9,8},{10,11... | collective-permute-start | bytes 3538952 | tf_op jit(solution)/shard_map/ppermute | solution.py:907
  130.4 14.1 %collective-permute-start.19 = (bf16[768,768]{1,0:T(8,128)(2,1)S(1)}, bf16[768,768]{1,0:T(8,128)(2,1)}, u32[]{:S(2)}, u32[]{:S(2)}) collective-permute-start(bf16[768,768]{1,0:T(8,128)(2,1)S(1)} %collective-permute-done.17.refs_8_), channel_id=1, source_target_pairs={{0,1},{1,0},{2,3},{3,2},{4,5},{5,4},{6,7},{7,6},{8,9},{9,8},{10,11... | collective-permute-start | bytes 3538952 | tf_op jit(solution)/shard_map/ppermute | solution.py:907
  130.4 9.9 %collective-permute-start.16 = (bf16[192,768]{1,0:T(8,128)(2,1)}, bf16[192,768]{1,0:T(8,128)(2,1)S(1)}, u32[]{:S(2)}, u32[]{:S(2)}) collective-permute-start(bf16[192,768]{1,0:T(8,128)(2,1)} %get-tuple-element.135), channel_id=1, source_target_pairs={{0,4},{4,0},{8,12},{12,8},{16,20},{20,16},{24,28},{28,24},{1,5},{5... | collective-permute-start | bytes 884744 | tf_op jit(solution)/shard_map/ppermute | solution.py:907
  132.4 32.3 %collective-permute-start.22 = (bf16[192,768]{1,0:T(8,128)(2,1)}, bf16[192,768]{1,0:T(8,128)(2,1)}, u32[]{:S(2)}, u32[]{:S(2)}) collective-permute-start(bf16[192,768]{1,0:T(8,128)(2,1)} %get-tuple-element.142), channel_id=1, source_target_pairs={{0,8},{4,12},{8,0},{12,4},{16,24},{20,28},{24,16},{28,20},{1,9},{5... | collective-permute-start | bytes 884744 | tf_op jit(solution)/shard_map/ppermute | solution.py:907
  133.8 31.5 %collective-permute-start.23 = (bf16[192,768]{1,0:T(8,128)(2,1)}, bf16[192,768]{1,0:T(8,128)(2,1)}, u32[]{:S(2)}, u32[]{:S(2)}) collective-permute-start(bf16[192,768]{1,0:T(8,128)(2,1)} %get-tuple-element.143), channel_id=1, source_target_pairs={{0,12},{4,8},{8,4},{12,0},{16,28},{20,24},{24,20},{28,16},{1,13},{... | collective-permute-start | bytes 884744 | tf_op jit(solution)/shard_map/ppermute | solution.py:907
  140.3 42.3 %collective-permute-start.27 = (bf16[192,768]{1,0:T(8,128)(2,1)}, bf16[192,768]{1,0:T(8,128)(2,1)S(1)}, u32[]{:S(2)}, u32[]{:S(2)}) collective-permute-start(bf16[192,768]{1,0:T(8,128)(2,1)} %get-tuple-element.156), channel_id=1, source_target_pairs={{0,16},{4,20},{8,24},{12,28},{16,0},{20,4},{24,8},{28,12},{1,17},{... | collective-permute-start | bytes 884744 | tf_op jit(solution)/shard_map/ppermute | solution.py:907
  142.9 42.6 %collective-permute-start.28 = (bf16[192,768]{1,0:T(8,128)(2,1)}, bf16[192,768]{1,0:T(8,128)(2,1)S(1)}, u32[]{:S(2)}, u32[]{:S(2)}) collective-permute-start(bf16[192,768]{1,0:T(8,128)(2,1)} %get-tuple-element.158), channel_id=1, source_target_pairs={{0,20},{4,16},{8,28},{12,24},{16,4},{20,0},{24,12},{28,8},{1,21},{... | collective-permute-start | bytes 884744 | tf_op jit(solution)/shard_map/ppermute | solution.py:907
  161.5 43.1 %collective-permute-start.20 = (bf16[192,768]{1,0:T(8,128)(2,1)S(1)}, bf16[192,768]{1,0:T(8,128)(2,1)S(1)}, u32[]{:S(2)}, u32[]{:S(2)}) collective-permute-start(bf16[192,768]{1,0:T(8,128)(2,1)S(1)} %copy-done.57), channel_id=1, source_target_pairs={{0,24},{4,28},{8,16},{12,20},{16,8},{20,12},{24,0},{28,4},{1,25},{... | collective-permute-start | bytes 884744 | tf_op jit(solution)/shard_map/ppermute | solution.py:907
  164.8 40.5 %collective-permute-start.21 = (bf16[192,768]{1,0:T(8,128)(2,1)}, bf16[192,768]{1,0:T(8,128)(2,1)S(1)}, u32[]{:S(2)}, u32[]{:S(2)}) collective-permute-start(bf16[192,768]{1,0:T(8,128)(2,1)} %get-tuple-element.141), channel_id=1, source_target_pairs={{0,4},{4,0},{8,12},{12,8},{16,20},{20,16},{24,28},{28,24},{1,5},{5... | collective-permute-start | bytes 884744 | tf_op jit(solution)/shard_map/ppermute | solution.py:907
  182.5 22.8 %collective-permute-start.24 = (bf16[192,768]{1,0:T(8,128)(2,1)}, bf16[192,768]{1,0:T(8,128)(2,1)S(1)}, u32[]{:S(2)}, u32[]{:S(2)}) collective-permute-start(bf16[192,768]{1,0:T(8,128)(2,1)} %get-tuple-element.150), channel_id=1, source_target_pairs={{0,8},{4,12},{8,0},{12,4},{16,24},{20,28},{24,16},{28,20},{1,9},{5... | collective-permute-start | bytes 884744 | tf_op jit(solution)/shard_map/ppermute | solution.py:907
  182.6 22.7 %collective-permute-start.25 = (bf16[192,768]{1,0:T(8,128)(2,1)}, bf16[192,768]{1,0:T(8,128)(2,1)S(1)}, u32[]{:S(2)}, u32[]{:S(2)}) collective-permute-start(bf16[192,768]{1,0:T(8,128)(2,1)} %get-tuple-element.151), channel_id=1, source_target_pairs={{0,12},{4,8},{8,4},{12,0},{16,28},{20,24},{24,20},{28,16},{1,13},{... | collective-permute-start | bytes 884744 | tf_op jit(solution)/shard_map/ppermute | solution.py:907
  185.5 19.8 %collective-permute-start.26 = (bf16[192,768]{1,0:T(8,128)(2,1)S(1)}, bf16[192,768]{1,0:T(8,128)(2,1)S(1)}, u32[]{:S(2)}, u32[]{:S(2)}) collective-permute-start(bf16[192,768]{1,0:T(8,128)(2,1)S(1)} %copy-done.56), channel_id=1, source_target_pairs={{0,28},{4,24},{8,20},{12,16},{16,12},{20,8},{24,4},{28,0},{1,29},{... | collective-permute-start | bytes 884744 | tf_op jit(solution)/shard_map/ppermute | solution.py:907
  204.6 33.4 %collective-permute-start.29 = (bf16[384,768]{1,0:T(8,128)(2,1)S(1)}, bf16[384,768]{1,0:T(8,128)(2,1)S(1)}, u32[]{:S(2)}, u32[]{:S(2)}) collective-permute-start(bf16[384,768]{1,0:T(8,128)(2,1)S(1)} %pad_maximum_fusion), channel_id=1, source_target_pairs={{0,16},{4,20},{8,24},{12,28},{16,0},{20,4},{24,8},{28,12},{1,17},{... | collective-permute-start | bytes 1769480 | tf_op jit(solution)/shard_map/ppermute | solution.py:907
  223.3 30.0 %collective-permute-start.31 = (bf16[192,768]{1,0:T(8,128)(2,1)}, bf16[192,768]{1,0:T(8,128)(2,1)S(1)}, u32[]{:S(2)}, u32[]{:S(2)}) collective-permute-start(bf16[192,768]{1,0:T(8,128)(2,1)} %get-tuple-element.179), channel_id=1, source_target_pairs={{0,24},{4,28},{8,16},{12,20},{16,8},{20,12},{24,0},{28,4},{1,25},{... | collective-permute-start | bytes 884744 | tf_op jit(solution)/shard_map/ppermute | solution.py:907
  238.1 15.2 %collective-permute-start.30 = (bf16[192,768]{1,0:T(8,128)(2,1)S(1)}, bf16[192,768]{1,0:T(8,128)(2,1)S(1)}, u32[]{:S(2)}, u32[]{:S(2)}) collective-permute-start(bf16[192,768]{1,0:T(8,128)(2,1)S(1)} %get-tuple-element.271), channel_id=1, source_target_pairs={{0,4},{4,0},{8,12},{12,8},{16,20},{20,16},{24,28},{28,24},{1,5},{5... | collective-permute-start | bytes 884744 | tf_op jit(solution)/shard_map/ppermute | solution.py:907
  241.1 12.2 %collective-permute-start.32 = (bf16[192,768]{1,0:T(8,128)(2,1)S(1)}, bf16[192,768]{1,0:T(8,128)(2,1)S(1)}, u32[]{:S(2)}, u32[]{:S(2)}) collective-permute-start(bf16[192,768]{1,0:T(8,128)(2,1)S(1)} %copy-done.58), channel_id=1, source_target_pairs={{0,28},{4,24},{8,20},{12,16},{16,12},{20,8},{24,4},{28,0},{1,29},{... | collective-permute-start | bytes 884744 | tf_op jit(solution)/shard_map/ppermute | solution.py:907
  254.9 3.5 collective-permute-start.33
  260.2 40.1 %collective-permute-start.34 = (bf16[1024,768]{1,0:T(8,128)(2,1)}, bf16[1024,768]{1,0:T(8,128)(2,1)}, u32[]{:S(2)}, u32[]{:S(2)}) collective-permute-start(bf16[1024,768]{1,0:T(8,128)(2,1)} %add_convert_fusion.1), channel_id=1, source_target_pairs={{0,2},{1,3},{2,0},{3,1},{4,6},{5,7},{6,4},{7,5},{8,10},{9,11},{10,... | collective-permute-start | bytes 4718600 | tf_op jit(solution)/shard_map/ppermute | solution.py:907
  286.4 6.9 %collective-permute-start.40 = (bf16[768,768]{1,0:T(8,128)(2,1)}, bf16[768,768]{1,0:T(8,128)(2,1)}, u32[]{:S(2)}, u32[]{:S(2)}) collective-permute-start(bf16[768,768]{1,0:T(8,128)(2,1)} %get-tuple-element.204), channel_id=1, source_target_pairs={{0,1},{1,0},{2,3},{3,2},{4,5},{5,4},{6,7},{7,6},{8,9},{9,8},{10,11... | collective-permute-start | bytes 3538952 | tf_op jit(solution)/shard_map/ppermute | solution.py:907
  286.4 6.9 %collective-permute-start.41 = (bf16[768,768]{1,0:T(8,128)(2,1)}, bf16[768,768]{1,0:T(8,128)(2,1)}, u32[]{:S(2)}, u32[]{:S(2)}) collective-permute-start(bf16[768,768]{1,0:T(8,128)(2,1)} %get-tuple-element.205), channel_id=1, source_target_pairs={{0,1},{1,0},{2,3},{3,2},{4,5},{5,4},{6,7},{7,6},{8,9},{9,8},{10,11... | collective-permute-start | bytes 3538952 | tf_op jit(solution)/shard_map/ppermute | solution.py:907
  286.9 79.4 %all-to-all-start.2 = ((bf16[8,192,768]{2,1,0:T(8,128)(2,1)}), bf16[8,192,768]{2,1,0:T(8,128)(2,1)S(1)}, u32[]{:S(2)}, u32[]{:S(2)}) async-start(bf16[8,192,768]{2,1,0:T(8,128)(2,1)} %bitcast.72), calls=%async_computation.2 | async-start | bytes 4718592 | tf_op jit(solution)/shard_map/all_to_all | solution.py:1063
  303.6 57.4 %collective-permute-start.42 = (bf16[2,768,768]{2,1,0:T(8,128)(2,1)}, bf16[2,768,768]{2,1,0:T(8,128)(2,1)}, u32[]{:S(2)}, u32[]{:S(2)}) collective-permute-start(bf16[2,768,768]{2,1,0:T(8,128)(2,1)} %shard_map.207), channel_id=1, source_target_pairs={{4,6},{5,7},{6,4},{7,5},{12,14},{13,15},{14,12},{15,13},{20,22},{2... | collective-permute-start | bytes 7077896 | tf_op jit(solution)/shard_map/ppermute | solution.py:915
  305.8 3.4 collective-permute-start.35
  310.3 51.3 %copy-start.44 = (f32[768,8]{1,0:T(8,128)S(1)}, f32[768,8]{1,0:T(8,128)}, u32[]{:S(2)}) copy-start(f32[768,8]{1,0:T(8,128)} %get-tuple-element.212) | copy-start | bytes 73732
  361.0 3.3 collective-permute-start.43
  361.2 20.2 %collective-permute-start.47 = (bf16[768,768]{1,0:T(8,128)(2,1)}, bf16[768,768]{1,0:T(8,128)(2,1)}, u32[]{:S(2)}, u32[]{:S(2)}) collective-permute-start(bf16[768,768]{1,0:T(8,128)(2,1)} %get-tuple-element.213), channel_id=1, source_target_pairs={{0,1},{1,0},{2,3},{3,2},{4,5},{5,4},{6,7},{7,6},{8,9},{9,8},{10,11... | collective-permute-start | bytes 3538952 | tf_op jit(solution)/shard_map/ppermute | solution.py:907
  361.5 19.8 %collective-permute-start.48 = (bf16[768,768]{1,0:T(8,128)(2,1)}, bf16[768,768]{1,0:T(8,128)(2,1)}, u32[]{:S(2)}, u32[]{:S(2)}) collective-permute-start(bf16[768,768]{1,0:T(8,128)(2,1)} %get-tuple-element.214), channel_id=1, source_target_pairs={{0,1},{1,0},{2,3},{3,2},{4,5},{5,4},{6,7},{7,6},{8,9},{9,8},{10,11... | collective-permute-start | bytes 3538952 | tf_op jit(solution)/shard_map/ppermute | solution.py:907
  361.8 19.4 %collective-permute-start.49 = (bf16[4,96,768]{2,1,0:T(8,128)(2,1)}, bf16[4,96,768]{2,1,0:T(8,128)(2,1)S(1)}, u32[]{:S(2)}, u32[]{:S(2)}) collective-permute-start(bf16[4,96,768]{2,1,0:T(8,128)(2,1)} %get-tuple-element.194), channel_id=1, source_target_pairs={{0,4},{4,0},{8,12},{12,8},{16,20},{20,16},{24,28},{28,24},{1,5},{5... | collective-permute-start | bytes 1769480 | tf_op jit(solution)/shard_map/ppermute | solution.py:907
  366.1 10.9 %collective-permute-start.45 = (f32[10,768]{1,0:T(8,128)S(1)}, f32[10,768]{1,0:T(8,128)S(1)}, u32[]{:S(2)}, u32[]{:S(2)}) collective-permute-start(f32[10,768]{1,0:T(8,128)S(1)} %pad_maximum_fusion.3), channel_id=1, source_target_pairs={{0,1},{1,0},{2,3},{3,2},{4,5},{5,4},{6,7},{7,6},{8,9},{9,8},{10,11... | collective-permute-start | bytes 92168 | tf_op jit(solution)/shard_map/ppermute | solution.py:907
  376.6 25.2 %collective-permute-start.37 = (bf16[512,768]{1,0:T(8,128)(2,1)S(1)}, bf16[512,768]{1,0:T(8,128)(2,1)S(1)}, u32[]{:S(2)}, u32[]{:S(2)}) collective-permute-start(bf16[512,768]{1,0:T(8,128)(2,1)S(1)} %get-tuple-element.199), channel_id=1, source_target_pairs={{0,1},{1,0},{2,3},{3,2},{4,5},{5,4},{6,7},{7,6},{8,9},{9,8},{10,11... | collective-permute-start | bytes 2359304 | tf_op jit(solution)/shard_map/ppermute | solution.py:907
  377.1 4.2 collective-permute-start.46
  385.7 14.3 %collective-permute-start.50 = (bf16[384,768]{1,0:T(8,128)(2,1)S(1)}, bf16[384,768]{1,0:T(8,128)(2,1)S(1)}, u32[]{:S(2)}, u32[]{:S(2)}) collective-permute-start(bf16[384,768]{1,0:T(8,128)(2,1)S(1)} %get-tuple-element.218), channel_id=1, source_target_pairs={{0,4},{4,0},{8,12},{12,8},{16,20},{20,16},{24,28},{28,24},{1,5},{5... | collective-permute-start | bytes 1769480 | tf_op jit(solution)/shard_map/ppermute | solution.py:907
  387.6 32.9 %collective-permute-start.39 = (bf16[512,768]{1,0:T(8,128)(2,1)S(1)}, bf16[512,768]{1,0:T(8,128)(2,1)S(1)}, u32[]{:S(2)}, u32[]{:S(2)}) collective-permute-start(bf16[512,768]{1,0:T(8,128)(2,1)S(1)} %copy-done.55), channel_id=1, source_target_pairs={{0,1},{1,0},{2,3},{3,2},{4,5},{5,4},{6,7},{7,6},{8,9},{9,8},{10,11... | collective-permute-start | bytes 2359304 | tf_op jit(solution)/shard_map/ppermute | solution.py:907
  387.6 32.9 %collective-permute-start.44 = (bf16[512,768]{1,0:T(8,128)(2,1)S(1)}, bf16[512,768]{1,0:T(8,128)(2,1)S(1)}, u32[]{:S(2)}, u32[]{:S(2)}) collective-permute-start(bf16[512,768]{1,0:T(8,128)(2,1)S(1)} %add_convert_fusion.3), channel_id=1, source_target_pairs={{0,2},{1,3},{2,0},{3,1},{4,6},{5,7},{6,4},{7,5},{8,10},{9,11},{10,... | collective-permute-start | bytes 2359304 | tf_op jit(solution)/shard_map/ppermute | solution.py:907
  389.1 18.3 %collective-permute-start.54 = (bf16[2,96,768]{2,1,0:T(8,128)(2,1)S(1)}, bf16[2,96,768]{2,1,0:T(8,128)(2,1)S(1)}, u32[]{:S(2)}, u32[]{:S(2)}) collective-permute-start(bf16[2,96,768]{2,1,0:T(8,128)(2,1)S(1)} %slice.155), channel_id=1, source_target_pairs={{0,8},{4,12},{8,0},{12,4},{16,24},{20,28},{24,16},{28,20},{1,9},{5... | collective-permute-start | bytes 884744 | tf_op jit(solution)/shard_map/ppermute | solution.py:907
  400.1 13.9 %collective-permute-start.56 = (bf16[384,768]{1,0:T(8,128)(2,1)S(1)}, bf16[384,768]{1,0:T(8,128)(2,1)S(1)}, u32[]{:S(2)}, u32[]{:S(2)}) collective-permute-start(bf16[384,768]{1,0:T(8,128)(2,1)S(1)} %get-tuple-element.221), channel_id=1, source_target_pairs={{0,4},{4,0},{8,12},{12,8},{16,20},{20,16},{24,28},{28,24},{1,5},{5... | collective-permute-start | bytes 1769480 | tf_op jit(solution)/shard_map/ppermute | solution.py:907
  401.8 4.1 collective-permute-start.51
  405.9 20.0 %collective-permute-start.38 = (bf16[512,768]{1,0:T(8,128)(2,1)S(1)}, bf16[512,768]{1,0:T(8,128)(2,1)}, u32[]{:S(2)}, u32[]{:S(2)}) collective-permute-start(bf16[512,768]{1,0:T(8,128)(2,1)S(1)} %add_convert_fusion.5), channel_id=1, source_target_pairs={{0,2},{1,3},{2,0},{3,1},{4,6},{5,7},{6,4},{7,5},{8,10},{9,11},{10,... | collective-permute-start | bytes 2359304 | tf_op jit(solution)/shard_map/ppermute | solution.py:907
  407.4 5.1 %collective-permute-start.52 = (f32[10,768]{1,0:T(8,128)S(1)}, f32[10,768]{1,0:T(8,128)S(1)}, u32[]{:S(2)}, u32[]{:S(2)}) collective-permute-start(f32[10,768]{1,0:T(8,128)S(1)} %add.131), channel_id=1, source_target_pairs={{0,16},{4,20},{8,24},{12,28},{16,0},{20,4},{24,8},{28,12},{1,17},{... | collective-permute-start | bytes 92168 | tf_op jit(solution)/shard_map/ppermute | solution.py:907
  412.5 4.2 collective-permute-start.53
  413.9 13.6 %collective-permute-start.36 = (bf16[512,768]{1,0:T(8,128)(2,1)}, bf16[512,768]{1,0:T(8,128)(2,1)}, u32[]{:S(2)}, u32[]{:S(2)}) collective-permute-start(bf16[512,768]{1,0:T(8,128)(2,1)} %get-tuple-element.197), channel_id=1, source_target_pairs={{0,1},{1,0},{2,3},{3,2},{4,5},{5,4},{6,7},{7,6},{8,9},{9,8},{10,11... | collective-permute-start | bytes 2359304 | tf_op jit(solution)/shard_map/ppermute | solution.py:907
  416.6 9.3 %collective-permute-start.55 = (bf16[1,96,768]{2,1,0:T(8,128)(2,1)S(1)}, bf16[1,96,768]{2,1,0:T(8,128)(2,1)S(1)}, u32[]{:S(2)}, u32[]{:S(2)}) collective-permute-start(bf16[1,96,768]{2,1,0:T(8,128)(2,1)S(1)} %slice.156), channel_id=1, source_target_pairs={{0,16},{4,20},{8,24},{12,28},{16,0},{20,4},{24,8},{28,12},{1,17},{... | collective-permute-start | bytes 442376 | tf_op jit(solution)/shard_map/ppermute | solution.py:907
  (58 other events, 480.9 us)

commit v5 on v4

--- a/solution.py
+++ b/solution.py
@@ -778,7 +778,7 @@
         in_specs=[pl.BlockSpec((1, 1, rows, features), lambda m: (1, m, 0, 0)), whole, whole],
         out_specs=pl.BlockSpec((1, rows, features), lambda m: (m, 0, 0)),
         out_shape=jax.ShapeDtypeStruct((halves, rows, features), LOW),
-        compiler_params=pltpu.CompilerParams(vmem_limit_bytes=40 * 2**20),
+        compiler_params=pltpu.CompilerParams(vmem_limit_bytes=60 * 2**20),
         cost_estimate=LITTLE,
     )(keep, *give)
 
@@ -874,7 +874,7 @@
         out_specs=[pl.BlockSpec((BLOCK, features), lambda i: (0, 0))] * 4,
         out_shape=[jax.ShapeDtypeStruct((BLOCK, features), LOW)] * 2
         + [jax.ShapeDtypeStruct((BLOCK, features), WIDE)] * 2,
-        compiler_params=pltpu.CompilerParams(vmem_limit_bytes=40 * 2**20),
+        compiler_params=pltpu.CompilerParams(vmem_limit_bytes=60 * 2**20),
         cost_estimate=LITTLE,
     )(hot, rows)
 

time: 439 us -> 433 us (0.986)
  local copies, waits for them, and re-layouts: 29.1 us -> 21.6 us
    unnamed x132 -> x126, local copies, waits for them, and re-layouts: 22.9 us -> 16.7 us
  transfers between devices with their start and end apart: 60 -> 60, of which waited for: 21 -> 21; matrix products, arithmetic and copies ran while one was open for 6% -> 5% of each run, Pallas kernels for 50% -> 52%
where the time goes in v5:
time: 433 us; the launch traced here: 425 us
  Pallas kernels  220 us (51%)
  waiting for transfers between devices  81.7 us (19%)
  starting transfers between devices  78.7 us (18%)
  local copies, waits for them, and re-layouts  21.6 us (5%)
  other arithmetic  11.7 us (3%)
  matrix products  9.07 us (2%)
    ppermute x56, waiting for transfers between devices, flip(): return lax.ppermute(array, axis, [(i, i ^ bits) for i in range(size)])  80.4 us
    pallas_call x4, Pallas kernels, run_experts(): pl.pallas_call(functools.partial(expert_kernel, count), grid_spec=grid_sp...  68.2 us
    ppermute x56, starting transfers between devices, flip(): return lax.ppermute(array, axis, [(i, i ^ bits) for i in range(size)])  60.9 us
    pallas_call x1, Pallas kernels, attend_back(): pl.pallas_call(attend_back_kernel, grid_spec=grid_spec, out_shape=[jax.Sh...  50.6 us
    pallas_call x1, Pallas kernels, attend(): pl.pallas_call(attend_kernel, grid_spec=grid_spec, out_shape=[jax.ShapeDt...  25.7 us
    pallas_call x1, Pallas kernels, expert_grads(): pl.pallas_call(expert_grads_kernel, grid=(4,), in_specs=[piece, piece, al...  24.7 us
    unnamed x126, local copies, waits for them, and re-layouts  16.7 us
    pallas_call x1, Pallas kernels, mix(): pl.pallas_call(functools.partial(mix_kernel, count), grid=(4,), in_specs=...  16.4 us
  transfers between devices with their start and end apart: 60, of which 21 were waited for; matrix products, arithmetic and copies ran while one was open for 5% of the time, Pallas kernels for 52%

profile of v5, /device:TPU:0, one launch (start us, length us, event | category | flops | bytes accessed | tf_op | source)
XLA Modules:
  0.0 425.2 jit_solution(12736057124649813704)
XLA Ops:
  0.6 3.0 collective-permute-start
  7.0 5.8 %all-to-all-start = ((bf16[8,96,768]{2,1,0:T(8,128)(2,1)}), bf16[8,96,768]{2,1,0:T(8,128)(2,1)}, u32[]{:S(2)}, u32[]{:S(2)}) async-start(bf16[8,96,768]{2,1,0:T(8,128)(2,1)} %broadcast_in_dim.59), calls=%async_computation | async-start | bytes 2359296 | tf_op jit(solution)/shard_map/all_to_all | solution.py:959
  13.7 1.5 fusion.16
  15.4 6.0 %collective-permute-done.c_1_ref = bf16[512,768]{1,0:T(8,128)(2,1)S(1)} collective-permute-done((bf16[512,768]{1,0:T(8,128)(2,1)}, bf16[512,768]{1,0:T(8,128)(2,1)S(1)}, u32[]{:S(2)}, u32[]{:S(2)}) %collective-permute-start) | collective-permute-done | bytes 786464 | tf_op jit(solution)/shard_map/ppermute | solution.py:907
  23.1 1.8 collective-permute-start.1
  25.2 9.9 %shard_map.197 = (bf16[8,208,768]{2,1,0:T(8,128)(2,1)S(1)}, bf16[1536,2048]{1,0:T(8,128)(2,1)S(1)}, bf16[1536,2048]{1,0:T(8,128)(2,1)}) custom-call(s32[1]{0:T(128)} %bitcast.1.index_ref, s32[8,2048]{1,0:T(8,128)S(1)} %pad.5.placed_ref, bf16[512,768]{1,0:T(8,128)(2,1)S(1)} %copy-done.10, bf16[512,768]{1,0:T(8,128)(2,1)S(1)} %collective-permute-done.c_1_ref, ...), custom_call_target="tpu_custom_call" | custom-call | flops 40000000000 | bytes 10000000 | tf_op jit(solution)/shard_map/pallas_call | solution.py:435
  35.2 2.6 copy-done.2
  37.8 1.6 copy-done.5
  40.9 1.3 all-to-all-done
  42.2 4.9 %all-to-all-start.1 = ((bf16[8,208,768]{2,1,0:T(8,128)(2,1)}), bf16[8,208,768]{2,1,0:T(8,128)(2,1)}, u32[]{:S(2)}, u32[]{:S(2)}) async-start(bf16[8,208,768]{2,1,0:T(8,128)(2,1)} %copy-done.5), calls=%async_computation.1 | async-start | bytes 5111808 | tf_op jit(solution)/shard_map/all_to_all | solution.py:1016
  47.1 1.5 collective-permute-start.4
  49.2 2.0 collective-permute-start.12
  54.2 25.7 %shard_map.198 = (bf16[2048,768]{1,0:T(8,128)(2,1)}, bf16[3,64,2048]{2,1,0:T(8,128)(2,1)S(1)}, bf16[3,2048,64]{2,1,0:T(8,128)(2,1)}, bf16[3,2048,64]{2,1,0:T(8,1...) custom-call(s32[7]{0:T(128)S(1)} %pad_add_fusion.1.meta_ref, ...), custom_call_target="tpu_custom_call" | custom-call | flops 1000000 | bytes 100000 | tf_op jit(solution)/shard_map/pallas_call | solution.py:170
  82.3 1.7 collective-permute-done.9.refs_5_
  84.0 1.5 collective-permute-start.10
  86.1 16.5 %collective-permute-done.12.refs_6_ = bf16[768,768]{1,0:T(8,128)(2,1)} collective-permute-done((bf16[768,768]{1,0:T(8,128)(2,1)}, bf16[768,768]{1,0:T(8,128)(2,1)}, u32[]{:S(2)}, u32[]{:S(2)}) %collective-permute-start.12) | collective-permute-done | bytes 1179680 | tf_op jit(solution)/shard_map/ppermute | solution.py:907
  103.3 1.5 collective-permute-start.17
  108.3 16.4 %shard_map.199 = (f32[2048,768]{1,0:T(8,128)}, bf16[192,768]{1,0:T(8,128)(2,1)}, bf16[192,768]{1,0:T(8,128)(2,1)}, bf16[192,768]{1,0:T(8,128)(2,1)}, bf16[192,76...) custom-call(f32[1,768]{1,0:T(1,128)} %broadcast_in_dim.29.gain_ref, ...), custom_call_target="tpu_custom_call" | custom-call | flops 1000000 | bytes 100000 | tf_op jit(solution)/shard_map/pallas_call | solution.py:516
  124.9 5.5 %collective-permute-done.17.refs_8_ = bf16[768,768]{1,0:T(8,128)(2,1)S(1)} collective-permute-done((bf16[768,768]{1,0:T(8,128)(2,1)}, bf16[768,768]{1,0:T(8,128)(2,1)S(1)}, u32[]{:S(2)}, u32[]{:S(2)}) %collective-permute-start.17) | collective-permute-done | bytes 1179680 | tf_op jit(solution)/shard_map/ppermute | solution.py:907
  130.4 2.1 collective-permute-start.16
  132.5 1.4 collective-permute-start.22
  134.0 6.4 %collective-permute-done.16.refs_1_ = bf16[192,768]{1,0:T(8,128)(2,1)S(1)} collective-permute-done((bf16[192,768]{1,0:T(8,128)(2,1)}, bf16[192,768]{1,0:T(8,128)(2,1)S(1)}, u32[]{:S(2)}, u32[]{:S(2)}) %collective-permute-start.16) | collective-permute-done | bytes 294944 | tf_op jit(solution)/shard_map/ppermute | solution.py:907
  140.4 2.5 collective-permute-start.27
  142.9 1.6 collective-permute-start.28
  144.5 17.0 %shard_map.200 = (bf16[1536,3072]{1,0:T(8,128)(2,1)}, bf16[1536,3072]{1,0:T(8,128)(2,1)}, bf16[1536,768]{1,0:T(8,128)(2,1)}, bf16[1536,768]{1,0:T(8,128)(2,1)}, ...) custom-call(s32[7]{0:T(128)} %copy-done.18, ...), custom_call_target="tpu_custom_call" | custom-call | flops 1000000 | bytes 100000 | tf_op jit(solution)/shard_map/pallas_call | solution.py:689
  161.5 3.3 collective-permute-start.20
  165.4 17.1 %shard_map.201 = (bf16[1536,3072]{1,0:T(8,128)(2,1)}, bf16[1536,3072]{1,0:T(8,128)(2,1)}, bf16[1536,768]{1,0:T(8,128)(2,1)}, bf16[1536,768]{1,0:T(8,128)(2,1)}, ...) custom-call(s32[7]{0:T(128)} %copy-done.18, ...), custom_call_target="tpu_custom_call", output_to_operand_aliasing={{0}: (14, {}), {1}: (15, {}), {2}: (16, {}), {3}: (17, {}),... | custom-call | flops 1000000 | bytes 100000 | tf_op jit(solution)/shard_map/pallas_call | solution.py:689
  182.6 2.9 collective-permute-start.25
  186.5 16.9 %shard_map.202 = (bf16[1536,3072]{1,0:T(8,128)(2,1)}, bf16[1536,3072]{1,0:T(8,128)(2,1)}, bf16[1536,768]{1,0:T(8,128)(2,1)}, bf16[1536,768]{1,0:T(8,128)(2,1)}, ...) custom-call(s32[7]{0:T(128)} %copy-done.18, ...), custom_call_target="tpu_custom_call", output_to_operand_aliasing={{0}: (14, {}), {1}: (15, {}), {2}: (16, {}), {3}: (17, {}),... | custom-call | flops 1000000 | bytes 100000 | tf_op jit(solution)/shard_map/pallas_call | solution.py:689
  206.1 17.2 %shard_map.203 = (bf16[1536,3072]{1,0:T(8,128)(2,1)}, bf16[1536,3072]{1,0:T(8,128)(2,1)}, bf16[1536,768]{1,0:T(8,128)(2,1)}, bf16[1536,768]{1,0:T(8,128)(2,1)}, ...) custom-call(s32[7]{0:T(128)} %copy-done.18, ...), custom_call_target="tpu_custom_call", output_to_operand_aliasing={{0}: (14, {}), {1}: (15, {}), {2}: (16, {}), {3}: (17, {}),... | custom-call | flops 1000000 | bytes 100000 | tf_op jit(solution)/shard_map/pallas_call | solution.py:689
  223.3 2.8 collective-permute-start.31
  226.2 3.0 fusion.10
  229.2 8.8 %collective-permute-done.29 = bf16[384,768]{1,0:T(8,128)(2,1)S(1)} collective-permute-done((bf16[384,768]{1,0:T(8,128)(2,1)S(1)}, bf16[384,768]{1,0:T(8,128)(2,1)S(1)}, u32[]{:S(2)}, u32[]{:S(2)}) %collective-permute-start.29) | collective-permute-done | bytes 589856 | tf_op jit(solution)/shard_map/ppermute | solution.py:907
  238.1 1.6 collective-permute-start.30
  239.7 1.5 fusion.14
  241.2 1.5 collective-permute-start.32
  242.8 10.4 %collective-permute-done.30 = bf16[192,768]{1,0:T(8,128)(2,1)S(1)} collective-permute-done((bf16[192,768]{1,0:T(8,128)(2,1)S(1)}, bf16[192,768]{1,0:T(8,128)(2,1)S(1)}, u32[]{:S(2)}, u32[]{:S(2)}) %collective-permute-start.30) | collective-permute-done | bytes 294944 | tf_op jit(solution)/shard_map/ppermute | solution.py:907
  253.3 1.5 add_convert_fusion.2
  254.9 1.5 fusion.12
  256.4 1.9 collective-permute-done.33
  258.9 1.6 collective-permute-start.34
  260.6 24.7 %shard_map.204 = (bf16[768,768]{1,0:T(8,128)(2,1)}, bf16[768,768]{1,0:T(8,128)(2,1)}, bf16[768,768]{1,0:T(8,128)(2,1)}, bf16[768,768]{1,0:T(8,128)(2,1)}, f32[2,2,768,768]{3,2,1,0:T(8,128)}, /*index=5*/f32[768,8]{1,0:T(8,128)}) custom-call(bf16[1536,3072]{1,0:T(8,128)(2,1)} %get-tuple-element.172.a_ref, bf16[1536,3072]{1,0:T(8,128)(2,1)} %get-tuple-element.173.du_ref, ...), custom_call_target="tpu_custom_call" | custom-call | flops 1000000 | bytes 100000 | tf_op jit(solution)/shard_map/pallas_call | solution.py:745
  285.8 6.3 %all-to-all-start.2 = ((bf16[8,192,768]{2,1,0:T(8,128)(2,1)}), bf16[8,192,768]{2,1,0:T(8,128)(2,1)}, u32[]{:S(2)}, u32[]{:S(2)}) async-start(bf16[8,192,768]{2,1,0:T(8,128)(2,1)} %bitcast.26), calls=%async_computation.2 | async-start | bytes 4718592 | tf_op jit(solution)/shard_map/all_to_all | solution.py:1063
  292.2 4.3 %shard_map.207 = bf16[2,768,768]{2,1,0:T(8,128)(2,1)} custom-call(f32[2,2,768,768]{3,2,1,0:T(8,128)} %get-tuple-element.184.keep_ref, bf16[768,768]{1,0:T(8,128)(2,1)} %collective-permute-done.40.give_0_ref, bf16[768,768]{1,0:T(8,128)(2,1)} %collective-permute-done.41.give_1_ref), custom_call_target="tpu_custom_call" | custom-call | flops 1000000 | bytes 100000 | tf_op jit(solution)/shard_map/pallas_call | solution.py:775
  298.2 3.4 collective-permute-done.35.dh_near_ref
  302.8 50.6 %shard_map.205 = (f32[512,768]{1,0:T(8,128)}, f32[1,768]{1,0:T(1,128)}, bf16[512,768]{1,0:T(8,128)(2,1)}, bf16[512,768]{1,0:T(8,128)(2,1)}, f32[512,768]{1,0:T(8...) custom-call(s32[7]{0:T(128)} %copy-done.18, ...), custom_call_target="tpu_custom_call" | custom-call | flops 1000000 | bytes 100000 | tf_op jit(solution)/shard_map/pallas_call | solution.py:368
  354.3 3.5 collective-permute-start.49
  359.8 10.5 %shard_map.206 = (bf16[512,768]{1,0:T(8,128)(2,1)}, bf16[512,768]{1,0:T(8,128)(2,1)}, f32[512,768]{1,0:T(8,128)}, f32[512,768]{1,0:T(8,128)}) custom-call(bf16[1536,2048]{1,0:T(8,128)(2,1)} %copy-done.2, bf16[1536,768]{1,0:T(8,128)(2,1)} %bitcast.27.rows_ref), custom_call_target="tpu_custom_call" | custom-call | flops 1000000 | bytes 100000 | tf_op jit(solution)/shard_map/pallas_call | solution.py:867
  370.8 1.5 collective-permute-start.46
  372.4 1.9 add_convert_fusion.3
  375.2 3.8 shard_map.209
  379.0 1.9 collective-permute-start.50
  380.8 1.5 collective-permute-start.44
  382.4 2.6 collective-permute-start.54
  384.9 8.6 %collective-permute-done.50.other_0_ref = bf16[384,768]{1,0:T(8,128)(2,1)S(1)} collective-permute-done((bf16[384,768]{1,0:T(8,128)(2,1)S(1)}, bf16[384,768]{1,0:T(8,128)(2,1)S(1)}, u32[]{:S(2)}, u32[]{:S(2)}) %collective-permute-start.50) | collective-permute-done | bytes 589856 | tf_op jit(solution)/shard_map/ppermute | solution.py:907
  393.5 1.7 collective-permute-start.56
  395.3 3.2 collective-permute-start.51
  398.7 1.9 collective-permute-done.51
  401.4 2.2 collective-permute-start.52
  403.5 2.9 collective-permute-done.52
  407.6 1.7 shard_map.210
  410.6 2.2 collective-permute-start.55
  415.1 4.1 shard_map.208
  421.7 3.1 add_convert_fusion.4
  (256 shorter events, 39.7 us)
Async XLA Ops:
  0.6 20.8 %collective-permute-start = (bf16[512,768]{1,0:T(8,128)(2,1)}, bf16[512,768]{1,0:T(8,128)(2,1)S(1)}, u32[]{:S(2)}, u32[]{:S(2)}) collective-permute-start(bf16[512,768]{1,0:T(8,128)(2,1)} %c_0_ref.3), channel_id=1, source_target_pairs={{0,2},{1,3},{2,0},{3,1},{4,6},{5,7},{6,4},{7,5},{8,10},{9,11},{10,... | collective-permute-start | bytes 2359304 | tf_op jit(solution)/shard_map/ppermute | solution.py:907
  3.6 21.2 %collective-permute-start.2 = (bf16[512,768]{1,0:T(8,128)(2,1)}, bf16[512,768]{1,0:T(8,128)(2,1)}, u32[]{:S(2)}, u32[]{:S(2)}) collective-permute-start(bf16[512,768]{1,0:T(8,128)(2,1)} %c_0_ref.3), channel_id=1, source_target_pairs={{0,1},{1,0},{2,3},{3,2},{4,5},{5,4},{6,7},{7,6},{8,9},{9,8},{10,11... | collective-permute-start | bytes 2359304 | tf_op jit(solution)/shard_map/ppermute | solution.py:907
  7.0 35.2 %all-to-all-start = ((bf16[8,96,768]{2,1,0:T(8,128)(2,1)}), bf16[8,96,768]{2,1,0:T(8,128)(2,1)}, u32[]{:S(2)}, u32[]{:S(2)}) async-start(bf16[8,96,768]{2,1,0:T(8,128)(2,1)} %broadcast_in_dim.59), calls=%async_computation | async-start | bytes 2359296 | tf_op jit(solution)/shard_map/all_to_all | solution.py:959
  13.1 39.9 %copy-start.16 = (s32[2048]{0:T(1024)}, s32[2048]{0:T(1024)S(1)}, u32[]{:S(2)}) copy-start(s32[2048]{0:T(1024)S(1)} %select_reduce_fusion) | copy-start | bytes 24580
  22.9 2.3 collective-permute-start.3
  23.1 24.0 %collective-permute-start.1 = (bf16[512,768]{1,0:T(8,128)(2,1)S(1)}, bf16[512,768]{1,0:T(8,128)(2,1)S(1)}, u32[]{:S(2)}, u32[]{:S(2)}) collective-permute-start(bf16[512,768]{1,0:T(8,128)(2,1)S(1)} %copy-done.1), channel_id=1, source_target_pairs={{0,2},{1,3},{2,0},{3,1},{4,6},{5,7},{6,4},{7,5},{8,10},{9,11},{10,... | collective-permute-start | bytes 2359304 | tf_op jit(solution)/shard_map/ppermute | solution.py:907
  42.2 102.3 %all-to-all-start.1 = ((bf16[8,208,768]{2,1,0:T(8,128)(2,1)}), bf16[8,208,768]{2,1,0:T(8,128)(2,1)}, u32[]{:S(2)}, u32[]{:S(2)}) async-start(bf16[8,208,768]{2,1,0:T(8,128)(2,1)} %copy-done.5), calls=%async_computation.1 | async-start | bytes 5111808 | tf_op jit(solution)/shard_map/all_to_all | solution.py:1016
  47.1 35.2 %collective-permute-start.8 = (bf16[768,768]{1,0:T(8,128)(2,1)S(1)}, bf16[768,768]{1,0:T(8,128)(2,1)S(1)}, u32[]{:S(2)}, u32[]{:S(2)}) collective-permute-start(bf16[768,768]{1,0:T(8,128)(2,1)S(1)} %get-tuple-element.125.refs_5_), channel_id=1, source_target_pairs={{0,1},{1,0},{2,3},{3,2},{4,5},{5,4},{6,7},{7,6},{8,9},{9,8},{10,11... | collective-permute-start | bytes 3538952 | tf_op jit(solution)/shard_map/ppermute | solution.py:907
  47.1 36.8 %collective-permute-start.4 = (bf16[768,768]{1,0:T(8,128)(2,1)S(1)}, bf16[768,768]{1,0:T(8,128)(2,1)S(1)}, u32[]{:S(2)}, u32[]{:S(2)}) collective-permute-start(bf16[768,768]{1,0:T(8,128)(2,1)S(1)} %get-tuple-element.125.refs_5_), channel_id=1, source_target_pairs={{0,2},{1,3},{2,0},{3,1},{4,6},{5,7},{6,4},{7,5},{8,10},{9,11},{10,... | collective-permute-start | bytes 3538952 | tf_op jit(solution)/shard_map/ppermute | solution.py:907
  48.7 3.7 collective-permute-start.6
  48.9 4.2 collective-permute-start.7
  49.2 53.3 %collective-permute-start.12 = (bf16[768,768]{1,0:T(8,128)(2,1)}, bf16[768,768]{1,0:T(8,128)(2,1)}, u32[]{:S(2)}, u32[]{:S(2)}) collective-permute-start(bf16[768,768]{1,0:T(8,128)(2,1)} %copy-done.20), channel_id=1, source_target_pairs={{0,4},{4,0},{8,12},{12,8},{16,20},{20,16},{24,28},{28,24},{1,5},{5... | collective-permute-start | bytes 3538952 | tf_op jit(solution)/shard_map/ppermute | solution.py:907
  52.4 55.9 %copy-start.29 = (bf16[768,192]{1,0:T(8,128)(2,1)}, bf16[768,192]{1,0:T(8,128)(2,1)S(1)}, u32[]{:S(2)}) copy-start(bf16[768,192]{1,0:T(8,128)(2,1)S(1)} %slice.113.refs_4_) | copy-start | bytes 884740
  52.4 31.6 %collective-permute-start.9 = (bf16[768,192]{1,0:T(8,128)(2,1)S(1)}, bf16[768,192]{1,0:T(8,128)(2,1)S(1)}, u32[]{:S(2)}, u32[]{:S(2)}) collective-permute-start(bf16[768,192]{1,0:T(8,128)(2,1)S(1)} %slice.113.refs_4_), channel_id=1, source_target_pairs={{0,2},{1,3},{2,0},{3,1},{4,6},{5,7},{6,4},{7,5},{8,10},{9,11},{10,... | collective-permute-start | bytes 884744 | tf_op jit(solution)/shard_map/ppermute | solution.py:907
  53.0 52.3 %copy-start.51 = (f32[768]{0:T(1024)S(1)}, f32[768]{0:T(1024)}, u32[]{:S(2)}) copy-start(f32[768]{0:T(1024)} %param.15) | copy-start | bytes 9220
  84.0 19.3 %collective-permute-start.10 = (bf16[192,2048]{1,0:T(8,128)(2,1)S(1)}, bf16[192,2048]{1,0:T(8,128)(2,1)S(1)}, u32[]{:S(2)}, u32[]{:S(2)}) collective-permute-start(bf16[192,2048]{1,0:T(8,128)(2,1)S(1)} %get-tuple-element.128.refs_0_.ctx_ref), channel_id=1, source_target_pairs={{0,2},{1,3},{2,0},{3,1},{4,6},{5,7},{6,4},{7,5},{8,10},{9,11},{10,... | collective-permute-start | bytes 2359304 | tf_op jit(solution)/shard_map/ppermute | solution.py:907
  85.5 20.4 %collective-permute-start.5 = (bf16[768,768]{1,0:T(8,128)(2,1)S(1)}, bf16[768,768]{1,0:T(8,128)(2,1)S(1)}, u32[]{:S(2)}, u32[]{:S(2)}) collective-permute-start(bf16[768,768]{1,0:T(8,128)(2,1)S(1)} %collective-permute-done.4.refs_7_), channel_id=1, source_target_pairs={{0,1},{1,0},{2,3},{3,2},{4,5},{5,4},{6,7},{7,6},{8,9},{9,8},{10,11... | collective-permute-start | bytes 3538952 | tf_op jit(solution)/shard_map/ppermute | solution.py:907
  85.5 19.2 %collective-permute-start.13 = (bf16[768,192]{1,0:T(8,128)(2,1)S(1)}, bf16[768,192]{1,0:T(8,128)(2,1)S(1)}, u32[]{:S(2)}, u32[]{:S(2)}) collective-permute-start(bf16[768,192]{1,0:T(8,128)(2,1)S(1)} %slice.113.refs_4_), channel_id=1, source_target_pairs={{0,1},{1,0},{2,3},{3,2},{4,5},{5,4},{6,7},{7,6},{8,9},{9,8},{10,11... | collective-permute-start | bytes 884744 | tf_op jit(solution)/shard_map/ppermute | solution.py:907
  86.1 18.7 %collective-permute-start.14 = (bf16[768,192]{1,0:T(8,128)(2,1)S(1)}, bf16[768,192]{1,0:T(8,128)(2,1)S(1)}, u32[]{:S(2)}, u32[]{:S(2)}) collective-permute-start(bf16[768,192]{1,0:T(8,128)(2,1)S(1)} %collective-permute-done.9.refs_5_), channel_id=1, source_target_pairs={{0,1},{1,0},{2,3},{3,2},{4,5},{5,4},{6,7},{7,6},{8,9},{9,8},{10,11... | collective-permute-start | bytes 884744 | tf_op jit(solution)/shard_map/ppermute | solution.py:907
  103.3 27.1 %collective-permute-start.17 = (bf16[768,768]{1,0:T(8,128)(2,1)}, bf16[768,768]{1,0:T(8,128)(2,1)S(1)}, u32[]{:S(2)}, u32[]{:S(2)}) collective-permute-start(bf16[768,768]{1,0:T(8,128)(2,1)} %collective-permute-done.12.refs_6_), channel_id=1, source_target_pairs={{0,2},{1,3},{2,0},{3,1},{4,6},{5,7},{6,4},{7,5},{8,10},{9,11},{10,... | collective-permute-start | bytes 3538952 | tf_op jit(solution)/shard_map/ppermute | solution.py:907
  104.8 2.4 collective-permute-start.11
  104.8 3.5 collective-permute-start.15
  124.7 18.2 %collective-permute-start.18 = (bf16[768,768]{1,0:T(8,128)(2,1)}, bf16[768,768]{1,0:T(8,128)(2,1)S(1)}, u32[]{:S(2)}, u32[]{:S(2)}) collective-permute-start(bf16[768,768]{1,0:T(8,128)(2,1)} %collective-permute-done.12.refs_6_), channel_id=1, source_target_pairs={{0,1},{1,0},{2,3},{3,2},{4,5},{5,4},{6,7},{7,6},{8,9},{9,8},{10,11... | collective-permute-start | bytes 3538952 | tf_op jit(solution)/shard_map/ppermute | solution.py:907
  130.4 14.1 %collective-permute-start.19 = (bf16[768,768]{1,0:T(8,128)(2,1)S(1)}, bf16[768,768]{1,0:T(8,128)(2,1)}, u32[]{:S(2)}, u32[]{:S(2)}) collective-permute-start(bf16[768,768]{1,0:T(8,128)(2,1)S(1)} %collective-permute-done.17.refs_8_), channel_id=1, source_target_pairs={{0,1},{1,0},{2,3},{3,2},{4,5},{5,4},{6,7},{7,6},{8,9},{9,8},{10,11... | collective-permute-start | bytes 3538952 | tf_op jit(solution)/shard_map/ppermute | solution.py:907
  130.4 9.9 %collective-permute-start.16 = (bf16[192,768]{1,0:T(8,128)(2,1)}, bf16[192,768]{1,0:T(8,128)(2,1)S(1)}, u32[]{:S(2)}, u32[]{:S(2)}) collective-permute-start(bf16[192,768]{1,0:T(8,128)(2,1)} %get-tuple-element.135), channel_id=1, source_target_pairs={{0,4},{4,0},{8,12},{12,8},{16,20},{20,16},{24,28},{28,24},{1,5},{5... | collective-permute-start | bytes 884744 | tf_op jit(solution)/shard_map/ppermute | solution.py:907
  132.5 32.4 %collective-permute-start.22 = (bf16[192,768]{1,0:T(8,128)(2,1)}, bf16[192,768]{1,0:T(8,128)(2,1)}, u32[]{:S(2)}, u32[]{:S(2)}) collective-permute-start(bf16[192,768]{1,0:T(8,128)(2,1)} %get-tuple-element.142), channel_id=1, source_target_pairs={{0,8},{4,12},{8,0},{12,4},{16,24},{20,28},{24,16},{28,20},{1,9},{5... | collective-permute-start | bytes 884744 | tf_op jit(solution)/shard_map/ppermute | solution.py:907
  133.8 31.6 %collective-permute-start.23 = (bf16[192,768]{1,0:T(8,128)(2,1)}, bf16[192,768]{1,0:T(8,128)(2,1)}, u32[]{:S(2)}, u32[]{:S(2)}) collective-permute-start(bf16[192,768]{1,0:T(8,128)(2,1)} %get-tuple-element.143), channel_id=1, source_target_pairs={{0,12},{4,8},{8,4},{12,0},{16,28},{20,24},{24,20},{28,16},{1,13},{... | collective-permute-start | bytes 884744 | tf_op jit(solution)/shard_map/ppermute | solution.py:907
  140.4 42.3 %collective-permute-start.27 = (bf16[192,768]{1,0:T(8,128)(2,1)}, bf16[192,768]{1,0:T(8,128)(2,1)S(1)}, u32[]{:S(2)}, u32[]{:S(2)}) collective-permute-start(bf16[192,768]{1,0:T(8,128)(2,1)} %get-tuple-element.156), channel_id=1, source_target_pairs={{0,16},{4,20},{8,24},{12,28},{16,0},{20,4},{24,8},{28,12},{1,17},{... | collective-permute-start | bytes 884744 | tf_op jit(solution)/shard_map/ppermute | solution.py:907
  142.9 42.6 %collective-permute-start.28 = (bf16[192,768]{1,0:T(8,128)(2,1)}, bf16[192,768]{1,0:T(8,128)(2,1)S(1)}, u32[]{:S(2)}, u32[]{:S(2)}) collective-permute-start(bf16[192,768]{1,0:T(8,128)(2,1)} %get-tuple-element.158), channel_id=1, source_target_pairs={{0,20},{4,16},{8,28},{12,24},{16,4},{20,0},{24,12},{28,8},{1,21},{... | collective-permute-start | bytes 884744 | tf_op jit(solution)/shard_map/ppermute | solution.py:907
  161.5 43.1 %collective-permute-start.20 = (bf16[192,768]{1,0:T(8,128)(2,1)S(1)}, bf16[192,768]{1,0:T(8,128)(2,1)S(1)}, u32[]{:S(2)}, u32[]{:S(2)}) collective-permute-start(bf16[192,768]{1,0:T(8,128)(2,1)S(1)} %copy-done.54), channel_id=1, source_target_pairs={{0,24},{4,28},{8,16},{12,20},{16,8},{20,12},{24,0},{28,4},{1,25},{... | collective-permute-start | bytes 884744 | tf_op jit(solution)/shard_map/ppermute | solution.py:907
  164.8 40.5 %collective-permute-start.21 = (bf16[192,768]{1,0:T(8,128)(2,1)}, bf16[192,768]{1,0:T(8,128)(2,1)S(1)}, u32[]{:S(2)}, u32[]{:S(2)}) collective-permute-start(bf16[192,768]{1,0:T(8,128)(2,1)} %get-tuple-element.141), channel_id=1, source_target_pairs={{0,4},{4,0},{8,12},{12,8},{16,20},{20,16},{24,28},{28,24},{1,5},{5... | collective-permute-start | bytes 884744 | tf_op jit(solution)/shard_map/ppermute | solution.py:907
  182.5 22.8 %collective-permute-start.24 = (bf16[192,768]{1,0:T(8,128)(2,1)}, bf16[192,768]{1,0:T(8,128)(2,1)S(1)}, u32[]{:S(2)}, u32[]{:S(2)}) collective-permute-start(bf16[192,768]{1,0:T(8,128)(2,1)} %get-tuple-element.150), channel_id=1, source_target_pairs={{0,8},{4,12},{8,0},{12,4},{16,24},{20,28},{24,16},{28,20},{1,9},{5... | collective-permute-start | bytes 884744 | tf_op jit(solution)/shard_map/ppermute | solution.py:907
  182.6 22.7 %collective-permute-start.25 = (bf16[192,768]{1,0:T(8,128)(2,1)}, bf16[192,768]{1,0:T(8,128)(2,1)S(1)}, u32[]{:S(2)}, u32[]{:S(2)}) collective-permute-start(bf16[192,768]{1,0:T(8,128)(2,1)} %get-tuple-element.151), channel_id=1, source_target_pairs={{0,12},{4,8},{8,4},{12,0},{16,28},{20,24},{24,20},{28,16},{1,13},{... | collective-permute-start | bytes 884744 | tf_op jit(solution)/shard_map/ppermute | solution.py:907
  185.5 19.8 %collective-permute-start.26 = (bf16[192,768]{1,0:T(8,128)(2,1)S(1)}, bf16[192,768]{1,0:T(8,128)(2,1)S(1)}, u32[]{:S(2)}, u32[]{:S(2)}) collective-permute-start(bf16[192,768]{1,0:T(8,128)(2,1)S(1)} %copy-done.53), channel_id=1, source_target_pairs={{0,28},{4,24},{8,20},{12,16},{16,12},{20,8},{24,4},{28,0},{1,29},{... | collective-permute-start | bytes 884744 | tf_op jit(solution)/shard_map/ppermute | solution.py:907
  204.6 33.5 %collective-permute-start.29 = (bf16[384,768]{1,0:T(8,128)(2,1)S(1)}, bf16[384,768]{1,0:T(8,128)(2,1)S(1)}, u32[]{:S(2)}, u32[]{:S(2)}) collective-permute-start(bf16[384,768]{1,0:T(8,128)(2,1)S(1)} %pad_maximum_fusion), channel_id=1, source_target_pairs={{0,16},{4,20},{8,24},{12,28},{16,0},{20,4},{24,8},{28,12},{1,17},{... | collective-permute-start | bytes 1769480 | tf_op jit(solution)/shard_map/ppermute | solution.py:907
  223.3 30.0 %collective-permute-start.31 = (bf16[192,768]{1,0:T(8,128)(2,1)}, bf16[192,768]{1,0:T(8,128)(2,1)S(1)}, u32[]{:S(2)}, u32[]{:S(2)}) collective-permute-start(bf16[192,768]{1,0:T(8,128)(2,1)} %get-tuple-element.179), channel_id=1, source_target_pairs={{0,24},{4,28},{8,16},{12,20},{16,8},{20,12},{24,0},{28,4},{1,25},{... | collective-permute-start | bytes 884744 | tf_op jit(solution)/shard_map/ppermute | solution.py:907
  238.1 15.1 %collective-permute-start.30 = (bf16[192,768]{1,0:T(8,128)(2,1)S(1)}, bf16[192,768]{1,0:T(8,128)(2,1)S(1)}, u32[]{:S(2)}, u32[]{:S(2)}) collective-permute-start(bf16[192,768]{1,0:T(8,128)(2,1)S(1)} %get-tuple-element.271), channel_id=1, source_target_pairs={{0,4},{4,0},{8,12},{12,8},{16,20},{20,16},{24,28},{28,24},{1,5},{5... | collective-permute-start | bytes 884744 | tf_op jit(solution)/shard_map/ppermute | solution.py:907
  241.2 12.1 %collective-permute-start.32 = (bf16[192,768]{1,0:T(8,128)(2,1)S(1)}, bf16[192,768]{1,0:T(8,128)(2,1)S(1)}, u32[]{:S(2)}, u32[]{:S(2)}) collective-permute-start(bf16[192,768]{1,0:T(8,128)(2,1)S(1)} %copy-done.55), channel_id=1, source_target_pairs={{0,28},{4,24},{8,20},{12,16},{16,12},{20,8},{24,4},{28,0},{1,29},{... | collective-permute-start | bytes 884744 | tf_op jit(solution)/shard_map/ppermute | solution.py:907
  254.9 3.5 collective-permute-start.33
  258.9 37.6 %collective-permute-start.34 = (bf16[1024,768]{1,0:T(8,128)(2,1)S(1)}, bf16[1024,768]{1,0:T(8,128)(2,1)S(1)}, u32[]{:S(2)}, u32[]{:S(2)}) collective-permute-start(bf16[1024,768]{1,0:T(8,128)(2,1)S(1)} %add_convert_fusion.1), channel_id=1, source_target_pairs={{0,2},{1,3},{2,0},{3,1},{4,6},{5,7},{6,4},{7,5},{8,10},{9,11},{10,... | collective-permute-start | bytes 4718600 | tf_op jit(solution)/shard_map/ppermute | solution.py:907
  285.3 6.8 %collective-permute-start.40 = (bf16[768,768]{1,0:T(8,128)(2,1)}, bf16[768,768]{1,0:T(8,128)(2,1)}, u32[]{:S(2)}, u32[]{:S(2)}) collective-permute-start(bf16[768,768]{1,0:T(8,128)(2,1)} %get-tuple-element.204), channel_id=1, source_target_pairs={{0,1},{1,0},{2,3},{3,2},{4,5},{5,4},{6,7},{7,6},{8,9},{9,8},{10,11... | collective-permute-start | bytes 3538952 | tf_op jit(solution)/shard_map/ppermute | solution.py:907
  285.3 6.8 %collective-permute-start.41 = (bf16[768,768]{1,0:T(8,128)(2,1)}, bf16[768,768]{1,0:T(8,128)(2,1)}, u32[]{:S(2)}, u32[]{:S(2)}) collective-permute-start(bf16[768,768]{1,0:T(8,128)(2,1)} %get-tuple-element.205), channel_id=1, source_target_pairs={{0,1},{1,0},{2,3},{3,2},{4,5},{5,4},{6,7},{7,6},{8,9},{9,8},{10,11... | collective-permute-start | bytes 3538952 | tf_op jit(solution)/shard_map/ppermute | solution.py:907
  285.8 74.0 %all-to-all-start.2 = ((bf16[8,192,768]{2,1,0:T(8,128)(2,1)}), bf16[8,192,768]{2,1,0:T(8,128)(2,1)}, u32[]{:S(2)}, u32[]{:S(2)}) async-start(bf16[8,192,768]{2,1,0:T(8,128)(2,1)} %bitcast.26), calls=%async_computation.2 | async-start | bytes 4718592 | tf_op jit(solution)/shard_map/all_to_all | solution.py:1063
  297.1 56.4 %collective-permute-start.42 = (bf16[2,768,768]{2,1,0:T(8,128)(2,1)}, bf16[2,768,768]{2,1,0:T(8,128)(2,1)S(1)}, u32[]{:S(2)}, u32[]{:S(2)}) collective-permute-start(bf16[2,768,768]{2,1,0:T(8,128)(2,1)} %shard_map.207), channel_id=1, source_target_pairs={{4,6},{5,7},{6,4},{7,5},{12,14},{13,15},{14,12},{15,13},{20,22},{2... | collective-permute-start | bytes 7077896 | tf_op jit(solution)/shard_map/ppermute | solution.py:915
  298.2 3.4 collective-permute-start.35
  302.8 51.4 %copy-start.41 = (f32[768,8]{1,0:T(8,128)S(1)}, f32[768,8]{1,0:T(8,128)}, u32[]{:S(2)}) copy-start(f32[768,8]{1,0:T(8,128)} %get-tuple-element.212) | copy-start | bytes 73732
  353.5 4.3 %collective-permute-start.43 = (bf16[512,768]{1,0:T(8,128)(2,1)}, bf16[512,768]{1,0:T(8,128)(2,1)}, u32[]{:S(2)}, u32[]{:S(2)}) collective-permute-start(bf16[512,768]{1,0:T(8,128)(2,1)} %get-tuple-element.207), channel_id=1, source_target_pairs={{0,1},{1,0},{2,3},{3,2},{4,5},{5,4},{6,7},{7,6},{8,9},{9,8},{10,11... | collective-permute-start | bytes 2359304 | tf_op jit(solution)/shard_map/ppermute | solution.py:907
  353.7 21.5 %collective-permute-start.47 = (bf16[768,768]{1,0:T(8,128)(2,1)}, bf16[768,768]{1,0:T(8,128)(2,1)}, u32[]{:S(2)}, u32[]{:S(2)}) collective-permute-start(bf16[768,768]{1,0:T(8,128)(2,1)} %get-tuple-element.213), channel_id=1, source_target_pairs={{0,1},{1,0},{2,3},{3,2},{4,5},{5,4},{6,7},{7,6},{8,9},{9,8},{10,11... | collective-permute-start | bytes 3538952 | tf_op jit(solution)/shard_map/ppermute | solution.py:907
  354.0 21.1 %collective-permute-start.48 = (bf16[768,768]{1,0:T(8,128)(2,1)}, bf16[768,768]{1,0:T(8,128)(2,1)}, u32[]{:S(2)}, u32[]{:S(2)}) collective-permute-start(bf16[768,768]{1,0:T(8,128)(2,1)} %get-tuple-element.214), channel_id=1, source_target_pairs={{0,1},{1,0},{2,3},{3,2},{4,5},{5,4},{6,7},{7,6},{8,9},{9,8},{10,11... | collective-permute-start | bytes 3538952 | tf_op jit(solution)/shard_map/ppermute | solution.py:907
  354.3 20.7 %collective-permute-start.49 = (bf16[4,96,768]{2,1,0:T(8,128)(2,1)}, bf16[4,96,768]{2,1,0:T(8,128)(2,1)S(1)}, u32[]{:S(2)}, u32[]{:S(2)}) collective-permute-start(bf16[4,96,768]{2,1,0:T(8,128)(2,1)} %get-tuple-element.194), channel_id=1, source_target_pairs={{0,4},{4,0},{8,12},{12,8},{16,20},{20,16},{24,28},{28,24},{1,5},{5... | collective-permute-start | bytes 1769480 | tf_op jit(solution)/shard_map/ppermute | solution.py:907
  359.7 11.1 %collective-permute-start.45 = (f32[10,768]{1,0:T(8,128)S(1)}, f32[10,768]{1,0:T(8,128)S(1)}, u32[]{:S(2)}, u32[]{:S(2)}) collective-permute-start(f32[10,768]{1,0:T(8,128)S(1)} %pad_maximum_fusion.3), channel_id=1, source_target_pairs={{0,1},{1,0},{2,3},{3,2},{4,5},{5,4},{6,7},{7,6},{8,9},{9,8},{10,11... | collective-permute-start | bytes 92168 | tf_op jit(solution)/shard_map/ppermute | solution.py:907
  370.4 24.9 %collective-permute-start.37 = (bf16[512,768]{1,0:T(8,128)(2,1)}, bf16[512,768]{1,0:T(8,128)(2,1)S(1)}, u32[]{:S(2)}, u32[]{:S(2)}) collective-permute-start(bf16[512,768]{1,0:T(8,128)(2,1)} %get-tuple-element.199), channel_id=1, source_target_pairs={{0,1},{1,0},{2,3},{3,2},{4,5},{5,4},{6,7},{7,6},{8,9},{9,8},{10,11... | collective-permute-start | bytes 2359304 | tf_op jit(solution)/shard_map/ppermute | solution.py:907
  370.8 4.2 collective-permute-start.46
  379.0 14.5 %collective-permute-start.50 = (bf16[384,768]{1,0:T(8,128)(2,1)S(1)}, bf16[384,768]{1,0:T(8,128)(2,1)S(1)}, u32[]{:S(2)}, u32[]{:S(2)}) collective-permute-start(bf16[384,768]{1,0:T(8,128)(2,1)S(1)} %get-tuple-element.218), channel_id=1, source_target_pairs={{0,4},{4,0},{8,12},{12,8},{16,20},{20,16},{24,28},{28,24},{1,5},{5... | collective-permute-start | bytes 1769480 | tf_op jit(solution)/shard_map/ppermute | solution.py:907
  380.8 33.1 %collective-permute-start.39 = (bf16[512,768]{1,0:T(8,128)(2,1)S(1)}, bf16[512,768]{1,0:T(8,128)(2,1)S(1)}, u32[]{:S(2)}, u32[]{:S(2)}) collective-permute-start(bf16[512,768]{1,0:T(8,128)(2,1)S(1)} %copy-done.52), channel_id=1, source_target_pairs={{0,1},{1,0},{2,3},{3,2},{4,5},{5,4},{6,7},{7,6},{8,9},{9,8},{10,11... | collective-permute-start | bytes 2359304 | tf_op jit(solution)/shard_map/ppermute | solution.py:907
  380.8 33.1 %collective-permute-start.44 = (bf16[512,768]{1,0:T(8,128)(2,1)S(1)}, bf16[512,768]{1,0:T(8,128)(2,1)S(1)}, u32[]{:S(2)}, u32[]{:S(2)}) collective-permute-start(bf16[512,768]{1,0:T(8,128)(2,1)S(1)} %add_convert_fusion.3), channel_id=1, source_target_pairs={{0,2},{1,3},{2,0},{3,1},{4,6},{5,7},{6,4},{7,5},{8,10},{9,11},{10,... | collective-permute-start | bytes 2359304 | tf_op jit(solution)/shard_map/ppermute | solution.py:907
  382.4 19.0 %collective-permute-start.54 = (bf16[2,96,768]{2,1,0:T(8,128)(2,1)S(1)}, bf16[2,96,768]{2,1,0:T(8,128)(2,1)S(1)}, u32[]{:S(2)}, u32[]{:S(2)}) collective-permute-start(bf16[2,96,768]{2,1,0:T(8,128)(2,1)S(1)} %slice.155), channel_id=1, source_target_pairs={{0,8},{4,12},{8,0},{12,4},{16,24},{20,28},{24,16},{28,20},{1,9},{5... | collective-permute-start | bytes 884744 | tf_op jit(solution)/shard_map/ppermute | solution.py:907
  393.5 14.1 %collective-permute-start.56 = (bf16[384,768]{1,0:T(8,128)(2,1)S(1)}, bf16[384,768]{1,0:T(8,128)(2,1)S(1)}, u32[]{:S(2)}, u32[]{:S(2)}) collective-permute-start(bf16[384,768]{1,0:T(8,128)(2,1)S(1)} %get-tuple-element.221), channel_id=1, source_target_pairs={{0,4},{4,0},{8,12},{12,8},{16,20},{20,16},{24,28},{28,24},{1,5},{5... | collective-permute-start | bytes 1769480 | tf_op jit(solution)/shard_map/ppermute | solution.py:907
  395.3 5.3 %collective-permute-start.51 = (f32[10,768]{1,0:T(8,128)S(1)}, f32[10,768]{1,0:T(8,128)S(1)}, u32[]{:S(2)}, u32[]{:S(2)}) collective-permute-start(f32[10,768]{1,0:T(8,128)S(1)} %add.129), channel_id=1, source_target_pairs={{0,8},{4,12},{8,0},{12,4},{16,24},{20,28},{24,16},{28,20},{1,9},{5... | collective-permute-start | bytes 92168 | tf_op jit(solution)/shard_map/ppermute | solution.py:907
  400.6 19.5 %collective-permute-start.38 = (bf16[512,768]{1,0:T(8,128)(2,1)S(1)}, bf16[512,768]{1,0:T(8,128)(2,1)}, u32[]{:S(2)}, u32[]{:S(2)}) collective-permute-start(bf16[512,768]{1,0:T(8,128)(2,1)S(1)} %add_convert_fusion.5), channel_id=1, source_target_pairs={{0,2},{1,3},{2,0},{3,1},{4,6},{5,7},{6,4},{7,5},{8,10},{9,11},{10,... | collective-permute-start | bytes 2359304 | tf_op jit(solution)/shard_map/ppermute | solution.py:907
  401.4 5.1 %collective-permute-start.52 = (f32[10,768]{1,0:T(8,128)S(1)}, f32[10,768]{1,0:T(8,128)S(1)}, u32[]{:S(2)}, u32[]{:S(2)}) collective-permute-start(f32[10,768]{1,0:T(8,128)S(1)} %add.131), channel_id=1, source_target_pairs={{0,16},{4,20},{8,24},{12,28},{16,0},{20,4},{24,8},{28,12},{1,17},{... | collective-permute-start | bytes 92168 | tf_op jit(solution)/shard_map/ppermute | solution.py:907
  406.4 4.1 collective-permute-start.53
  407.6 14.1 %collective-permute-start.36 = (bf16[512,768]{1,0:T(8,128)(2,1)}, bf16[512,768]{1,0:T(8,128)(2,1)}, u32[]{:S(2)}, u32[]{:S(2)}) collective-permute-start(bf16[512,768]{1,0:T(8,128)(2,1)} %get-tuple-element.197), channel_id=1, source_target_pairs={{0,1},{1,0},{2,3},{3,2},{4,5},{5,4},{6,7},{7,6},{8,9},{9,8},{10,11... | collective-permute-start | bytes 2359304 | tf_op jit(solution)/shard_map/ppermute | solution.py:907
  410.6 9.5 %collective-permute-start.55 = (bf16[1,96,768]{2,1,0:T(8,128)(2,1)S(1)}, bf16[1,96,768]{2,1,0:T(8,128)(2,1)S(1)}, u32[]{:S(2)}, u32[]{:S(2)}) collective-permute-start(bf16[1,96,768]{2,1,0:T(8,128)(2,1)S(1)} %slice.156), channel_id=1, source_target_pairs={{0,16},{4,20},{8,24},{12,28},{16,0},{20,4},{24,8},{28,12},{1,17},{... | collective-permute-start | bytes 442376 | tf_op jit(solution)/shard_map/ppermute | solution.py:907
  (55 other events, 486.9 us)
